TPU v7x, 32 devices: a whole 2x2x4 slice. The times are simulated.
32 devices in a mesh: parts: 2 (over x), store: 8 (over z, y), tensor: 2 (over core).
Axes of the slice: x: 2, y: 2, z: 4, core: 2. Of those that a mesh axis runs over, the one named last changes fastest.
Arguments:
- hidden: bfloat16 [512, 28672], P(('parts', 'store'), 'tensor'), parts along dimension 0, may hold values from -6 to 6
- down_weight: bfloat16 [28672, 8192], P('tensor', 'store'), may hold values from -0.03125 to 0.03125
- shrink_weight: bfloat16 [32, 28672, 64], P(('parts', 'store'), 'tensor'), parts along dimension 0, may hold values from -0.03125 to 0.03125
- expand_weight: bfloat16 [32, 64, 8192], P(('parts', 'store')), parts along dimension 0, may hold values from -0.75 to 0.75
- row_adapter: int32 [512], P('parts'), parts along dimension 0, may hold values from 0 to 15
- adapter_slot: int32 [32], P('parts'), parts along dimension 0, may hold values from 0 to 15, each once
Outputs:
- mixed: bfloat16 [512, 8192], P('parts', ('store', 'tensor')), parts along dimension 0
There are 2 independent parts, one for each index of `parts`. A program takes and returns all parts, laid end to end along the dimension named above; an argument that names none is the same for every part. Nothing has to cross between parts.
Inputs may be any that keep to these rules, and one draw needn't show every extreme that they name: `row_adapter`: every row names one of the 16 adapter ids. `adapter_slot`: each storage slot holds exactly one adapter id.
All inputs are finite; a program needn't handle non-finite values.
Results may differ from a plain program's by a relative error of at most 0.004.
Values may be sent and summed in bfloat16 or wider, within the bound.
No kernel may reach another device: no remote copies, remote signals or barrier semaphores. Data moves between devices by JAX's collectives and lax.ppermute only.
A program may use at most 128 MiB of HBM per device.

v0:
```python
import jax
import jax.numpy as jnp
from jax import lax
from jax.sharding import PartitionSpec as P


def shards(hidden, down_weight, shrink_weight, expand_weight, row_adapter, adapter_slot):
    owned = shrink_weight.shape[0]
    half_units = shrink_weight.shape[1]
    rank_width = shrink_weight.shape[2]
    columns = down_weight.shape[1]
    owner = lax.axis_index("store")
    row_slot = adapter_slot[row_adapter]
    local_slots = owner * owned + jnp.arange(owned, dtype=jnp.int32)
    stacked = jnp.transpose(shrink_weight, (1, 0, 2)).reshape(half_units, owned * rank_width)
    piece = lax.all_gather(hidden, "store", axis=0, tiled=True)
    plain = jnp.dot(piece, down_weight, preferred_element_type=jnp.float32)
    narrow = jnp.dot(piece, stacked, preferred_element_type=jnp.float32)
    terms = jnp.concatenate([plain, narrow], axis=1)
    base = terms[:, :columns]
    raw_shrunk = terms[:, columns:].reshape(terms.shape[0], owned, rank_width)
    ownership = row_slot[:, None] == local_slots[None, :]
    partial_shrunk = jnp.sum(
        jnp.where(ownership[:, :, None], raw_shrunk, jnp.zeros((), jnp.float32)), axis=1
    )
    shrunk = lax.psum(partial_shrunk, ("store", "tensor")).astype(jnp.bfloat16)
    second_factors = lax.all_to_all(expand_weight, "store", split_axis=2, concat_axis=0, tiled=True)
    total_adapters = second_factors.shape[0]
    picks = row_slot[:, None] == jnp.arange(total_adapters, dtype=jnp.int32)[None, :]
    spread = jnp.where(picks[:, :, None], shrunk[:, None, :], jnp.zeros((), jnp.bfloat16))
    spread = spread.reshape(spread.shape[0], total_adapters * rank_width)
    share = columns // lax.axis_size("tensor")
    tensor_place = lax.axis_index("tensor")
    own_factors = lax.dynamic_slice_in_dim(second_factors, tensor_place * share, share, 2)
    extra = jnp.dot(
        spread,
        own_factors.reshape(total_adapters * rank_width, share),
        preferred_element_type=jnp.float32,
    )
    kept_base = lax.psum_scatter(base, "tensor", scatter_dimension=1, tiled=True)
    mixed = kept_base + extra
    return mixed.astype(jnp.bfloat16)


def solution(mesh):
    in_specs = (
        P(("parts", "store"), "tensor"),
        P("tensor", "store"),
        P(("parts", "store"), "tensor", None),
        P(("parts", "store"), None, None),
        P("parts"),
        P("parts"),
    )
    out_specs = P("parts", ("store", "tensor"))
    return jax.shard_map(shards, mesh=mesh, in_specs=in_specs, out_specs=out_specs, check_vma=False)
```

profile of v0, /device:TPU:0, one launch (start us, length us, event | category | flops | bytes accessed | tf_op | source)
XLA Modules:
  0.0 275.5 jit_solution(6426494558007238017)
XLA Ops:
  6.5 0.0 all-gather.2.cloned.1.call-start
  6.5 0.7 all-gather.2.cloned.1.call-update
  7.3 9.5 %copy.10 = bf16[2,64,8192]{1,0,2:T(2,128)(2,1)} copy(bf16[2,64,8192]{2,1,0:T(8,128)(2,1)} %param.9) | data formatting | bytes 4194304 | tf_op args[3]
  16.8 7.6 %reshape.86 = bf16[8,2,65536]{2,1,0:T(2,128)(2,1)} reshape(bf16[8192,2,64]{2,1,0:T(2,128)(2,1)} %bitcast.51) | data formatting | bytes 4194304
  24.4 7.3 %all-to-all-start = ((bf16[8,2,65536]{2,1,0:T(2,128)(2,1)}), bf16[8,2,65536]{2,1,0:T(2,128)(2,1)S(1)}, u32[]{:S(2)}, u32[]{:S(2)}) async-start(bf16[8,2,65536]{2,1,0:T(2,128)(2,1)} %reshape.86), calls=%async_computation.1 | async-start | bytes 4194304 | tf_op jit(solution)/shard_map/all_to_all | solution.py:27
  31.7 0.0 copy-start
  31.7 0.0 copy-start.1
  31.7 0.0 reduce-scatter.2.cloned.1.call-start
  31.8 128.4 %all-gather.2.cloned.1.call-done = bf16[256,14336]{1,0:T(8,128)(2,1)} async-done(((bf16[32,14336]{1,0:T(8,128)(2,1)}), bf16[256,14336]{1,0:T(8,128)(2,1)}) %all-gather.2.cloned.1.call-update) | async-done | bytes 7340048 | tf_op jit(solution)/shard_map/all_gather | solution.py:16
  160.2 16.2 %fusion.23 = f32[256,1024]{1,0:T(8,128)} fusion(bf16[256,14336]{1,0:T(8,128)(2,1)} %all-gather.2.cloned.1.call-done, bf16[14336,1024]{1,0:T(8,128)(2,1)} %param.7), kind=kOutput, calls=%fused_computation.35 | convolution fusion | flops 7516192768 | bytes 37748736 | tf_op jit(solution)/shard_map/dot_general | solution.py:17
  176.4 0.0 reduce-scatter.2.cloned.1.call-update
  176.4 0.0 copy-done
  176.4 0.7 fusion.22
  177.1 0.0 copy-done.1
  177.1 10.1 %compare_select_fusion.1 = s32[256]{0:T(256)S(1)} fusion(s32[256]{0:T(256)S(1)} %copy-done.1, s32[]{:T(128)} %bitcast, s32[]{:T(128)} %bitcast.1, s32[]{:T(128)} %bitcast.2, s32[]{:T(128)} %bitcast.3, s32[]{:T(128)} %bitcast.4, s32[]{:T(128)} %bitcast.5, s32[]{:T(128)} %bitcast.6, s32[]{:T(128)} %bitcast.7, s32[]{:T(128)} %bitcast.8, s32[]{:T(128)} %bitcast.9, ...), kind=kLoop, calls=%fused_computation.15 | loop fusion | flops 8448 | bytes 2112 | tf_op jit(solution)/shard_map/gather | solution.py:13
  187.3 0.1 broadcast_compare_fusion
  187.3 0.0 all-to-all-done
  187.3 5.1 %reshape.87 = bf16[8192,2,64]{2,1,0:T(2,128)(2,1)} reshape(bf16[8,2,65536]{2,1,0:T(2,128)(2,1)S(1)} %all-to-all-done) | data formatting | bytes 4194304
  192.4 9.1 %copy.11 = bf16[2,64,8,1024]{3,1,0,2:T(8,128)(2,1)S(1)} copy(bf16[2,64,8,1024]{1,0,3,2:T(2,128)(2,1)} %bitcast.50) | data formatting | bytes 4194304 | tf_op jit(solution)/shard_map/all_to_all | solution.py:27
  201.5 6.7 %fusion.10 = f32[256,64]{0,1:T(8,128)S(1)} fusion(bf16[2,14336,64]{1,2,0:T(8,128)(2,1)} %param.8, bf16[256,14336]{1,0:T(8,128)(2,1)} %all-gather.2.cloned.1.call-done, pred[256,2]{0,1:T(4,128)(4,1)S(1)} %broadcast_compare_fusion), kind=kOutput, calls=%fused_computation.7 | convolution fusion | flops 939573248 | bytes 11076096 | tf_op jit(solution)/shard_map/dot_general | solution.py:18
  208.2 58.2 %psum.7 = bf16[256,64]{0,1:T(8,128)(2,1)S(1)} all-reduce(f32[256,64]{0,1:T(8,128)S(1)} %fusion.10), channel_id=1, replica_groups=mesh['parts'=2,'store'=8,'tensor'=2] {'store','tensor'}, use_global_device_ids=true, to_apply=%region_2.3 | all-reduce | flops 16384 | bytes 98304 | tf_op jit(solution)/shard_map/psum | solution.py:26
  266.4 0.0 reduce-scatter.2.cloned.1.call-done
  266.4 2.2 fusion.4
  (2 shorter events, 0.0 us)
Async XLA Ops:
  6.5 153.6 %all-gather.2.cloned.1.call-start = ((), (), s32[]{:S(2)}) async-start(), calls=%async_computation.2 | async-start | bytes 8257536 | tf_op jit(solution)/shard_map/all_gather | solution.py:16
  24.4 162.9 %all-to-all-start = ((bf16[8,2,65536]{2,1,0:T(2,128)(2,1)}), bf16[8,2,65536]{2,1,0:T(2,128)(2,1)S(1)}, u32[]{:S(2)}, u32[]{:S(2)}) async-start(bf16[8,2,65536]{2,1,0:T(2,128)(2,1)} %reshape.86), calls=%async_computation.1 | async-start | bytes 4194304 | tf_op jit(solution)/shard_map/all_to_all | solution.py:27
  31.7 144.7 %copy-start = (s32[16]{0:T(128)S(1)}, s32[16]{0:T(128)}, u32[]{:S(2)}) copy-start(s32[16]{0:T(128)} %param.11) | copy-start | bytes 196
  31.7 145.4 %copy-start.1 = (s32[256]{0:T(256)S(1)}, s32[256]{0:T(256)}, u32[]{:S(2)}) copy-start(s32[256]{0:T(256)} %param.10) | copy-start | bytes 3076
  31.7 234.7 %reduce-scatter.2.cloned.1.call-start = ((), (), s32[]{:S(2)}) async-start(), calls=%async_computation.3 | async-start | bytes 1572864 | tf_op jit(solution)/shard_map/reduce_scatter | solution.py:40
Sparse Core Ops, SparseCore 0:
  9.5 150.5 all-gather.1
  176.5 7.7 reduce-scatter.1
where the time goes:
time: 276 us
  waiting for transfers between devices  129 us (47%)
  blocking collectives  58.2 us (21%)
  local copies, waits for them, and re-layouts  32 us (12%)
  matrix products  25.1 us (9%)
  between operations  13.5 us (5%)
  other arithmetic  10.2 us (4%)
  starting transfers between devices  7.37 us (3%)
    all_gather x1, waiting for transfers between devices, shards(): piece = lax.all_gather(hidden, 'store', axis=0, tiled=True)  128 us
    psum x1, blocking collectives, shards(): shrunk = lax.psum(partial_shrunk, ('store', 'tensor')).astype(jnp.bfloat16)  58.2 us
    unnamed x7, local copies, waits for them, and re-layouts  22.2 us
    dot_general x1, matrix products, shards(): plain = jnp.dot(piece, down_weight, preferred_element_type=jnp.float32)  16.2 us
    gather x1, other arithmetic, shards(): row_slot = adapter_slot[row_adapter]  10.1 us
    all_to_all x1, local copies, waits for them, and re-layouts, shards(): lax.all_to_all(expand_weight, 'store', split_axis=2, concat_axis=0, tiled...  9.09 us
    all_to_all x1, starting transfers between devices, shards(): lax.all_to_all(expand_weight, 'store', split_axis=2, concat_axis=0, tiled...  7.33 us
    dot_general x1, matrix products, shards(): narrow = jnp.dot(piece, stacked, preferred_element_type=jnp.float32)  6.71 us
  transfers between devices with their start and end apart: 3, of which 1 were waited for; matrix products, arithmetic and copies ran while one was open for 24% of the time, Pallas kernels for 0%

commit v1 on v0

v1 whole, which is shorter than its diff:
```python
import functools

import jax
import jax.numpy as jnp
from jax import lax
from jax.experimental import pallas as pl
from jax.experimental.pallas import tpu as pltpu
from jax.sharding import PartitionSpec as P

F32, BF16 = jnp.float32, jnp.bfloat16
CHUNKS = 4
VMEM = 48 * 2**20


def ring_order(n):
    return list(range(0, n, 2)) + list(range(1, n, 2))[::-1]


def split_kernel(place, src, dst):
    dst[...] = src[...][None]


def expand_blocks(expand, n, parts_of_columns, tensor_place):
    owned, rank, width = expand.shape
    rows = owned * rank
    share = width // (n * parts_of_columns)
    return pl.pallas_call(
        split_kernel,
        grid_spec=pltpu.PrefetchScalarGridSpec(
            num_scalar_prefetch=1,
            grid=(n,),
            in_specs=[pl.BlockSpec((rows, share), lambda s, t: (0, s * parts_of_columns + t[0]))],
            out_specs=pl.BlockSpec((1, rows, share), lambda s, t: (s, 0, 0)),
        ),
        out_shape=jax.ShapeDtypeStruct((n, rows, share), BF16),
        compiler_params=pltpu.CompilerParams(vmem_limit_bytes=VMEM),
        cost_estimate=pl.CostEstimate(flops=0, bytes_accessed=4 * n * rows * share, transcendentals=0),
        name="expand_blocks",
    )(tensor_place.reshape(1), expand.reshape(rows, width))


def matmul_kernel(n, steps, has_narrow, sides, has_acc, owned, places, *refs):
    refs = list(refs)
    pieces = [refs.pop(0) for _ in range(n)]
    weights = [refs.pop(0) for _ in range(sides)]
    shrink = refs.pop(0) if has_narrow else None
    count = sides + (1 if has_narrow else 0)
    before = [refs.pop(0) for _ in range(count)] if has_acc else None
    after = [refs.pop(0) for _ in range(count)]
    lhs = refs.pop(0)
    step = pl.program_id(0)
    rows = pieces[0].shape[0]

    @pl.when(step == 0)
    def _():
        for i in range(count):
            after[i][...] = before[i][...] if has_acc else jnp.zeros_like(after[i])

    for i in range(n):
        at = pl.multiple_of(places[i] * rows, rows)
        lhs[pl.ds(at, rows), :] = pieces[i][...]
    if has_narrow:
        after[-1][...] += lax.dot_general(
            shrink[...], lhs[...], (((1,), (1,)), ((), ())), preferred_element_type=F32
        )
    for i in range(sides):
        after[i][...] += jnp.dot(lhs[...], weights[i][...], preferred_element_type=F32)


def chunk_matmul(scalars, pieces, down, shrink, acc, chunk, width, tile, sides, narrow, label):
    n = len(pieces)
    rows = pieces[0].shape[0] * n
    share = down.shape[1] // 2
    steps = width // tile
    first = chunk * steps
    narrow_rows = shrink.shape[0]
    in_specs = [pl.BlockSpec((rows // n, tile), lambda k, s: (0, k)) for _ in pieces]
    args = list(pieces)
    for side in sides:
        in_specs.append(pl.BlockSpec((tile, share), functools.partial(lambda side, k, s: (first + k, s[n + side]), side)))
        args.append(down)
    if narrow:
        in_specs.append(pl.BlockSpec((narrow_rows, tile), lambda k, s: (0, first + k)))
        args.append(shrink)
    shapes = [(rows, share)] * len(sides) + ([(narrow_rows, rows)] if narrow else [])
    whole = [pl.BlockSpec(shape, lambda k, s: (0, 0)) for shape in shapes]
    aliases = {}
    if acc is not None:
        aliases = {1 + len(args) + i: i for i in range(len(shapes))}
        in_specs += whole
        args += list(acc)
    columns = share * len(sides) + (narrow_rows if narrow else 0)
    return pl.pallas_call(
        functools.partial(matmul_kernel, n, steps, narrow, len(sides), acc is not None, 0),
        grid_spec=pltpu.PrefetchScalarGridSpec(
            num_scalar_prefetch=1,
            grid=(steps,),
            in_specs=in_specs,
            out_specs=whole,
            scratch_shapes=[pltpu.VMEM((rows, tile), BF16)],
        ),
        out_shape=[jax.ShapeDtypeStruct(shape, F32) for shape in shapes],
        input_output_aliases=aliases,
        compiler_params=pltpu.CompilerParams(vmem_limit_bytes=VMEM),
        cost_estimate=pl.CostEstimate(
            flops=2 * rows * width * columns,
            bytes_accessed=2 * width * (columns + rows) + 8 * rows * columns,
            transcendentals=0,
        ),
        name=label,
    )(scalars, *args)


def final_kernel(n, rank, owned, owners, *refs):
    pieces, (slot, factors, kept, other, out, spread) = refs[:n], refs[n:]
    wide = owned * rank
    lane = lax.broadcasted_iota(jnp.int32, (out.shape[0], wide), 1) // rank
    for i in range(n):
        owner = owners[i]
        own = pieces[i][...].astype(F32).T
        pair = jnp.concatenate([own] * owned, axis=1)
        block = jnp.where(slot[...] == owner * owned + lane, pair, 0.0).astype(BF16)
        spread[:, i * wide:(i + 1) * wide] = block
    total = kept[...] + other[...]
    for i in range(n):
        total += jnp.dot(spread[:, i * wide:(i + 1) * wide], factors[owners[i]], preferred_element_type=F32)
    out[...] = total.astype(BF16)


def final(owners, pieces, slot_column, factors, kept, other, owned):
    n = len(pieces)
    rank = pieces[0].shape[0]
    rows, share = kept.shape
    return pl.pallas_call(
        functools.partial(final_kernel, n, rank, owned),
        grid_spec=pltpu.PrefetchScalarGridSpec(
            num_scalar_prefetch=1,
            grid=(1,),
            in_specs=[pl.BlockSpec(p.shape, lambda k, s: (0, 0)) for p in pieces]
            + [
                pl.BlockSpec((rows, 1), lambda k, s: (0, 0)),
                pl.BlockSpec(factors.shape, lambda k, s: (0, 0, 0)),
                pl.BlockSpec((rows, share), lambda k, s: (0, 0)),
                pl.BlockSpec((rows, share), lambda k, s: (0, 0)),
            ],
            out_specs=pl.BlockSpec((rows, share), lambda k, s: (0, 0)),
            scratch_shapes=[pltpu.VMEM((rows, n * owned * rank), BF16)],
        ),
        out_shape=jax.ShapeDtypeStruct((rows, share), BF16),
        compiler_params=pltpu.CompilerParams(vmem_limit_bytes=VMEM),
        cost_estimate=pl.CostEstimate(
            flops=2 * rows * share * n * owned * rank,
            bytes_accessed=2 * n * owned * rank * share + 10 * rows * share,
            transcendentals=0,
        ),
        name="expand_and_add",
    )(owners, *pieces, slot_column, factors, kept, other)


def make_shards(n, cores):
    order = ring_order(n)
    place_of = {store: place for place, store in enumerate(order)}
    clockwise = [(order[i], order[(i + 1) % n]) for i in range(n)]
    counter = [(order[i], order[i - 1]) for i in range(n)]
    long, short = n // 2, (n - 1) // 2
    swap = [(t, (t + 1) % cores) for t in range(cores)]

    def shards(hidden, down, shrink, expand, row_adapter, adapter_slot):
        owned, units, rank = shrink.shape
        width = units // CHUNKS
        tile = width // 7
        store, tensor = lax.axis_index("store"), lax.axis_index("tensor")
        place = jnp.asarray([place_of[s] for s in range(n)], jnp.int32)[store]
        at = jnp.asarray(order, jnp.int32)
        shrink_rows = jnp.transpose(shrink, (0, 2, 1)).reshape(owned * rank, units)

        blocks = expand_blocks(expand, n, cores, tensor)
        slots = jnp.arange(adapter_slot.shape[0], dtype=jnp.int32)
        row_slot = jnp.sum(jnp.where(row_adapter[None, :] == slots[:, None], adapter_slot[:, None], 0), axis=0)

        acc = None
        for chunk in range(CHUNKS):
            own = hidden[:, chunk * width:(chunk + 1) * width]
            steps = (long, short) if chunk % 2 == 0 else (short, long)
            pieces, shifts = [own], [0]
            for length, pairs, sign in zip(steps, (clockwise, counter), (-1, 1)):
                moving = own
                for step in range(1, length + 1):
                    moving = lax.ppermute(moving, "store", pairs)
                    pieces.append(moving)
                    shifts.append(sign * step)
            places = at[(place + jnp.asarray(shifts, jnp.int32)) % n]
            scalars = jnp.concatenate([places, jnp.stack([tensor, 1 - tensor])]).astype(jnp.int32)
            if chunk < CHUNKS - 1:
                acc = chunk_matmul(scalars, pieces, down, shrink_rows, acc, chunk, width, tile, (0, 1), True, f"chunk_{chunk}")
            else:
                send, narrow = chunk_matmul(
                    scalars, pieces, down, shrink_rows, acc and acc[1:], chunk, width, tile, (1,), True, "last_sent"
                )
                kept, = chunk_matmul(
                    scalars, pieces, down, shrink_rows, acc and acc[:1], chunk, width, tile, (0,), False, "last_kept"
                )
        mine = [
            jnp.where((row_slot == store * owned + i)[None, :], narrow[i * rank:(i + 1) * rank], 0.0)
            for i in range(owned)
        ]
        mine = sum(mine[1:], mine[0])
        shrunk = (mine + lax.ppermute(mine, "tensor", swap)).astype(BF16)
        other = lax.ppermute(send, "tensor", swap)
        everyone, owners = [shrunk], [store]
        for shift in range(1, n):
            everyone.append(lax.ppermute(shrunk, "store", [(s, (s + shift) % n) for s in range(n)]))
            owners.append((store - shift) % n)
        factors = lax.all_to_all(blocks, "store", 0, 0)
        return final(jnp.stack(owners).astype(jnp.int32), everyone, row_slot[:, None], factors, kept, other, owned)

    return shards


def solution(mesh):
    in_specs = (
        P(("parts", "store"), "tensor"),
        P("tensor", "store"),
        P(("parts", "store"), "tensor", None),
        P(("parts", "store"), None, None),
        P("parts"),
        P("parts"),
    )
    out_specs = P("parts", ("store", "tensor"))
    shards = make_shards(mesh.shape["store"], mesh.shape["tensor"])
    return jax.shard_map(shards, mesh=mesh, in_specs=in_specs, out_specs=out_specs, check_vma=False)
```

time: 276 us -> 150 us (0.54)
  waiting for transfers between devices: 129 us -> 32.4 us
  blocking collectives: 58.2 us -> 0 us
  starting transfers between devices: 7.37 us -> 60.9 us
  Pallas kernels: 0 us -> 44.3 us
  matrix products: 25.1 us -> 0 us
  local copies, waits for them, and re-layouts: 32 us -> 10.2 us
  between operations: 13.5 us -> 0.41 us
  other arithmetic: 10.2 us -> 0.94 us
    all_gather x1 -> x0, waiting for transfers between devices: 128 us -> none  [shards(): piece = lax.all_gather(hidden, 'store', axis=0, tiled=True)]
    psum x1 -> x0, blocking collectives: 58.2 us -> none  [shards(): shrunk = lax.psum(partial_shrunk, ('store', 'tensor')).astype(jnp.bfloat16)]
    ppermute x0 -> x37, starting transfers between devices: none -> 57.4 us  [the longest x28 47.6 us: shards(): moving = lax.ppermute(moving, 'store', pairs)]
    pallas_call x0 -> x7, Pallas kernels: none -> 44.3 us  [the longest x5 38.1 us: chunk_matmul(): pl.pallas_call(functools.partial(matmul_kernel, n, steps, narrow, len(sid...]
    ppermute x0 -> x37, waiting for transfers between devices: none -> 32.4 us  [the longest x28 30.3 us: shards(): moving = lax.ppermute(moving, 'store', pairs)]
    dot_general x3 -> x0, matrix products: 25.1 us -> none  [the longest x1 16.2 us: shards(): plain = jnp.dot(piece, down_weight, preferred_element_type=jnp.float32)]
    unnamed x7 -> x52, local copies, waits for them, and re-layouts: 22.2 us -> 6.07 us
    gather x1 -> x2, other arithmetic: 10.1 us -> 0.01 us  [shards(): places = at[(place + jnp.asarray(shifts, jnp.int32)) % n]]
  transfers between devices with their start and end apart: 3 -> 38, of which waited for: 1 -> 8; matrix products, arithmetic and copies ran while one was open for 24% -> 2% of each run, Pallas kernels for 0% -> 27%
where the time goes in v1:
time: 150 us; the launch traced here: 149 us
  starting transfers between devices  60.9 us (41%)
  Pallas kernels  44.3 us (30%)
  waiting for transfers between devices  32.4 us (22%)
  local copies, waits for them, and re-layouts  10.2 us (7%)
    ppermute x28, starting transfers between devices, shards(): moving = lax.ppermute(moving, 'store', pairs)  47.6 us
    pallas_call x5, Pallas kernels, chunk_matmul(): pl.pallas_call(functools.partial(matmul_kernel, n, steps, narrow, len(sid...  38.1 us
    ppermute x28, waiting for transfers between devices, shards(): moving = lax.ppermute(moving, 'store', pairs)  30.3 us
    ppermute x7, starting transfers between devices, shards(): lax.ppermute(shrunk, 'store', [(s, (s + shift) % n) for s in range(n)])  9.13 us
    unnamed x52, local copies, waits for them, and re-layouts  6.07 us
    all_to_all x1, starting transfers between devices, shards(): factors = lax.all_to_all(blocks, 'store', 0, 0)  3.56 us
    pallas_call x1, Pallas kernels, final(): pl.pallas_call(functools.partial(final_kernel, n, rank, owned), grid_spec...  3.5 us
  transfers between devices with their start and end apart: 38, of which 8 were waited for; matrix products, arithmetic and copies ran while one was open for 2% of the time, Pallas kernels for 27%

profile of v1, /device:TPU:0, one launch (start us, length us, event | category | flops | bytes accessed | tf_op | source)
XLA Modules:
  0.0 149.2 jit_solution(7751983601648830406)
XLA Ops:
  1.4 3.1 %collective-permute-start.21 = (bf16[32,3584]{1,0:T(8,128)(2,1)S(1)}, bf16[32,3584]{1,0:T(8,128)(2,1)}, u32[]{:S(2)}, u32[]{:S(2)}) collective-permute-start(bf16[32,3584]{1,0:T(8,128)(2,1)S(1)} %get-tuple-element.27.refs_0_), channel_id=1, source_target_pairs={{0,4},{4,8},{8,12},{12,14},{14,10},{10,6},{6,2},{2,0},{1,5},{5,9},... | collective-permute-start | bytes 688136 | tf_op jit(solution)/shard_map/ppermute | solution.py:189
  4.5 2.0 %collective-permute-start.17 = (bf16[32,3584]{1,0:T(8,128)(2,1)S(1)}, bf16[32,3584]{1,0:T(8,128)(2,1)S(1)}, u32[]{:S(2)}, u32[]{:S(2)}) collective-permute-start(bf16[32,3584]{1,0:T(8,128)(2,1)S(1)} %get-tuple-element.30.refs_0_), channel_id=1, source_target_pairs={{0,2},{4,0},{8,4},{12,8},{14,12},{10,14},{6,10},{2,6},{1,3},{5,1},... | collective-permute-start | bytes 688136 | tf_op jit(solution)/shard_map/ppermute | solution.py:189
  6.6 2.0 %collective-permute-start.7 = (bf16[32,3584]{1,0:T(8,128)(2,1)S(1)}, bf16[32,3584]{1,0:T(8,128)(2,1)S(1)}, u32[]{:S(2)}, u32[]{:S(2)}) collective-permute-start(bf16[32,3584]{1,0:T(8,128)(2,1)S(1)} %get-tuple-element.28.refs_0_), channel_id=1, source_target_pairs={{0,4},{4,8},{8,12},{12,14},{14,10},{10,6},{6,2},{2,0},{1,5},{5,9},... | collective-permute-start | bytes 688136 | tf_op jit(solution)/shard_map/ppermute | solution.py:189
  8.6 2.4 %collective-permute-done.21.refs_1_ = bf16[32,3584]{1,0:T(8,128)(2,1)} collective-permute-done((bf16[32,3584]{1,0:T(8,128)(2,1)S(1)}, bf16[32,3584]{1,0:T(8,128)(2,1)}, u32[]{:S(2)}, u32[]{:S(2)}) %collective-permute-start.21) | collective-permute-done | bytes 229408 | tf_op jit(solution)/shard_map/ppermute | solution.py:189
  11.0 2.1 %collective-permute-start.11 = (bf16[32,3584]{1,0:T(8,128)(2,1)S(1)}, bf16[32,3584]{1,0:T(8,128)(2,1)S(1)}, u32[]{:S(2)}, u32[]{:S(2)}) collective-permute-start(bf16[32,3584]{1,0:T(8,128)(2,1)S(1)} %get-tuple-element.28.refs_0_), channel_id=1, source_target_pairs={{0,2},{4,0},{8,4},{12,8},{14,12},{10,14},{6,10},{2,6},{1,3},{5,1},... | collective-permute-start | bytes 688136 | tf_op jit(solution)/shard_map/ppermute | solution.py:189
  15.3 2.6 %collective-permute-done.17.refs_4_ = bf16[32,3584]{1,0:T(8,128)(2,1)S(1)} collective-permute-done((bf16[32,3584]{1,0:T(8,128)(2,1)S(1)}, bf16[32,3584]{1,0:T(8,128)(2,1)S(1)}, u32[]{:S(2)}, u32[]{:S(2)}) %collective-permute-start.17) | collective-permute-done | bytes 229408 | tf_op jit(solution)/shard_map/ppermute | solution.py:189
  17.9 1.6 %collective-permute-start = (bf16[32,3584]{1,0:T(8,128)(2,1)S(1)}, bf16[32,3584]{1,0:T(8,128)(2,1)S(1)}, u32[]{:S(2)}, u32[]{:S(2)}) collective-permute-start(bf16[32,3584]{1,0:T(8,128)(2,1)S(1)} %get-tuple-element.29.refs_0_), channel_id=1, source_target_pairs={{0,4},{4,8},{8,12},{12,14},{14,10},{10,6},{6,2},{2,0},{1,5},{5,9},... | collective-permute-start | bytes 688136 | tf_op jit(solution)/shard_map/ppermute | solution.py:189
  21.1 1.6 %copy-done.1 = bf16[2,64,8192]{2,1,0:T(8,128)(2,1)S(1)} copy-done((bf16[2,64,8192]{2,1,0:T(8,128)(2,1)S(1)}, bf16[2,64,8192]{2,1,0:T(8,128)(2,1)}, u32[]{:S(2)}) %copy-start.1) | copy-done | bytes 2097176
  22.7 2.7 %expand_blocks.1 = bf16[8,128,512]{2,1,0:T(8,128)(2,1)} custom-call(s32[1]{0:T(128)} %bitcast.9.place, bf16[128,8192]{1,0:T(8,128)(2,1)S(1)} %bitcast.20), custom_call_target="tpu_custom_call" | custom-call | bytes 2097152 | tf_op jit(solution)/shard_map/expand_blocks/pallas_call | solution.py:27
  25.4 3.6 %all-to-all-start = ((bf16[8,128,512]{2,1,0:T(8,128)(2,1)}), bf16[8,128,512]{2,1,0:T(8,128)(2,1)S(1)}, u32[]{:S(2)}, u32[]{:S(2)}) async-start(bf16[8,128,512]{2,1,0:T(8,128)(2,1)} %expand_blocks.1), calls=%async_computation | async-start | bytes 2097152 | tf_op jit(solution)/shard_map/all_to_all | solution.py:214
  29.0 2.0 %collective-permute-start.26 = (bf16[32,3584]{1,0:T(8,128)(2,1)}, bf16[32,3584]{1,0:T(8,128)(2,1)}, u32[]{:S(2)}, u32[]{:S(2)}) collective-permute-start(bf16[32,3584]{1,0:T(8,128)(2,1)} %copy-done.18), channel_id=1, source_target_pairs={{0,2},{4,0},{8,4},{12,8},{14,12},{10,14},{6,10},{2,6},{1,3},{5,1},... | collective-permute-start | bytes 688136 | tf_op jit(solution)/shard_map/ppermute | solution.py:189
  33.3 1.9 %collective-permute-start.12 = (bf16[32,3584]{1,0:T(8,128)(2,1)S(1)}, bf16[32,3584]{1,0:T(8,128)(2,1)}, u32[]{:S(2)}, u32[]{:S(2)}) collective-permute-start(bf16[32,3584]{1,0:T(8,128)(2,1)S(1)} %collective-permute-done.11.refs_5_), channel_id=1, source_target_pairs={{0,2},{4,0},{8,4},{12,8},{14,12},{10,14},{6,10},{2,6},{1,3},{5,1},... | collective-permute-start | bytes 688136 | tf_op jit(solution)/shard_map/ppermute | solution.py:189
  35.8 16.8 %collective-permute-done.26.refs_6_ = bf16[32,3584]{1,0:T(8,128)(2,1)} collective-permute-done((bf16[32,3584]{1,0:T(8,128)(2,1)}, bf16[32,3584]{1,0:T(8,128)(2,1)}, u32[]{:S(2)}, u32[]{:S(2)}) %collective-permute-start.26) | collective-permute-done | bytes 229408 | tf_op jit(solution)/shard_map/ppermute | solution.py:189
  52.5 1.6 %collective-permute-start.4 = (bf16[32,3584]{1,0:T(8,128)(2,1)S(1)}, bf16[32,3584]{1,0:T(8,128)(2,1)}, u32[]{:S(2)}, u32[]{:S(2)}) collective-permute-start(bf16[32,3584]{1,0:T(8,128)(2,1)S(1)} %collective-permute-done.3.refs_4_), channel_id=1, source_target_pairs={{0,2},{4,0},{8,4},{12,8},{14,12},{10,14},{6,10},{2,6},{1,3},{5,1},... | collective-permute-start | bytes 688136 | tf_op jit(solution)/shard_map/ppermute | solution.py:189
  54.2 4.4 %collective-permute-done.18.refs_5_ = bf16[32,3584]{1,0:T(8,128)(2,1)} collective-permute-done((bf16[32,3584]{1,0:T(8,128)(2,1)S(1)}, bf16[32,3584]{1,0:T(8,128)(2,1)}, u32[]{:S(2)}, u32[]{:S(2)}) %collective-permute-start.18) | collective-permute-done | bytes 229408 | tf_op jit(solution)/shard_map/ppermute | solution.py:189
  58.6 6.6 %collective-permute-start.23 = (bf16[32,3584]{1,0:T(8,128)(2,1)}, bf16[32,3584]{1,0:T(8,128)(2,1)}, u32[]{:S(2)}, u32[]{:S(2)}) collective-permute-start(bf16[32,3584]{1,0:T(8,128)(2,1)} %collective-permute-done.22.refs_2_), channel_id=1, source_target_pairs={{0,4},{4,8},{8,12},{12,14},{14,10},{10,6},{6,2},{2,0},{1,5},{5,9},... | collective-permute-start | bytes 688136 | tf_op jit(solution)/shard_map/ppermute | solution.py:189
  66.0 2.0 %collective-permute-start.27 = (bf16[32,3584]{1,0:T(8,128)(2,1)}, bf16[32,3584]{1,0:T(8,128)(2,1)}, u32[]{:S(2)}, u32[]{:S(2)}) collective-permute-start(bf16[32,3584]{1,0:T(8,128)(2,1)} %collective-permute-done.26.refs_6_), channel_id=1, source_target_pairs={{0,2},{4,0},{8,4},{12,8},{14,12},{10,14},{6,10},{2,6},{1,3},{5,1},... | collective-permute-start | bytes 688136 | tf_op jit(solution)/shard_map/ppermute | solution.py:189
  68.1 7.0 %collective-permute-start.9 = (bf16[32,3584]{1,0:T(8,128)(2,1)}, bf16[32,3584]{1,0:T(8,128)(2,1)}, u32[]{:S(2)}, u32[]{:S(2)}) collective-permute-start(bf16[32,3584]{1,0:T(8,128)(2,1)} %collective-permute-done.8.refs_2_), channel_id=1, source_target_pairs={{0,4},{4,8},{8,12},{12,14},{14,10},{10,6},{6,2},{2,0},{1,5},{5,9},... | collective-permute-start | bytes 688136 | tf_op jit(solution)/shard_map/ppermute | solution.py:189
  76.5 2.0 %collective-permute-start.5 = (bf16[32,3584]{1,0:T(8,128)(2,1)}, bf16[32,3584]{1,0:T(8,128)(2,1)S(1)}, u32[]{:S(2)}, u32[]{:S(2)}) collective-permute-start(bf16[32,3584]{1,0:T(8,128)(2,1)} %collective-permute-done.4.refs_5_), channel_id=1, source_target_pairs={{0,2},{4,0},{8,4},{12,8},{14,12},{10,14},{6,10},{2,6},{1,3},{5,1},... | collective-permute-start | bytes 688136 | tf_op jit(solution)/shard_map/ppermute | solution.py:189
  78.6 2.0 %collective-permute-start.20 = (bf16[32,3584]{1,0:T(8,128)(2,1)}, bf16[32,3584]{1,0:T(8,128)(2,1)S(1)}, u32[]{:S(2)}, u32[]{:S(2)}) collective-permute-start(bf16[32,3584]{1,0:T(8,128)(2,1)} %collective-permute-done.19.refs_6_), channel_id=1, source_target_pairs={{0,2},{4,0},{8,4},{12,8},{14,12},{10,14},{6,10},{2,6},{1,3},{5,1},... | collective-permute-start | bytes 688136 | tf_op jit(solution)/shard_map/ppermute | solution.py:189
  81.4 1.7 %collective-permute-start.13 = (bf16[32,3584]{1,0:T(8,128)(2,1)}, bf16[32,3584]{1,0:T(8,128)(2,1)S(1)}, u32[]{:S(2)}, u32[]{:S(2)}) collective-permute-start(bf16[32,3584]{1,0:T(8,128)(2,1)} %collective-permute-done.12.refs_6_), channel_id=1, source_target_pairs={{0,2},{4,0},{8,4},{12,8},{14,12},{10,14},{6,10},{2,6},{1,3},{5,1},... | collective-permute-start | bytes 688136 | tf_op jit(solution)/shard_map/ppermute | solution.py:189
  83.1 3.2 %collective-permute-done.24.refs_4_ = bf16[32,3584]{1,0:T(8,128)(2,1)} collective-permute-done((bf16[32,3584]{1,0:T(8,128)(2,1)}, bf16[32,3584]{1,0:T(8,128)(2,1)}, u32[]{:S(2)}, u32[]{:S(2)}) %collective-permute-start.24) | collective-permute-done | bytes 229408 | tf_op jit(solution)/shard_map/ppermute | solution.py:189
  86.3 2.5 %collective-permute-start.10 = (bf16[32,3584]{1,0:T(8,128)(2,1)}, bf16[32,3584]{1,0:T(8,128)(2,1)S(1)}, u32[]{:S(2)}, u32[]{:S(2)}) collective-permute-start(bf16[32,3584]{1,0:T(8,128)(2,1)} %collective-permute-done.9.refs_3_), channel_id=1, source_target_pairs={{0,4},{4,8},{8,12},{12,14},{14,10},{10,6},{6,2},{2,0},{1,5},{5,9},... | collective-permute-start | bytes 688136 | tf_op jit(solution)/shard_map/ppermute | solution.py:189
  89.7 8.3 %chunk_0.1 = (f32[256,512]{1,0:T(8,128)S(1)}, f32[256,512]{1,0:T(8,128)S(1)}, f32[128,256]{1,0:T(8,128)S(1)}) custom-call(s32[10]{0:T(128)S(1)} %add_add_fusion.1.places, bf16[32,3584]{1,0:T(8,128)(2,1)S(1)} %get-tuple-element.27.refs_0_, bf16[32,3584]{1,0:T(8,128)(2,1)} %collective-permute-done.21.refs_1_, ...), custom_call_target="tpu_custom_call" | custom-call | flops 2113929216 | bytes 12451840 | tf_op jit(solution)/shard_map/chunk_0/pallas_call | solution.py:93
  98.2 2.0 %collective-permute-start.6 = (bf16[32,3584]{1,0:T(8,128)(2,1)S(1)}, bf16[32,3584]{1,0:T(8,128)(2,1)S(1)}, u32[]{:S(2)}, u32[]{:S(2)}) collective-permute-start(bf16[32,3584]{1,0:T(8,128)(2,1)S(1)} %collective-permute-done.5.refs_6_), channel_id=1, source_target_pairs={{0,2},{4,0},{8,4},{12,8},{14,12},{10,14},{6,10},{2,6},{1,3},{5,1},... | collective-permute-start | bytes 688136 | tf_op jit(solution)/shard_map/ppermute | solution.py:189
  100.2 8.2 %chunk_1.1 = (f32[256,512]{1,0:T(8,128)S(1)}, f32[256,512]{1,0:T(8,128)S(1)}, f32[128,256]{1,0:T(8,128)S(1)}) custom-call(s32[10]{0:T(128)S(1)} %add_add_fusion.places, bf16[32,3584]{1,0:T(8,128)(2,1)S(1)} %get-tuple-element.30.refs_0_, bf16[32,3584]{1,0:T(8,128)(2,1)S(1)} %copy-done.17, ...), custom_call_target="tpu_custom_call", output_to_operand_aliasing={{0}: (12, {}), {1}: (13, {}), {2}: (14, {})} | custom-call | flops 2113929216 | bytes 12451840 | tf_op jit(solution)/shard_map/chunk_1/pallas_call | solution.py:93
  108.4 8.5 %chunk_2.1 = (f32[256,512]{1,0:T(8,128)S(1)}, f32[256,512]{1,0:T(8,128)S(1)}, f32[128,256]{1,0:T(8,128)S(1)}) custom-call(s32[10]{0:T(128)S(1)} %add_add_fusion.1.places, bf16[32,3584]{1,0:T(8,128)(2,1)S(1)} %get-tuple-element.28.refs_0_, bf16[32,3584]{1,0:T(8,128)(2,1)S(1)} %copy-done.11, ...), custom_call_target="tpu_custom_call", output_to_operand_aliasing={{0}: (12, {}), {1}: (13, {}), {2}: (14, {})} | custom-call | flops 2113929216 | bytes 12451840 | tf_op jit(solution)/shard_map/chunk_2/pallas_call | solution.py:93
  117.0 6.8 %last_sent.1 = (f32[256,512]{1,0:T(8,128)S(1)}, f32[128,256]{1,0:T(8,128)S(1)}) custom-call(s32[10]{0:T(128)S(1)} %add_add_fusion.places, bf16[32,3584]{1,0:T(8,128)(2,1)S(1)} %get-tuple-element.29.refs_0_, bf16[32,3584]{1,0:T(8,128)(2,1)S(1)} %collective-permute-done.refs_1_, ...), custom_call_target="tpu_custom_call", output_to_operand_aliasing={{0}: (11, {}), {1}: (12, {})} | custom-call | flops 1174405120 | bytes 7733248 | tf_op jit(solution)/shard_map/last_sent/pallas_call | solution.py:93
  128.4 3.7 %collective-permute-start.32 = (bf16[64,256]{1,0:T(8,128)(2,1)S(1)}, bf16[64,256]{1,0:T(8,128)(2,1)S(1)}, u32[]{:S(2)}, u32[]{:S(2)}) collective-permute-start(bf16[64,256]{1,0:T(8,128)(2,1)S(1)} %add_convert_fusion.refs_0_), channel_id=1, source_target_pairs={{0,8},{2,10},{4,12},{6,14},{8,0},{10,2},{12,4},{14,6},{1,9},{3,11}... | collective-permute-start | bytes 98312 | tf_op jit(solution)/shard_map/ppermute | solution.py:212
  132.8 2.2 %collective-permute-start.34 = (bf16[64,256]{1,0:T(8,128)(2,1)S(1)}, bf16[64,256]{1,0:T(8,128)(2,1)S(1)}, u32[]{:S(2)}, u32[]{:S(2)}) collective-permute-start(bf16[64,256]{1,0:T(8,128)(2,1)S(1)} %add_convert_fusion.refs_0_), channel_id=1, source_target_pairs={{0,12},{2,14},{4,0},{6,2},{8,4},{10,6},{12,8},{14,10},{1,13},{3,15... | collective-permute-start | bytes 98312 | tf_op jit(solution)/shard_map/ppermute | solution.py:212
  138.4 6.3 %last_kept.1.refs_10_ = f32[256,512]{1,0:T(8,128)S(1)} custom-call(s32[10]{0:T(128)S(1)} %add_add_fusion.places, bf16[32,3584]{1,0:T(8,128)(2,1)S(1)} %get-tuple-element.29.refs_0_, bf16[32,3584]{1,0:T(8,128)(2,1)S(1)} %collective-permute-done.refs_1_, bf16[32,3584]{1,0:T(8,128)(2,1)S(1)} %copy-done.4, ...), custom_call_target="tpu_custom_call", output_to_operand_aliasing={{}: (10, {})} | custom-call | flops 939524096 | bytes 6553600 | tf_op jit(solution)/shard_map/last_kept/pallas_call | solution.py:93
  145.7 3.5 %expand_and_add.1 = bf16[256,512]{1,0:T(8,128)(2,1)} custom-call(s32[8]{0:T(128)S(1)} %stack.47.owners, bf16[64,256]{1,0:T(8,128)(2,1)S(1)} %add_convert_fusion.refs_0_, bf16[64,256]{1,0:T(8,128)(2,1)S(1)} %collective-permute-done.29.refs_1_, bf16[64,256]{1,0:T(8,128)(2,1)S(1)} %collective-permute-done.30.refs_2_, ...), custom_call_target="tpu_custom_call" | custom-call | flops 268435456 | bytes 2359296 | tf_op jit(solution)/shard_map/expand_and_add/pallas_call | solution.py:134
  (118 shorter events, 22.1 us)
Async XLA Ops:
  4.5 13.4 %collective-permute-start.17 = (bf16[32,3584]{1,0:T(8,128)(2,1)S(1)}, bf16[32,3584]{1,0:T(8,128)(2,1)S(1)}, u32[]{:S(2)}, u32[]{:S(2)}) collective-permute-start(bf16[32,3584]{1,0:T(8,128)(2,1)S(1)} %get-tuple-element.30.refs_0_), channel_id=1, source_target_pairs={{0,2},{4,0},{8,4},{12,8},{14,12},{10,14},{6,10},{2,6},{1,3},{5,1},... | collective-permute-start | bytes 688136 | tf_op jit(solution)/shard_map/ppermute | solution.py:189
  6.5 13.1 %collective-permute-start.14 = (bf16[32,3584]{1,0:T(8,128)(2,1)S(1)}, bf16[32,3584]{1,0:T(8,128)(2,1)S(1)}, u32[]{:S(2)}, u32[]{:S(2)}) collective-permute-start(bf16[32,3584]{1,0:T(8,128)(2,1)S(1)} %get-tuple-element.30.refs_0_), channel_id=1, source_target_pairs={{0,4},{4,8},{8,12},{12,14},{14,10},{10,6},{6,2},{2,0},{1,5},{5,9},... | collective-permute-start | bytes 688136 | tf_op jit(solution)/shard_map/ppermute | solution.py:189
  6.6 22.4 %collective-permute-start.7 = (bf16[32,3584]{1,0:T(8,128)(2,1)S(1)}, bf16[32,3584]{1,0:T(8,128)(2,1)S(1)}, u32[]{:S(2)}, u32[]{:S(2)}) collective-permute-start(bf16[32,3584]{1,0:T(8,128)(2,1)S(1)} %get-tuple-element.28.refs_0_), channel_id=1, source_target_pairs={{0,4},{4,8},{8,12},{12,14},{14,10},{10,6},{6,2},{2,0},{1,5},{5,9},... | collective-permute-start | bytes 688136 | tf_op jit(solution)/shard_map/ppermute | solution.py:189
  11.0 20.0 %collective-permute-start.11 = (bf16[32,3584]{1,0:T(8,128)(2,1)S(1)}, bf16[32,3584]{1,0:T(8,128)(2,1)S(1)}, u32[]{:S(2)}, u32[]{:S(2)}) collective-permute-start(bf16[32,3584]{1,0:T(8,128)(2,1)S(1)} %get-tuple-element.28.refs_0_), channel_id=1, source_target_pairs={{0,2},{4,0},{8,4},{12,8},{14,12},{10,14},{6,10},{2,6},{1,3},{5,1},... | collective-permute-start | bytes 688136 | tf_op jit(solution)/shard_map/ppermute | solution.py:189
  13.7 18.8 %collective-permute-start.3 = (bf16[32,3584]{1,0:T(8,128)(2,1)S(1)}, bf16[32,3584]{1,0:T(8,128)(2,1)S(1)}, u32[]{:S(2)}, u32[]{:S(2)}) collective-permute-start(bf16[32,3584]{1,0:T(8,128)(2,1)S(1)} %get-tuple-element.29.refs_0_), channel_id=1, source_target_pairs={{0,2},{4,0},{8,4},{12,8},{14,12},{10,14},{6,10},{2,6},{1,3},{5,1},... | collective-permute-start | bytes 688136 | tf_op jit(solution)/shard_map/ppermute | solution.py:189
  17.9 15.2 %collective-permute-start = (bf16[32,3584]{1,0:T(8,128)(2,1)S(1)}, bf16[32,3584]{1,0:T(8,128)(2,1)S(1)}, u32[]{:S(2)}, u32[]{:S(2)}) collective-permute-start(bf16[32,3584]{1,0:T(8,128)(2,1)S(1)} %get-tuple-element.29.refs_0_), channel_id=1, source_target_pairs={{0,4},{4,8},{8,12},{12,14},{14,10},{10,6},{6,2},{2,0},{1,5},{5,9},... | collective-permute-start | bytes 688136 | tf_op jit(solution)/shard_map/ppermute | solution.py:189
  19.5 13.7 %collective-permute-start.22 = (bf16[32,3584]{1,0:T(8,128)(2,1)}, bf16[32,3584]{1,0:T(8,128)(2,1)}, u32[]{:S(2)}, u32[]{:S(2)}) collective-permute-start(bf16[32,3584]{1,0:T(8,128)(2,1)} %collective-permute-done.21.refs_1_), channel_id=1, source_target_pairs={{0,4},{4,8},{8,12},{12,14},{14,10},{10,6},{6,2},{2,0},{1,5},{5,9},... | collective-permute-start | bytes 688136 | tf_op jit(solution)/shard_map/ppermute | solution.py:189
  25.4 119.4 %all-to-all-start = ((bf16[8,128,512]{2,1,0:T(8,128)(2,1)}), bf16[8,128,512]{2,1,0:T(8,128)(2,1)S(1)}, u32[]{:S(2)}, u32[]{:S(2)}) async-start(bf16[8,128,512]{2,1,0:T(8,128)(2,1)} %expand_blocks.1), calls=%async_computation | async-start | bytes 2097152 | tf_op jit(solution)/shard_map/all_to_all | solution.py:214
  29.0 23.5 %collective-permute-start.26 = (bf16[32,3584]{1,0:T(8,128)(2,1)}, bf16[32,3584]{1,0:T(8,128)(2,1)}, u32[]{:S(2)}, u32[]{:S(2)}) collective-permute-start(bf16[32,3584]{1,0:T(8,128)(2,1)} %copy-done.18), channel_id=1, source_target_pairs={{0,2},{4,0},{8,4},{12,8},{14,12},{10,14},{6,10},{2,6},{1,3},{5,1},... | collective-permute-start | bytes 688136 | tf_op jit(solution)/shard_map/ppermute | solution.py:189
  31.0 27.6 %collective-permute-start.18 = (bf16[32,3584]{1,0:T(8,128)(2,1)S(1)}, bf16[32,3584]{1,0:T(8,128)(2,1)}, u32[]{:S(2)}, u32[]{:S(2)}) collective-permute-start(bf16[32,3584]{1,0:T(8,128)(2,1)S(1)} %collective-permute-done.17.refs_4_), channel_id=1, source_target_pairs={{0,2},{4,0},{8,4},{12,8},{14,12},{10,14},{6,10},{2,6},{1,3},{5,1},... | collective-permute-start | bytes 688136 | tf_op jit(solution)/shard_map/ppermute | solution.py:189
  32.6 33.3 %collective-permute-start.15 = (bf16[32,3584]{1,0:T(8,128)(2,1)S(1)}, bf16[32,3584]{1,0:T(8,128)(2,1)}, u32[]{:S(2)}, u32[]{:S(2)}) collective-permute-start(bf16[32,3584]{1,0:T(8,128)(2,1)S(1)} %collective-permute-done.14.refs_1_), channel_id=1, source_target_pairs={{0,4},{4,8},{8,12},{12,14},{14,10},{10,6},{6,2},{2,0},{1,5},{5,9},... | collective-permute-start | bytes 688136 | tf_op jit(solution)/shard_map/ppermute | solution.py:189
  33.2 32.8 %collective-permute-start.8 = (bf16[32,3584]{1,0:T(8,128)(2,1)S(1)}, bf16[32,3584]{1,0:T(8,128)(2,1)}, u32[]{:S(2)}, u32[]{:S(2)}) collective-permute-start(bf16[32,3584]{1,0:T(8,128)(2,1)S(1)} %collective-permute-done.7.refs_1_), channel_id=1, source_target_pairs={{0,4},{4,8},{8,12},{12,14},{14,10},{10,6},{6,2},{2,0},{1,5},{5,9},... | collective-permute-start | bytes 688136 | tf_op jit(solution)/shard_map/ppermute | solution.py:189
  33.3 34.7 %collective-permute-start.12 = (bf16[32,3584]{1,0:T(8,128)(2,1)S(1)}, bf16[32,3584]{1,0:T(8,128)(2,1)}, u32[]{:S(2)}, u32[]{:S(2)}) collective-permute-start(bf16[32,3584]{1,0:T(8,128)(2,1)S(1)} %collective-permute-done.11.refs_5_), channel_id=1, source_target_pairs={{0,2},{4,0},{8,4},{12,8},{14,12},{10,14},{6,10},{2,6},{1,3},{5,1},... | collective-permute-start | bytes 688136 | tf_op jit(solution)/shard_map/ppermute | solution.py:189
  52.5 15.5 %collective-permute-start.4 = (bf16[32,3584]{1,0:T(8,128)(2,1)S(1)}, bf16[32,3584]{1,0:T(8,128)(2,1)}, u32[]{:S(2)}, u32[]{:S(2)}) collective-permute-start(bf16[32,3584]{1,0:T(8,128)(2,1)S(1)} %collective-permute-done.3.refs_4_), channel_id=1, source_target_pairs={{0,2},{4,0},{8,4},{12,8},{14,12},{10,14},{6,10},{2,6},{1,3},{5,1},... | collective-permute-start | bytes 688136 | tf_op jit(solution)/shard_map/ppermute | solution.py:189
  58.6 16.4 %collective-permute-start.23 = (bf16[32,3584]{1,0:T(8,128)(2,1)}, bf16[32,3584]{1,0:T(8,128)(2,1)}, u32[]{:S(2)}, u32[]{:S(2)}) collective-permute-start(bf16[32,3584]{1,0:T(8,128)(2,1)} %collective-permute-done.22.refs_2_), channel_id=1, source_target_pairs={{0,4},{4,8},{8,12},{12,14},{14,10},{10,6},{6,2},{2,0},{1,5},{5,9},... | collective-permute-start | bytes 688136 | tf_op jit(solution)/shard_map/ppermute | solution.py:189
  65.9 10.6 %collective-permute-start.1 = (bf16[32,3584]{1,0:T(8,128)(2,1)S(1)}, bf16[32,3584]{1,0:T(8,128)(2,1)S(1)}, u32[]{:S(2)}, u32[]{:S(2)}) collective-permute-start(bf16[32,3584]{1,0:T(8,128)(2,1)S(1)} %collective-permute-done.refs_1_), channel_id=1, source_target_pairs={{0,4},{4,8},{8,12},{12,14},{14,10},{10,6},{6,2},{2,0},{1,5},{5,9},... | collective-permute-start | bytes 688136 | tf_op jit(solution)/shard_map/ppermute | solution.py:189
  66.0 10.5 %collective-permute-start.27 = (bf16[32,3584]{1,0:T(8,128)(2,1)}, bf16[32,3584]{1,0:T(8,128)(2,1)}, u32[]{:S(2)}, u32[]{:S(2)}) collective-permute-start(bf16[32,3584]{1,0:T(8,128)(2,1)} %collective-permute-done.26.refs_6_), channel_id=1, source_target_pairs={{0,2},{4,0},{8,4},{12,8},{14,12},{10,14},{6,10},{2,6},{1,3},{5,1},... | collective-permute-start | bytes 688136 | tf_op jit(solution)/shard_map/ppermute | solution.py:189
  68.0 10.6 %collective-permute-start.19 = (bf16[32,3584]{1,0:T(8,128)(2,1)}, bf16[32,3584]{1,0:T(8,128)(2,1)}, u32[]{:S(2)}, u32[]{:S(2)}) collective-permute-start(bf16[32,3584]{1,0:T(8,128)(2,1)} %collective-permute-done.18.refs_5_), channel_id=1, source_target_pairs={{0,2},{4,0},{8,4},{12,8},{14,12},{10,14},{6,10},{2,6},{1,3},{5,1},... | collective-permute-start | bytes 688136 | tf_op jit(solution)/shard_map/ppermute | solution.py:189
  68.1 13.4 %collective-permute-start.9 = (bf16[32,3584]{1,0:T(8,128)(2,1)}, bf16[32,3584]{1,0:T(8,128)(2,1)}, u32[]{:S(2)}, u32[]{:S(2)}) collective-permute-start(bf16[32,3584]{1,0:T(8,128)(2,1)} %collective-permute-done.8.refs_2_), channel_id=1, source_target_pairs={{0,4},{4,8},{8,12},{12,14},{14,10},{10,6},{6,2},{2,0},{1,5},{5,9},... | collective-permute-start | bytes 688136 | tf_op jit(solution)/shard_map/ppermute | solution.py:189
  75.0 11.2 %collective-permute-start.24 = (bf16[32,3584]{1,0:T(8,128)(2,1)}, bf16[32,3584]{1,0:T(8,128)(2,1)}, u32[]{:S(2)}, u32[]{:S(2)}) collective-permute-start(bf16[32,3584]{1,0:T(8,128)(2,1)} %collective-permute-done.23.refs_3_), channel_id=1, source_target_pairs={{0,4},{4,8},{8,12},{12,14},{14,10},{10,6},{6,2},{2,0},{1,5},{5,9},... | collective-permute-start | bytes 688136 | tf_op jit(solution)/shard_map/ppermute | solution.py:189
  76.5 21.6 %collective-permute-start.16 = (bf16[32,3584]{1,0:T(8,128)(2,1)}, bf16[32,3584]{1,0:T(8,128)(2,1)S(1)}, u32[]{:S(2)}, u32[]{:S(2)}) collective-permute-start(bf16[32,3584]{1,0:T(8,128)(2,1)} %collective-permute-done.15.refs_2_), channel_id=1, source_target_pairs={{0,4},{4,8},{8,12},{12,14},{14,10},{10,6},{6,2},{2,0},{1,5},{5,9},... | collective-permute-start | bytes 688136 | tf_op jit(solution)/shard_map/ppermute | solution.py:189
  76.5 21.7 %collective-permute-start.5 = (bf16[32,3584]{1,0:T(8,128)(2,1)}, bf16[32,3584]{1,0:T(8,128)(2,1)S(1)}, u32[]{:S(2)}, u32[]{:S(2)}) collective-permute-start(bf16[32,3584]{1,0:T(8,128)(2,1)} %collective-permute-done.4.refs_5_), channel_id=1, source_target_pairs={{0,2},{4,0},{8,4},{12,8},{14,12},{10,14},{6,10},{2,6},{1,3},{5,1},... | collective-permute-start | bytes 688136 | tf_op jit(solution)/shard_map/ppermute | solution.py:189
  78.6 21.6 %collective-permute-start.20 = (bf16[32,3584]{1,0:T(8,128)(2,1)}, bf16[32,3584]{1,0:T(8,128)(2,1)S(1)}, u32[]{:S(2)}, u32[]{:S(2)}) collective-permute-start(bf16[32,3584]{1,0:T(8,128)(2,1)} %collective-permute-done.19.refs_6_), channel_id=1, source_target_pairs={{0,2},{4,0},{8,4},{12,8},{14,12},{10,14},{6,10},{2,6},{1,3},{5,1},... | collective-permute-start | bytes 688136 | tf_op jit(solution)/shard_map/ppermute | solution.py:189
  81.4 27.0 %collective-permute-start.13 = (bf16[32,3584]{1,0:T(8,128)(2,1)}, bf16[32,3584]{1,0:T(8,128)(2,1)S(1)}, u32[]{:S(2)}, u32[]{:S(2)}) collective-permute-start(bf16[32,3584]{1,0:T(8,128)(2,1)} %collective-permute-done.12.refs_6_), channel_id=1, source_target_pairs={{0,2},{4,0},{8,4},{12,8},{14,12},{10,14},{6,10},{2,6},{1,3},{5,1},... | collective-permute-start | bytes 688136 | tf_op jit(solution)/shard_map/ppermute | solution.py:189
  86.3 22.1 %collective-permute-start.10 = (bf16[32,3584]{1,0:T(8,128)(2,1)}, bf16[32,3584]{1,0:T(8,128)(2,1)S(1)}, u32[]{:S(2)}, u32[]{:S(2)}) collective-permute-start(bf16[32,3584]{1,0:T(8,128)(2,1)} %collective-permute-done.9.refs_3_), channel_id=1, source_target_pairs={{0,4},{4,8},{8,12},{12,14},{14,10},{10,6},{6,2},{2,0},{1,5},{5,9},... | collective-permute-start | bytes 688136 | tf_op jit(solution)/shard_map/ppermute | solution.py:189
  98.0 18.9 %collective-permute-start.2 = (bf16[32,3584]{1,0:T(8,128)(2,1)S(1)}, bf16[32,3584]{1,0:T(8,128)(2,1)S(1)}, u32[]{:S(2)}, u32[]{:S(2)}) collective-permute-start(bf16[32,3584]{1,0:T(8,128)(2,1)S(1)} %copy-done.3), channel_id=1, source_target_pairs={{0,4},{4,8},{8,12},{12,14},{14,10},{10,6},{6,2},{2,0},{1,5},{5,9},... | collective-permute-start | bytes 688136 | tf_op jit(solution)/shard_map/ppermute | solution.py:189
  98.2 18.8 %collective-permute-start.6 = (bf16[32,3584]{1,0:T(8,128)(2,1)S(1)}, bf16[32,3584]{1,0:T(8,128)(2,1)S(1)}, u32[]{:S(2)}, u32[]{:S(2)}) collective-permute-start(bf16[32,3584]{1,0:T(8,128)(2,1)S(1)} %collective-permute-done.5.refs_6_), channel_id=1, source_target_pairs={{0,2},{4,0},{8,4},{12,8},{14,12},{10,14},{6,10},{2,6},{1,3},{5,1},... | collective-permute-start | bytes 688136 | tf_op jit(solution)/shard_map/ppermute | solution.py:189
  123.8 21.0 %collective-permute-start.36 = (f32[256,512]{1,0:T(8,128)S(1)}, f32[256,512]{1,0:T(8,128)}, u32[]{:S(2)}, u32[]{:S(2)}) collective-permute-start(f32[256,512]{1,0:T(8,128)S(1)} %get-tuple-element.26), channel_id=1, source_target_pairs={{0,1},{1,0},{2,3},{3,2},{4,5},{5,4},{6,7},{7,6},{8,9},{9,8},{10,11... | collective-permute-start | bytes 1572872 | tf_op jit(solution)/shard_map/ppermute | solution.py:209
  128.4 16.3 %collective-permute-start.32 = (bf16[64,256]{1,0:T(8,128)(2,1)S(1)}, bf16[64,256]{1,0:T(8,128)(2,1)S(1)}, u32[]{:S(2)}, u32[]{:S(2)}) collective-permute-start(bf16[64,256]{1,0:T(8,128)(2,1)S(1)} %add_convert_fusion.refs_0_), channel_id=1, source_target_pairs={{0,8},{2,10},{4,12},{6,14},{8,0},{10,2},{12,4},{14,6},{1,9},{3,11}... | collective-permute-start | bytes 98312 | tf_op jit(solution)/shard_map/ppermute | solution.py:212
  132.8 11.9 %collective-permute-start.33 = (bf16[64,256]{1,0:T(8,128)(2,1)S(1)}, bf16[64,256]{1,0:T(8,128)(2,1)S(1)}, u32[]{:S(2)}, u32[]{:S(2)}) collective-permute-start(bf16[64,256]{1,0:T(8,128)(2,1)S(1)} %add_convert_fusion.refs_0_), channel_id=1, source_target_pairs={{0,10},{2,12},{4,14},{6,0},{8,2},{10,4},{12,6},{14,8},{1,11},{3,13... | collective-permute-start | bytes 98312 | tf_op jit(solution)/shard_map/ppermute | solution.py:212
  132.8 11.9 %collective-permute-start.34 = (bf16[64,256]{1,0:T(8,128)(2,1)S(1)}, bf16[64,256]{1,0:T(8,128)(2,1)S(1)}, u32[]{:S(2)}, u32[]{:S(2)}) collective-permute-start(bf16[64,256]{1,0:T(8,128)(2,1)S(1)} %add_convert_fusion.refs_0_), channel_id=1, source_target_pairs={{0,12},{2,14},{4,0},{6,2},{8,4},{10,6},{12,8},{14,10},{1,13},{3,15... | collective-permute-start | bytes 98312 | tf_op jit(solution)/shard_map/ppermute | solution.py:212
  135.1 9.7 %collective-permute-start.35 = (bf16[64,256]{1,0:T(8,128)(2,1)S(1)}, bf16[64,256]{1,0:T(8,128)(2,1)S(1)}, u32[]{:S(2)}, u32[]{:S(2)}) collective-permute-start(bf16[64,256]{1,0:T(8,128)(2,1)S(1)} %add_convert_fusion.refs_0_), channel_id=1, source_target_pairs={{0,14},{2,0},{4,2},{6,4},{8,6},{10,8},{12,10},{14,12},{1,15},{3,1}... | collective-permute-start | bytes 98312 | tf_op jit(solution)/shard_map/ppermute | solution.py:212
  (32 other events, 701.0 us)

commit v2 on v1

v2 whole, which is shorter than its diff:
```python
import functools

import jax
import jax.numpy as jnp
import numpy as np
from jax import lax
from jax.experimental import pallas as pl
from jax.experimental.pallas import tpu as pltpu
from jax.sharding import PartitionSpec as P

F32, BF16 = jnp.float32, jnp.bfloat16
TILE = 512
MIB = 2**20


def params(mib):
    return pltpu.CompilerParams(vmem_limit_bytes=mib * MIB)


def ring_order(n):
    return list(range(0, n, 2)) + list(range(1, n, 2))[::-1]


def take_kernel(start, width, src, *refs):
    *_, dst, sem = refs
    copy = pltpu.make_async_copy(src.at[:, pl.ds(start, width)], dst, sem)
    copy.start()
    copy.wait()


def take(hidden, start, width, after):
    rows = hidden.shape[0]
    return pl.pallas_call(
        functools.partial(take_kernel, start, width),
        in_specs=[pl.BlockSpec(memory_space=pl.ANY)] * (1 + len(after)),
        out_specs=pl.BlockSpec(memory_space=pl.ANY),
        scratch_shapes=[pltpu.SemaphoreType.DMA],
        out_shape=jax.ShapeDtypeStruct((rows, width), BF16),
        compiler_params=params(1),
        cost_estimate=pl.CostEstimate(flops=0, bytes_accessed=4 * rows * width, transcendentals=0),
        name=f"take_{start}",
    )(hidden, *after)


def split_kernel(scalars, src, after, dst):
    dst[...] = src[...][None]


def expand_blocks(scalars, half, expand, n, cores, after):
    owned, rank, width = expand.shape
    rows = owned * rank
    share = width // (n * cores)
    return pl.pallas_call(
        split_kernel,
        grid_spec=pltpu.PrefetchScalarGridSpec(
            num_scalar_prefetch=1,
            grid=(n,),
            in_specs=[
                pl.BlockSpec((rows, share), lambda s, t: (0, s * cores + t[half])),
                pl.BlockSpec(memory_space=pl.ANY),
            ],
            out_specs=pl.BlockSpec((1, rows, share), lambda s, t: (s, 0, 0)),
        ),
        out_shape=jax.ShapeDtypeStruct((n, rows, share), BF16),
        compiler_params=params(8),
        cost_estimate=pl.CostEstimate(flops=0, bytes_accessed=4 * n * rows * share, transcendentals=0),
        name="expand_blocks",
    )(scalars, expand.reshape(rows, width), after)


def matmul_kernel(n, base, sides, narrow, has_acc, scalars, *refs):
    refs = list(refs)
    pieces = [refs.pop(0) for _ in range(n)]
    weights = [refs.pop(0) for _ in range(sides)]
    shrink = refs.pop(0) if narrow else None
    count = sides + narrow
    before = [refs.pop(0) for _ in range(count)] if has_acc else None
    after = [refs.pop(0) for _ in range(count)]
    lhs, sems = refs
    step = pl.program_id(0)
    rows = pieces[0].shape[0]
    tile = lhs.shape[2]

    @pl.when(step == 0)
    def _():
        copies = []
        for i in range(n):
            at = pl.multiple_of(scalars[base + i] * rows, rows)
            for j in range(lhs.shape[0]):
                copies.append(
                    pltpu.make_async_copy(
                        pieces[i].at[:, pl.ds(j * tile, tile)], lhs.at[j, pl.ds(at, rows), :], sems.at[i, j]
                    )
                )
        for copy in copies:
            copy.start()
        for i in range(count):
            after[i][...] = before[i][...] if has_acc else jnp.zeros_like(after[i])
        for copy in copies:
            copy.wait()

    left = lhs[step]
    if narrow:
        after[-1][...] += lax.dot_general(
            shrink[...], left, (((1,), (1,)), ((), ())), preferred_element_type=F32
        )
    for i in range(sides):
        after[i][...] += jnp.dot(left, weights[i][...], preferred_element_type=F32)


def chunk_matmul(scalars, base, half, pieces, down, shrink, acc, start, sides, narrow, label):
    n = len(pieces)
    rows, width = pieces[0].shape[0] * n, pieces[0].shape[1]
    share = down.shape[1] // 2
    steps = width // TILE
    first = start // TILE
    ranks = shrink.shape[0]
    in_specs = [pl.BlockSpec(memory_space=pl.ANY) for _ in pieces]
    args = list(pieces)
    for side in sides:
        in_specs.append(pl.BlockSpec((TILE, share), functools.partial(lambda side, k, s: (first + k, s[half + side]), side)))
        args.append(down)
    if narrow:
        in_specs.append(pl.BlockSpec((ranks, TILE), lambda k, s: (0, first + k)))
        args.append(shrink)
    shapes = [(rows, share)] * len(sides) + [(ranks, rows)] * narrow
    whole = [pl.BlockSpec(shape, lambda k, s: (0, 0)) for shape in shapes]
    aliases = {}
    if acc is not None:
        aliases = {1 + len(args) + i: i for i in range(len(shapes))}
        in_specs += whole
        args += list(acc)
    columns = share * len(sides) + ranks * narrow
    return pl.pallas_call(
        functools.partial(matmul_kernel, n, base, len(sides), narrow, acc is not None),
        grid_spec=pltpu.PrefetchScalarGridSpec(
            num_scalar_prefetch=1,
            grid=(steps,),
            in_specs=in_specs,
            out_specs=whole,
            scratch_shapes=[pltpu.VMEM((steps, rows, TILE), BF16), pltpu.SemaphoreType.DMA((n, steps))],
        ),
        out_shape=[jax.ShapeDtypeStruct(shape, F32) for shape in shapes],
        input_output_aliases=aliases,
        compiler_params=params(24),
        cost_estimate=pl.CostEstimate(
            flops=4 * rows * width * columns,
            bytes_accessed=2 * width * (columns + rows) + 8 * rows * columns,
            transcendentals=0,
        ),
        name=label,
    )(scalars, *args)


def final_kernel(n, owned, shrunk, slot, factors, kept, other, out, spread):
    rank = shrunk.shape[0]
    wide = owned * rank
    rows = out.shape[0]
    lane = lax.broadcasted_iota(jnp.int32, (rows, wide), 1) // rank
    own = shrunk[...].astype(F32).T
    pair = jnp.concatenate([own] * owned, axis=1)
    place = slot[...] - lane
    for i in range(n):
        spread[:, i * wide:(i + 1) * wide] = jnp.where(place == i * owned, pair, 0.0).astype(BF16)
    extra = jnp.dot(spread[...], factors[...], preferred_element_type=F32)
    out[...] = (kept[...] + other[...] + extra).astype(BF16)


def final(shrunk, slot_column, factors, kept, other, owned):
    n, wide, share = factors.shape
    rows = kept.shape[0]
    return pl.pallas_call(
        functools.partial(final_kernel, n, owned),
        in_specs=[pl.BlockSpec(memory_space=pltpu.VMEM)] * 5,
        out_specs=pl.BlockSpec(memory_space=pltpu.VMEM),
        scratch_shapes=[pltpu.VMEM((rows, n * wide), BF16)],
        out_shape=jax.ShapeDtypeStruct((rows, share), BF16),
        compiler_params=params(24),
        cost_estimate=pl.CostEstimate(
            flops=2 * rows * share * n * wide,
            bytes_accessed=2 * n * wide * share + 10 * rows * share,
            transcendentals=0,
        ),
        name="expand_and_add",
    )(shrunk, slot_column, factors.reshape(n * wide, share), kept, other)


def make_shards(n, cores):
    order = ring_order(n)
    place_of = {store: place for place, store in enumerate(order)}
    clockwise = [(order[i], order[(i + 1) % n]) for i in range(n)]
    counter = [(order[i], order[i - 1]) for i in range(n)]
    long, short = n // 2, (n - 1) // 2
    swap = [(t, (t + 1) % cores) for t in range(cores)]
    hops = [[0] + [-i for i in range(1, a + 1)] + list(range(1, b + 1)) for a, b in ((long, short), (short, long))]
    table = np.array(
        [
            [order[(place_of[s] + hop) % n] for way in hops for hop in way] + [t, 1 - t]
            for s in range(n)
            for t in range(cores)
        ],
        np.int32,
    )
    half = 2 * n

    def shards(hidden, down, shrink, expand, row_adapter, adapter_slot):
        owned, units, rank = shrink.shape
        store, tensor = lax.axis_index("store"), lax.axis_index("tensor")
        scalars = lax.dynamic_slice_in_dim(jnp.asarray(table), store * cores + tensor, 1, 0)[0]
        shrink_rows = jnp.transpose(shrink, (0, 2, 1)).reshape(owned * rank, units)

        slots = jnp.arange(adapter_slot.shape[0], dtype=jnp.int32)
        row_slot = jnp.sum(jnp.where(row_adapter[None, :] == slots[:, None], adapter_slot[:, None], 0), axis=0)

        tiles = units // TILE
        small = tiles // 7
        widths = [(tiles - small) // 3 * TILE] * 3 + [small * TILE]
        widths[0] += units - sum(widths)

        acc, ends = None, []
        start = 0
        for chunk, width in enumerate(widths):
            own = hidden[:, :width] if chunk == 0 else take(hidden, start, width, after)
            way = chunk % 2
            pieces = [own]
            for length, pairs in zip(((long, short), (short, long))[way], (clockwise, counter)):
                moving = own
                for step in range(length):
                    moving = lax.ppermute(moving, "store", pairs)
                    pieces.append(moving)
            turn = (long, short)[way]
            after = [pieces[2], pieces[turn + 2], *ends]
            ends = [pieces[turn], pieces[-1]]
            if chunk == 1:
                after.append(blocks)
            if chunk == 2:
                after.append(factors)
            if chunk == 0:
                blocks = expand_blocks(scalars, half, expand, n, cores, pieces[1])
                factors = lax.all_to_all(blocks, "store", 0, 0)
            call = functools.partial(chunk_matmul, scalars, way * n, half, pieces, down, shrink_rows)
            if chunk < len(widths) - 1:
                acc = call(acc, start, (0, 1), True, f"chunk_{chunk}")
            else:
                narrow, = call(acc[2:], start, (), True, "last_narrow")
                send, = call(acc[1:2], start, (1,), False, "last_sent")
                kept, = call(acc[:1], start, (0,), False, "last_kept")
            start += width
        mine = [
            jnp.where((row_slot == store * owned + i)[None, :], narrow[i * rank:(i + 1) * rank], 0.0)
            for i in range(owned)
        ]
        mine = sum(mine[1:], mine[0])
        shrunk = (mine + lax.ppermute(mine, "tensor", swap)).astype(BF16)
        other = lax.ppermute(send, "tensor", swap)
        bit = 1
        while bit < n:
            shrunk = shrunk + lax.ppermute(shrunk, "store", [(s, s ^ bit) for s in range(n)])
            bit *= 2
        return final(shrunk, row_slot[:, None], factors, kept, other, owned)

    return shards


def solution(mesh):
    in_specs = (
        P(("parts", "store"), "tensor"),
        P("tensor", "store"),
        P(("parts", "store"), "tensor", None),
        P(("parts", "store"), None, None),
        P("parts"),
        P("parts"),
    )
    out_specs = P("parts", ("store", "tensor"))
    shards = make_shards(mesh.shape["store"], mesh.shape["tensor"])
    return jax.shard_map(shards, mesh=mesh, in_specs=in_specs, out_specs=out_specs, check_vma=False)
```

time: 150 us -> 198 us (1.32)
  waiting for transfers between devices: 32.4 us -> 69.6 us
  local copies, waits for them, and re-layouts: 10.2 us -> 35.5 us
  starting transfers between devices: 60.9 us -> 46.5 us
    ppermute x28, waiting for transfers between devices: 30.3 us -> 64.1 us  [shards(): moving = lax.ppermute(moving, 'store', pairs)]
    unnamed x52 -> x70, local copies, waits for them, and re-layouts: 6.07 us -> 33.6 us
    ppermute x28, starting transfers between devices: 47.6 us -> 34.6 us  [shards(): moving = lax.ppermute(moving, 'store', pairs)]
    ppermute x7 -> x3, starting transfers between devices: 9.13 us -> 5.01 us  [shards(): lax.ppermute(shrunk, 'store', [(s, s ^ bit) for s in range(n)])]
    ppermute x7 -> x3, waiting for transfers between devices: 0.69 us -> 4.54 us  [shards(): lax.ppermute(shrunk, 'store', [(s, s ^ bit) for s in range(n)])]
    all_to_all x1, starting transfers between devices: 3.56 us -> 6.19 us  [shards(): factors = lax.all_to_all(blocks, 'store', 0, 0)]
    pallas_call x6 -> x10, Pallas kernels: 41.6 us -> 41.3 us  [the longest x6 38.9 us: chunk_matmul(): pl.pallas_call(functools.partial(matmul_kernel, n, base, len(sides), narr...]
  transfers between devices with their start and end apart: 38 -> 34, of which waited for: 8 -> 15; matrix products, arithmetic and copies ran while one was open for 2% -> 0% of each run, Pallas kernels for 27% -> 18%
where the time goes in v2:
time: 198 us; the launch traced here: 197 us
  waiting for transfers between devices  69.6 us (35%)
  starting transfers between devices  46.5 us (23%)
  Pallas kernels  44.7 us (23%)
  local copies, waits for them, and re-layouts  35.5 us (18%)
    ppermute x28, waiting for transfers between devices, shards(): moving = lax.ppermute(moving, 'store', pairs)  64.1 us
    pallas_call x6, Pallas kernels, chunk_matmul(): pl.pallas_call(functools.partial(matmul_kernel, n, base, len(sides), narr...  38.9 us
    ppermute x28, starting transfers between devices, shards(): moving = lax.ppermute(moving, 'store', pairs)  34.6 us
    unnamed x70, local copies, waits for them, and re-layouts  33.6 us
    all_to_all x1, starting transfers between devices, shards(): factors = lax.all_to_all(blocks, 'store', 0, 0)  6.19 us
    ppermute x3, starting transfers between devices, shards(): lax.ppermute(shrunk, 'store', [(s, s ^ bit) for s in range(n)])  5.01 us
    ppermute x3, waiting for transfers between devices, shards(): lax.ppermute(shrunk, 'store', [(s, s ^ bit) for s in range(n)])  4.54 us
  transfers between devices with their start and end apart: 34, of which 15 were waited for; matrix products, arithmetic and copies ran while one was open for 0% of the time, Pallas kernels for 18%

profile of v2, /device:TPU:0, one launch (start us, length us, event | category | flops | bytes accessed | tf_op | source)
XLA Modules:
  0.0 196.6 jit_solution(9308552196922193076)
XLA Ops:
  1.1 3.1 %collective-permute-start = (bf16[32,4096]{1,0:T(8,128)(2,1)S(1)}, bf16[32,4096]{1,0:T(8,128)(2,1)S(1)}, u32[]{:S(2)}, u32[]{:S(2)}) collective-permute-start(bf16[32,4096]{1,0:T(8,128)(2,1)S(1)} %slice.9.refs_0_), channel_id=1, source_target_pairs={{0,4},{4,8},{8,12},{12,14},{14,10},{10,6},{6,2},{2,0},{1,5},{5,9},... | collective-permute-start | bytes 786440 | tf_op jit(solution)/shard_map/ppermute | solution.py:229
  4.8 5.6 %collective-permute-done.after.refs_1_ = bf16[32,4096]{1,0:T(8,128)(2,1)S(1)} collective-permute-done((bf16[32,4096]{1,0:T(8,128)(2,1)S(1)}, bf16[32,4096]{1,0:T(8,128)(2,1)S(1)}, u32[]{:S(2)}, u32[]{:S(2)}) %collective-permute-start) | collective-permute-done | bytes 262176 | tf_op jit(solution)/shard_map/ppermute | solution.py:229
  12.0 3.3 %expand_blocks.1.refs_4_ = bf16[8,128,512]{2,1,0:T(8,128)(2,1)} custom-call(s32[18]{0:T(128)S(1)} %dynamic-slice_bitcast_fusion.scalars, bf16[128,8192]{1,0:T(8,128)(2,1)S(1)} %bitcast.13, bf16[32,4096]{1,0:T(8,128)(2,1)S(1)} %collective-permute-done.after.refs_1_), custom_call_target="tpu_custom_call" | custom-call | bytes 2097152 | tf_op jit(solution)/shard_map/expand_blocks/pallas_call | solution.py:53
  15.3 6.2 %all-to-all-start = ((bf16[8,128,512]{2,1,0:T(8,128)(2,1)}), bf16[8,128,512]{2,1,0:T(8,128)(2,1)S(1)}, u32[]{:S(2)}, u32[]{:S(2)}) async-start(bf16[8,128,512]{2,1,0:T(8,128)(2,1)} %expand_blocks.1.refs_4_), calls=%async_computation | async-start | bytes 2097152 | tf_op jit(solution)/shard_map/all_to_all | solution.py:240
  21.5 2.0 %collective-permute-start.2 = (bf16[32,4096]{1,0:T(8,128)(2,1)S(1)}, bf16[32,4096]{1,0:T(8,128)(2,1)S(1)}, u32[]{:S(2)}, u32[]{:S(2)}) collective-permute-start(bf16[32,4096]{1,0:T(8,128)(2,1)S(1)} %slice.9.refs_0_), channel_id=1, source_target_pairs={{0,2},{4,0},{8,4},{12,8},{14,12},{10,14},{6,10},{2,6},{1,3},{5,1},... | collective-permute-start | bytes 786440 | tf_op jit(solution)/shard_map/ppermute | solution.py:229
  23.5 18.4 %collective-permute-done.2.refs_5_ = bf16[32,4096]{1,0:T(8,128)(2,1)S(1)} collective-permute-done((bf16[32,4096]{1,0:T(8,128)(2,1)S(1)}, bf16[32,4096]{1,0:T(8,128)(2,1)S(1)}, u32[]{:S(2)}, u32[]{:S(2)}) %collective-permute-start.2) | collective-permute-done | bytes 262176 | tf_op jit(solution)/shard_map/ppermute | solution.py:229
  41.9 3.2 %collective-permute-start.3 = (bf16[32,4096]{1,0:T(8,128)(2,1)S(1)}, bf16[32,4096]{1,0:T(8,128)(2,1)S(1)}, u32[]{:S(2)}, u32[]{:S(2)}) collective-permute-start(bf16[32,4096]{1,0:T(8,128)(2,1)S(1)} %collective-permute-done.2.refs_5_), channel_id=1, source_target_pairs={{0,2},{4,0},{8,4},{12,8},{14,12},{10,14},{6,10},{2,6},{1,3},{5,1},... | collective-permute-start | bytes 786440 | tf_op jit(solution)/shard_map/ppermute | solution.py:229
  45.8 11.5 %collective-permute-done.3.refs_1_.refs_6_ = bf16[32,4096]{1,0:T(8,128)(2,1)S(1)} collective-permute-done((bf16[32,4096]{1,0:T(8,128)(2,1)S(1)}, bf16[32,4096]{1,0:T(8,128)(2,1)S(1)}, u32[]{:S(2)}, u32[]{:S(2)}) %collective-permute-start.3) | collective-permute-done | bytes 262176 | tf_op jit(solution)/shard_map/ppermute | solution.py:229
  59.7 2.0 collective-permute-start.4
  62.4 4.3 %collective-permute-done.6.refs_4_ = bf16[32,4096]{1,0:T(8,128)(2,1)S(1)} collective-permute-done((bf16[32,4096]{1,0:T(8,128)(2,1)S(1)}, bf16[32,4096]{1,0:T(8,128)(2,1)S(1)}, u32[]{:S(2)}, u32[]{:S(2)}) %collective-permute-start.6) | collective-permute-done | bytes 262176 | tf_op jit(solution)/shard_map/ppermute | solution.py:229
  69.6 3.6 %collective-permute-done.4.refs_1_ = bf16[32,4096]{1,0:T(8,128)(2,1)S(1)} collective-permute-done((bf16[32,4096]{1,0:T(8,128)(2,1)S(1)}, bf16[32,4096]{1,0:T(8,128)(2,1)S(1)}, u32[]{:S(2)}, u32[]{:S(2)}) %collective-permute-start.4) | collective-permute-done | bytes 262176 | tf_op jit(solution)/shard_map/ppermute | solution.py:229
  76.5 2.3 %collective-permute-done.9.refs_2_.refs_4_ = bf16[32,4096]{1,0:T(8,128)(2,1)S(1)} collective-permute-done((bf16[32,4096]{1,0:T(8,128)(2,1)S(1)}, bf16[32,4096]{1,0:T(8,128)(2,1)S(1)}, u32[]{:S(2)}, u32[]{:S(2)}) %collective-permute-start.9) | collective-permute-done | bytes 262176 | tf_op jit(solution)/shard_map/ppermute | solution.py:229
  78.8 3.8 %collective-permute-done.5.refs_0_.refs_2_ = bf16[32,4096]{1,0:T(8,128)(2,1)S(1)} collective-permute-done((bf16[32,4096]{1,0:T(8,128)(2,1)S(1)}, bf16[32,4096]{1,0:T(8,128)(2,1)S(1)}, u32[]{:S(2)}, u32[]{:S(2)}) %collective-permute-start.5) | collective-permute-done | bytes 262176 | tf_op jit(solution)/shard_map/ppermute | solution.py:229
  82.7 2.5 %collective-permute-start.13 = (bf16[32,4096]{1,0:T(8,128)(2,1)S(1)}, bf16[32,4096]{1,0:T(8,128)(2,1)}, u32[]{:S(2)}, u32[]{:S(2)}) collective-permute-start(bf16[32,4096]{1,0:T(8,128)(2,1)S(1)} %take_8192.1.refs_0_), channel_id=1, source_target_pairs={{0,2},{4,0},{8,4},{12,8},{14,12},{10,14},{6,10},{2,6},{1,3},{5,1},... | collective-permute-start | bytes 786440 | tf_op jit(solution)/shard_map/ppermute | solution.py:229
  85.3 2.0 %collective-permute-start.17 = (bf16[32,4096]{1,0:T(8,128)(2,1)}, bf16[32,4096]{1,0:T(8,128)(2,1)}, u32[]{:S(2)}, u32[]{:S(2)}) collective-permute-start(bf16[32,4096]{1,0:T(8,128)(2,1)} %collective-permute-done.16.refs_6_), channel_id=1, source_target_pairs={{0,2},{4,0},{8,4},{12,8},{14,12},{10,14},{6,10},{2,6},{1,3},{5,1},... | collective-permute-start | bytes 786440 | tf_op jit(solution)/shard_map/ppermute | solution.py:229
  87.3 5.2 %collective-permute-done.11.refs_1_ = bf16[32,4096]{1,0:T(8,128)(2,1)} collective-permute-done((bf16[32,4096]{1,0:T(8,128)(2,1)S(1)}, bf16[32,4096]{1,0:T(8,128)(2,1)}, u32[]{:S(2)}, u32[]{:S(2)}) %collective-permute-start.11) | collective-permute-done | bytes 262176 | tf_op jit(solution)/shard_map/ppermute | solution.py:229
  92.5 2.1 %collective-permute-start.14 = (bf16[32,4096]{1,0:T(8,128)(2,1)}, bf16[32,4096]{1,0:T(8,128)(2,1)S(1)}, u32[]{:S(2)}, u32[]{:S(2)}) collective-permute-start(bf16[32,4096]{1,0:T(8,128)(2,1)} %collective-permute-done.13.refs_5_), channel_id=1, source_target_pairs={{0,2},{4,0},{8,4},{12,8},{14,12},{10,14},{6,10},{2,6},{1,3},{5,1},... | collective-permute-start | bytes 786440 | tf_op jit(solution)/shard_map/ppermute | solution.py:229
  94.7 3.3 %collective-permute-done.15.refs_2_.refs_3_ = bf16[32,4096]{1,0:T(8,128)(2,1)S(1)} collective-permute-done((bf16[32,4096]{1,0:T(8,128)(2,1)S(1)}, bf16[32,4096]{1,0:T(8,128)(2,1)S(1)}, u32[]{:S(2)}, u32[]{:S(2)}) %collective-permute-start.15) | collective-permute-done | bytes 262176 | tf_op jit(solution)/shard_map/ppermute | solution.py:229
  98.7 2.5 %collective-permute-done.12.refs_0_.refs_2_ = bf16[32,4096]{1,0:T(8,128)(2,1)} collective-permute-done((bf16[32,4096]{1,0:T(8,128)(2,1)}, bf16[32,4096]{1,0:T(8,128)(2,1)}, u32[]{:S(2)}, u32[]{:S(2)}) %collective-permute-start.12) | collective-permute-done | bytes 262176 | tf_op jit(solution)/shard_map/ppermute | solution.py:229
  105.2 3.2 %collective-permute-done.21.refs_4_ = bf16[32,2048]{1,0:T(8,128)(2,1)S(1)} collective-permute-done((bf16[32,2048]{1,0:T(8,128)(2,1)S(1)}, bf16[32,2048]{1,0:T(8,128)(2,1)S(1)}, u32[]{:S(2)}, u32[]{:S(2)}) %collective-permute-start.21) | collective-permute-done | bytes 131104 | tf_op jit(solution)/shard_map/ppermute | solution.py:229
  110.3 2.0 %copy-done.2 = bf16[2,14336,64]{1,2,0:T(8,128)(2,1)S(1)} copy-done((bf16[2,14336,64]{1,2,0:T(8,128)(2,1)S(1)}, bf16[2,14336,64]{1,2,0:T(8,128)(2,1)}, u32[]{:S(2)}) %copy-start.2) | copy-done | bytes 3670040
  119.0 10.3 %chunk_0.1 = (f32[256,512]{1,0:T(8,128)S(1)}, f32[256,512]{1,0:T(8,128)S(1)}, f32[128,256]{1,0:T(8,128)S(1)}) custom-call(s32[18]{0:T(128)S(1)} %dynamic-slice_bitcast_fusion.scalars, bf16[32,4096]{1,0:T(8,128)(2,1)S(1)} %copy-done.18, bf16[32,4096]{1,0:T(8,128)(2,1)S(1)} %collective-permute-done.after.refs_1_, bf16[32,4096]{1,0:T(8,128)(2,1)S(1)} %copy-done.22, ...), custom_call_target="tpu_custom_call" | custom-call | flops 4831838208 | bytes 13893632 | tf_op jit(solution)/shard_map/chunk_0/pallas_call | solution.py:134
  133.4 10.6 %chunk_1.1 = (f32[256,512]{1,0:T(8,128)S(1)}, f32[256,512]{1,0:T(8,128)S(1)}, f32[128,256]{1,0:T(8,128)S(1)}) custom-call(s32[18]{0:T(128)S(1)} %dynamic-slice_bitcast_fusion.scalars, bf16[32,4096]{1,0:T(8,128)(2,1)S(1)} %copy-done.20, bf16[32,4096]{1,0:T(8,128)(2,1)S(1)} %copy-done.28, ...), custom_call_target="tpu_custom_call", output_to_operand_aliasing={{0}: (12, {}), {1}: (13, {}), {2}: (14, {})} | custom-call | flops 4831838208 | bytes 13893632 | tf_op jit(solution)/shard_map/chunk_1/pallas_call | solution.py:134
  146.1 10.2 %chunk_2.1 = (f32[256,512]{1,0:T(8,128)S(1)}, f32[256,512]{1,0:T(8,128)S(1)}, f32[128,256]{1,0:T(8,128)S(1)}) custom-call(s32[18]{0:T(128)S(1)} %dynamic-slice_bitcast_fusion.scalars, bf16[32,4096]{1,0:T(8,128)(2,1)S(1)} %take_8192.1.refs_0_, ...), custom_call_target="tpu_custom_call", output_to_operand_aliasing={{0}: (12, {}), {1}: (13, {}), {2}: (14, {})} | custom-call | flops 4831838208 | bytes 13893632 | tf_op jit(solution)/shard_map/chunk_2/pallas_call | solution.py:134
  156.3 9.3 %copy-done = bf16[14336,1024]{1,0:T(8,128)(2,1)S(1)} copy-done((bf16[14336,1024]{1,0:T(8,128)(2,1)S(1)}, bf16[14336,1024]{1,0:T(8,128)(2,1)}, u32[]{:S(2)}) %copy-start) | copy-done | bytes 29360152
  165.6 2.8 %last_sent.1 = f32[256,512]{1,0:T(8,128)S(1)} custom-call(s32[18]{0:T(128)S(1)} %dynamic-slice_bitcast_fusion.scalars, bf16[32,2048]{1,0:T(8,128)(2,1)S(1)} %take_12288.1.refs_0_, bf16[32,2048]{1,0:T(8,128)(2,1)S(1)} %collective-permute-done.18.refs_1_, bf16[32,2048]{1,0:T(8,128)(2,1)S(1)} %collective-permute-done.19.refs_2_, ...), custom_call_target="tpu_custom_call", output_to_operand_aliasing={{}: (10, {})} | custom-call | flops 1073741824 | bytes 4194304 | tf_op jit(solution)/shard_map/last_sent/pallas_call | solution.py:134
  168.5 2.3 %last_narrow.1 = f32[128,256]{1,0:T(8,128)S(1)} custom-call(s32[18]{0:T(128)S(1)} %dynamic-slice_bitcast_fusion.scalars, bf16[32,2048]{1,0:T(8,128)(2,1)S(1)} %take_12288.1.refs_0_, bf16[32,2048]{1,0:T(8,128)(2,1)S(1)} %collective-permute-done.18.refs_1_, bf16[32,2048]{1,0:T(8,128)(2,1)S(1)} %collective-permute-done.19.refs_2_, ...), custom_call_target="tpu_custom_call", output_to_operand_aliasing={{}: (10, {})} | custom-call | flops 268435456 | bytes 1835008 | tf_op jit(solution)/shard_map/last_narrow/pallas_call | solution.py:134
  174.3 2.0 %collective-permute-done.29 = bf16[64,256]{1,0:T(8,128)(2,1)S(1)} collective-permute-done((bf16[64,256]{1,0:T(8,128)(2,1)S(1)}, bf16[64,256]{1,0:T(8,128)(2,1)S(1)}, u32[]{:S(2)}, u32[]{:S(2)}) %collective-permute-start.29) | collective-permute-done | bytes 32800 | tf_op jit(solution)/shard_map/ppermute | solution.py:258
  177.8 2.5 %collective-permute-done.30 = bf16[64,256]{1,0:T(8,128)(2,1)S(1)} collective-permute-done((bf16[64,256]{1,0:T(8,128)(2,1)S(1)}, bf16[64,256]{1,0:T(8,128)(2,1)S(1)}, u32[]{:S(2)}, u32[]{:S(2)}) %collective-permute-start.30) | collective-permute-done | bytes 32800 | tf_op jit(solution)/shard_map/ppermute | solution.py:258
  182.1 9.3 %copy-done.1 = bf16[14336,1024]{1,0:T(8,128)(2,1)S(1)} copy-done((bf16[14336,1024]{1,0:T(8,128)(2,1)S(1)}, bf16[14336,1024]{1,0:T(8,128)(2,1)}, u32[]{:S(2)}) %copy-start.1) | copy-done | bytes 29360152
  191.4 2.8 %last_kept.1.kept = f32[256,512]{1,0:T(8,128)S(1)} custom-call(s32[18]{0:T(128)S(1)} %dynamic-slice_bitcast_fusion.scalars, bf16[32,2048]{1,0:T(8,128)(2,1)S(1)} %take_12288.1.refs_0_, bf16[32,2048]{1,0:T(8,128)(2,1)S(1)} %collective-permute-done.18.refs_1_, bf16[32,2048]{1,0:T(8,128)(2,1)S(1)} %collective-permute-done.19.refs_2_, ...), custom_call_target="tpu_custom_call", output_to_operand_aliasing={{}: (10, {})} | custom-call | flops 1073741824 | bytes 4194304 | tf_op jit(solution)/shard_map/last_kept/pallas_call | solution.py:134
  194.2 2.4 %expand_and_add.1 = bf16[256,512]{1,0:T(8,128)(2,1)} custom-call(bf16[64,256]{1,0:T(8,128)(2,1)S(1)} %add.31.shrunk, s32[256,1]{1,0:T(8,128)S(1)} %copy.18.slot, bf16[1024,512]{1,0:T(8,128)(2,1)S(1)} %bitcast.12, f32[256,512]{1,0:T(8,128)S(1)} %last_kept.1.kept, f32[256,512]{1,0:T(8,128)} %collective-permute-done.32.other), custom_call_target="tpu_custom_call" | custom-call | flops 268435456 | bytes 2359296 | tf_op jit(solution)/shard_map/expand_and_add/pallas_call | solution.py:172
  (127 shorter events, 39.8 us)
Async XLA Ops:
  1.1 9.3 %collective-permute-start = (bf16[32,4096]{1,0:T(8,128)(2,1)S(1)}, bf16[32,4096]{1,0:T(8,128)(2,1)S(1)}, u32[]{:S(2)}, u32[]{:S(2)}) collective-permute-start(bf16[32,4096]{1,0:T(8,128)(2,1)S(1)} %slice.9.refs_0_), channel_id=1, source_target_pairs={{0,4},{4,8},{8,12},{12,14},{14,10},{10,6},{6,2},{2,0},{1,5},{5,9},... | collective-permute-start | bytes 786440 | tf_op jit(solution)/shard_map/ppermute | solution.py:229
  15.3 85.9 %all-to-all-start = ((bf16[8,128,512]{2,1,0:T(8,128)(2,1)}), bf16[8,128,512]{2,1,0:T(8,128)(2,1)S(1)}, u32[]{:S(2)}, u32[]{:S(2)}) async-start(bf16[8,128,512]{2,1,0:T(8,128)(2,1)} %expand_blocks.1.refs_4_), calls=%async_computation | async-start | bytes 2097152 | tf_op jit(solution)/shard_map/all_to_all | solution.py:240
  21.5 20.4 %collective-permute-start.2 = (bf16[32,4096]{1,0:T(8,128)(2,1)S(1)}, bf16[32,4096]{1,0:T(8,128)(2,1)S(1)}, u32[]{:S(2)}, u32[]{:S(2)}) collective-permute-start(bf16[32,4096]{1,0:T(8,128)(2,1)S(1)} %slice.9.refs_0_), channel_id=1, source_target_pairs={{0,2},{4,0},{8,4},{12,8},{14,12},{10,14},{6,10},{2,6},{1,3},{5,1},... | collective-permute-start | bytes 786440 | tf_op jit(solution)/shard_map/ppermute | solution.py:229
  23.5 22.3 %collective-permute-start.1 = (bf16[32,4096]{1,0:T(8,128)(2,1)S(1)}, bf16[32,4096]{1,0:T(8,128)(2,1)S(1)}, u32[]{:S(2)}, u32[]{:S(2)}) collective-permute-start(bf16[32,4096]{1,0:T(8,128)(2,1)S(1)} %collective-permute-done.after.refs_1_), channel_id=1, source_target_pairs={{0,4},{4,8},{8,12},{12,14},{14,10},{10,6},{6,2},{2,0},{1,5},{5,9},... | collective-permute-start | bytes 786440 | tf_op jit(solution)/shard_map/ppermute | solution.py:229
  41.9 15.4 %collective-permute-start.3 = (bf16[32,4096]{1,0:T(8,128)(2,1)S(1)}, bf16[32,4096]{1,0:T(8,128)(2,1)S(1)}, u32[]{:S(2)}, u32[]{:S(2)}) collective-permute-start(bf16[32,4096]{1,0:T(8,128)(2,1)S(1)} %collective-permute-done.2.refs_5_), channel_id=1, source_target_pairs={{0,2},{4,0},{8,4},{12,8},{14,12},{10,14},{6,10},{2,6},{1,3},{5,1},... | collective-permute-start | bytes 786440 | tf_op jit(solution)/shard_map/ppermute | solution.py:229
  57.3 9.4 %collective-permute-start.6 = (bf16[32,4096]{1,0:T(8,128)(2,1)S(1)}, bf16[32,4096]{1,0:T(8,128)(2,1)S(1)}, u32[]{:S(2)}, u32[]{:S(2)}) collective-permute-start(bf16[32,4096]{1,0:T(8,128)(2,1)S(1)} %take_4096.1.refs_0_), channel_id=1, source_target_pairs={{0,2},{4,0},{8,4},{12,8},{14,12},{10,14},{6,10},{2,6},{1,3},{5,1},... | collective-permute-start | bytes 786440 | tf_op jit(solution)/shard_map/ppermute | solution.py:229
  57.9 9.7 %collective-permute-start.8 = (bf16[32,4096]{1,0:T(8,128)(2,1)S(1)}, bf16[32,4096]{1,0:T(8,128)(2,1)S(1)}, u32[]{:S(2)}, u32[]{:S(2)}) collective-permute-start(bf16[32,4096]{1,0:T(8,128)(2,1)S(1)} %collective-permute-done.1.refs_0_.refs_2_), channel_id=1, source_target_pairs={{0,4},{4,8},{8,12},{12,14},{14,10},{10,6},{6,2},{2,0},{1,5},{5,9},... | collective-permute-start | bytes 786440 | tf_op jit(solution)/shard_map/ppermute | solution.py:229
  59.7 13.5 %collective-permute-start.4 = (bf16[32,4096]{1,0:T(8,128)(2,1)S(1)}, bf16[32,4096]{1,0:T(8,128)(2,1)S(1)}, u32[]{:S(2)}, u32[]{:S(2)}) collective-permute-start(bf16[32,4096]{1,0:T(8,128)(2,1)S(1)} %take_4096.1.refs_0_), channel_id=1, source_target_pairs={{0,4},{4,8},{8,12},{12,14},{14,10},{10,6},{6,2},{2,0},{1,5},{5,9},... | collective-permute-start | bytes 786440 | tf_op jit(solution)/shard_map/ppermute | solution.py:229
  62.3 14.2 %collective-permute-start.10 = (bf16[32,4096]{1,0:T(8,128)(2,1)S(1)}, bf16[32,4096]{1,0:T(8,128)(2,1)S(1)}, u32[]{:S(2)}, u32[]{:S(2)}) collective-permute-start(bf16[32,4096]{1,0:T(8,128)(2,1)S(1)} %collective-permute-done.3.refs_1_.refs_6_), channel_id=1, source_target_pairs={{0,2},{4,0},{8,4},{12,8},{14,12},{10,14},{6,10},{2,6},{1,3},{5,1},... | collective-permute-start | bytes 786440 | tf_op jit(solution)/shard_map/ppermute | solution.py:229
  66.7 8.6 %collective-permute-start.7 = (bf16[32,4096]{1,0:T(8,128)(2,1)S(1)}, bf16[32,4096]{1,0:T(8,128)(2,1)S(1)}, u32[]{:S(2)}, u32[]{:S(2)}) collective-permute-start(bf16[32,4096]{1,0:T(8,128)(2,1)S(1)} %collective-permute-done.6.refs_4_), channel_id=1, source_target_pairs={{0,2},{4,0},{8,4},{12,8},{14,12},{10,14},{6,10},{2,6},{1,3},{5,1},... | collective-permute-start | bytes 786440 | tf_op jit(solution)/shard_map/ppermute | solution.py:229
  67.6 11.2 %collective-permute-start.9 = (bf16[32,4096]{1,0:T(8,128)(2,1)S(1)}, bf16[32,4096]{1,0:T(8,128)(2,1)S(1)}, u32[]{:S(2)}, u32[]{:S(2)}) collective-permute-start(bf16[32,4096]{1,0:T(8,128)(2,1)S(1)} %collective-permute-done.8.refs_3_), channel_id=1, source_target_pairs={{0,4},{4,8},{8,12},{12,14},{14,10},{10,6},{6,2},{2,0},{1,5},{5,9},... | collective-permute-start | bytes 786440 | tf_op jit(solution)/shard_map/ppermute | solution.py:229
  73.2 9.4 %collective-permute-start.5 = (bf16[32,4096]{1,0:T(8,128)(2,1)S(1)}, bf16[32,4096]{1,0:T(8,128)(2,1)S(1)}, u32[]{:S(2)}, u32[]{:S(2)}) collective-permute-start(bf16[32,4096]{1,0:T(8,128)(2,1)S(1)} %collective-permute-done.4.refs_1_), channel_id=1, source_target_pairs={{0,4},{4,8},{8,12},{12,14},{14,10},{10,6},{6,2},{2,0},{1,5},{5,9},... | collective-permute-start | bytes 786440 | tf_op jit(solution)/shard_map/ppermute | solution.py:229
  75.3 10.0 %collective-permute-start.16 = (bf16[32,4096]{1,0:T(8,128)(2,1)S(1)}, bf16[32,4096]{1,0:T(8,128)(2,1)}, u32[]{:S(2)}, u32[]{:S(2)}) collective-permute-start(bf16[32,4096]{1,0:T(8,128)(2,1)S(1)} %collective-permute-done.7.refs_1_.refs_5_), channel_id=1, source_target_pairs={{0,2},{4,0},{8,4},{12,8},{14,12},{10,14},{6,10},{2,6},{1,3},{5,1},... | collective-permute-start | bytes 786440 | tf_op jit(solution)/shard_map/ppermute | solution.py:229
  82.6 9.9 %collective-permute-start.11 = (bf16[32,4096]{1,0:T(8,128)(2,1)S(1)}, bf16[32,4096]{1,0:T(8,128)(2,1)}, u32[]{:S(2)}, u32[]{:S(2)}) collective-permute-start(bf16[32,4096]{1,0:T(8,128)(2,1)S(1)} %take_8192.1.refs_0_), channel_id=1, source_target_pairs={{0,4},{4,8},{8,12},{12,14},{14,10},{10,6},{6,2},{2,0},{1,5},{5,9},... | collective-permute-start | bytes 786440 | tf_op jit(solution)/shard_map/ppermute | solution.py:229
  82.7 9.8 %collective-permute-start.13 = (bf16[32,4096]{1,0:T(8,128)(2,1)S(1)}, bf16[32,4096]{1,0:T(8,128)(2,1)}, u32[]{:S(2)}, u32[]{:S(2)}) collective-permute-start(bf16[32,4096]{1,0:T(8,128)(2,1)S(1)} %take_8192.1.refs_0_), channel_id=1, source_target_pairs={{0,2},{4,0},{8,4},{12,8},{14,12},{10,14},{6,10},{2,6},{1,3},{5,1},... | collective-permute-start | bytes 786440 | tf_op jit(solution)/shard_map/ppermute | solution.py:229
  85.2 12.8 %collective-permute-start.15 = (bf16[32,4096]{1,0:T(8,128)(2,1)S(1)}, bf16[32,4096]{1,0:T(8,128)(2,1)S(1)}, u32[]{:S(2)}, u32[]{:S(2)}) collective-permute-start(bf16[32,4096]{1,0:T(8,128)(2,1)S(1)} %collective-permute-done.5.refs_0_.refs_2_), channel_id=1, source_target_pairs={{0,4},{4,8},{8,12},{12,14},{14,10},{10,6},{6,2},{2,0},{1,5},{5,9},... | collective-permute-start | bytes 786440 | tf_op jit(solution)/shard_map/ppermute | solution.py:229
  85.3 13.5 %collective-permute-start.17 = (bf16[32,4096]{1,0:T(8,128)(2,1)}, bf16[32,4096]{1,0:T(8,128)(2,1)}, u32[]{:S(2)}, u32[]{:S(2)}) collective-permute-start(bf16[32,4096]{1,0:T(8,128)(2,1)} %collective-permute-done.16.refs_6_), channel_id=1, source_target_pairs={{0,2},{4,0},{8,4},{12,8},{14,12},{10,14},{6,10},{2,6},{1,3},{5,1},... | collective-permute-start | bytes 786440 | tf_op jit(solution)/shard_map/ppermute | solution.py:229
  92.5 8.7 %collective-permute-start.12 = (bf16[32,4096]{1,0:T(8,128)(2,1)}, bf16[32,4096]{1,0:T(8,128)(2,1)}, u32[]{:S(2)}, u32[]{:S(2)}) collective-permute-start(bf16[32,4096]{1,0:T(8,128)(2,1)} %collective-permute-done.11.refs_1_), channel_id=1, source_target_pairs={{0,4},{4,8},{8,12},{12,14},{14,10},{10,6},{6,2},{2,0},{1,5},{5,9},... | collective-permute-start | bytes 786440 | tf_op jit(solution)/shard_map/ppermute | solution.py:229
  92.5 8.7 %collective-permute-start.14 = (bf16[32,4096]{1,0:T(8,128)(2,1)}, bf16[32,4096]{1,0:T(8,128)(2,1)S(1)}, u32[]{:S(2)}, u32[]{:S(2)}) collective-permute-start(bf16[32,4096]{1,0:T(8,128)(2,1)} %collective-permute-done.13.refs_5_), channel_id=1, source_target_pairs={{0,2},{4,0},{8,4},{12,8},{14,12},{10,14},{6,10},{2,6},{1,3},{5,1},... | collective-permute-start | bytes 786440 | tf_op jit(solution)/shard_map/ppermute | solution.py:229
  102.3 6.0 %collective-permute-start.21 = (bf16[32,2048]{1,0:T(8,128)(2,1)S(1)}, bf16[32,2048]{1,0:T(8,128)(2,1)S(1)}, u32[]{:S(2)}, u32[]{:S(2)}) collective-permute-start(bf16[32,2048]{1,0:T(8,128)(2,1)S(1)} %take_12288.1.refs_0_), channel_id=1, source_target_pairs={{0,2},{4,0},{8,4},{12,8},{14,12},{10,14},{6,10},{2,6},{1,3},{5,1},... | collective-permute-start | bytes 393224 | tf_op jit(solution)/shard_map/ppermute | solution.py:229
  104.1 27.1 %collective-permute-start.25 = (bf16[32,4096]{1,0:T(8,128)(2,1)}, bf16[32,4096]{1,0:T(8,128)(2,1)S(1)}, u32[]{:S(2)}, u32[]{:S(2)}) collective-permute-start(bf16[32,4096]{1,0:T(8,128)(2,1)} %collective-permute-done.12.refs_0_.refs_2_), channel_id=1, source_target_pairs={{0,4},{4,8},{8,12},{12,14},{14,10},{10,6},{6,2},{2,0},{1,5},{5,9},... | collective-permute-start | bytes 786440 | tf_op jit(solution)/shard_map/ppermute | solution.py:229
  104.4 26.9 %collective-permute-start.18 = (bf16[32,2048]{1,0:T(8,128)(2,1)S(1)}, bf16[32,2048]{1,0:T(8,128)(2,1)S(1)}, u32[]{:S(2)}, u32[]{:S(2)}) collective-permute-start(bf16[32,2048]{1,0:T(8,128)(2,1)S(1)} %take_12288.1.refs_0_), channel_id=1, source_target_pairs={{0,4},{4,8},{8,12},{12,14},{14,10},{10,6},{6,2},{2,0},{1,5},{5,9},... | collective-permute-start | bytes 393224 | tf_op jit(solution)/shard_map/ppermute | solution.py:229
  108.4 23.1 %collective-permute-start.22 = (bf16[32,2048]{1,0:T(8,128)(2,1)S(1)}, bf16[32,2048]{1,0:T(8,128)(2,1)S(1)}, u32[]{:S(2)}, u32[]{:S(2)}) collective-permute-start(bf16[32,2048]{1,0:T(8,128)(2,1)S(1)} %collective-permute-done.21.refs_4_), channel_id=1, source_target_pairs={{0,2},{4,0},{8,4},{12,8},{14,12},{10,14},{6,10},{2,6},{1,3},{5,1},... | collective-permute-start | bytes 393224 | tf_op jit(solution)/shard_map/ppermute | solution.py:229
  129.3 16.8 %collective-permute-start.27 = (bf16[32,4096]{1,0:T(8,128)(2,1)S(1)}, bf16[32,4096]{1,0:T(8,128)(2,1)S(1)}, u32[]{:S(2)}, u32[]{:S(2)}) collective-permute-start(bf16[32,4096]{1,0:T(8,128)(2,1)S(1)} %copy-done.9), channel_id=1, source_target_pairs={{0,2},{4,0},{8,4},{12,8},{14,12},{10,14},{6,10},{2,6},{1,3},{5,1},... | collective-permute-start | bytes 786440 | tf_op jit(solution)/shard_map/ppermute | solution.py:229
  131.2 14.9 %collective-permute-start.26 = (bf16[32,4096]{1,0:T(8,128)(2,1)S(1)}, bf16[32,4096]{1,0:T(8,128)(2,1)S(1)}, u32[]{:S(2)}, u32[]{:S(2)}) collective-permute-start(bf16[32,4096]{1,0:T(8,128)(2,1)S(1)} %collective-permute-done.25.refs_3_), channel_id=1, source_target_pairs={{0,4},{4,8},{8,12},{12,14},{14,10},{10,6},{6,2},{2,0},{1,5},{5,9},... | collective-permute-start | bytes 786440 | tf_op jit(solution)/shard_map/ppermute | solution.py:229
  131.4 12.6 %collective-permute-start.19 = (bf16[32,2048]{1,0:T(8,128)(2,1)S(1)}, bf16[32,2048]{1,0:T(8,128)(2,1)S(1)}, u32[]{:S(2)}, u32[]{:S(2)}) collective-permute-start(bf16[32,2048]{1,0:T(8,128)(2,1)S(1)} %collective-permute-done.18.refs_1_), channel_id=1, source_target_pairs={{0,4},{4,8},{8,12},{12,14},{14,10},{10,6},{6,2},{2,0},{1,5},{5,9},... | collective-permute-start | bytes 393224 | tf_op jit(solution)/shard_map/ppermute | solution.py:229
  131.5 12.7 %collective-permute-start.23 = (bf16[32,2048]{1,0:T(8,128)(2,1)S(1)}, bf16[32,2048]{1,0:T(8,128)(2,1)S(1)}, u32[]{:S(2)}, u32[]{:S(2)}) collective-permute-start(bf16[32,2048]{1,0:T(8,128)(2,1)S(1)} %collective-permute-done.22.refs_5_), channel_id=1, source_target_pairs={{0,2},{4,0},{8,4},{12,8},{14,12},{10,14},{6,10},{2,6},{1,3},{5,1},... | collective-permute-start | bytes 393224 | tf_op jit(solution)/shard_map/ppermute | solution.py:229
  144.0 12.3 %collective-permute-start.20 = (bf16[32,2048]{1,0:T(8,128)(2,1)S(1)}, bf16[32,2048]{1,0:T(8,128)(2,1)S(1)}, u32[]{:S(2)}, u32[]{:S(2)}) collective-permute-start(bf16[32,2048]{1,0:T(8,128)(2,1)S(1)} %collective-permute-done.19.refs_2_), channel_id=1, source_target_pairs={{0,4},{4,8},{8,12},{12,14},{14,10},{10,6},{6,2},{2,0},{1,5},{5,9},... | collective-permute-start | bytes 393224 | tf_op jit(solution)/shard_map/ppermute | solution.py:229
  144.2 12.1 %collective-permute-start.24 = (bf16[32,2048]{1,0:T(8,128)(2,1)S(1)}, bf16[32,2048]{1,0:T(8,128)(2,1)S(1)}, u32[]{:S(2)}, u32[]{:S(2)}) collective-permute-start(bf16[32,2048]{1,0:T(8,128)(2,1)S(1)} %collective-permute-done.23.refs_6_), channel_id=1, source_target_pairs={{0,2},{4,0},{8,4},{12,8},{14,12},{10,14},{6,10},{2,6},{1,3},{5,1},... | collective-permute-start | bytes 393224 | tf_op jit(solution)/shard_map/ppermute | solution.py:229
  168.4 25.8 %collective-permute-start.32 = (f32[256,512]{1,0:T(8,128)S(1)}, f32[256,512]{1,0:T(8,128)}, u32[]{:S(2)}, u32[]{:S(2)}) collective-permute-start(f32[256,512]{1,0:T(8,128)S(1)} %last_sent.1), channel_id=1, source_target_pairs={{0,1},{1,0},{2,3},{3,2},{4,5},{5,4},{6,7},{7,6},{8,9},{9,8},{10,11... | collective-permute-start | bytes 1572872 | tf_op jit(solution)/shard_map/ppermute | solution.py:255
  172.3 4.0 %collective-permute-start.29 = (bf16[64,256]{1,0:T(8,128)(2,1)S(1)}, bf16[64,256]{1,0:T(8,128)(2,1)S(1)}, u32[]{:S(2)}, u32[]{:S(2)}) collective-permute-start(bf16[64,256]{1,0:T(8,128)(2,1)S(1)} %add_convert_fusion), channel_id=1, source_target_pairs={{0,2},{2,0},{4,6},{6,4},{8,10},{10,8},{12,14},{14,12},{1,3},{3,1},... | collective-permute-start | bytes 98312 | tf_op jit(solution)/shard_map/ppermute | solution.py:258
  180.3 13.9 %collective-permute-start.31 = (bf16[64,256]{1,0:T(8,128)(2,1)S(1)}, bf16[64,256]{1,0:T(8,128)(2,1)S(1)}, u32[]{:S(2)}, u32[]{:S(2)}) collective-permute-start(bf16[64,256]{1,0:T(8,128)(2,1)S(1)} %add.30), channel_id=1, source_target_pairs={{0,8},{2,10},{4,12},{6,14},{8,0},{10,2},{12,4},{14,6},{1,9},{3,11}... | collective-permute-start | bytes 98312 | tf_op jit(solution)/shard_map/ppermute | solution.py:258
  (37 other events, 570.3 us)

commit v3 on v2

--- a/solution.py
+++ b/solution.py
@@ -9,7 +9,7 @@
 from jax.sharding import PartitionSpec as P
 
 F32, BF16 = jnp.float32, jnp.bfloat16
-TILE = 512
+TILE = 1024
 MIB = 2**20
 
 
@@ -36,17 +36,17 @@
         out_specs=pl.BlockSpec(memory_space=pl.ANY),
         scratch_shapes=[pltpu.SemaphoreType.DMA],
         out_shape=jax.ShapeDtypeStruct((rows, width), BF16),
-        compiler_params=params(1),
+        compiler_params=params(40),
         cost_estimate=pl.CostEstimate(flops=0, bytes_accessed=4 * rows * width, transcendentals=0),
         name=f"take_{start}",
     )(hidden, *after)
 
 
-def split_kernel(scalars, src, after, dst):
+def split_kernel(scalars, src, dst):
     dst[...] = src[...][None]
 
 
-def expand_blocks(scalars, half, expand, n, cores, after):
+def expand_blocks(scalars, half, expand, n, cores):
     owned, rank, width = expand.shape
     rows = owned * rank
     share = width // (n * cores)
@@ -55,21 +55,18 @@
         grid_spec=pltpu.PrefetchScalarGridSpec(
             num_scalar_prefetch=1,
             grid=(n,),
-            in_specs=[
-                pl.BlockSpec((rows, share), lambda s, t: (0, s * cores + t[half])),
-                pl.BlockSpec(memory_space=pl.ANY),
-            ],
+            in_specs=[pl.BlockSpec((rows, share), lambda s, t: (0, s * cores + t[half]))],
             out_specs=pl.BlockSpec((1, rows, share), lambda s, t: (s, 0, 0)),
         ),
         out_shape=jax.ShapeDtypeStruct((n, rows, share), BF16),
-        compiler_params=params(8),
+        compiler_params=params(40),
         cost_estimate=pl.CostEstimate(flops=0, bytes_accessed=4 * n * rows * share, transcendentals=0),
         name="expand_blocks",
-    )(scalars, expand.reshape(rows, width), after)
-
-
-def matmul_kernel(n, base, sides, narrow, has_acc, scalars, *refs):
-    refs = list(refs)
+    )(scalars, expand.reshape(rows, width))
+
+
+def matmul_kernel(n, base, sides, narrow, has_acc, waits, scalars, *refs):
+    refs = list(refs)[waits:]
     pieces = [refs.pop(0) for _ in range(n)]
     weights = [refs.pop(0) for _ in range(sides)]
     shrink = refs.pop(0) if narrow else None
@@ -108,15 +105,15 @@
         after[i][...] += jnp.dot(left, weights[i][...], preferred_element_type=F32)
 
 
-def chunk_matmul(scalars, base, half, pieces, down, shrink, acc, start, sides, narrow, label):
+def chunk_matmul(scalars, base, half, pieces, down, shrink, acc, start, sides, narrow, label, after=()):
     n = len(pieces)
     rows, width = pieces[0].shape[0] * n, pieces[0].shape[1]
     share = down.shape[1] // 2
     steps = width // TILE
     first = start // TILE
     ranks = shrink.shape[0]
-    in_specs = [pl.BlockSpec(memory_space=pl.ANY) for _ in pieces]
-    args = list(pieces)
+    in_specs = [pl.BlockSpec(memory_space=pl.ANY) for _ in (*after, *pieces)]
+    args = [*after, *pieces]
     for side in sides:
         in_specs.append(pl.BlockSpec((TILE, share), functools.partial(lambda side, k, s: (first + k, s[half + side]), side)))
         args.append(down)
@@ -132,7 +129,7 @@
         args += list(acc)
     columns = share * len(sides) + ranks * narrow
     return pl.pallas_call(
-        functools.partial(matmul_kernel, n, base, len(sides), narrow, acc is not None),
+        functools.partial(matmul_kernel, n, base, len(sides), narrow, acc is not None, len(after)),
         grid_spec=pltpu.PrefetchScalarGridSpec(
             num_scalar_prefetch=1,
             grid=(steps,),
@@ -142,7 +139,7 @@
         ),
         out_shape=[jax.ShapeDtypeStruct(shape, F32) for shape in shapes],
         input_output_aliases=aliases,
-        compiler_params=params(24),
+        compiler_params=params(40),
         cost_estimate=pl.CostEstimate(
             flops=4 * rows * width * columns,
             bytes_accessed=2 * width * (columns + rows) + 8 * rows * columns,
@@ -175,7 +172,7 @@
         out_specs=pl.BlockSpec(memory_space=pltpu.VMEM),
         scratch_shapes=[pltpu.VMEM((rows, n * wide), BF16)],
         out_shape=jax.ShapeDtypeStruct((rows, share), BF16),
-        compiler_params=params(24),
+        compiler_params=params(40),
         cost_estimate=pl.CostEstimate(
             flops=2 * rows * share * n * wide,
             bytes_accessed=2 * n * wide * share + 10 * rows * share,
@@ -213,14 +210,17 @@
         row_slot = jnp.sum(jnp.where(row_adapter[None, :] == slots[:, None], adapter_slot[:, None], 0), axis=0)
 
         tiles = units // TILE
-        small = tiles // 7
-        widths = [(tiles - small) // 3 * TILE] * 3 + [small * TILE]
-        widths[0] += units - sum(widths)
-
-        acc, ends = None, []
+        large = (tiles + 2) // 4 * TILE
+        small = (units - 2 * large) // (2 * TILE) * TILE
+        widths = [units - 2 * large - small, large, large, small]
+
+        acc = None
         start = 0
+        after = {}
+        blocks = expand_blocks(scalars, half, expand, n, cores)
+        factors = lax.all_to_all(blocks, "store", 0, 0)
         for chunk, width in enumerate(widths):
-            own = hidden[:, :width] if chunk == 0 else take(hidden, start, width, after)
+            own = take(hidden, start, width, after[chunk]) if chunk in after else hidden[:, start:start + width]
             way = chunk % 2
             pieces = [own]
             for length, pairs in zip(((long, short), (short, long))[way], (clockwise, counter)):
@@ -228,29 +228,23 @@
                 for step in range(length):
                     moving = lax.ppermute(moving, "store", pairs)
                     pieces.append(moving)
-            turn = (long, short)[way]
-            after = [pieces[2], pieces[turn + 2], *ends]
-            ends = [pieces[turn], pieces[-1]]
+            if chunk == 0:
+                after[2] = [pieces[(long, short)[way]], pieces[-1], blocks]
             if chunk == 1:
-                after.append(blocks)
-            if chunk == 2:
-                after.append(factors)
-            if chunk == 0:
-                blocks = expand_blocks(scalars, half, expand, n, cores, pieces[1])
-                factors = lax.all_to_all(blocks, "store", 0, 0)
+                after[3] = [pieces[(long, short)[way]], pieces[-1], factors]
             call = functools.partial(chunk_matmul, scalars, way * n, half, pieces, down, shrink_rows)
             if chunk < len(widths) - 1:
                 acc = call(acc, start, (0, 1), True, f"chunk_{chunk}")
             else:
                 narrow, = call(acc[2:], start, (), True, "last_narrow")
-                send, = call(acc[1:2], start, (1,), False, "last_sent")
-                kept, = call(acc[:1], start, (0,), False, "last_kept")
+                mine = [
+                    jnp.where((row_slot == store * owned + i)[None, :], narrow[i * rank:(i + 1) * rank], 0.0)
+                    for i in range(owned)
+                ]
+                mine = sum(mine[1:], mine[0])
+                send, = call(acc[1:2], start, (1,), False, "last_sent", [mine])
+                kept, = call(acc[:1], start, (0,), False, "last_kept", [send])
             start += width
-        mine = [
-            jnp.where((row_slot == store * owned + i)[None, :], narrow[i * rank:(i + 1) * rank], 0.0)
-            for i in range(owned)
-        ]
-        mine = sum(mine[1:], mine[0])
         shrunk = (mine + lax.ppermute(mine, "tensor", swap)).astype(BF16)
         other = lax.ppermute(send, "tensor", swap)
         bit = 1

time: 198 us -> 161 us (0.81)
  waiting for transfers between devices: 69.6 us -> 38.8 us
  local copies, waits for them, and re-layouts: 35.5 us -> 18.7 us
  starting transfers between devices: 46.5 us -> 60.5 us
  Pallas kernels: 44.7 us -> 40.9 us
    ppermute x28, waiting for transfers between devices: 64.1 us -> 32.2 us  [shards(): moving = lax.ppermute(moving, 'store', pairs)]
    unnamed x70 -> x74, local copies, waits for them, and re-layouts: 33.6 us -> 17.1 us
    ppermute x28, starting transfers between devices: 34.6 us -> 49 us  [shards(): moving = lax.ppermute(moving, 'store', pairs)]
    pallas_call x6, Pallas kernels: 38.9 us -> 35.1 us  [chunk_matmul(): pl.pallas_call(functools.partial(matmul_kernel, n, base, len(sides), narr...]
  transfers between devices with their start and end apart: 34 -> 34, of which waited for: 15 -> 11; matrix products, arithmetic and copies ran while one was open for 0% -> 1% of each run, Pallas kernels for 18% -> 17%
where the time goes in v3:
time: 161 us; the launch traced here: 160 us
  starting transfers between devices  60.5 us (38%)
  Pallas kernels  40.9 us (25%)
  waiting for transfers between devices  38.8 us (24%)
  local copies, waits for them, and re-layouts  18.7 us (12%)
    ppermute x28, starting transfers between devices, shards(): moving = lax.ppermute(moving, 'store', pairs)  49 us
    pallas_call x6, Pallas kernels, chunk_matmul(): pl.pallas_call(functools.partial(matmul_kernel, n, base, len(sides), narr...  35.1 us
    ppermute x28, waiting for transfers between devices, shards(): moving = lax.ppermute(moving, 'store', pairs)  32.2 us
    unnamed x74, local copies, waits for them, and re-layouts  17.1 us
    all_to_all x1, starting transfers between devices, shards(): factors = lax.all_to_all(blocks, 'store', 0, 0)  7.28 us
    ppermute x3, waiting for transfers between devices, shards(): lax.ppermute(shrunk, 'store', [(s, s ^ bit) for s in range(n)])  5.1 us
    ppermute x3, starting transfers between devices, shards(): lax.ppermute(shrunk, 'store', [(s, s ^ bit) for s in range(n)])  3.71 us
    pallas_call x1, Pallas kernels, expand_blocks(): pl.pallas_call(split_kernel, grid_spec=pltpu.PrefetchScalarGridSpec(num_s...  3.33 us
  transfers between devices with their start and end apart: 34, of which 11 were waited for; matrix products, arithmetic and copies ran while one was open for 1% of the time, Pallas kernels for 17%

profile of v3, /device:TPU:0, one launch (start us, length us, event | category | flops | bytes accessed | tf_op | source)
XLA Modules:
  0.0 160.2 jit_solution(15997237294177360704)
XLA Ops:
  2.4 3.3 %expand_blocks.1.refs_2_ = bf16[8,128,512]{2,1,0:T(8,128)(2,1)} custom-call(s32[18]{0:T(128)S(1)} %dynamic-slice_bitcast_fusion.scalars, bf16[128,8192]{1,0:T(8,128)(2,1)S(1)} %bitcast.13), custom_call_target="tpu_custom_call" | custom-call | bytes 2097152 | tf_op jit(solution)/shard_map/expand_blocks/pallas_call | solution.py:53
  5.7 7.3 %all-to-all-start = ((bf16[8,128,512]{2,1,0:T(8,128)(2,1)}), bf16[8,128,512]{2,1,0:T(8,128)(2,1)S(1)}, u32[]{:S(2)}, u32[]{:S(2)}) async-start(bf16[8,128,512]{2,1,0:T(8,128)(2,1)} %expand_blocks.1.refs_2_), calls=%async_computation | async-start | bytes 2097152 | tf_op jit(solution)/shard_map/all_to_all | solution.py:221
  13.0 2.1 %collective-permute-start.14 = (bf16[32,3072]{1,0:T(8,128)(2,1)S(1)}, bf16[32,3072]{1,0:T(8,128)(2,1)S(1)}, u32[]{:S(2)}, u32[]{:S(2)}) collective-permute-start(bf16[32,3072]{1,0:T(8,128)(2,1)S(1)} %slice.13.refs_0_), channel_id=1, source_target_pairs={{0,4},{4,8},{8,12},{12,14},{14,10},{10,6},{6,2},{2,0},{1,5},{5,9},... | collective-permute-start | bytes 589832 | tf_op jit(solution)/shard_map/ppermute | solution.py:229
  15.2 2.0 %collective-permute-start.18 = (bf16[32,3072]{1,0:T(8,128)(2,1)S(1)}, bf16[32,3072]{1,0:T(8,128)(2,1)S(1)}, u32[]{:S(2)}, u32[]{:S(2)}) collective-permute-start(bf16[32,3072]{1,0:T(8,128)(2,1)S(1)} %slice.13.refs_0_), channel_id=1, source_target_pairs={{0,2},{4,0},{8,4},{12,8},{14,12},{10,14},{6,10},{2,6},{1,3},{5,1},... | collective-permute-start | bytes 589832 | tf_op jit(solution)/shard_map/ppermute | solution.py:229
  17.2 17.1 %collective-permute-done.14.refs_1_ = bf16[32,3072]{1,0:T(8,128)(2,1)S(1)} collective-permute-done((bf16[32,3072]{1,0:T(8,128)(2,1)S(1)}, bf16[32,3072]{1,0:T(8,128)(2,1)S(1)}, u32[]{:S(2)}, u32[]{:S(2)}) %collective-permute-start.14) | collective-permute-done | bytes 196640 | tf_op jit(solution)/shard_map/ppermute | solution.py:229
  34.3 7.0 %collective-permute-start.15 = (bf16[32,3072]{1,0:T(8,128)(2,1)S(1)}, bf16[32,3072]{1,0:T(8,128)(2,1)S(1)}, u32[]{:S(2)}, u32[]{:S(2)}) collective-permute-start(bf16[32,3072]{1,0:T(8,128)(2,1)S(1)} %collective-permute-done.14.refs_1_), channel_id=1, source_target_pairs={{0,4},{4,8},{8,12},{12,14},{14,10},{10,6},{6,2},{2,0},{1,5},{5,9},... | collective-permute-start | bytes 589832 | tf_op jit(solution)/shard_map/ppermute | solution.py:229
  42.0 2.5 %collective-permute-start = (bf16[32,4096]{1,0:T(8,128)(2,1)S(1)}, bf16[32,4096]{1,0:T(8,128)(2,1)S(1)}, u32[]{:S(2)}, u32[]{:S(2)}) collective-permute-start(bf16[32,4096]{1,0:T(8,128)(2,1)S(1)} %slice.12.refs_0_), channel_id=1, source_target_pairs={{0,4},{4,8},{8,12},{12,14},{14,10},{10,6},{6,2},{2,0},{1,5},{5,9},... | collective-permute-start | bytes 786440 | tf_op jit(solution)/shard_map/ppermute | solution.py:229
  47.0 4.3 %collective-permute-start.16 = (bf16[32,3072]{1,0:T(8,128)(2,1)S(1)}, bf16[32,3072]{1,0:T(8,128)(2,1)S(1)}, u32[]{:S(2)}, u32[]{:S(2)}) collective-permute-start(bf16[32,3072]{1,0:T(8,128)(2,1)S(1)} %collective-permute-done.15.refs_2_), channel_id=1, source_target_pairs={{0,4},{4,8},{8,12},{12,14},{14,10},{10,6},{6,2},{2,0},{1,5},{5,9},... | collective-permute-start | bytes 589832 | tf_op jit(solution)/shard_map/ppermute | solution.py:229
  52.0 4.4 %collective-permute-done.19.refs_6_ = bf16[32,3072]{1,0:T(8,128)(2,1)S(1)} collective-permute-done((bf16[32,3072]{1,0:T(8,128)(2,1)S(1)}, bf16[32,3072]{1,0:T(8,128)(2,1)S(1)}, u32[]{:S(2)}, u32[]{:S(2)}) %collective-permute-start.19) | collective-permute-done | bytes 196640 | tf_op jit(solution)/shard_map/ppermute | solution.py:229
  57.3 2.4 %collective-permute-start.17 = (bf16[32,3072]{1,0:T(8,128)(2,1)S(1)}, bf16[32,3072]{1,0:T(8,128)(2,1)S(1)}, u32[]{:S(2)}, u32[]{:S(2)}) collective-permute-start(bf16[32,3072]{1,0:T(8,128)(2,1)S(1)} %collective-permute-done.16.refs_3_), channel_id=1, source_target_pairs={{0,4},{4,8},{8,12},{12,14},{14,10},{10,6},{6,2},{2,0},{1,5},{5,9},... | collective-permute-start | bytes 589832 | tf_op jit(solution)/shard_map/ppermute | solution.py:229
  60.4 2.0 %collective-permute-start.1 = (bf16[32,4096]{1,0:T(8,128)(2,1)S(1)}, bf16[32,4096]{1,0:T(8,128)(2,1)}, u32[]{:S(2)}, u32[]{:S(2)}) collective-permute-start(bf16[32,4096]{1,0:T(8,128)(2,1)S(1)} %collective-permute-done.refs_1_), channel_id=1, source_target_pairs={{0,4},{4,8},{8,12},{12,14},{14,10},{10,6},{6,2},{2,0},{1,5},{5,9},... | collective-permute-start | bytes 786440 | tf_op jit(solution)/shard_map/ppermute | solution.py:229
  62.8 2.3 %collective-permute-done.17.refs_0_.refs_4_ = bf16[32,3072]{1,0:T(8,128)(2,1)S(1)} collective-permute-done((bf16[32,3072]{1,0:T(8,128)(2,1)S(1)}, bf16[32,3072]{1,0:T(8,128)(2,1)S(1)}, u32[]{:S(2)}, u32[]{:S(2)}) %collective-permute-start.17) | collective-permute-done | bytes 196640 | tf_op jit(solution)/shard_map/ppermute | solution.py:229
  65.1 2.5 %collective-permute-start.21 = (bf16[32,4096]{1,0:T(8,128)(2,1)S(1)}, bf16[32,4096]{1,0:T(8,128)(2,1)}, u32[]{:S(2)}, u32[]{:S(2)}) collective-permute-start(bf16[32,4096]{1,0:T(8,128)(2,1)S(1)} %take_7168.1.refs_0_), channel_id=1, source_target_pairs={{0,4},{4,8},{8,12},{12,14},{14,10},{10,6},{6,2},{2,0},{1,5},{5,9},... | collective-permute-start | bytes 786440 | tf_op jit(solution)/shard_map/ppermute | solution.py:229
  67.6 3.2 %collective-permute-done.1.refs_2_ = bf16[32,4096]{1,0:T(8,128)(2,1)} collective-permute-done((bf16[32,4096]{1,0:T(8,128)(2,1)S(1)}, bf16[32,4096]{1,0:T(8,128)(2,1)}, u32[]{:S(2)}, u32[]{:S(2)}) %collective-permute-start.1) | collective-permute-done | bytes 262176 | tf_op jit(solution)/shard_map/ppermute | solution.py:229
  70.8 2.4 %collective-permute-start.2 = (bf16[32,4096]{1,0:T(8,128)(2,1)}, bf16[32,4096]{1,0:T(8,128)(2,1)S(1)}, u32[]{:S(2)}, u32[]{:S(2)}) collective-permute-start(bf16[32,4096]{1,0:T(8,128)(2,1)} %collective-permute-done.1.refs_2_), channel_id=1, source_target_pairs={{0,4},{4,8},{8,12},{12,14},{14,10},{10,6},{6,2},{2,0},{1,5},{5,9},... | collective-permute-start | bytes 786440 | tf_op jit(solution)/shard_map/ppermute | solution.py:229
  73.2 2.1 %collective-permute-start.25 = (bf16[32,4096]{1,0:T(8,128)(2,1)S(1)}, bf16[32,4096]{1,0:T(8,128)(2,1)}, u32[]{:S(2)}, u32[]{:S(2)}) collective-permute-start(bf16[32,4096]{1,0:T(8,128)(2,1)S(1)} %take_7168.1.refs_0_), channel_id=1, source_target_pairs={{0,2},{4,0},{8,4},{12,8},{14,12},{10,14},{6,10},{2,6},{1,3},{5,1},... | collective-permute-start | bytes 786440 | tf_op jit(solution)/shard_map/ppermute | solution.py:229
  76.4 2.4 %collective-permute-start.22 = (bf16[32,4096]{1,0:T(8,128)(2,1)}, bf16[32,4096]{1,0:T(8,128)(2,1)}, u32[]{:S(2)}, u32[]{:S(2)}) collective-permute-start(bf16[32,4096]{1,0:T(8,128)(2,1)} %collective-permute-done.21.refs_1_), channel_id=1, source_target_pairs={{0,4},{4,8},{8,12},{12,14},{14,10},{10,6},{6,2},{2,0},{1,5},{5,9},... | collective-permute-start | bytes 786440 | tf_op jit(solution)/shard_map/ppermute | solution.py:229
  78.9 3.0 %collective-permute-done.2.refs_0_.refs_3_ = bf16[32,4096]{1,0:T(8,128)(2,1)S(1)} collective-permute-done((bf16[32,4096]{1,0:T(8,128)(2,1)}, bf16[32,4096]{1,0:T(8,128)(2,1)S(1)}, u32[]{:S(2)}, u32[]{:S(2)}) %collective-permute-start.2) | collective-permute-done | bytes 262176 | tf_op jit(solution)/shard_map/ppermute | solution.py:229
  82.1 2.4 %collective-permute-start.10 = (bf16[32,3072]{1,0:T(8,128)(2,1)S(1)}, bf16[32,3072]{1,0:T(8,128)(2,1)S(1)}, u32[]{:S(2)}, u32[]{:S(2)}) collective-permute-start(bf16[32,3072]{1,0:T(8,128)(2,1)S(1)} %take_11264.1.refs_0_.refs_1_), channel_id=1, source_target_pairs={{0,2},{4,0},{8,4},{12,8},{14,12},{10,14},{6,10},{2,6},{1,3},{5,1},... | collective-permute-start | bytes 589832 | tf_op jit(solution)/shard_map/ppermute | solution.py:229
  84.5 2.1 %collective-permute-start.26 = (bf16[32,4096]{1,0:T(8,128)(2,1)}, bf16[32,4096]{1,0:T(8,128)(2,1)S(1)}, u32[]{:S(2)}, u32[]{:S(2)}) collective-permute-start(bf16[32,4096]{1,0:T(8,128)(2,1)} %collective-permute-done.25.refs_5_), channel_id=1, source_target_pairs={{0,2},{4,0},{8,4},{12,8},{14,12},{10,14},{6,10},{2,6},{1,3},{5,1},... | collective-permute-start | bytes 786440 | tf_op jit(solution)/shard_map/ppermute | solution.py:229
  90.2 2.1 %collective-permute-start.11 = (bf16[32,3072]{1,0:T(8,128)(2,1)S(1)}, bf16[32,3072]{1,0:T(8,128)(2,1)S(1)}, u32[]{:S(2)}, u32[]{:S(2)}) collective-permute-start(bf16[32,3072]{1,0:T(8,128)(2,1)S(1)} %collective-permute-done.10.refs_4_.refs_5_), channel_id=1, source_target_pairs={{0,2},{4,0},{8,4},{12,8},{14,12},{10,14},{6,10},{2,6},{1,3},{5,1},... | collective-permute-start | bytes 589832 | tf_op jit(solution)/shard_map/ppermute | solution.py:229
  92.3 2.0 %copy-done = bf16[2,14336,64]{1,2,0:T(8,128)(2,1)S(1)} copy-done((bf16[2,14336,64]{1,2,0:T(8,128)(2,1)S(1)}, bf16[2,14336,64]{1,2,0:T(8,128)(2,1)}, u32[]{:S(2)}) %copy-start) | copy-done | bytes 3670040
  101.8 6.7 %chunk_0.1 = (f32[256,512]{1,0:T(8,128)S(1)}, f32[256,512]{1,0:T(8,128)S(1)}, f32[128,256]{1,0:T(8,128)S(1)}) custom-call(s32[18]{0:T(128)S(1)} %dynamic-slice_bitcast_fusion.scalars, bf16[32,3072]{1,0:T(8,128)(2,1)S(1)} %copy-done.17, bf16[32,3072]{1,0:T(8,128)(2,1)S(1)} %copy-done.26, bf16[32,3072]{1,0:T(8,128)(2,1)S(1)} %copy-done.30, ...), custom_call_target="tpu_custom_call" | custom-call | flops 3623878656 | bytes 11010048 | tf_op jit(solution)/shard_map/chunk_0/pallas_call | solution.py:131
  108.5 2.1 %collective-permute-start.27 = (bf16[32,4096]{1,0:T(8,128)(2,1)S(1)}, bf16[32,4096]{1,0:T(8,128)(2,1)S(1)}, u32[]{:S(2)}, u32[]{:S(2)}) collective-permute-start(bf16[32,4096]{1,0:T(8,128)(2,1)S(1)} %collective-permute-done.26.refs_6_), channel_id=1, source_target_pairs={{0,2},{4,0},{8,4},{12,8},{14,12},{10,14},{6,10},{2,6},{1,3},{5,1},... | collective-permute-start | bytes 786440 | tf_op jit(solution)/shard_map/ppermute | solution.py:229
  113.7 8.3 %chunk_1.1 = (f32[256,512]{1,0:T(8,128)S(1)}, f32[256,512]{1,0:T(8,128)S(1)}, f32[128,256]{1,0:T(8,128)S(1)}) custom-call(s32[18]{0:T(128)S(1)} %dynamic-slice_bitcast_fusion.scalars, bf16[32,4096]{1,0:T(8,128)(2,1)S(1)} %slice.12.refs_0_, bf16[32,4096]{1,0:T(8,128)(2,1)S(1)} %copy-done.22, ...), custom_call_target="tpu_custom_call", output_to_operand_aliasing={{0}: (12, {}), {1}: (13, {}), {2}: (14, {})} | custom-call | flops 4831838208 | bytes 13893632 | tf_op jit(solution)/shard_map/chunk_1/pallas_call | solution.py:131
  124.1 8.2 %chunk_2.1 = (f32[256,512]{1,0:T(8,128)S(1)}, f32[256,512]{1,0:T(8,128)S(1)}, f32[128,256]{1,0:T(8,128)S(1)}) custom-call(s32[18]{0:T(128)S(1)} %dynamic-slice_bitcast_fusion.scalars, bf16[32,4096]{1,0:T(8,128)(2,1)S(1)} %copy-done.7, ...), custom_call_target="tpu_custom_call", output_to_operand_aliasing={{0}: (12, {}), {1}: (13, {}), {2}: (14, {})} | custom-call | flops 4831838208 | bytes 13893632 | tf_op jit(solution)/shard_map/chunk_2/pallas_call | solution.py:131
  132.3 2.4 %last_narrow.1 = f32[128,256]{1,0:T(8,128)S(1)} custom-call(s32[18]{0:T(128)S(1)} %dynamic-slice_bitcast_fusion.scalars, bf16[32,3072]{1,0:T(8,128)(2,1)S(1)} %take_11264.1.refs_0_.refs_1_, bf16[32,3072]{1,0:T(8,128)(2,1)S(1)} %collective-permute-done.7.refs_1_.refs_2_, ...), custom_call_target="tpu_custom_call", output_to_operand_aliasing={{}: (10, {})} | custom-call | flops 402653184 | bytes 2621440 | tf_op jit(solution)/shard_map/last_narrow/pallas_call | solution.py:131
  134.8 4.8 %last_sent.1.refs_0_ = f32[256,512]{1,0:T(8,128)S(1)} custom-call(s32[18]{0:T(128)S(1)} %dynamic-slice_bitcast_fusion.scalars, f32[64,256]{1,0:T(8,128)S(1)} %fusion.refs_0_, bf16[32,3072]{1,0:T(8,128)(2,1)S(1)} %take_11264.1.refs_0_.refs_1_, bf16[32,3072]{1,0:T(8,128)(2,1)S(1)} %collective-permute-done.7.refs_1_.refs_2_, ...), custom_call_target="tpu_custom_call", output_to_operand_aliasing={{}: (11, {})} | custom-call | flops 1610612736 | bytes 5767168 | tf_op jit(solution)/shard_map/last_sent/pallas_call | solution.py:131
  141.7 2.0 %collective-permute-start.29 = (bf16[64,256]{1,0:T(8,128)(2,1)S(1)}, bf16[64,256]{1,0:T(8,128)(2,1)S(1)}, u32[]{:S(2)}, u32[]{:S(2)}) collective-permute-start(bf16[64,256]{1,0:T(8,128)(2,1)S(1)} %add_convert_fusion), channel_id=1, source_target_pairs={{0,2},{2,0},{4,6},{6,4},{8,10},{10,8},{12,14},{14,12},{1,3},{3,1},... | collective-permute-start | bytes 98312 | tf_op jit(solution)/shard_map/ppermute | solution.py:252
  146.6 3.1 %collective-permute-done.30 = bf16[64,256]{1,0:T(8,128)(2,1)} collective-permute-done((bf16[64,256]{1,0:T(8,128)(2,1)S(1)}, bf16[64,256]{1,0:T(8,128)(2,1)}, u32[]{:S(2)}, u32[]{:S(2)}) %collective-permute-start.30) | collective-permute-done | bytes 32800 | tf_op jit(solution)/shard_map/ppermute | solution.py:252
  153.0 4.7 %last_kept.1.kept = f32[256,512]{1,0:T(8,128)S(1)} custom-call(s32[18]{0:T(128)S(1)} %dynamic-slice_bitcast_fusion.scalars, f32[256,512]{1,0:T(8,128)S(1)} %last_sent.1.refs_0_, bf16[32,3072]{1,0:T(8,128)(2,1)S(1)} %take_11264.1.refs_0_.refs_1_, bf16[32,3072]{1,0:T(8,128)(2,1)S(1)} %collective-permute-done.7.refs_1_.refs_2_, ...), custom_call_target="tpu_custom_call", output_to_operand_aliasing={{}: (11, {})} | custom-call | flops 1610612736 | bytes 5767168 | tf_op jit(solution)/shard_map/last_kept/pallas_call | solution.py:131
  157.8 2.4 %expand_and_add.1 = bf16[256,512]{1,0:T(8,128)(2,1)} custom-call(bf16[64,256]{1,0:T(8,128)(2,1)S(1)} %add.31.shrunk, s32[256,1]{1,0:T(8,128)S(1)} %copy-done.18, bf16[1024,512]{1,0:T(8,128)(2,1)S(1)} %bitcast.12, f32[256,512]{1,0:T(8,128)S(1)} %last_kept.1.kept, f32[256,512]{1,0:T(8,128)} %collective-permute-done.32.other), custom_call_target="tpu_custom_call" | custom-call | flops 268435456 | bytes 2359296 | tf_op jit(solution)/shard_map/expand_and_add/pallas_call | solution.py:169
  (131 shorter events, 34.3 us)
Async XLA Ops:
  5.7 76.3 %all-to-all-start = ((bf16[8,128,512]{2,1,0:T(8,128)(2,1)}), bf16[8,128,512]{2,1,0:T(8,128)(2,1)S(1)}, u32[]{:S(2)}, u32[]{:S(2)}) async-start(bf16[8,128,512]{2,1,0:T(8,128)(2,1)} %expand_blocks.1.refs_2_), calls=%async_computation | async-start | bytes 2097152 | tf_op jit(solution)/shard_map/all_to_all | solution.py:221
  13.0 21.3 %collective-permute-start.14 = (bf16[32,3072]{1,0:T(8,128)(2,1)S(1)}, bf16[32,3072]{1,0:T(8,128)(2,1)S(1)}, u32[]{:S(2)}, u32[]{:S(2)}) collective-permute-start(bf16[32,3072]{1,0:T(8,128)(2,1)S(1)} %slice.13.refs_0_), channel_id=1, source_target_pairs={{0,4},{4,8},{8,12},{12,14},{14,10},{10,6},{6,2},{2,0},{1,5},{5,9},... | collective-permute-start | bytes 589832 | tf_op jit(solution)/shard_map/ppermute | solution.py:229
  15.1 29.3 %collective-permute-start.3 = (bf16[32,4096]{1,0:T(8,128)(2,1)S(1)}, bf16[32,4096]{1,0:T(8,128)(2,1)S(1)}, u32[]{:S(2)}, u32[]{:S(2)}) collective-permute-start(bf16[32,4096]{1,0:T(8,128)(2,1)S(1)} %slice.12.refs_0_), channel_id=1, source_target_pairs={{0,2},{4,0},{8,4},{12,8},{14,12},{10,14},{6,10},{2,6},{1,3},{5,1},... | collective-permute-start | bytes 786440 | tf_op jit(solution)/shard_map/ppermute | solution.py:229
  15.2 30.0 %collective-permute-start.18 = (bf16[32,3072]{1,0:T(8,128)(2,1)S(1)}, bf16[32,3072]{1,0:T(8,128)(2,1)S(1)}, u32[]{:S(2)}, u32[]{:S(2)}) collective-permute-start(bf16[32,3072]{1,0:T(8,128)(2,1)S(1)} %slice.13.refs_0_), channel_id=1, source_target_pairs={{0,2},{4,0},{8,4},{12,8},{14,12},{10,14},{6,10},{2,6},{1,3},{5,1},... | collective-permute-start | bytes 589832 | tf_op jit(solution)/shard_map/ppermute | solution.py:229
  34.3 12.7 %collective-permute-start.15 = (bf16[32,3072]{1,0:T(8,128)(2,1)S(1)}, bf16[32,3072]{1,0:T(8,128)(2,1)S(1)}, u32[]{:S(2)}, u32[]{:S(2)}) collective-permute-start(bf16[32,3072]{1,0:T(8,128)(2,1)S(1)} %collective-permute-done.14.refs_1_), channel_id=1, source_target_pairs={{0,4},{4,8},{8,12},{12,14},{14,10},{10,6},{6,2},{2,0},{1,5},{5,9},... | collective-permute-start | bytes 589832 | tf_op jit(solution)/shard_map/ppermute | solution.py:229
  42.0 18.5 %collective-permute-start = (bf16[32,4096]{1,0:T(8,128)(2,1)S(1)}, bf16[32,4096]{1,0:T(8,128)(2,1)S(1)}, u32[]{:S(2)}, u32[]{:S(2)}) collective-permute-start(bf16[32,4096]{1,0:T(8,128)(2,1)S(1)} %slice.12.refs_0_), channel_id=1, source_target_pairs={{0,4},{4,8},{8,12},{12,14},{14,10},{10,6},{6,2},{2,0},{1,5},{5,9},... | collective-permute-start | bytes 786440 | tf_op jit(solution)/shard_map/ppermute | solution.py:229
  44.4 18.0 %collective-permute-start.4 = (bf16[32,4096]{1,0:T(8,128)(2,1)S(1)}, bf16[32,4096]{1,0:T(8,128)(2,1)S(1)}, u32[]{:S(2)}, u32[]{:S(2)}) collective-permute-start(bf16[32,4096]{1,0:T(8,128)(2,1)S(1)} %collective-permute-done.3.refs_4_), channel_id=1, source_target_pairs={{0,2},{4,0},{8,4},{12,8},{14,12},{10,14},{6,10},{2,6},{1,3},{5,1},... | collective-permute-start | bytes 786440 | tf_op jit(solution)/shard_map/ppermute | solution.py:229
  45.1 11.2 %collective-permute-start.19 = (bf16[32,3072]{1,0:T(8,128)(2,1)S(1)}, bf16[32,3072]{1,0:T(8,128)(2,1)S(1)}, u32[]{:S(2)}, u32[]{:S(2)}) collective-permute-start(bf16[32,3072]{1,0:T(8,128)(2,1)S(1)} %collective-permute-done.18.refs_5_), channel_id=1, source_target_pairs={{0,2},{4,0},{8,4},{12,8},{14,12},{10,14},{6,10},{2,6},{1,3},{5,1},... | collective-permute-start | bytes 589832 | tf_op jit(solution)/shard_map/ppermute | solution.py:229
  47.0 10.3 %collective-permute-start.16 = (bf16[32,3072]{1,0:T(8,128)(2,1)S(1)}, bf16[32,3072]{1,0:T(8,128)(2,1)S(1)}, u32[]{:S(2)}, u32[]{:S(2)}) collective-permute-start(bf16[32,3072]{1,0:T(8,128)(2,1)S(1)} %collective-permute-done.15.refs_2_), channel_id=1, source_target_pairs={{0,4},{4,8},{8,12},{12,14},{14,10},{10,6},{6,2},{2,0},{1,5},{5,9},... | collective-permute-start | bytes 589832 | tf_op jit(solution)/shard_map/ppermute | solution.py:229
  56.3 6.4 %collective-permute-start.20 = (bf16[32,3072]{1,0:T(8,128)(2,1)S(1)}, bf16[32,3072]{1,0:T(8,128)(2,1)S(1)}, u32[]{:S(2)}, u32[]{:S(2)}) collective-permute-start(bf16[32,3072]{1,0:T(8,128)(2,1)S(1)} %collective-permute-done.19.refs_6_), channel_id=1, source_target_pairs={{0,2},{4,0},{8,4},{12,8},{14,12},{10,14},{6,10},{2,6},{1,3},{5,1},... | collective-permute-start | bytes 589832 | tf_op jit(solution)/shard_map/ppermute | solution.py:229
  57.3 7.8 %collective-permute-start.17 = (bf16[32,3072]{1,0:T(8,128)(2,1)S(1)}, bf16[32,3072]{1,0:T(8,128)(2,1)S(1)}, u32[]{:S(2)}, u32[]{:S(2)}) collective-permute-start(bf16[32,3072]{1,0:T(8,128)(2,1)S(1)} %collective-permute-done.16.refs_3_), channel_id=1, source_target_pairs={{0,4},{4,8},{8,12},{12,14},{14,10},{10,6},{6,2},{2,0},{1,5},{5,9},... | collective-permute-start | bytes 589832 | tf_op jit(solution)/shard_map/ppermute | solution.py:229
  60.4 10.4 %collective-permute-start.1 = (bf16[32,4096]{1,0:T(8,128)(2,1)S(1)}, bf16[32,4096]{1,0:T(8,128)(2,1)}, u32[]{:S(2)}, u32[]{:S(2)}) collective-permute-start(bf16[32,4096]{1,0:T(8,128)(2,1)S(1)} %collective-permute-done.refs_1_), channel_id=1, source_target_pairs={{0,4},{4,8},{8,12},{12,14},{14,10},{10,6},{6,2},{2,0},{1,5},{5,9},... | collective-permute-start | bytes 786440 | tf_op jit(solution)/shard_map/ppermute | solution.py:229
  62.4 10.8 %collective-permute-start.5 = (bf16[32,4096]{1,0:T(8,128)(2,1)S(1)}, bf16[32,4096]{1,0:T(8,128)(2,1)}, u32[]{:S(2)}, u32[]{:S(2)}) collective-permute-start(bf16[32,4096]{1,0:T(8,128)(2,1)S(1)} %collective-permute-done.4.refs_5_), channel_id=1, source_target_pairs={{0,2},{4,0},{8,4},{12,8},{14,12},{10,14},{6,10},{2,6},{1,3},{5,1},... | collective-permute-start | bytes 786440 | tf_op jit(solution)/shard_map/ppermute | solution.py:229
  65.1 11.3 %collective-permute-start.21 = (bf16[32,4096]{1,0:T(8,128)(2,1)S(1)}, bf16[32,4096]{1,0:T(8,128)(2,1)}, u32[]{:S(2)}, u32[]{:S(2)}) collective-permute-start(bf16[32,4096]{1,0:T(8,128)(2,1)S(1)} %take_7168.1.refs_0_), channel_id=1, source_target_pairs={{0,4},{4,8},{8,12},{12,14},{14,10},{10,6},{6,2},{2,0},{1,5},{5,9},... | collective-permute-start | bytes 786440 | tf_op jit(solution)/shard_map/ppermute | solution.py:229
  70.8 11.2 %collective-permute-start.2 = (bf16[32,4096]{1,0:T(8,128)(2,1)}, bf16[32,4096]{1,0:T(8,128)(2,1)S(1)}, u32[]{:S(2)}, u32[]{:S(2)}) collective-permute-start(bf16[32,4096]{1,0:T(8,128)(2,1)} %collective-permute-done.1.refs_2_), channel_id=1, source_target_pairs={{0,4},{4,8},{8,12},{12,14},{14,10},{10,6},{6,2},{2,0},{1,5},{5,9},... | collective-permute-start | bytes 786440 | tf_op jit(solution)/shard_map/ppermute | solution.py:229
  73.2 8.8 %collective-permute-start.6 = (bf16[32,4096]{1,0:T(8,128)(2,1)}, bf16[32,4096]{1,0:T(8,128)(2,1)S(1)}, u32[]{:S(2)}, u32[]{:S(2)}) collective-permute-start(bf16[32,4096]{1,0:T(8,128)(2,1)} %collective-permute-done.5.refs_6_), channel_id=1, source_target_pairs={{0,2},{4,0},{8,4},{12,8},{14,12},{10,14},{6,10},{2,6},{1,3},{5,1},... | collective-permute-start | bytes 786440 | tf_op jit(solution)/shard_map/ppermute | solution.py:229
  73.2 11.2 %collective-permute-start.25 = (bf16[32,4096]{1,0:T(8,128)(2,1)S(1)}, bf16[32,4096]{1,0:T(8,128)(2,1)}, u32[]{:S(2)}, u32[]{:S(2)}) collective-permute-start(bf16[32,4096]{1,0:T(8,128)(2,1)S(1)} %take_7168.1.refs_0_), channel_id=1, source_target_pairs={{0,2},{4,0},{8,4},{12,8},{14,12},{10,14},{6,10},{2,6},{1,3},{5,1},... | collective-permute-start | bytes 786440 | tf_op jit(solution)/shard_map/ppermute | solution.py:229
  76.4 10.2 %collective-permute-start.22 = (bf16[32,4096]{1,0:T(8,128)(2,1)}, bf16[32,4096]{1,0:T(8,128)(2,1)}, u32[]{:S(2)}, u32[]{:S(2)}) collective-permute-start(bf16[32,4096]{1,0:T(8,128)(2,1)} %collective-permute-done.21.refs_1_), channel_id=1, source_target_pairs={{0,4},{4,8},{8,12},{12,14},{14,10},{10,6},{6,2},{2,0},{1,5},{5,9},... | collective-permute-start | bytes 786440 | tf_op jit(solution)/shard_map/ppermute | solution.py:229
  82.1 8.2 %collective-permute-start.10 = (bf16[32,3072]{1,0:T(8,128)(2,1)S(1)}, bf16[32,3072]{1,0:T(8,128)(2,1)S(1)}, u32[]{:S(2)}, u32[]{:S(2)}) collective-permute-start(bf16[32,3072]{1,0:T(8,128)(2,1)S(1)} %take_11264.1.refs_0_.refs_1_), channel_id=1, source_target_pairs={{0,2},{4,0},{8,4},{12,8},{14,12},{10,14},{6,10},{2,6},{1,3},{5,1},... | collective-permute-start | bytes 589832 | tf_op jit(solution)/shard_map/ppermute | solution.py:229
  84.5 24.0 %collective-permute-start.26 = (bf16[32,4096]{1,0:T(8,128)(2,1)}, bf16[32,4096]{1,0:T(8,128)(2,1)S(1)}, u32[]{:S(2)}, u32[]{:S(2)}) collective-permute-start(bf16[32,4096]{1,0:T(8,128)(2,1)} %collective-permute-done.25.refs_5_), channel_id=1, source_target_pairs={{0,2},{4,0},{8,4},{12,8},{14,12},{10,14},{6,10},{2,6},{1,3},{5,1},... | collective-permute-start | bytes 786440 | tf_op jit(solution)/shard_map/ppermute | solution.py:229
  86.6 24.0 %collective-permute-start.23 = (bf16[32,4096]{1,0:T(8,128)(2,1)}, bf16[32,4096]{1,0:T(8,128)(2,1)S(1)}, u32[]{:S(2)}, u32[]{:S(2)}) collective-permute-start(bf16[32,4096]{1,0:T(8,128)(2,1)} %collective-permute-done.22.refs_2_), channel_id=1, source_target_pairs={{0,4},{4,8},{8,12},{12,14},{14,10},{10,6},{6,2},{2,0},{1,5},{5,9},... | collective-permute-start | bytes 786440 | tf_op jit(solution)/shard_map/ppermute | solution.py:229
  87.9 22.8 %collective-permute-start.7 = (bf16[32,3072]{1,0:T(8,128)(2,1)S(1)}, bf16[32,3072]{1,0:T(8,128)(2,1)S(1)}, u32[]{:S(2)}, u32[]{:S(2)}) collective-permute-start(bf16[32,3072]{1,0:T(8,128)(2,1)S(1)} %take_11264.1.refs_0_.refs_1_), channel_id=1, source_target_pairs={{0,4},{4,8},{8,12},{12,14},{14,10},{10,6},{6,2},{2,0},{1,5},{5,9},... | collective-permute-start | bytes 589832 | tf_op jit(solution)/shard_map/ppermute | solution.py:229
  90.2 20.6 %collective-permute-start.11 = (bf16[32,3072]{1,0:T(8,128)(2,1)S(1)}, bf16[32,3072]{1,0:T(8,128)(2,1)S(1)}, u32[]{:S(2)}, u32[]{:S(2)}) collective-permute-start(bf16[32,3072]{1,0:T(8,128)(2,1)S(1)} %collective-permute-done.10.refs_4_.refs_5_), channel_id=1, source_target_pairs={{0,2},{4,0},{8,4},{12,8},{14,12},{10,14},{6,10},{2,6},{1,3},{5,1},... | collective-permute-start | bytes 589832 | tf_op jit(solution)/shard_map/ppermute | solution.py:229
  108.5 15.6 %collective-permute-start.27 = (bf16[32,4096]{1,0:T(8,128)(2,1)S(1)}, bf16[32,4096]{1,0:T(8,128)(2,1)S(1)}, u32[]{:S(2)}, u32[]{:S(2)}) collective-permute-start(bf16[32,4096]{1,0:T(8,128)(2,1)S(1)} %collective-permute-done.26.refs_6_), channel_id=1, source_target_pairs={{0,2},{4,0},{8,4},{12,8},{14,12},{10,14},{6,10},{2,6},{1,3},{5,1},... | collective-permute-start | bytes 786440 | tf_op jit(solution)/shard_map/ppermute | solution.py:229
  110.6 13.5 %collective-permute-start.24 = (bf16[32,4096]{1,0:T(8,128)(2,1)S(1)}, bf16[32,4096]{1,0:T(8,128)(2,1)S(1)}, u32[]{:S(2)}, u32[]{:S(2)}) collective-permute-start(bf16[32,4096]{1,0:T(8,128)(2,1)S(1)} %collective-permute-done.23.refs_3_), channel_id=1, source_target_pairs={{0,4},{4,8},{8,12},{12,14},{14,10},{10,6},{6,2},{2,0},{1,5},{5,9},... | collective-permute-start | bytes 786440 | tf_op jit(solution)/shard_map/ppermute | solution.py:229
  110.6 11.4 %collective-permute-start.8 = (bf16[32,3072]{1,0:T(8,128)(2,1)S(1)}, bf16[32,3072]{1,0:T(8,128)(2,1)S(1)}, u32[]{:S(2)}, u32[]{:S(2)}) collective-permute-start(bf16[32,3072]{1,0:T(8,128)(2,1)S(1)} %collective-permute-done.7.refs_1_.refs_2_), channel_id=1, source_target_pairs={{0,4},{4,8},{8,12},{12,14},{14,10},{10,6},{6,2},{2,0},{1,5},{5,9},... | collective-permute-start | bytes 589832 | tf_op jit(solution)/shard_map/ppermute | solution.py:229
  110.8 11.4 %collective-permute-start.12 = (bf16[32,3072]{1,0:T(8,128)(2,1)S(1)}, bf16[32,3072]{1,0:T(8,128)(2,1)S(1)}, u32[]{:S(2)}, u32[]{:S(2)}) collective-permute-start(bf16[32,3072]{1,0:T(8,128)(2,1)S(1)} %collective-permute-done.11.refs_5_.refs_6_), channel_id=1, source_target_pairs={{0,2},{4,0},{8,4},{12,8},{14,12},{10,14},{6,10},{2,6},{1,3},{5,1},... | collective-permute-start | bytes 589832 | tf_op jit(solution)/shard_map/ppermute | solution.py:229
  122.0 10.3 %collective-permute-start.9 = (bf16[32,3072]{1,0:T(8,128)(2,1)S(1)}, bf16[32,3072]{1,0:T(8,128)(2,1)S(1)}, u32[]{:S(2)}, u32[]{:S(2)}) collective-permute-start(bf16[32,3072]{1,0:T(8,128)(2,1)S(1)} %collective-permute-done.8.refs_2_.refs_3_), channel_id=1, source_target_pairs={{0,4},{4,8},{8,12},{12,14},{14,10},{10,6},{6,2},{2,0},{1,5},{5,9},... | collective-permute-start | bytes 589832 | tf_op jit(solution)/shard_map/ppermute | solution.py:229
  122.2 10.1 %collective-permute-start.13 = (bf16[32,3072]{1,0:T(8,128)(2,1)S(1)}, bf16[32,3072]{1,0:T(8,128)(2,1)S(1)}, u32[]{:S(2)}, u32[]{:S(2)}) collective-permute-start(bf16[32,3072]{1,0:T(8,128)(2,1)S(1)} %collective-permute-done.12.refs_6_.refs_7_), channel_id=1, source_target_pairs={{0,2},{4,0},{8,4},{12,8},{14,12},{10,14},{6,10},{2,6},{1,3},{5,1},... | collective-permute-start | bytes 589832 | tf_op jit(solution)/shard_map/ppermute | solution.py:229
  139.6 18.2 %collective-permute-start.32 = (f32[256,512]{1,0:T(8,128)S(1)}, f32[256,512]{1,0:T(8,128)}, u32[]{:S(2)}, u32[]{:S(2)}) collective-permute-start(f32[256,512]{1,0:T(8,128)S(1)} %last_sent.1.refs_0_), channel_id=1, source_target_pairs={{0,1},{1,0},{2,3},{3,2},{4,5},{5,4},{6,7},{7,6},{8,9},{9,8},{10,11... | collective-permute-start | bytes 1572872 | tf_op jit(solution)/shard_map/ppermute | solution.py:249
  145.6 4.1 %collective-permute-start.30 = (bf16[64,256]{1,0:T(8,128)(2,1)S(1)}, bf16[64,256]{1,0:T(8,128)(2,1)}, u32[]{:S(2)}, u32[]{:S(2)}) collective-permute-start(bf16[64,256]{1,0:T(8,128)(2,1)S(1)} %add.29), channel_id=1, source_target_pairs={{0,4},{2,6},{4,0},{6,2},{8,12},{10,14},{12,8},{14,10},{1,5},{3,7},... | collective-permute-start | bytes 98312 | tf_op jit(solution)/shard_map/ppermute | solution.py:252
  150.5 7.2 %collective-permute-start.31 = (bf16[64,256]{1,0:T(8,128)(2,1)S(1)}, bf16[64,256]{1,0:T(8,128)(2,1)S(1)}, u32[]{:S(2)}, u32[]{:S(2)}) collective-permute-start(bf16[64,256]{1,0:T(8,128)(2,1)S(1)} %add.30), channel_id=1, source_target_pairs={{0,8},{2,10},{4,12},{6,14},{8,0},{10,2},{12,4},{14,6},{1,9},{3,11}... | collective-permute-start | bytes 98312 | tf_op jit(solution)/shard_map/ppermute | solution.py:252
  (39 other events, 414.1 us)

commit v4 on v3

v4 whole, which is shorter than its diff:
```python
import functools

import jax
import jax.numpy as jnp
import numpy as np
from jax import lax
from jax.experimental import pallas as pl
from jax.experimental.pallas import tpu as pltpu
from jax.sharding import Mesh, PartitionSpec as P

F32, BF16 = jnp.float32, jnp.bfloat16
TILE = 1024
MIB = 2**20


def params(mib):
    return pltpu.CompilerParams(vmem_limit_bytes=mib * MIB)


def split_kernel(scalars, src, dst):
    dst[...] = src[...][None]


def expand_blocks(scalars, half, expand, n, cores):
    owned, rank, width = expand.shape
    rows = owned * rank
    share = width // (n * cores)
    return pl.pallas_call(
        split_kernel,
        grid_spec=pltpu.PrefetchScalarGridSpec(
            num_scalar_prefetch=1,
            grid=(n,),
            in_specs=[pl.BlockSpec((rows, share), lambda s, t: (0, s * cores + t[half]))],
            out_specs=pl.BlockSpec((1, rows, share), lambda s, t: (s, 0, 0)),
        ),
        out_shape=jax.ShapeDtypeStruct((n, rows, share), BF16),
        compiler_params=params(40),
        cost_estimate=pl.CostEstimate(flops=0, bytes_accessed=4 * n * rows * share, transcendentals=0),
        name="expand_blocks",
    )(scalars, expand.reshape(rows, width))


def matmul_kernel(count, waits, layout, sides, narrow, has_acc, scalars, *refs):
    refs = list(refs)[waits:]
    pieces = [refs.pop(0) for _ in range(count)]
    weights = [refs.pop(0) for _ in range(sides)]
    shrink = refs.pop(0) if narrow else None
    outs = sides + narrow
    before = [refs.pop(0) for _ in range(outs)] if has_acc else None
    after = [refs.pop(0) for _ in range(outs)]
    lhs, sems = refs
    step = pl.program_id(0)
    steps, all_rows, tile = lhs.shape
    rows = all_rows // len(layout)

    @pl.when(step == 0)
    def _():
        copies = []
        for i, (piece, block, pair, which) in enumerate(layout):
            at = pl.multiple_of((2 * pair + scalars[which]) * rows, rows)
            for j in range(steps):
                copies.append(
                    pltpu.make_async_copy(
                        pieces[piece].at[pl.ds(block * rows, rows), pl.ds(j * tile, tile)],
                        lhs.at[j, pl.ds(at, rows), :],
                        sems.at[i, j],
                    )
                )
        for copy in copies:
            copy.start()
        for i in range(outs):
            after[i][...] = before[i][...] if has_acc else jnp.zeros_like(after[i])
        for copy in copies:
            copy.wait()

    left = lhs[step]
    if narrow:
        after[-1][...] += lax.dot_general(
            shrink[...], left, (((1,), (1,)), ((), ())), preferred_element_type=F32
        )
    for i in range(sides):
        after[i][...] += jnp.dot(left, weights[i][...], preferred_element_type=F32)


def chunk_matmul(scalars, pieces, layout, down, shrink, acc, start, sides, narrow, label, after=()):
    rows, width = sum(piece.shape[0] for piece in pieces), pieces[0].shape[1]
    share = down.shape[1] // 2
    steps = width // TILE
    first = start // TILE
    ranks = shrink.shape[0]
    in_specs = [pl.BlockSpec(memory_space=pl.ANY) for _ in after]
    in_specs += [pl.BlockSpec(memory_space=pltpu.HBM) for _ in pieces]
    args = [*after, *pieces]
    for side in sides:
        in_specs.append(pl.BlockSpec((TILE, share), functools.partial(lambda side, k, s: (first + k, s[2 + side]), side)))
        args.append(down)
    if narrow:
        in_specs.append(pl.BlockSpec((ranks, TILE), lambda k, s: (0, first + k)))
        args.append(shrink)
    shapes = [(rows, share)] * len(sides) + [(ranks, rows)] * narrow
    whole = [pl.BlockSpec(shape, lambda k, s: (0, 0)) for shape in shapes]
    aliases = {}
    if acc is not None:
        aliases = {1 + len(args) + i: i for i in range(len(shapes))}
        in_specs += whole
        args += list(acc)
    columns = share * len(sides) + ranks * narrow
    return pl.pallas_call(
        functools.partial(matmul_kernel, len(pieces), len(after), layout, len(sides), narrow, acc is not None),
        grid_spec=pltpu.PrefetchScalarGridSpec(
            num_scalar_prefetch=1,
            grid=(steps,),
            in_specs=in_specs,
            out_specs=whole,
            scratch_shapes=[pltpu.VMEM((steps, rows, TILE), BF16), pltpu.SemaphoreType.DMA((len(layout), steps))],
        ),
        out_shape=[jax.ShapeDtypeStruct(shape, F32) for shape in shapes],
        input_output_aliases=aliases,
        compiler_params=params(40),
        cost_estimate=pl.CostEstimate(
            flops=4 * rows * width * columns,
            bytes_accessed=2 * width * (columns + rows) + 8 * rows * columns,
            transcendentals=0,
        ),
        name=label,
    )(scalars, *args)


def final_kernel(n, owned, shrunk, slot, factors, kept, other, out, spread):
    rank = shrunk.shape[0]
    wide = owned * rank
    rows = out.shape[0]
    lane = lax.broadcasted_iota(jnp.int32, (rows, wide), 1) // rank
    own = shrunk[...].astype(F32).T
    pair = jnp.concatenate([own] * owned, axis=1)
    place = slot[...] - lane
    for i in range(n):
        spread[:, i * wide:(i + 1) * wide] = jnp.where(place == i * owned, pair, 0.0).astype(BF16)
    extra = jnp.dot(spread[...], factors[...], preferred_element_type=F32)
    out[...] = (kept[...] + other[...] + extra).astype(BF16)


def final(shrunk, slot_column, factors, kept, other, owned):
    n, wide, share = factors.shape
    rows = kept.shape[0]
    return pl.pallas_call(
        functools.partial(final_kernel, n, owned),
        in_specs=[pl.BlockSpec(memory_space=pltpu.VMEM)] * 5,
        out_specs=pl.BlockSpec(memory_space=pltpu.VMEM),
        scratch_shapes=[pltpu.VMEM((rows, n * wide), BF16)],
        out_shape=jax.ShapeDtypeStruct((rows, share), BF16),
        compiler_params=params(40),
        cost_estimate=pl.CostEstimate(
            flops=2 * rows * share * n * wide,
            bytes_accessed=2 * n * wide * share + 10 * rows * share,
            transcendentals=0,
        ),
        name="expand_and_add",
    )(shrunk, slot_column, factors.reshape(n * wide, share), kept, other)


def make_shards(depth, cores):
    n = 2 * depth
    swap_y, swap_core = [(0, 1), (1, 0)], [(t, (t + 1) % cores) for t in range(cores)]
    table = np.array([[y, 1 - y, t, 1 - t] for y in range(2) for t in range(cores)], np.int32)
    gathered_first = tuple((piece, z, z, piece) for z in range(depth) for piece in range(2))

    def shards(hidden, down, shrink, expand, row_adapter, adapter_slot):
        owned, units, rank = shrink.shape
        y, tensor = lax.axis_index("y"), lax.axis_index("tensor")
        store = 2 * lax.axis_index("z") + y
        scalars = lax.dynamic_slice_in_dim(jnp.asarray(table), y * cores + tensor, 1, 0)[0]
        shrink_rows = jnp.transpose(shrink, (0, 2, 1)).reshape(owned * rank, units)

        slots = jnp.arange(adapter_slot.shape[0], dtype=jnp.int32)
        row_slot = jnp.sum(jnp.where(row_adapter[None, :] == slots[:, None], adapter_slot[:, None], 0), axis=0)

        tiles = units // TILE
        large = (tiles + 2) // 4 * TILE
        small = (units - 2 * large) // (2 * TILE) * TILE
        widths = [units - 2 * large - small, large, large, small]

        blocks = expand_blocks(scalars, 2, expand, n, cores)
        factors = lax.all_to_all(blocks, ("z", "y"), 0, 0)
        acc = None
        start = 0
        for chunk, width in enumerate(widths):
            column = lax.all_gather(hidden[:, start:start + width], "z", axis=0, tiled=True)
            pieces = [column, lax.ppermute(column, "y", swap_y)]
            call = functools.partial(chunk_matmul, scalars, pieces, gathered_first, down, shrink_rows)
            if chunk < len(widths) - 1:
                acc = call(acc, start, (0, 1), True, f"chunk_{chunk}")
            else:
                narrow, = call(acc[2:], start, (), True, "last_narrow")
                mine = [
                    jnp.where((row_slot == store * owned + i)[None, :], narrow[i * rank:(i + 1) * rank], 0.0)
                    for i in range(owned)
                ]
                mine = sum(mine[1:], mine[0])
                send, = call(acc[1:2], start, (1,), False, "last_sent", [mine])
                kept, = call(acc[:1], start, (0,), False, "last_kept", [send])
            start += width
        shrunk = (mine + lax.ppermute(mine, "tensor", swap_core)).astype(BF16)
        other = lax.ppermute(send, "tensor", swap_core)
        bit = 1
        while bit < n:
            shrunk = shrunk + lax.ppermute(shrunk, ("z", "y"), [(s, s ^ bit) for s in range(n)])
            bit *= 2
        return final(shrunk, row_slot[:, None], factors, kept, other, owned)

    return shards


def solution(mesh):
    parts, stores, cores = (mesh.shape[name] for name in ("parts", "store", "tensor"))
    split = Mesh(mesh.devices.reshape(parts, stores // 2, 2, cores), ("parts", "z", "y", "tensor"))
    in_specs = (
        P(("parts", "z", "y"), "tensor"),
        P("tensor", ("z", "y")),
        P(("parts", "z", "y"), "tensor", None),
        P(("parts", "z", "y"), None, None),
        P("parts"),
        P("parts"),
    )
    out_specs = P("parts", ("z", "y", "tensor"))
    shards = make_shards(stores // 2, cores)
    return jax.shard_map(shards, mesh=split, in_specs=in_specs, out_specs=out_specs, check_vma=False)
```

time: 161 us -> 171 us (1.062)
  blocking collectives: 0 us -> 52.1 us
  starting transfers between devices: 60.5 us -> 18.2 us
  between operations: 0.33 us -> 13.6 us
  local copies, waits for them, and re-layouts: 18.7 us -> 7.38 us
    all_gather x0 -> x2, blocking collectives: none -> 52.1 us  [shards(): lax.all_gather(hidden[:, start:start + width], 'z', axis=0, tiled=True)]
    ppermute x33 -> x9, starting transfers between devices: 53.2 us -> 11.3 us  [the longest x3 5.88 us: shards(): lax.ppermute(shrunk, ('z', 'y'), [(s, s ^ bit) for s in range(n)])]
    unnamed x74 -> x14, local copies, waits for them, and re-layouts: 17.1 us -> 3.65 us
    ppermute x33 -> x9, waiting for transfers between devices: 38.8 us -> 29.8 us  [the longest x4 23.5 us: shards(): pieces = [column, lax.ppermute(column, 'y', swap_y)]]
    all_gather x0 -> x2, waiting for transfers between devices: none -> 6.72 us  [shards(): lax.all_gather(hidden[:, start:start + width], 'z', axis=0, tiled=True)]
    slice x2, local copies, waits for them, and re-layouts: 0.03 us -> 2.91 us  [shards(): hidden[:, start:start + width]]
    pallas_call x8 -> x6, Pallas kernels: 35.2 us -> 35.6 us  [chunk_matmul(): pl.pallas_call(functools.partial(matmul_kernel, len(pieces), len(after),...]
  transfers between devices with their start and end apart: 34 -> 12, of which waited for: 11 -> 5; matrix products, arithmetic and copies ran while one was open for 1% -> 1% of each run, Pallas kernels for 17% -> 23%
where the time goes in v4:
time: 171 us; the launch traced here: 170 us
  blocking collectives  52.1 us (30%)
  Pallas kernels  41.5 us (24%)
  waiting for transfers between devices  37.2 us (22%)
  starting transfers between devices  18.2 us (11%)
  between operations  13.6 us (8%)
  local copies, waits for them, and re-layouts  7.38 us (4%)
    all_gather x2, blocking collectives, shards(): lax.all_gather(hidden[:, start:start + width], 'z', axis=0, tiled=True)  52.1 us
    pallas_call x6, Pallas kernels, chunk_matmul(): pl.pallas_call(functools.partial(matmul_kernel, len(pieces), len(after),...  35.6 us
    ppermute x4, waiting for transfers between devices, shards(): pieces = [column, lax.ppermute(column, 'y', swap_y)]  23.5 us
    all_to_all x1, starting transfers between devices, shards(): factors = lax.all_to_all(blocks, ('z', 'y'), 0, 0)  6.85 us
    all_gather x2, waiting for transfers between devices, shards(): lax.all_gather(hidden[:, start:start + width], 'z', axis=0, tiled=True)  6.72 us
    ppermute x3, starting transfers between devices, shards(): lax.ppermute(shrunk, ('z', 'y'), [(s, s ^ bit) for s in range(n)])  5.88 us
    ppermute x4, starting transfers between devices, shards(): pieces = [column, lax.ppermute(column, 'y', swap_y)]  4.88 us
    ppermute x3, waiting for transfers between devices, shards(): lax.ppermute(shrunk, ('z', 'y'), [(s, s ^ bit) for s in range(n)])  4.83 us
  transfers between devices with their start and end apart: 12, of which 5 were waited for; matrix products, arithmetic and copies ran while one was open for 1% of the time, Pallas kernels for 23%

profile of v4, /device:TPU:0, one launch (start us, length us, event | category | flops | bytes accessed | tf_op | source)
XLA Modules:
  0.0 170.2 jit_solution(14004493557612981467)
XLA Ops:
  6.5 1.9 %fusion.2 = (bf16[32,4096]{1,0:T(8,128)(2,1)}, bf16[32,4096]{1,0:T(8,128)(2,1)}) fusion(bf16[32,14336]{1,0:T(8,128)(2,1)} %param.7), kind=kLoop, calls=%fused_computation.10 | loop fusion | bytes 1048576 | tf_op jit(solution)/shard_map/slice | solution.py:188
  8.5 0.7 all-gather.3.cloned.1.call-update
  9.2 1.1 fusion.1
  10.3 28.1 %all_gather.15.refs_0_ = bf16[128,3072]{1,0:T(8,128)(2,1)S(1)} all-gather(bf16[32,3072]{1,0:T(8,128)(2,1)S(1)} %get-tuple-element.23), channel_id=1, replica_groups=mesh['parts'=2,'z'=4,'y'=2,'tensor'=2] {'z'}, dimensions={0}, use_global_device_ids=true | all-gather | bytes 983040 | tf_op jit(solution)/shard_map/all_gather | solution.py:188
  38.4 1.4 collective-permute-start.3
  39.8 6.7 %all-gather.5.cloned.1.call-done.refs_0_ = bf16[128,4096]{1,0:T(8,128)(2,1)} async-done(((bf16[32,4096]{1,0:T(8,128)(2,1)}), bf16[128,4096]{1,0:T(8,128)(2,1)}) %all-gather.5.cloned.1.call-update) | async-done | bytes 1048592 | tf_op jit(solution)/shard_map/all_gather | solution.py:188
  46.5 1.5 collective-permute-start.2
  48.0 23.9 %all_gather.12.refs_0_.refs_1_ = bf16[128,3072]{1,0:T(8,128)(2,1)S(1)} all-gather(bf16[32,3072]{1,0:T(8,128)(2,1)S(1)} %get-tuple-element.24), channel_id=1, replica_groups=mesh['parts'=2,'z'=4,'y'=2,'tensor'=2] {'z'}, dimensions={0}, use_global_device_ids=true | all-gather | bytes 983040 | tf_op jit(solution)/shard_map/all_gather | solution.py:188
  71.9 0.7 dynamic-slice_bitcast_fusion.scalars
  72.6 1.6 copy-done.2
  74.2 3.3 %expand_blocks.1 = bf16[8,128,512]{2,1,0:T(8,128)(2,1)} custom-call(s32[4]{0:T(128)S(1)} %dynamic-slice_bitcast_fusion.scalars, bf16[128,8192]{1,0:T(8,128)(2,1)S(1)} %bitcast.12), custom_call_target="tpu_custom_call" | custom-call | bytes 2097152 | tf_op jit(solution)/shard_map/expand_blocks/pallas_call | solution.py:28
  77.5 6.9 %all-to-all-start = ((bf16[8,128,512]{2,1,0:T(8,128)(2,1)}), bf16[8,128,512]{2,1,0:T(8,128)(2,1)}, u32[]{:S(2)}, u32[]{:S(2)}) async-start(bf16[8,128,512]{2,1,0:T(8,128)(2,1)} %expand_blocks.1), calls=%async_computation | async-start | bytes 2097152 | tf_op jit(solution)/shard_map/all_to_all | solution.py:184
  84.4 2.0 %collective-permute-start.1 = (bf16[128,4096]{1,0:T(8,128)(2,1)}, bf16[128,4096]{1,0:T(8,128)(2,1)}, u32[]{:S(2)}, u32[]{:S(2)}) collective-permute-start(bf16[128,4096]{1,0:T(8,128)(2,1)} %all-gather.3.cloned.1.call-done.refs_0_), channel_id=1, source_target_pairs={{0,2},{2,0},{1,3},{3,1},{4,6},{6,4},{5,7},{7,5},{8,10},{10,8},{9,1... | collective-permute-start | bytes 3145736 | tf_op jit(solution)/shard_map/ppermute | solution.py:189
  86.4 0.1 select_reduce_fusion
  86.5 2.0 %copy-done = bf16[2,14336,64]{1,2,0:T(8,128)(2,1)S(1)} copy-done((bf16[2,14336,64]{1,2,0:T(8,128)(2,1)S(1)}, bf16[2,14336,64]{1,2,0:T(8,128)(2,1)}, u32[]{:S(2)}) %copy-start) | copy-done | bytes 3670040
  88.5 7.3 %chunk_0.1 = (f32[256,512]{1,0:T(8,128)S(1)}, f32[256,512]{1,0:T(8,128)S(1)}, f32[128,256]{1,0:T(8,128)S(1)}) custom-call(s32[4]{0:T(128)S(1)} %dynamic-slice_bitcast_fusion.scalars, bf16[128,3072]{1,0:T(8,128)(2,1)S(1)} %all_gather.15.refs_0_, bf16[128,3072]{1,0:T(8,128)(2,1)} %collective-permute-done.3.refs_1_, bf16[14336,1024]{1,0:T(8,128)(2,1)} %refs_3_.9, ...), custom_call_target="tpu_custom_call" | custom-call | flops 3623878656 | bytes 11010048 | tf_op jit(solution)/shard_map/chunk_0/pallas_call | solution.py:108
  95.9 8.2 %chunk_1.1 = (f32[256,512]{1,0:T(8,128)S(1)}, f32[256,512]{1,0:T(8,128)S(1)}, f32[128,256]{1,0:T(8,128)S(1)}) custom-call(s32[4]{0:T(128)S(1)} %dynamic-slice_bitcast_fusion.scalars, bf16[128,4096]{1,0:T(8,128)(2,1)S(1)} %copy-done.4, bf16[128,4096]{1,0:T(8,128)(2,1)} %collective-permute-done.2.refs_1_, ...), custom_call_target="tpu_custom_call", output_to_operand_aliasing={{0}: (6, {}), {1}: (7, {}), {2}: (8, {})} | custom-call | flops 4831838208 | bytes 13893632 | tf_op jit(solution)/shard_map/chunk_1/pallas_call | solution.py:108
  104.2 23.5 %collective-permute-done.1.refs_1_ = bf16[128,4096]{1,0:T(8,128)(2,1)} collective-permute-done((bf16[128,4096]{1,0:T(8,128)(2,1)}, bf16[128,4096]{1,0:T(8,128)(2,1)}, u32[]{:S(2)}, u32[]{:S(2)}) %collective-permute-start.1) | collective-permute-done | bytes 1048608 | tf_op jit(solution)/shard_map/ppermute | solution.py:189
  127.6 8.2 %chunk_2.1 = (f32[256,512]{1,0:T(8,128)S(1)}, f32[256,512]{1,0:T(8,128)S(1)}, f32[128,256]{1,0:T(8,128)S(1)}) custom-call(s32[4]{0:T(128)S(1)} %dynamic-slice_bitcast_fusion.scalars, bf16[128,4096]{1,0:T(8,128)(2,1)S(1)} %copy-done.3, bf16[128,4096]{1,0:T(8,128)(2,1)} %collective-permute-done.1.refs_1_, ...), custom_call_target="tpu_custom_call", output_to_operand_aliasing={{0}: (6, {}), {1}: (7, {}), {2}: (8, {})} | custom-call | flops 4831838208 | bytes 13893632 | tf_op jit(solution)/shard_map/chunk_2/pallas_call | solution.py:108
  135.9 2.4 %last_narrow.1 = f32[128,256]{1,0:T(8,128)S(1)} custom-call(s32[4]{0:T(128)S(1)} %dynamic-slice_bitcast_fusion.scalars, bf16[128,3072]{1,0:T(8,128)(2,1)S(1)} %all_gather.12.refs_0_.refs_1_, bf16[128,3072]{1,0:T(8,128)(2,1)S(1)} %collective-permute-done.refs_1_.refs_2_, bf16[128,14336]{1,0:T(8,128)(2,1)S(1)} %bitcast.11, ...), custom_call_target="tpu_custom_call", output_to_operand_aliasing={{}: (4, {})} | custom-call | flops 402653184 | bytes 2621440 | tf_op jit(solution)/shard_map/last_narrow/pallas_call | solution.py:108
  138.3 4.7 %last_sent.1.refs_0_ = f32[256,512]{1,0:T(8,128)S(1)} custom-call(s32[4]{0:T(128)S(1)} %dynamic-slice_bitcast_fusion.scalars, f32[64,256]{1,0:T(8,128)S(1)} %fusion.refs_0_, bf16[128,3072]{1,0:T(8,128)(2,1)S(1)} %all_gather.12.refs_0_.refs_1_, bf16[128,3072]{1,0:T(8,128)(2,1)S(1)} %collective-permute-done.refs_1_.refs_2_, ...), custom_call_target="tpu_custom_call", output_to_operand_aliasing={{}: (5, {})} | custom-call | flops 1610612736 | bytes 5767168 | tf_op jit(solution)/shard_map/last_sent/pallas_call | solution.py:108
  143.0 0.1 collective-permute-start.8
  143.1 0.5 collective-permute-start.4
  143.6 1.5 collective-permute-done.4
  145.1 1.4 collective-permute-start.5
  146.5 2.6 %collective-permute-done.5 = bf16[64,256]{1,0:T(8,128)(2,1)S(1)} collective-permute-done((bf16[64,256]{1,0:T(8,128)(2,1)S(1)}, bf16[64,256]{1,0:T(8,128)(2,1)S(1)}, u32[]{:S(2)}, u32[]{:S(2)}) %collective-permute-start.5) | collective-permute-done | bytes 32800 | tf_op jit(solution)/shard_map/ppermute | solution.py:207
  149.1 1.6 collective-permute-start.6
  150.7 0.1 copy.18.slot
  150.8 2.2 %collective-permute-done.6 = bf16[64,256]{1,0:T(8,128)(2,1)S(1)} collective-permute-done((bf16[64,256]{1,0:T(8,128)(2,1)S(1)}, bf16[64,256]{1,0:T(8,128)(2,1)S(1)}, u32[]{:S(2)}, u32[]{:S(2)}) %collective-permute-start.6) | collective-permute-done | bytes 32800 | tf_op jit(solution)/shard_map/ppermute | solution.py:207
  153.1 2.9 %collective-permute-start.7 = (bf16[64,256]{1,0:T(8,128)(2,1)S(1)}, bf16[64,256]{1,0:T(8,128)(2,1)S(1)}, u32[]{:S(2)}, u32[]{:S(2)}) collective-permute-start(bf16[64,256]{1,0:T(8,128)(2,1)S(1)} %add.34), channel_id=1, source_target_pairs={{0,8},{2,10},{4,12},{6,14},{8,0},{10,2},{12,4},{14,6},{1,9},{3,11}... | collective-permute-start | bytes 98312 | tf_op jit(solution)/shard_map/ppermute | solution.py:207
  156.0 4.7 %last_kept.1.kept = f32[256,512]{1,0:T(8,128)S(1)} custom-call(s32[4]{0:T(128)S(1)} %dynamic-slice_bitcast_fusion.scalars, f32[256,512]{1,0:T(8,128)S(1)} %last_sent.1.refs_0_, bf16[128,3072]{1,0:T(8,128)(2,1)S(1)} %all_gather.12.refs_0_.refs_1_, bf16[128,3072]{1,0:T(8,128)(2,1)S(1)} %collective-permute-done.refs_1_.refs_2_, ...), custom_call_target="tpu_custom_call", output_to_operand_aliasing={{}: (5, {})} | custom-call | flops 1610612736 | bytes 5767168 | tf_op jit(solution)/shard_map/last_kept/pallas_call | solution.py:108
  160.8 2.6 %expand_and_add.1 = bf16[256,512]{1,0:T(8,128)(2,1)} custom-call(bf16[64,256]{1,0:T(8,128)(2,1)S(1)} %add.35.shrunk, s32[256,1]{1,0:T(8,128)S(1)} %copy.18.slot, bf16[1024,512]{1,0:T(8,128)(2,1)} %bitcast.6.factors, f32[256,512]{1,0:T(8,128)S(1)} %last_kept.1.kept, f32[256,512]{1,0:T(8,128)S(1)} %collective-permute-done.8.other), custom_call_target="tpu_custom_call" | custom-call | flops 268435456 | bytes 2359296 | tf_op jit(solution)/shard_map/expand_and_add/pallas_call | solution.py:146
  (29 shorter events, 0.2 us)
Async XLA Ops:
  6.5 39.9 %all-gather.5.cloned.1.call-start = ((), (), s32[]{:S(2)}) async-start(), calls=%async_computation.2 | async-start | bytes 1310720 | tf_op jit(solution)/shard_map/all_gather | solution.py:188
  8.4 76.0 %all-gather.3.cloned.1.call-start = ((), (), s32[]{:S(2)}) async-start(), calls=%async_computation.1 | async-start | bytes 1310720 | tf_op jit(solution)/shard_map/all_gather | solution.py:188
  10.2 76.2 %copy-start.5 = (s32[256]{0:T(256)S(1)}, s32[256]{0:T(256)}, u32[]{:S(2)}) copy-start(s32[256]{0:T(256)} %param.11) | copy-start | bytes 3076
  10.2 76.2 %copy-start.6 = (s32[16]{0:T(128)S(1)}, s32[16]{0:T(128)}, u32[]{:S(2)}) copy-start(s32[16]{0:T(128)} %param.12) | copy-start | bytes 196
  38.4 48.1 %collective-permute-start.3 = (bf16[128,3072]{1,0:T(8,128)(2,1)S(1)}, bf16[128,3072]{1,0:T(8,128)(2,1)}, u32[]{:S(2)}, u32[]{:S(2)}) collective-permute-start(bf16[128,3072]{1,0:T(8,128)(2,1)S(1)} %all_gather.15.refs_0_), channel_id=1, source_target_pairs={{0,2},{2,0},{1,3},{3,1},{4,6},{6,4},{5,7},{7,5},{8,10},{10,8},{9,1... | collective-permute-start | bytes 2359304 | tf_op jit(solution)/shard_map/ppermute | solution.py:189
  46.5 49.4 %collective-permute-start.2 = (bf16[128,4096]{1,0:T(8,128)(2,1)}, bf16[128,4096]{1,0:T(8,128)(2,1)}, u32[]{:S(2)}, u32[]{:S(2)}) collective-permute-start(bf16[128,4096]{1,0:T(8,128)(2,1)} %all-gather.5.cloned.1.call-done.refs_0_), channel_id=1, source_target_pairs={{0,2},{2,0},{1,3},{3,1},{4,6},{6,4},{5,7},{7,5},{8,10},{10,8},{9,1... | collective-permute-start | bytes 3145736 | tf_op jit(solution)/shard_map/ppermute | solution.py:189
  71.9 64.0 %collective-permute-start = (bf16[128,3072]{1,0:T(8,128)(2,1)S(1)}, bf16[128,3072]{1,0:T(8,128)(2,1)S(1)}, u32[]{:S(2)}, u32[]{:S(2)}) collective-permute-start(bf16[128,3072]{1,0:T(8,128)(2,1)S(1)} %all_gather.12.refs_0_.refs_1_), channel_id=1, source_target_pairs={{0,2},{2,0},{1,3},{3,1},{4,6},{6,4},{5,7},{7,5},{8,10},{10,8},{9,1... | collective-permute-start | bytes 2359304 | tf_op jit(solution)/shard_map/ppermute | solution.py:189
  72.6 1.6 copy-start.2
  77.5 83.2 %all-to-all-start = ((bf16[8,128,512]{2,1,0:T(8,128)(2,1)}), bf16[8,128,512]{2,1,0:T(8,128)(2,1)}, u32[]{:S(2)}, u32[]{:S(2)}) async-start(bf16[8,128,512]{2,1,0:T(8,128)(2,1)} %expand_blocks.1), calls=%async_computation | async-start | bytes 2097152 | tf_op jit(solution)/shard_map/all_to_all | solution.py:184
  84.4 43.2 %collective-permute-start.1 = (bf16[128,4096]{1,0:T(8,128)(2,1)}, bf16[128,4096]{1,0:T(8,128)(2,1)}, u32[]{:S(2)}, u32[]{:S(2)}) collective-permute-start(bf16[128,4096]{1,0:T(8,128)(2,1)} %all-gather.3.cloned.1.call-done.refs_0_), channel_id=1, source_target_pairs={{0,2},{2,0},{1,3},{3,1},{4,6},{6,4},{5,7},{7,5},{8,10},{10,8},{9,1... | collective-permute-start | bytes 3145736 | tf_op jit(solution)/shard_map/ppermute | solution.py:189
  86.5 2.0 %copy-start = (bf16[2,14336,64]{1,2,0:T(8,128)(2,1)S(1)}, bf16[2,14336,64]{1,2,0:T(8,128)(2,1)}, u32[]{:S(2)}) copy-start(bf16[2,14336,64]{1,2,0:T(8,128)(2,1)} %param.9) | copy-start | bytes 11010052
  88.5 7.4 %copy-start.1 = (bf16[2,14336,64]{1,2,0:T(8,128)(2,1)S(1)}, bf16[2,14336,64]{1,2,0:T(8,128)(2,1)}, u32[]{:S(2)}) copy-start(bf16[2,14336,64]{1,2,0:T(8,128)(2,1)} %param.9) | copy-start | bytes 11010052
  88.5 7.4 %copy-start.4 = (bf16[128,4096]{1,0:T(8,128)(2,1)S(1)}, bf16[128,4096]{1,0:T(8,128)(2,1)}, u32[]{:S(2)}) copy-start(bf16[128,4096]{1,0:T(8,128)(2,1)} %all-gather.5.cloned.1.call-done.refs_0_) | copy-start | bytes 3145732
  95.9 31.7 %copy-start.3 = (bf16[128,4096]{1,0:T(8,128)(2,1)S(1)}, bf16[128,4096]{1,0:T(8,128)(2,1)}, u32[]{:S(2)}) copy-start(bf16[128,4096]{1,0:T(8,128)(2,1)} %all-gather.3.cloned.1.call-done.refs_0_) | copy-start | bytes 3145732
  143.0 17.7 %collective-permute-start.8 = (f32[256,512]{1,0:T(8,128)S(1)}, f32[256,512]{1,0:T(8,128)S(1)}, u32[]{:S(2)}, u32[]{:S(2)}) collective-permute-start(f32[256,512]{1,0:T(8,128)S(1)} %last_sent.1.refs_0_), channel_id=1, source_target_pairs={{0,1},{1,0},{2,3},{3,2},{4,5},{5,4},{6,7},{7,6},{8,9},{9,8},{10,11... | collective-permute-start | bytes 1572872 | tf_op jit(solution)/shard_map/ppermute | solution.py:204
  143.1 2.0 %collective-permute-start.4 = (f32[64,256]{1,0:T(8,128)S(1)}, f32[64,256]{1,0:T(8,128)S(1)}, u32[]{:S(2)}, u32[]{:S(2)}) collective-permute-start(f32[64,256]{1,0:T(8,128)S(1)} %fusion.refs_0_), channel_id=1, source_target_pairs={{0,1},{1,0},{2,3},{3,2},{4,5},{5,4},{6,7},{7,6},{8,9},{9,8},{10,11... | collective-permute-start | bytes 196616 | tf_op jit(solution)/shard_map/ppermute | solution.py:203
  145.1 4.0 %collective-permute-start.5 = (bf16[64,256]{1,0:T(8,128)(2,1)S(1)}, bf16[64,256]{1,0:T(8,128)(2,1)S(1)}, u32[]{:S(2)}, u32[]{:S(2)}) collective-permute-start(bf16[64,256]{1,0:T(8,128)(2,1)S(1)} %add_convert_fusion), channel_id=1, source_target_pairs={{0,2},{2,0},{4,6},{6,4},{8,10},{10,8},{12,14},{14,12},{1,3},{3,1},... | collective-permute-start | bytes 98312 | tf_op jit(solution)/shard_map/ppermute | solution.py:207
  149.1 4.0 %collective-permute-start.6 = (bf16[64,256]{1,0:T(8,128)(2,1)S(1)}, bf16[64,256]{1,0:T(8,128)(2,1)S(1)}, u32[]{:S(2)}, u32[]{:S(2)}) collective-permute-start(bf16[64,256]{1,0:T(8,128)(2,1)S(1)} %add.33), channel_id=1, source_target_pairs={{0,4},{2,6},{4,0},{6,2},{8,12},{10,14},{12,8},{14,10},{1,5},{3,7},... | collective-permute-start | bytes 98312 | tf_op jit(solution)/shard_map/ppermute | solution.py:207
  153.1 7.6 %collective-permute-start.7 = (bf16[64,256]{1,0:T(8,128)(2,1)S(1)}, bf16[64,256]{1,0:T(8,128)(2,1)S(1)}, u32[]{:S(2)}, u32[]{:S(2)}) collective-permute-start(bf16[64,256]{1,0:T(8,128)(2,1)S(1)} %add.34), channel_id=1, source_target_pairs={{0,8},{2,10},{4,12},{6,14},{8,0},{10,2},{12,4},{14,6},{1,9},{3,11}... | collective-permute-start | bytes 98312 | tf_op jit(solution)/shard_map/ppermute | solution.py:207
Sparse Core Ops, SparseCore 0:
  8.9 37.4 all-gather.4
  48.0 33.5 all-gather.2

commit v5 on v3

--- a/solution.py
+++ b/solution.py
@@ -11,6 +11,7 @@
 F32, BF16 = jnp.float32, jnp.bfloat16
 TILE = 1024
 MIB = 2**20
+MATMUL_MIB = 56
 
 
 def params(mib):
@@ -42,11 +43,13 @@
     )(hidden, *after)
 
 
-def split_kernel(scalars, src, dst):
+def split_kernel(scalars, src, *refs):
+    *_, dst, mark = refs
     dst[...] = src[...][None]
-
-
-def expand_blocks(scalars, half, expand, n, cores):
+    mark[...] = jnp.zeros_like(mark)
+
+
+def expand_blocks(scalars, half, expand, n, cores, after):
     owned, rank, width = expand.shape
     rows = owned * rank
     share = width // (n * cores)
@@ -55,64 +58,62 @@
         grid_spec=pltpu.PrefetchScalarGridSpec(
             num_scalar_prefetch=1,
             grid=(n,),
-            in_specs=[pl.BlockSpec((rows, share), lambda s, t: (0, s * cores + t[half]))],
-            out_specs=pl.BlockSpec((1, rows, share), lambda s, t: (s, 0, 0)),
-        ),
-        out_shape=jax.ShapeDtypeStruct((n, rows, share), BF16),
+            in_specs=[pl.BlockSpec((rows, share), lambda s, t: (0, s * cores + t[half]))]
+            + [pl.BlockSpec(memory_space=pl.ANY)] * len(after),
+            out_specs=[pl.BlockSpec((1, rows, share), lambda s, t: (s, 0, 0)), pl.BlockSpec((8, 128), lambda s, t: (0, 0))],
+        ),
+        out_shape=[jax.ShapeDtypeStruct((n, rows, share), BF16), jax.ShapeDtypeStruct((8, 128), F32)],
         compiler_params=params(40),
         cost_estimate=pl.CostEstimate(flops=0, bytes_accessed=4 * n * rows * share, transcendentals=0),
         name="expand_blocks",
-    )(scalars, expand.reshape(rows, width))
-
-
-def matmul_kernel(n, base, sides, narrow, has_acc, waits, scalars, *refs):
+    )(scalars, expand.reshape(rows, width), *after)
+
+
+def matmul_kernel(n, waits, base, sides, narrow, has_acc, token, scalars, *refs):
     refs = list(refs)[waits:]
     pieces = [refs.pop(0) for _ in range(n)]
     weights = [refs.pop(0) for _ in range(sides)]
     shrink = refs.pop(0) if narrow else None
-    count = sides + narrow
-    before = [refs.pop(0) for _ in range(count)] if has_acc else None
-    after = [refs.pop(0) for _ in range(count)]
+    outs = sides + narrow
+    before = [refs.pop(0) for _ in range(outs)] if has_acc else None
+    acc = [refs.pop(0) for _ in range(outs)]
+    if token:
+        refs.pop(0)[...] = jnp.zeros((8, 128), F32)
     lhs, sems = refs
     step = pl.program_id(0)
     rows = pieces[0].shape[0]
-    tile = lhs.shape[2]
 
     @pl.when(step == 0)
     def _():
         copies = []
         for i in range(n):
             at = pl.multiple_of(scalars[base + i] * rows, rows)
-            for j in range(lhs.shape[0]):
-                copies.append(
-                    pltpu.make_async_copy(
-                        pieces[i].at[:, pl.ds(j * tile, tile)], lhs.at[j, pl.ds(at, rows), :], sems.at[i, j]
-                    )
-                )
+            copies.append(pltpu.make_async_copy(pieces[i], lhs.at[pl.ds(at, rows), :], sems.at[i]))
         for copy in copies:
             copy.start()
-        for i in range(count):
-            after[i][...] = before[i][...] if has_acc else jnp.zeros_like(after[i])
+        for i, out in enumerate(acc):
+            out[...] = before[i][...] if has_acc else jnp.zeros_like(out)
         for copy in copies:
             copy.wait()
 
-    left = lhs[step]
+    left = lhs[:, pl.ds(pl.multiple_of(step * TILE, TILE), TILE)]
     if narrow:
-        after[-1][...] += lax.dot_general(
+        acc[-1][...] += lax.dot_general(
             shrink[...], left, (((1,), (1,)), ((), ())), preferred_element_type=F32
         )
     for i in range(sides):
-        after[i][...] += jnp.dot(left, weights[i][...], preferred_element_type=F32)
-
-
-def chunk_matmul(scalars, base, half, pieces, down, shrink, acc, start, sides, narrow, label, after=()):
+        acc[i][...] += jnp.dot(left, weights[i][...], preferred_element_type=F32)
+
+
+def chunk_matmul(scalars, base, half, pieces, down, shrink, acc, start, sides, narrow, label, after=(), token=False):
     n = len(pieces)
     rows, width = pieces[0].shape[0] * n, pieces[0].shape[1]
     share = down.shape[1] // 2
     steps = width // TILE
     first = start // TILE
     ranks = shrink.shape[0]
-    in_specs = [pl.BlockSpec(memory_space=pl.ANY) for _ in (*after, *pieces)]
+    in_specs = [pl.BlockSpec(memory_space=pl.ANY) for _ in after]
+    in_specs += [pl.BlockSpec(memory_space=pltpu.HBM) for _ in pieces]
     args = [*after, *pieces]
     for side in sides:
         in_specs.append(pl.BlockSpec((TILE, share), functools.partial(lambda side, k, s: (first + k, s[half + side]), side)))
@@ -128,18 +129,19 @@
         in_specs += whole
         args += list(acc)
     columns = share * len(sides) + ranks * narrow
-    return pl.pallas_call(
-        functools.partial(matmul_kernel, n, base, len(sides), narrow, acc is not None, len(after)),
+    marks = [(8, 128)] * token
+    return pl.pallas_call(
+        functools.partial(matmul_kernel, n, len(after), base, len(sides), narrow, acc is not None, token),
         grid_spec=pltpu.PrefetchScalarGridSpec(
             num_scalar_prefetch=1,
             grid=(steps,),
             in_specs=in_specs,
-            out_specs=whole,
-            scratch_shapes=[pltpu.VMEM((steps, rows, TILE), BF16), pltpu.SemaphoreType.DMA((n, steps))],
-        ),
-        out_shape=[jax.ShapeDtypeStruct(shape, F32) for shape in shapes],
+            out_specs=whole + [pl.BlockSpec((8, 128), lambda k, s: (0, 0))] * token,
+            scratch_shapes=[pltpu.VMEM((rows, width), BF16), pltpu.SemaphoreType.DMA((n,))],
+        ),
+        out_shape=[jax.ShapeDtypeStruct(shape, F32) for shape in shapes + marks],
         input_output_aliases=aliases,
-        compiler_params=params(40),
+        compiler_params=params(MATMUL_MIB),
         cost_estimate=pl.CostEstimate(
             flops=4 * rows * width * columns,
             bytes_accessed=2 * width * (columns + rows) + 8 * rows * columns,
@@ -217,24 +219,28 @@
         acc = None
         start = 0
         after = {}
-        blocks = expand_blocks(scalars, half, expand, n, cores)
-        factors = lax.all_to_all(blocks, "store", 0, 0)
         for chunk, width in enumerate(widths):
             own = take(hidden, start, width, after[chunk]) if chunk in after else hidden[:, start:start + width]
             way = chunk % 2
             pieces = [own]
-            for length, pairs in zip(((long, short), (short, long))[way], (clockwise, counter)):
+            lengths = ((long, short), (short, long))[way]
+            for length, pairs in zip(lengths, (clockwise, counter)):
                 moving = own
                 for step in range(length):
                     moving = lax.ppermute(moving, "store", pairs)
                     pieces.append(moving)
-            if chunk == 0:
-                after[2] = [pieces[(long, short)[way]], pieces[-1], blocks]
-            if chunk == 1:
-                after[3] = [pieces[(long, short)[way]], pieces[-1], factors]
             call = functools.partial(chunk_matmul, scalars, way * n, half, pieces, down, shrink_rows)
             if chunk < len(widths) - 1:
-                acc = call(acc, start, (0, 1), True, f"chunk_{chunk}")
+                ends, late = [pieces[lengths[0]], pieces[-1]], [pieces[lengths[0] - 1], pieces[-2]]
+                first = []
+                if chunk == 2:
+                    blocks, *first = expand_blocks(scalars, half, expand, n, cores, [*late, token])
+                    factors = lax.all_to_all(blocks, "store", 0, 0)
+                *acc, token = call(acc, start, (0, 1), True, f"chunk_{chunk}", first, True)
+                if chunk == 0:
+                    after[2], after[3] = ends, [token]
+                if chunk == 1:
+                    after[3] += ends
             else:
                 narrow, = call(acc[2:], start, (), True, "last_narrow")
                 mine = [

time: 161 us -> 159 us (0.988)
  Pallas kernels: 40.9 us -> 51.5 us
  starting transfers between devices: 60.5 us -> 50.6 us
  local copies, waits for them, and re-layouts: 18.7 us -> 9.05 us
  waiting for transfers between devices: 38.8 us -> 44.4 us
    pallas_call x6, Pallas kernels: 35.1 us -> 46.7 us  [chunk_matmul(): pl.pallas_call(functools.partial(matmul_kernel, n, len(after), base, len(...]
    unnamed x74 -> x86, local copies, waits for them, and re-layouts: 17.1 us -> 5.79 us
    ppermute x28, starting transfers between devices: 49 us -> 38.4 us  [shards(): moving = lax.ppermute(moving, 'store', pairs)]
    ppermute x28, waiting for transfers between devices: 32.2 us -> 39.2 us  [shards(): moving = lax.ppermute(moving, 'store', pairs)]
    ppermute x3, starting transfers between devices: 3.71 us -> 6.78 us  [shards(): lax.ppermute(shrunk, 'store', [(s, s ^ bit) for s in range(n)])]
    all_to_all x1, starting transfers between devices: 7.28 us -> 4.82 us  [shards(): factors = lax.all_to_all(blocks, 'store', 0, 0)]
    slice x2, local copies, waits for them, and re-layouts: 0.03 us -> 1.91 us  [shards(): hidden[:, start:start + width]]
  transfers between devices with their start and end apart: 34 -> 34, of which waited for: 11 -> 13; matrix products, arithmetic and copies ran while one was open for 1% -> 3% of each run, Pallas kernels for 17% -> 32%
where the time goes in v5:
time: 159 us; the launch traced here: 158 us
  Pallas kernels  51.5 us (32%)
  starting transfers between devices  50.6 us (32%)
  waiting for transfers between devices  44.4 us (28%)
  local copies, waits for them, and re-layouts  9.05 us (6%)
  other arithmetic  1.65 us (1%)
    pallas_call x6, Pallas kernels, chunk_matmul(): pl.pallas_call(functools.partial(matmul_kernel, n, len(after), base, len(...  46.7 us
    ppermute x28, waiting for transfers between devices, shards(): moving = lax.ppermute(moving, 'store', pairs)  39.2 us
    ppermute x28, starting transfers between devices, shards(): moving = lax.ppermute(moving, 'store', pairs)  38.4 us
    ppermute x3, starting transfers between devices, shards(): lax.ppermute(shrunk, 'store', [(s, s ^ bit) for s in range(n)])  6.78 us
    unnamed x86, local copies, waits for them, and re-layouts  5.79 us
    all_to_all x1, starting transfers between devices, shards(): factors = lax.all_to_all(blocks, 'store', 0, 0)  4.82 us
    ppermute x3, waiting for transfers between devices, shards(): lax.ppermute(shrunk, 'store', [(s, s ^ bit) for s in range(n)])  3.71 us
    pallas_call x1, Pallas kernels, expand_blocks(): pl.pallas_call(split_kernel, grid_spec=pltpu.PrefetchScalarGridSpec(num_s...  3.36 us
  transfers between devices with their start and end apart: 34, of which 13 were waited for; matrix products, arithmetic and copies ran while one was open for 3% of the time, Pallas kernels for 32%

profile of v5, /device:TPU:0, one launch (start us, length us, event | category | flops | bytes accessed | tf_op | source)
XLA Modules:
  0.0 157.7 jit_solution(720982681702760570)
XLA Ops:
  1.0 3.1 %collective-permute-start = (bf16[32,3072]{1,0:T(8,128)(2,1)S(1)}, bf16[32,3072]{1,0:T(8,128)(2,1)S(1)}, u32[]{:S(2)}, u32[]{:S(2)}) collective-permute-start(bf16[32,3072]{1,0:T(8,128)(2,1)S(1)} %slice.12.refs_0_), channel_id=1, source_target_pairs={{0,4},{4,8},{8,12},{12,14},{14,10},{10,6},{6,2},{2,0},{1,5},{5,9},... | collective-permute-start | bytes 589832 | tf_op jit(solution)/shard_map/ppermute | solution.py:230
  4.0 4.8 %collective-permute-done.refs_1_ = bf16[32,3072]{1,0:T(8,128)(2,1)S(1)} collective-permute-done((bf16[32,3072]{1,0:T(8,128)(2,1)S(1)}, bf16[32,3072]{1,0:T(8,128)(2,1)S(1)}, u32[]{:S(2)}, u32[]{:S(2)}) %collective-permute-start) | collective-permute-done | bytes 196640 | tf_op jit(solution)/shard_map/ppermute | solution.py:230
  8.9 1.8 %collective-permute-start.1 = (bf16[32,3072]{1,0:T(8,128)(2,1)S(1)}, bf16[32,3072]{1,0:T(8,128)(2,1)S(1)}, u32[]{:S(2)}, u32[]{:S(2)}) collective-permute-start(bf16[32,3072]{1,0:T(8,128)(2,1)S(1)} %collective-permute-done.refs_1_), channel_id=1, source_target_pairs={{0,4},{4,8},{8,12},{12,14},{14,10},{10,6},{6,2},{2,0},{1,5},{5,9},... | collective-permute-start | bytes 589832 | tf_op jit(solution)/shard_map/ppermute | solution.py:230
  11.9 1.7 %collective-permute-start.5 = (bf16[32,3072]{1,0:T(8,128)(2,1)S(1)}, bf16[32,3072]{1,0:T(8,128)(2,1)S(1)}, u32[]{:S(2)}, u32[]{:S(2)}) collective-permute-start(bf16[32,3072]{1,0:T(8,128)(2,1)S(1)} %collective-permute-done.4.refs_5_), channel_id=1, source_target_pairs={{0,2},{4,0},{8,4},{12,8},{14,12},{10,14},{6,10},{2,6},{1,3},{5,1},... | collective-permute-start | bytes 589832 | tf_op jit(solution)/shard_map/ppermute | solution.py:230
  18.0 2.9 %collective-permute-done.10.refs_4_ = bf16[32,4096]{1,0:T(8,128)(2,1)S(1)} collective-permute-done((bf16[32,4096]{1,0:T(8,128)(2,1)S(1)}, bf16[32,4096]{1,0:T(8,128)(2,1)S(1)}, u32[]{:S(2)}, u32[]{:S(2)}) %collective-permute-start.10) | collective-permute-done | bytes 262176 | tf_op jit(solution)/shard_map/ppermute | solution.py:230
  21.2 4.0 %collective-permute-done.5.refs_6_ = bf16[32,3072]{1,0:T(8,128)(2,1)S(1)} collective-permute-done((bf16[32,3072]{1,0:T(8,128)(2,1)S(1)}, bf16[32,3072]{1,0:T(8,128)(2,1)S(1)}, u32[]{:S(2)}, u32[]{:S(2)}) %collective-permute-start.5) | collective-permute-done | bytes 196640 | tf_op jit(solution)/shard_map/ppermute | solution.py:230
  25.4 1.8 %collective-permute-start.3 = (bf16[32,3072]{1,0:T(8,128)(2,1)S(1)}, bf16[32,3072]{1,0:T(8,128)(2,1)S(1)}, u32[]{:S(2)}, u32[]{:S(2)}) collective-permute-start(bf16[32,3072]{1,0:T(8,128)(2,1)S(1)} %collective-permute-done.2.refs_3_), channel_id=1, source_target_pairs={{0,4},{4,8},{8,12},{12,14},{14,10},{10,6},{6,2},{2,0},{1,5},{5,9},... | collective-permute-start | bytes 589832 | tf_op jit(solution)/shard_map/ppermute | solution.py:230
  28.8 1.9 %collective-permute-done.11.refs_5_ = bf16[32,4096]{1,0:T(8,128)(2,1)S(1)} collective-permute-done((bf16[32,4096]{1,0:T(8,128)(2,1)S(1)}, bf16[32,4096]{1,0:T(8,128)(2,1)S(1)}, u32[]{:S(2)}, u32[]{:S(2)}) %collective-permute-start.11) | collective-permute-done | bytes 262176 | tf_op jit(solution)/shard_map/ppermute | solution.py:230
  31.0 4.0 %collective-permute-done.6.refs_7_.refs_1_ = bf16[32,3072]{1,0:T(8,128)(2,1)S(1)} collective-permute-done((bf16[32,3072]{1,0:T(8,128)(2,1)S(1)}, bf16[32,3072]{1,0:T(8,128)(2,1)S(1)}, u32[]{:S(2)}, u32[]{:S(2)}) %collective-permute-start.6) | collective-permute-done | bytes 196640 | tf_op jit(solution)/shard_map/ppermute | solution.py:230
  36.3 1.6 %collective-permute-start.21 = (bf16[32,4096]{1,0:T(8,128)(2,1)S(1)}, bf16[32,4096]{1,0:T(8,128)(2,1)S(1)}, u32[]{:S(2)}, u32[]{:S(2)}) collective-permute-start(bf16[32,4096]{1,0:T(8,128)(2,1)S(1)} %take_7168.1.refs_1_), channel_id=1, source_target_pairs={{0,4},{4,8},{8,12},{12,14},{14,10},{10,6},{6,2},{2,0},{1,5},{5,9},... | collective-permute-start | bytes 786440 | tf_op jit(solution)/shard_map/ppermute | solution.py:230
  39.2 1.6 %collective-permute-start.9 = (bf16[32,4096]{1,0:T(8,128)(2,1)S(1)}, bf16[32,4096]{1,0:T(8,128)(2,1)S(1)}, u32[]{:S(2)}, u32[]{:S(2)}) collective-permute-start(bf16[32,4096]{1,0:T(8,128)(2,1)S(1)} %collective-permute-done.8.refs_2_), channel_id=1, source_target_pairs={{0,4},{4,8},{8,12},{12,14},{14,10},{10,6},{6,2},{2,0},{1,5},{5,9},... | collective-permute-start | bytes 786440 | tf_op jit(solution)/shard_map/ppermute | solution.py:230
  41.7 3.9 %collective-permute-done.21.refs_2_ = bf16[32,4096]{1,0:T(8,128)(2,1)S(1)} collective-permute-done((bf16[32,4096]{1,0:T(8,128)(2,1)S(1)}, bf16[32,4096]{1,0:T(8,128)(2,1)S(1)}, u32[]{:S(2)}, u32[]{:S(2)}) %collective-permute-start.21) | collective-permute-done | bytes 262176 | tf_op jit(solution)/shard_map/ppermute | solution.py:230
  47.2 8.2 %chunk_0.1 = (f32[256,512]{1,0:T(8,128)}, f32[256,512]{1,0:T(8,128)}, f32[128,256]{1,0:T(8,128)}, f32[8,128]{1,0:T(8,128)}) custom-call(s32[18]{0:T(128)} %dynamic-slice_bitcast_fusion.scalars, bf16[32,3072]{1,0:T(8,128)(2,1)} %copy-done.25, bf16[32,3072]{1,0:T(8,128)(2,1)} %copy-done.36, bf16[32,3072]{1,0:T(8,128)(2,1)} %copy-done.38, ...), custom_call_target="tpu_custom_call" | custom-call | flops 3623878656 | bytes 11010048 | tf_op jit(solution)/shard_map/chunk_0/pallas_call | solution.py:133
  57.1 1.8 %collective-permute-start.23 = (bf16[32,4096]{1,0:T(8,128)(2,1)S(1)}, bf16[32,4096]{1,0:T(8,128)(2,1)S(1)}, u32[]{:S(2)}, u32[]{:S(2)}) collective-permute-start(bf16[32,4096]{1,0:T(8,128)(2,1)S(1)} %collective-permute-done.22.refs_3_), channel_id=1, source_target_pairs={{0,4},{4,8},{8,12},{12,14},{14,10},{10,6},{6,2},{2,0},{1,5},{5,9},... | collective-permute-start | bytes 786440 | tf_op jit(solution)/shard_map/ppermute | solution.py:230
  58.9 10.1 %chunk_1.1 = (f32[256,512]{1,0:T(8,128)}, f32[256,512]{1,0:T(8,128)}, f32[128,256]{1,0:T(8,128)}, f32[8,128]{1,0:T(8,128)}) custom-call(s32[18]{0:T(128)} %dynamic-slice_bitcast_fusion.scalars, bf16[32,4096]{1,0:T(8,128)(2,1)} %copy-done.24, bf16[32,4096]{1,0:T(8,128)(2,1)} %copy-done.29, ...), custom_call_target="tpu_custom_call", output_to_operand_aliasing={{0}: (12, {}), {1}: (13, {}), {2}: (14, {})} | custom-call | flops 4831838208 | bytes 13893632 | tf_op jit(solution)/shard_map/chunk_1/pallas_call | solution.py:133
  69.8 3.4 %expand_blocks.1 = (bf16[8,128,512]{2,1,0:T(8,128)(2,1)}, f32[8,128]{1,0:T(8,128)S(1)}) custom-call(s32[18]{0:T(128)S(1)} %copy-done.12, bf16[128,8192]{1,0:T(8,128)(2,1)S(1)} %bitcast.9, bf16[32,4096]{1,0:T(8,128)(2,1)S(1)} %collective-permute-done.23.refs_0_.refs_4_, bf16[32,4096]{1,0:T(8,128)(2,1)S(1)} %collective-permute-done.25.refs_1_.refs_7_, ...), custom_call_target="tpu_custom_call" | custom-call | bytes 2097152 | tf_op jit(solution)/shard_map/expand_blocks/pallas_call | solution.py:56
  73.7 4.8 %all-to-all-start = ((bf16[8,128,512]{2,1,0:T(8,128)(2,1)}), bf16[8,128,512]{2,1,0:T(8,128)(2,1)S(1)}, u32[]{:S(2)}, u32[]{:S(2)}) async-start(bf16[8,128,512]{2,1,0:T(8,128)(2,1)} %get-tuple-element.28), calls=%async_computation | async-start | bytes 2097152 | tf_op jit(solution)/shard_map/all_to_all | solution.py:238
  78.5 2.0 %collective-permute-start.14 = (bf16[32,3072]{1,0:T(8,128)(2,1)S(1)}, bf16[32,3072]{1,0:T(8,128)(2,1)S(1)}, u32[]{:S(2)}, u32[]{:S(2)}) collective-permute-start(bf16[32,3072]{1,0:T(8,128)(2,1)S(1)} %take_11264.1.refs_0_.refs_1_), channel_id=1, source_target_pairs={{0,4},{4,8},{8,12},{12,14},{14,10},{10,6},{6,2},{2,0},{1,5},{5,9},... | collective-permute-start | bytes 589832 | tf_op jit(solution)/shard_map/ppermute | solution.py:230
  80.6 2.0 %collective-permute-start.27 = (bf16[32,4096]{1,0:T(8,128)(2,1)S(1)}, bf16[32,4096]{1,0:T(8,128)(2,1)S(1)}, u32[]{:S(2)}, u32[]{:S(2)}) collective-permute-start(bf16[32,4096]{1,0:T(8,128)(2,1)S(1)} %collective-permute-done.25.refs_1_.refs_7_), channel_id=1, source_target_pairs={{0,2},{4,0},{8,4},{12,8},{14,12},{10,14},{6,10},{2,6},{1,3},{5,1},... | collective-permute-start | bytes 786440 | tf_op jit(solution)/shard_map/ppermute | solution.py:230
  82.8 12.7 %collective-permute-done.14.refs_1_.refs_2_ = bf16[32,3072]{1,0:T(8,128)(2,1)S(1)} collective-permute-done((bf16[32,3072]{1,0:T(8,128)(2,1)S(1)}, bf16[32,3072]{1,0:T(8,128)(2,1)S(1)}, u32[]{:S(2)}, u32[]{:S(2)}) %collective-permute-start.14) | collective-permute-done | bytes 196640 | tf_op jit(solution)/shard_map/ppermute | solution.py:230
  95.4 7.3 %collective-permute-start.15 = (bf16[32,3072]{1,0:T(8,128)(2,1)S(1)}, bf16[32,3072]{1,0:T(8,128)(2,1)S(1)}, u32[]{:S(2)}, u32[]{:S(2)}) collective-permute-start(bf16[32,3072]{1,0:T(8,128)(2,1)S(1)} %collective-permute-done.14.refs_1_.refs_2_), channel_id=1, source_target_pairs={{0,4},{4,8},{8,12},{12,14},{14,10},{10,6},{6,2},{2,0},{1,5},{5,9},... | collective-permute-start | bytes 589832 | tf_op jit(solution)/shard_map/ppermute | solution.py:230
  102.8 3.2 %collective-permute-done.15.refs_2_.refs_3_ = bf16[32,3072]{1,0:T(8,128)(2,1)S(1)} collective-permute-done((bf16[32,3072]{1,0:T(8,128)(2,1)S(1)}, bf16[32,3072]{1,0:T(8,128)(2,1)S(1)}, u32[]{:S(2)}, u32[]{:S(2)}) %collective-permute-start.15) | collective-permute-done | bytes 196640 | tf_op jit(solution)/shard_map/ppermute | solution.py:230
  105.9 3.8 %collective-permute-start.16 = (bf16[32,3072]{1,0:T(8,128)(2,1)S(1)}, bf16[32,3072]{1,0:T(8,128)(2,1)S(1)}, u32[]{:S(2)}, u32[]{:S(2)}) collective-permute-start(bf16[32,3072]{1,0:T(8,128)(2,1)S(1)} %collective-permute-done.15.refs_2_.refs_3_), channel_id=1, source_target_pairs={{0,4},{4,8},{8,12},{12,14},{14,10},{10,6},{6,2},{2,0},{1,5},{5,9},... | collective-permute-start | bytes 589832 | tf_op jit(solution)/shard_map/ppermute | solution.py:230
  111.8 9.9 %chunk_2.1 = (f32[256,512]{1,0:T(8,128)}, f32[256,512]{1,0:T(8,128)}, f32[128,256]{1,0:T(8,128)}, f32[8,128]{1,0:T(8,128)}) custom-call(s32[18]{0:T(128)} %dynamic-slice_bitcast_fusion.scalars, f32[8,128]{1,0:T(8,128)} %copy-done.13, bf16[32,4096]{1,0:T(8,128)(2,1)} %copy-done.9, ...), custom_call_target="tpu_custom_call", output_to_operand_aliasing={{0}: (13, {}), {1}: (14, {}), {2}: (15, {})} | custom-call | flops 4831838208 | bytes 13893632 | tf_op jit(solution)/shard_map/chunk_2/pallas_call | solution.py:133
  122.5 5.4 %last_narrow.1 = f32[128,256]{1,0:T(8,128)} custom-call(s32[18]{0:T(128)} %dynamic-slice_bitcast_fusion.scalars, bf16[32,3072]{1,0:T(8,128)(2,1)} %copy-done.3, bf16[32,3072]{1,0:T(8,128)(2,1)} %copy-done.18, bf16[32,3072]{1,0:T(8,128)(2,1)} %copy-done.20, bf16[32,3072]{1,0:T(8,128)(2,1)} %copy-done.22, ...), custom_call_target="tpu_custom_call", output_to_operand_aliasing={{}: (10, {})} | custom-call | flops 402653184 | bytes 2621440 | tf_op jit(solution)/shard_map/last_narrow/pallas_call | solution.py:133
  129.4 6.6 %last_sent.1.refs_0_ = f32[256,512]{1,0:T(8,128)} custom-call(s32[18]{0:T(128)} %dynamic-slice_bitcast_fusion.scalars, f32[64,256]{1,0:T(8,128)} %fusion.refs_0_, bf16[32,3072]{1,0:T(8,128)(2,1)} %copy-done.3, bf16[32,3072]{1,0:T(8,128)(2,1)} %copy-done.18, bf16[32,3072]{1,0:T(8,128)(2,1)} %copy-done.20, ...), custom_call_target="tpu_custom_call", output_to_operand_aliasing={{}: (11, {})} | custom-call | flops 1610612736 | bytes 5767168 | tf_op jit(solution)/shard_map/last_sent/pallas_call | solution.py:133
  138.1 2.8 %collective-permute-start.29 = (bf16[64,256]{1,0:T(8,128)(2,1)S(1)}, bf16[64,256]{1,0:T(8,128)(2,1)S(1)}, u32[]{:S(2)}, u32[]{:S(2)}) collective-permute-start(bf16[64,256]{1,0:T(8,128)(2,1)S(1)} %add_convert_fusion), channel_id=1, source_target_pairs={{0,2},{2,0},{4,6},{6,4},{8,10},{10,8},{12,14},{14,12},{1,3},{3,1},... | collective-permute-start | bytes 98312 | tf_op jit(solution)/shard_map/ppermute | solution.py:258
  140.9 1.9 %collective-permute-done.29 = bf16[64,256]{1,0:T(8,128)(2,1)S(1)} collective-permute-done((bf16[64,256]{1,0:T(8,128)(2,1)S(1)}, bf16[64,256]{1,0:T(8,128)(2,1)S(1)}, u32[]{:S(2)}, u32[]{:S(2)}) %collective-permute-start.29) | collective-permute-done | bytes 32800 | tf_op jit(solution)/shard_map/ppermute | solution.py:258
  142.8 2.0 %collective-permute-start.30 = (bf16[64,256]{1,0:T(8,128)(2,1)S(1)}, bf16[64,256]{1,0:T(8,128)(2,1)S(1)}, u32[]{:S(2)}, u32[]{:S(2)}) collective-permute-start(bf16[64,256]{1,0:T(8,128)(2,1)S(1)} %add.29), channel_id=1, source_target_pairs={{0,4},{2,6},{4,0},{6,2},{8,12},{10,14},{12,8},{14,10},{1,5},{3,7},... | collective-permute-start | bytes 98312 | tf_op jit(solution)/shard_map/ppermute | solution.py:258
  145.0 1.8 %collective-permute-done.30 = bf16[64,256]{1,0:T(8,128)(2,1)S(1)} collective-permute-done((bf16[64,256]{1,0:T(8,128)(2,1)S(1)}, bf16[64,256]{1,0:T(8,128)(2,1)S(1)}, u32[]{:S(2)}, u32[]{:S(2)}) %collective-permute-start.30) | collective-permute-done | bytes 32800 | tf_op jit(solution)/shard_map/ppermute | solution.py:258
  146.8 2.0 %collective-permute-start.31 = (bf16[64,256]{1,0:T(8,128)(2,1)S(1)}, bf16[64,256]{1,0:T(8,128)(2,1)S(1)}, u32[]{:S(2)}, u32[]{:S(2)}) collective-permute-start(bf16[64,256]{1,0:T(8,128)(2,1)S(1)} %add.30), channel_id=1, source_target_pairs={{0,8},{2,10},{4,12},{6,14},{8,0},{10,2},{12,4},{14,6},{1,9},{3,11}... | collective-permute-start | bytes 98312 | tf_op jit(solution)/shard_map/ppermute | solution.py:258
  148.8 6.5 %last_kept.1.kept = f32[256,512]{1,0:T(8,128)} custom-call(s32[18]{0:T(128)} %dynamic-slice_bitcast_fusion.scalars, f32[256,512]{1,0:T(8,128)} %last_sent.1.refs_0_, bf16[32,3072]{1,0:T(8,128)(2,1)} %copy-done.3, bf16[32,3072]{1,0:T(8,128)(2,1)} %copy-done.18, bf16[32,3072]{1,0:T(8,128)(2,1)} %copy-done.20, ...), custom_call_target="tpu_custom_call", output_to_operand_aliasing={{}: (11, {})} | custom-call | flops 1610612736 | bytes 5767168 | tf_op jit(solution)/shard_map/last_kept/pallas_call | solution.py:133
  (143 shorter events, 25.9 us)
Async XLA Ops:
  1.0 7.9 %collective-permute-start = (bf16[32,3072]{1,0:T(8,128)(2,1)S(1)}, bf16[32,3072]{1,0:T(8,128)(2,1)S(1)}, u32[]{:S(2)}, u32[]{:S(2)}) collective-permute-start(bf16[32,3072]{1,0:T(8,128)(2,1)S(1)} %slice.12.refs_0_), channel_id=1, source_target_pairs={{0,4},{4,8},{8,12},{12,14},{14,10},{10,6},{6,2},{2,0},{1,5},{5,9},... | collective-permute-start | bytes 589832 | tf_op jit(solution)/shard_map/ppermute | solution.py:230
  4.0 7.9 %collective-permute-start.4 = (bf16[32,3072]{1,0:T(8,128)(2,1)S(1)}, bf16[32,3072]{1,0:T(8,128)(2,1)S(1)}, u32[]{:S(2)}, u32[]{:S(2)}) collective-permute-start(bf16[32,3072]{1,0:T(8,128)(2,1)S(1)} %slice.12.refs_0_), channel_id=1, source_target_pairs={{0,2},{4,0},{8,4},{12,8},{14,12},{10,14},{6,10},{2,6},{1,3},{5,1},... | collective-permute-start | bytes 589832 | tf_op jit(solution)/shard_map/ppermute | solution.py:230
  8.9 6.1 %collective-permute-start.1 = (bf16[32,3072]{1,0:T(8,128)(2,1)S(1)}, bf16[32,3072]{1,0:T(8,128)(2,1)S(1)}, u32[]{:S(2)}, u32[]{:S(2)}) collective-permute-start(bf16[32,3072]{1,0:T(8,128)(2,1)S(1)} %collective-permute-done.refs_1_), channel_id=1, source_target_pairs={{0,4},{4,8},{8,12},{12,14},{14,10},{10,6},{6,2},{2,0},{1,5},{5,9},... | collective-permute-start | bytes 589832 | tf_op jit(solution)/shard_map/ppermute | solution.py:230
  11.7 9.3 %collective-permute-start.10 = (bf16[32,4096]{1,0:T(8,128)(2,1)S(1)}, bf16[32,4096]{1,0:T(8,128)(2,1)S(1)}, u32[]{:S(2)}, u32[]{:S(2)}) collective-permute-start(bf16[32,4096]{1,0:T(8,128)(2,1)S(1)} %slice.13.refs_0_), channel_id=1, source_target_pairs={{0,2},{4,0},{8,4},{12,8},{14,12},{10,14},{6,10},{2,6},{1,3},{5,1},... | collective-permute-start | bytes 786440 | tf_op jit(solution)/shard_map/ppermute | solution.py:230
  11.9 13.2 %collective-permute-start.5 = (bf16[32,3072]{1,0:T(8,128)(2,1)S(1)}, bf16[32,3072]{1,0:T(8,128)(2,1)S(1)}, u32[]{:S(2)}, u32[]{:S(2)}) collective-permute-start(bf16[32,3072]{1,0:T(8,128)(2,1)S(1)} %collective-permute-done.4.refs_5_), channel_id=1, source_target_pairs={{0,2},{4,0},{8,4},{12,8},{14,12},{10,14},{6,10},{2,6},{1,3},{5,1},... | collective-permute-start | bytes 589832 | tf_op jit(solution)/shard_map/ppermute | solution.py:230
  15.0 10.4 %collective-permute-start.2 = (bf16[32,3072]{1,0:T(8,128)(2,1)S(1)}, bf16[32,3072]{1,0:T(8,128)(2,1)S(1)}, u32[]{:S(2)}, u32[]{:S(2)}) collective-permute-start(bf16[32,3072]{1,0:T(8,128)(2,1)S(1)} %collective-permute-done.1.refs_2_), channel_id=1, source_target_pairs={{0,4},{4,8},{8,12},{12,14},{14,10},{10,6},{6,2},{2,0},{1,5},{5,9},... | collective-permute-start | bytes 589832 | tf_op jit(solution)/shard_map/ppermute | solution.py:230
  16.4 11.2 %collective-permute-start.7 = (bf16[32,4096]{1,0:T(8,128)(2,1)S(1)}, bf16[32,4096]{1,0:T(8,128)(2,1)S(1)}, u32[]{:S(2)}, u32[]{:S(2)}) collective-permute-start(bf16[32,4096]{1,0:T(8,128)(2,1)S(1)} %slice.13.refs_0_), channel_id=1, source_target_pairs={{0,4},{4,8},{8,12},{12,14},{14,10},{10,6},{6,2},{2,0},{1,5},{5,9},... | collective-permute-start | bytes 786440 | tf_op jit(solution)/shard_map/ppermute | solution.py:230
  21.0 9.8 %collective-permute-start.11 = (bf16[32,4096]{1,0:T(8,128)(2,1)S(1)}, bf16[32,4096]{1,0:T(8,128)(2,1)S(1)}, u32[]{:S(2)}, u32[]{:S(2)}) collective-permute-start(bf16[32,4096]{1,0:T(8,128)(2,1)S(1)} %collective-permute-done.10.refs_4_), channel_id=1, source_target_pairs={{0,2},{4,0},{8,4},{12,8},{14,12},{10,14},{6,10},{2,6},{1,3},{5,1},... | collective-permute-start | bytes 786440 | tf_op jit(solution)/shard_map/ppermute | solution.py:230
  25.2 9.8 %collective-permute-start.6 = (bf16[32,3072]{1,0:T(8,128)(2,1)S(1)}, bf16[32,3072]{1,0:T(8,128)(2,1)S(1)}, u32[]{:S(2)}, u32[]{:S(2)}) collective-permute-start(bf16[32,3072]{1,0:T(8,128)(2,1)S(1)} %collective-permute-done.5.refs_6_), channel_id=1, source_target_pairs={{0,2},{4,0},{8,4},{12,8},{14,12},{10,14},{6,10},{2,6},{1,3},{5,1},... | collective-permute-start | bytes 589832 | tf_op jit(solution)/shard_map/ppermute | solution.py:230
  25.4 9.6 %collective-permute-start.3 = (bf16[32,3072]{1,0:T(8,128)(2,1)S(1)}, bf16[32,3072]{1,0:T(8,128)(2,1)S(1)}, u32[]{:S(2)}, u32[]{:S(2)}) collective-permute-start(bf16[32,3072]{1,0:T(8,128)(2,1)S(1)} %collective-permute-done.2.refs_3_), channel_id=1, source_target_pairs={{0,4},{4,8},{8,12},{12,14},{14,10},{10,6},{6,2},{2,0},{1,5},{5,9},... | collective-permute-start | bytes 589832 | tf_op jit(solution)/shard_map/ppermute | solution.py:230
  27.7 11.5 %collective-permute-start.8 = (bf16[32,4096]{1,0:T(8,128)(2,1)S(1)}, bf16[32,4096]{1,0:T(8,128)(2,1)S(1)}, u32[]{:S(2)}, u32[]{:S(2)}) collective-permute-start(bf16[32,4096]{1,0:T(8,128)(2,1)S(1)} %collective-permute-done.7.refs_1_), channel_id=1, source_target_pairs={{0,4},{4,8},{8,12},{12,14},{14,10},{10,6},{6,2},{2,0},{1,5},{5,9},... | collective-permute-start | bytes 786440 | tf_op jit(solution)/shard_map/ppermute | solution.py:230
  30.8 10.0 %collective-permute-start.12 = (bf16[32,4096]{1,0:T(8,128)(2,1)S(1)}, bf16[32,4096]{1,0:T(8,128)(2,1)S(1)}, u32[]{:S(2)}, u32[]{:S(2)}) collective-permute-start(bf16[32,4096]{1,0:T(8,128)(2,1)S(1)} %collective-permute-done.11.refs_5_), channel_id=1, source_target_pairs={{0,2},{4,0},{8,4},{12,8},{14,12},{10,14},{6,10},{2,6},{1,3},{5,1},... | collective-permute-start | bytes 786440 | tf_op jit(solution)/shard_map/ppermute | solution.py:230
  36.3 9.3 %collective-permute-start.21 = (bf16[32,4096]{1,0:T(8,128)(2,1)S(1)}, bf16[32,4096]{1,0:T(8,128)(2,1)S(1)}, u32[]{:S(2)}, u32[]{:S(2)}) collective-permute-start(bf16[32,4096]{1,0:T(8,128)(2,1)S(1)} %take_7168.1.refs_1_), channel_id=1, source_target_pairs={{0,4},{4,8},{8,12},{12,14},{14,10},{10,6},{6,2},{2,0},{1,5},{5,9},... | collective-permute-start | bytes 786440 | tf_op jit(solution)/shard_map/ppermute | solution.py:230
  39.2 16.3 %collective-permute-start.9 = (bf16[32,4096]{1,0:T(8,128)(2,1)S(1)}, bf16[32,4096]{1,0:T(8,128)(2,1)S(1)}, u32[]{:S(2)}, u32[]{:S(2)}) collective-permute-start(bf16[32,4096]{1,0:T(8,128)(2,1)S(1)} %collective-permute-done.8.refs_2_), channel_id=1, source_target_pairs={{0,4},{4,8},{8,12},{12,14},{14,10},{10,6},{6,2},{2,0},{1,5},{5,9},... | collective-permute-start | bytes 786440 | tf_op jit(solution)/shard_map/ppermute | solution.py:230
  40.8 14.8 %collective-permute-start.13 = (bf16[32,4096]{1,0:T(8,128)(2,1)S(1)}, bf16[32,4096]{1,0:T(8,128)(2,1)S(1)}, u32[]{:S(2)}, u32[]{:S(2)}) collective-permute-start(bf16[32,4096]{1,0:T(8,128)(2,1)S(1)} %collective-permute-done.12.refs_6_), channel_id=1, source_target_pairs={{0,2},{4,0},{8,4},{12,8},{14,12},{10,14},{6,10},{2,6},{1,3},{5,1},... | collective-permute-start | bytes 786440 | tf_op jit(solution)/shard_map/ppermute | solution.py:230
  41.3 15.6 %collective-permute-start.24 = (bf16[32,4096]{1,0:T(8,128)(2,1)S(1)}, bf16[32,4096]{1,0:T(8,128)(2,1)S(1)}, u32[]{:S(2)}, u32[]{:S(2)}) collective-permute-start(bf16[32,4096]{1,0:T(8,128)(2,1)S(1)} %take_7168.1.refs_1_), channel_id=1, source_target_pairs={{0,2},{4,0},{8,4},{12,8},{14,12},{10,14},{6,10},{2,6},{1,3},{5,1},... | collective-permute-start | bytes 786440 | tf_op jit(solution)/shard_map/ppermute | solution.py:230
  45.6 11.5 %collective-permute-start.22 = (bf16[32,4096]{1,0:T(8,128)(2,1)S(1)}, bf16[32,4096]{1,0:T(8,128)(2,1)S(1)}, u32[]{:S(2)}, u32[]{:S(2)}) collective-permute-start(bf16[32,4096]{1,0:T(8,128)(2,1)S(1)} %collective-permute-done.21.refs_2_), channel_id=1, source_target_pairs={{0,4},{4,8},{8,12},{12,14},{14,10},{10,6},{6,2},{2,0},{1,5},{5,9},... | collective-permute-start | bytes 786440 | tf_op jit(solution)/shard_map/ppermute | solution.py:230
  56.3 24.2 %collective-permute-start.17 = (bf16[32,3072]{1,0:T(8,128)(2,1)S(1)}, bf16[32,3072]{1,0:T(8,128)(2,1)S(1)}, u32[]{:S(2)}, u32[]{:S(2)}) collective-permute-start(bf16[32,3072]{1,0:T(8,128)(2,1)S(1)} %take_11264.1.refs_0_.refs_1_), channel_id=1, source_target_pairs={{0,2},{4,0},{8,4},{12,8},{14,12},{10,14},{6,10},{2,6},{1,3},{5,1},... | collective-permute-start | bytes 589832 | tf_op jit(solution)/shard_map/ppermute | solution.py:230
  56.8 12.2 %collective-permute-start.25 = (bf16[32,4096]{1,0:T(8,128)(2,1)S(1)}, bf16[32,4096]{1,0:T(8,128)(2,1)S(1)}, u32[]{:S(2)}, u32[]{:S(2)}) collective-permute-start(bf16[32,4096]{1,0:T(8,128)(2,1)S(1)} %collective-permute-done.24.refs_6_), channel_id=1, source_target_pairs={{0,2},{4,0},{8,4},{12,8},{14,12},{10,14},{6,10},{2,6},{1,3},{5,1},... | collective-permute-start | bytes 786440 | tf_op jit(solution)/shard_map/ppermute | solution.py:230
  57.1 12.0 %collective-permute-start.23 = (bf16[32,4096]{1,0:T(8,128)(2,1)S(1)}, bf16[32,4096]{1,0:T(8,128)(2,1)S(1)}, u32[]{:S(2)}, u32[]{:S(2)}) collective-permute-start(bf16[32,4096]{1,0:T(8,128)(2,1)S(1)} %collective-permute-done.22.refs_3_), channel_id=1, source_target_pairs={{0,4},{4,8},{8,12},{12,14},{14,10},{10,6},{6,2},{2,0},{1,5},{5,9},... | collective-permute-start | bytes 786440 | tf_op jit(solution)/shard_map/ppermute | solution.py:230
  73.7 81.6 %all-to-all-start = ((bf16[8,128,512]{2,1,0:T(8,128)(2,1)}), bf16[8,128,512]{2,1,0:T(8,128)(2,1)S(1)}, u32[]{:S(2)}, u32[]{:S(2)}) async-start(bf16[8,128,512]{2,1,0:T(8,128)(2,1)} %get-tuple-element.28), calls=%async_computation | async-start | bytes 2097152 | tf_op jit(solution)/shard_map/all_to_all | solution.py:238
  78.5 16.9 %collective-permute-start.14 = (bf16[32,3072]{1,0:T(8,128)(2,1)S(1)}, bf16[32,3072]{1,0:T(8,128)(2,1)S(1)}, u32[]{:S(2)}, u32[]{:S(2)}) collective-permute-start(bf16[32,3072]{1,0:T(8,128)(2,1)S(1)} %take_11264.1.refs_0_.refs_1_), channel_id=1, source_target_pairs={{0,4},{4,8},{8,12},{12,14},{14,10},{10,6},{6,2},{2,0},{1,5},{5,9},... | collective-permute-start | bytes 589832 | tf_op jit(solution)/shard_map/ppermute | solution.py:230
  80.6 22.2 %collective-permute-start.18 = (bf16[32,3072]{1,0:T(8,128)(2,1)S(1)}, bf16[32,3072]{1,0:T(8,128)(2,1)S(1)}, u32[]{:S(2)}, u32[]{:S(2)}) collective-permute-start(bf16[32,3072]{1,0:T(8,128)(2,1)S(1)} %collective-permute-done.17.refs_4_.refs_5_), channel_id=1, source_target_pairs={{0,2},{4,0},{8,4},{12,8},{14,12},{10,14},{6,10},{2,6},{1,3},{5,1},... | collective-permute-start | bytes 589832 | tf_op jit(solution)/shard_map/ppermute | solution.py:230
  80.6 30.4 %collective-permute-start.27 = (bf16[32,4096]{1,0:T(8,128)(2,1)S(1)}, bf16[32,4096]{1,0:T(8,128)(2,1)S(1)}, u32[]{:S(2)}, u32[]{:S(2)}) collective-permute-start(bf16[32,4096]{1,0:T(8,128)(2,1)S(1)} %collective-permute-done.25.refs_1_.refs_7_), channel_id=1, source_target_pairs={{0,2},{4,0},{8,4},{12,8},{14,12},{10,14},{6,10},{2,6},{1,3},{5,1},... | collective-permute-start | bytes 786440 | tf_op jit(solution)/shard_map/ppermute | solution.py:230
  82.6 28.4 %collective-permute-start.26 = (bf16[32,4096]{1,0:T(8,128)(2,1)S(1)}, bf16[32,4096]{1,0:T(8,128)(2,1)}, u32[]{:S(2)}, u32[]{:S(2)}) collective-permute-start(bf16[32,4096]{1,0:T(8,128)(2,1)S(1)} %collective-permute-done.23.refs_0_.refs_4_), channel_id=1, source_target_pairs={{0,4},{4,8},{8,12},{12,14},{14,10},{10,6},{6,2},{2,0},{1,5},{5,9},... | collective-permute-start | bytes 786440 | tf_op jit(solution)/shard_map/ppermute | solution.py:230
  95.4 10.5 %collective-permute-start.15 = (bf16[32,3072]{1,0:T(8,128)(2,1)S(1)}, bf16[32,3072]{1,0:T(8,128)(2,1)S(1)}, u32[]{:S(2)}, u32[]{:S(2)}) collective-permute-start(bf16[32,3072]{1,0:T(8,128)(2,1)S(1)} %collective-permute-done.14.refs_1_.refs_2_), channel_id=1, source_target_pairs={{0,4},{4,8},{8,12},{12,14},{14,10},{10,6},{6,2},{2,0},{1,5},{5,9},... | collective-permute-start | bytes 589832 | tf_op jit(solution)/shard_map/ppermute | solution.py:230
  102.7 6.9 %collective-permute-start.19 = (bf16[32,3072]{1,0:T(8,128)(2,1)S(1)}, bf16[32,3072]{1,0:T(8,128)(2,1)S(1)}, u32[]{:S(2)}, u32[]{:S(2)}) collective-permute-start(bf16[32,3072]{1,0:T(8,128)(2,1)S(1)} %collective-permute-done.18.refs_5_.refs_6_), channel_id=1, source_target_pairs={{0,2},{4,0},{8,4},{12,8},{14,12},{10,14},{6,10},{2,6},{1,3},{5,1},... | collective-permute-start | bytes 589832 | tf_op jit(solution)/shard_map/ppermute | solution.py:230
  105.9 15.8 %collective-permute-start.16 = (bf16[32,3072]{1,0:T(8,128)(2,1)S(1)}, bf16[32,3072]{1,0:T(8,128)(2,1)S(1)}, u32[]{:S(2)}, u32[]{:S(2)}) collective-permute-start(bf16[32,3072]{1,0:T(8,128)(2,1)S(1)} %collective-permute-done.15.refs_2_.refs_3_), channel_id=1, source_target_pairs={{0,4},{4,8},{8,12},{12,14},{14,10},{10,6},{6,2},{2,0},{1,5},{5,9},... | collective-permute-start | bytes 589832 | tf_op jit(solution)/shard_map/ppermute | solution.py:230
  109.7 12.1 %collective-permute-start.20 = (bf16[32,3072]{1,0:T(8,128)(2,1)S(1)}, bf16[32,3072]{1,0:T(8,128)(2,1)S(1)}, u32[]{:S(2)}, u32[]{:S(2)}) collective-permute-start(bf16[32,3072]{1,0:T(8,128)(2,1)S(1)} %collective-permute-done.19.refs_6_.refs_7_), channel_id=1, source_target_pairs={{0,2},{4,0},{8,4},{12,8},{14,12},{10,14},{6,10},{2,6},{1,3},{5,1},... | collective-permute-start | bytes 589832 | tf_op jit(solution)/shard_map/ppermute | solution.py:230
  136.0 19.2 %collective-permute-start.32 = (f32[256,512]{1,0:T(8,128)}, f32[256,512]{1,0:T(8,128)S(1)}, u32[]{:S(2)}, u32[]{:S(2)}) collective-permute-start(f32[256,512]{1,0:T(8,128)} %last_sent.1.refs_0_), channel_id=1, source_target_pairs={{0,1},{1,0},{2,3},{3,2},{4,5},{5,4},{6,7},{7,6},{8,9},{9,8},{10,11... | collective-permute-start | bytes 1572872 | tf_op jit(solution)/shard_map/ppermute | solution.py:255
  138.1 4.6 %collective-permute-start.29 = (bf16[64,256]{1,0:T(8,128)(2,1)S(1)}, bf16[64,256]{1,0:T(8,128)(2,1)S(1)}, u32[]{:S(2)}, u32[]{:S(2)}) collective-permute-start(bf16[64,256]{1,0:T(8,128)(2,1)S(1)} %add_convert_fusion), channel_id=1, source_target_pairs={{0,2},{2,0},{4,6},{6,4},{8,10},{10,8},{12,14},{14,12},{1,3},{3,1},... | collective-permute-start | bytes 98312 | tf_op jit(solution)/shard_map/ppermute | solution.py:258
  146.8 8.5 %collective-permute-start.31 = (bf16[64,256]{1,0:T(8,128)(2,1)S(1)}, bf16[64,256]{1,0:T(8,128)(2,1)S(1)}, u32[]{:S(2)}, u32[]{:S(2)}) collective-permute-start(bf16[64,256]{1,0:T(8,128)(2,1)S(1)} %add.30), channel_id=1, source_target_pairs={{0,8},{2,10},{4,12},{6,14},{8,0},{10,2},{12,4},{14,6},{1,9},{3,11}... | collective-permute-start | bytes 98312 | tf_op jit(solution)/shard_map/ppermute | solution.py:258
  (45 other events, 665.8 us)

commit v6 on v5

v6 whole, which is shorter than its diff:
```python
import functools

import jax
import jax.numpy as jnp
import numpy as np
from jax import lax
from jax.experimental import pallas as pl
from jax.experimental.pallas import tpu as pltpu
from jax.sharding import PartitionSpec as P

F32, BF16 = jnp.float32, jnp.bfloat16
TILE = 1024
MIB = 2**20
MATMUL_MIB = 48


def params(mib):
    return pltpu.CompilerParams(vmem_limit_bytes=mib * MIB)


def ring_order(n):
    return list(range(0, n, 2)) + list(range(1, n, 2))[::-1]


def take_kernel(start, width, src, *refs):
    *_, dst, sem = refs
    copy = pltpu.make_async_copy(src.at[:, pl.ds(start, width)], dst, sem)
    copy.start()
    copy.wait()


def take(hidden, start, width, after):
    rows = hidden.shape[0]
    return pl.pallas_call(
        functools.partial(take_kernel, start, width),
        in_specs=[pl.BlockSpec(memory_space=pl.ANY)] * (1 + len(after)),
        out_specs=pl.BlockSpec(memory_space=pl.ANY),
        scratch_shapes=[pltpu.SemaphoreType.DMA],
        out_shape=jax.ShapeDtypeStruct((rows, width), BF16),
        compiler_params=params(MATMUL_MIB),
        cost_estimate=pl.CostEstimate(flops=0, bytes_accessed=4 * rows * width, transcendentals=0),
        name=f"take_{start}",
    )(hidden, *after)


def split_kernel(scalars, src, dst):
    dst[...] = src[...][None]


def expand_blocks(scalars, half, expand, n, cores):
    owned, rank, width = expand.shape
    rows = owned * rank
    share = width // (n * cores)
    return pl.pallas_call(
        split_kernel,
        grid_spec=pltpu.PrefetchScalarGridSpec(
            num_scalar_prefetch=1,
            grid=(n,),
            in_specs=[pl.BlockSpec((rows, share), lambda s, t: (0, s * cores + t[half]))],
            out_specs=pl.BlockSpec((1, rows, share), lambda s, t: (s, 0, 0)),
        ),
        out_shape=jax.ShapeDtypeStruct((n, rows, share), BF16),
        compiler_params=params(MATMUL_MIB),
        cost_estimate=pl.CostEstimate(flops=0, bytes_accessed=4 * n * rows * share, transcendentals=0),
        name="expand_blocks",
    )(scalars, expand.reshape(rows, width))


def tie_kernel(*refs):
    pass


def tie(array, after):
    return pl.pallas_call(
        tie_kernel,
        in_specs=[pl.BlockSpec(memory_space=pl.ANY)] * (1 + len(after)),
        out_specs=pl.BlockSpec(memory_space=pl.ANY),
        out_shape=jax.ShapeDtypeStruct(array.shape, array.dtype),
        input_output_aliases={0: 0},
        compiler_params=params(MATMUL_MIB),
        name="tie",
    )(array, *after)


def matmul_kernel(n, waits, base, half, start, tiles, sides, narrow, has_acc, token, scalars, *refs):
    refs = list(refs)[waits:]
    pieces = [refs.pop(0) for _ in range(n)]
    down = refs.pop(0)
    shrink = refs.pop(0)
    outs = len(sides) + narrow
    before = [refs.pop(0) for _ in range(outs)] if has_acc else []
    acc = [refs.pop(0) for _ in range(outs)]
    if token:
        refs.pop(0)[...] = jnp.zeros((8, 128), F32)
    lefts = [refs.pop(0) for _ in tiles]
    weights = [[refs.pop(0) for _ in tiles] for _ in sides]
    ranks = [refs.pop(0) for _ in tiles] if narrow else []
    earlier = [refs.pop(0) for _ in before]
    sems, old_sems = refs
    rows = pieces[0].shape[0]
    share = down.shape[1] // 2

    copies = []
    at = 0
    for k, tile in enumerate(tiles):
        group = []
        for i in range(n):
            to = pl.multiple_of(scalars[base + i] * rows, rows)
            group.append((pieces[i].at[:, pl.ds(at, tile)], lefts[k].at[pl.ds(to, rows), :]))
        if narrow:
            group.append((shrink.at[:, pl.ds(start + at, tile)], ranks[k]))
        for i, side in enumerate(sides):
            column = pl.multiple_of(scalars[half + side] * share, share)
            group.append((down.at[pl.ds(start + at, tile), pl.ds(column, share)], weights[i][k]))
        copies.append([pltpu.make_async_copy(*pair, sems.at[k, i]) for i, pair in enumerate(group)])
        for copy in copies[-1]:
            copy.start()
        at += tile
    old = [pltpu.make_async_copy(a, b, old_sems.at[i]) for i, (a, b) in enumerate(zip(before, earlier))]
    for copy in old:
        copy.start()

    for k in range(len(tiles)):
        for copy in copies[k]:
            copy.wait()
        left = lefts[k][...]
        terms = [jnp.dot(left, weights[i][k][...], preferred_element_type=F32) for i in range(len(sides))]
        if narrow:
            terms.append(
                lax.dot_general(ranks[k][...], left, (((1,), (1,)), ((), ())), preferred_element_type=F32)
            )
        for i, term in enumerate(terms):
            acc[i][...] = term if k == 0 else acc[i][...] + term
    for i, copy in enumerate(old):
        copy.wait()
        acc[i][...] += earlier[i][...]


def chunk_matmul(scalars, base, half, pieces, down, shrink, acc, start, sides, narrow, label, after=(), token=False):
    n = len(pieces)
    rows, width = pieces[0].shape[0] * n, pieces[0].shape[1]
    share = down.shape[1] // 2
    ranks = shrink.shape[0]
    tiles = [TILE // 2] * 2 + [TILE] * (width // TILE - 1)
    anywhere = pl.BlockSpec(memory_space=pl.ANY)
    args = [*after, *pieces, down, shrink, *(acc or ())]
    shapes = [(rows, share)] * len(sides) + [(ranks, rows)] * narrow
    columns = share * len(sides) + ranks * narrow
    marks = [(8, 128)] * token
    return pl.pallas_call(
        functools.partial(
            matmul_kernel, n, len(after), base, half, start, tiles, sides, narrow, acc is not None, token
        ),
        grid_spec=pltpu.PrefetchScalarGridSpec(
            num_scalar_prefetch=1,
            grid=(),
            in_specs=[anywhere] * len(args),
            out_specs=[pl.BlockSpec(memory_space=pltpu.VMEM)] * len(shapes + marks),
            scratch_shapes=[pltpu.VMEM((rows, tile), BF16) for tile in tiles]
            + [pltpu.VMEM((tile, share), BF16) for _ in sides for tile in tiles]
            + [pltpu.VMEM((ranks, tile), BF16) for tile in tiles if narrow]
            + [pltpu.VMEM(shape, F32) for shape in shapes if acc is not None]
            + [pltpu.SemaphoreType.DMA((len(tiles), n + 3)), pltpu.SemaphoreType.DMA((3,))],
        ),
        out_shape=[jax.ShapeDtypeStruct(shape, F32) for shape in shapes + marks],
        compiler_params=params(MATMUL_MIB),
        cost_estimate=pl.CostEstimate(
            flops=4 * rows * width * columns,
            bytes_accessed=2 * width * (columns + rows) + 8 * rows * columns,
            transcendentals=0,
        ),
        name=label,
    )(scalars, *args)


def final_kernel(n, owned, shrunk, slot, factors, kept, other, out, spread):
    rank = shrunk.shape[0]
    wide = owned * rank
    rows = out.shape[0]
    lane = lax.broadcasted_iota(jnp.int32, (rows, wide), 1) // rank
    own = shrunk[...].astype(F32).T
    pair = jnp.concatenate([own] * owned, axis=1)
    place = slot[...] - lane
    for i in range(n):
        spread[:, i * wide:(i + 1) * wide] = jnp.where(place == i * owned, pair, 0.0).astype(BF16)
    extra = jnp.dot(spread[...], factors[...], preferred_element_type=F32)
    out[...] = (kept[...] + other[...] + extra).astype(BF16)


def final(shrunk, slot_column, factors, kept, other, owned):
    n, wide, share = factors.shape
    rows = kept.shape[0]
    return pl.pallas_call(
        functools.partial(final_kernel, n, owned),
        in_specs=[pl.BlockSpec(memory_space=pltpu.VMEM)] * 5,
        out_specs=pl.BlockSpec(memory_space=pltpu.VMEM),
        scratch_shapes=[pltpu.VMEM((rows, n * wide), BF16)],
        out_shape=jax.ShapeDtypeStruct((rows, share), BF16),
        compiler_params=params(MATMUL_MIB),
        cost_estimate=pl.CostEstimate(
            flops=2 * rows * share * n * wide,
            bytes_accessed=2 * n * wide * share + 10 * rows * share,
            transcendentals=0,
        ),
        name="expand_and_add",
    )(shrunk, slot_column, factors.reshape(n * wide, share), kept, other)


def make_shards(n, cores):
    order = ring_order(n)
    place_of = {store: place for place, store in enumerate(order)}
    clockwise = [(order[i], order[(i + 1) % n]) for i in range(n)]
    counter = [(order[i], order[i - 1]) for i in range(n)]
    long, short = n // 2, (n - 1) // 2
    swap = [(t, (t + 1) % cores) for t in range(cores)]
    hops = [[0] + [-i for i in range(1, a + 1)] + list(range(1, b + 1)) for a, b in ((long, short), (short, long))]
    table = np.array(
        [
            [order[(place_of[s] + hop) % n] for way in hops for hop in way] + [t, 1 - t]
            for s in range(n)
            for t in range(cores)
        ],
        np.int32,
    )
    half = 2 * n

    def shards(hidden, down, shrink, expand, row_adapter, adapter_slot):
        owned, units, rank = shrink.shape
        store, tensor = lax.axis_index("store"), lax.axis_index("tensor")
        scalars = lax.dynamic_slice_in_dim(jnp.asarray(table), store * cores + tensor, 1, 0)[0]
        shrink_rows = jnp.transpose(shrink, (0, 2, 1)).reshape(owned * rank, units)

        slots = jnp.arange(adapter_slot.shape[0], dtype=jnp.int32)
        row_slot = jnp.sum(jnp.where(row_adapter[None, :] == slots[:, None], adapter_slot[:, None], 0), axis=0)

        large = 2 * (units // (7 * TILE)) * TILE
        widths = [units - 3 * large, large, large, large]

        blocks = expand_blocks(scalars, half, expand, n, cores)
        acc = None
        start = 0
        after = {}
        for chunk, width in enumerate(widths):
            own = take(hidden, start, width, after[chunk]) if chunk in after else hidden[:, start:start + width]
            way = chunk % 2
            pieces = [own]
            lengths = ((long, short), (short, long))[way]
            for length, pairs in zip(lengths, (clockwise, counter)):
                moving = own
                for step in range(length):
                    moving = lax.ppermute(moving, "store", pairs)
                    pieces.append(moving)
            ends = [pieces[lengths[0]], pieces[-1]]
            call = functools.partial(chunk_matmul, scalars, way * n, half, pieces, down, shrink_rows)
            if chunk < len(widths) - 1:
                *acc, token = call(acc, start, (0, 1), True, f"chunk_{chunk}", token=True)
                if chunk == 0:
                    after[3] = ends
            else:
                factors = lax.all_to_all(tie(blocks, ends), "store", 0, 0)
                narrow, = call(acc[2:], start, (), True, "last_narrow")
                mine = [
                    jnp.where((row_slot == store * owned + i)[None, :], narrow[i * rank:(i + 1) * rank], 0.0)
                    for i in range(owned)
                ]
                mine = sum(mine[1:], mine[0])
                send, = call(acc[1:2], start, (1,), False, "last_sent", [mine])
                kept, = call(acc[:1], start, (0,), False, "last_kept", [send])
            start += width
        where = [(s, t) for s in range(n) for t in range(cores)]
        whole = mine
        for ds in range(2):
            for dt in range(cores):
                if ds or dt:
                    pairs = [(s * cores + t, (s ^ ds) * cores + (t + dt) % cores) for s, t in where]
                    whole = whole + lax.ppermute(mine, ("store", "tensor"), pairs)
        column = whole.astype(BF16)
        shrunk = column
        for ds in range(2, n, 2):
            shrunk = shrunk + lax.ppermute(column, "store", [(s, (s + ds) % n) for s in range(n)])
        other = lax.ppermute(send, "tensor", swap)
        return final(shrunk, row_slot[:, None], factors, kept, other, owned)

    return shards


def solution(mesh):
    in_specs = (
        P(("parts", "store"), "tensor"),
        P("tensor", "store"),
        P(("parts", "store"), "tensor", None),
        P(("parts", "store"), None, None),
        P("parts"),
        P("parts"),
    )
    out_specs = P("parts", ("store", "tensor"))
    shards = make_shards(mesh.shape["store"], mesh.shape["tensor"])
    return jax.shard_map(shards, mesh=mesh, in_specs=in_specs, out_specs=out_specs, check_vma=False)
```

time: 159 us -> 142 us (0.89)
  local copies, waits for them, and re-layouts: 9.05 us -> 26.4 us
  Pallas kernels: 51.5 us -> 35.2 us
  waiting for transfers between devices: 44.4 us -> 31.6 us
  starting transfers between devices: 50.6 us -> 47.3 us
    unnamed x86 -> x64, local copies, waits for them, and re-layouts: 5.79 us -> 23.6 us
    pallas_call x6 -> x7, Pallas kernels: 46.7 us -> 30.5 us  [the longest x6 30.5 us: chunk_matmul(): pl.pallas_call(functools.partial(matmul_kernel, n, len(after), base, half...]
    ppermute x28, waiting for transfers between devices: 39.2 us -> 31.5 us  [shards(): moving = lax.ppermute(moving, 'store', pairs)]
    ppermute x4 -> x6, waiting for transfers between devices: 5.2 us -> 0.02 us  [the longest x3 0.01 us: shards(): whole = whole + lax.ppermute(mine, ('store', 'tensor'), pairs)]
    ppermute x28, starting transfers between devices: 38.4 us -> 33.6 us  [shards(): moving = lax.ppermute(moving, 'store', pairs)]
    ppermute x4 -> x6, starting transfers between devices: 7.27 us -> 8.03 us  [the longest x3 5.81 us: shards(): lax.ppermute(column, 'store', [(s, (s + ds) % n) for s in range(n)])]
  transfers between devices with their start and end apart: 34 -> 36, of which waited for: 13 -> 11; matrix products, arithmetic and copies ran while one was open for 3% -> 2% of each run, Pallas kernels for 32% -> 24%
where the time goes in v6:
time: 142 us
  starting transfers between devices  47.3 us (33%)
  Pallas kernels  35.2 us (25%)
  waiting for transfers between devices  31.6 us (22%)
  local copies, waits for them, and re-layouts  26.4 us (19%)
    ppermute x28, starting transfers between devices, shards(): moving = lax.ppermute(moving, 'store', pairs)  33.6 us
    ppermute x28, waiting for transfers between devices, shards(): moving = lax.ppermute(moving, 'store', pairs)  31.5 us
    pallas_call x6, Pallas kernels, chunk_matmul(): pl.pallas_call(functools.partial(matmul_kernel, n, len(after), base, half...  30.5 us
    unnamed x64, local copies, waits for them, and re-layouts  23.6 us
    ppermute x3, starting transfers between devices, shards(): lax.ppermute(column, 'store', [(s, (s + ds) % n) for s in range(n)])  5.81 us
    all_to_all x1, starting transfers between devices, shards(): factors = lax.all_to_all(tie(blocks, ends), 'store', 0, 0)  5.38 us
    pallas_call x1, Pallas kernels, expand_blocks(): pl.pallas_call(split_kernel, grid_spec=pltpu.PrefetchScalarGridSpec(num_s...  3.31 us
  transfers between devices with their start and end apart: 36, of which 11 were waited for; matrix products, arithmetic and copies ran while one was open for 2% of the time, Pallas kernels for 24%

profile of v6, /device:TPU:0, one launch (start us, length us, event | category | flops | bytes accessed | tf_op | source)
XLA Modules:
  0.0 141.6 jit_solution(14990658158613450236)
XLA Ops:
  0.9 3.1 %collective-permute-start = (bf16[32,2048]{1,0:T(8,128)(2,1)S(1)}, bf16[32,2048]{1,0:T(8,128)(2,1)S(1)}, u32[]{:S(2)}, u32[]{:S(2)}) collective-permute-start(bf16[32,2048]{1,0:T(8,128)(2,1)S(1)} %slice.15.refs_0_), channel_id=1, source_target_pairs={{0,4},{4,8},{8,12},{12,14},{14,10},{10,6},{6,2},{2,0},{1,5},{5,9},... | collective-permute-start | bytes 393224 | tf_op jit(solution)/shard_map/ppermute | solution.py:251
  4.0 3.4 %collective-permute-done.refs_1_ = bf16[32,2048]{1,0:T(8,128)(2,1)S(1)} collective-permute-done((bf16[32,2048]{1,0:T(8,128)(2,1)S(1)}, bf16[32,2048]{1,0:T(8,128)(2,1)S(1)}, u32[]{:S(2)}, u32[]{:S(2)}) %collective-permute-start) | collective-permute-done | bytes 131104 | tf_op jit(solution)/shard_map/ppermute | solution.py:251
  7.4 1.8 %collective-permute-start.1 = (bf16[32,2048]{1,0:T(8,128)(2,1)S(1)}, bf16[32,2048]{1,0:T(8,128)(2,1)S(1)}, u32[]{:S(2)}, u32[]{:S(2)}) collective-permute-start(bf16[32,2048]{1,0:T(8,128)(2,1)S(1)} %collective-permute-done.refs_1_), channel_id=1, source_target_pairs={{0,4},{4,8},{8,12},{12,14},{14,10},{10,6},{6,2},{2,0},{1,5},{5,9},... | collective-permute-start | bytes 393224 | tf_op jit(solution)/shard_map/ppermute | solution.py:251
  10.1 2.3 %collective-permute-done.1.refs_2_ = bf16[32,2048]{1,0:T(8,128)(2,1)S(1)} collective-permute-done((bf16[32,2048]{1,0:T(8,128)(2,1)S(1)}, bf16[32,2048]{1,0:T(8,128)(2,1)S(1)}, u32[]{:S(2)}, u32[]{:S(2)}) %collective-permute-start.1) | collective-permute-done | bytes 131104 | tf_op jit(solution)/shard_map/ppermute | solution.py:251
  12.4 1.8 %collective-permute-start.2 = (bf16[32,2048]{1,0:T(8,128)(2,1)S(1)}, bf16[32,2048]{1,0:T(8,128)(2,1)S(1)}, u32[]{:S(2)}, u32[]{:S(2)}) collective-permute-start(bf16[32,2048]{1,0:T(8,128)(2,1)S(1)} %collective-permute-done.1.refs_2_), channel_id=1, source_target_pairs={{0,4},{4,8},{8,12},{12,14},{14,10},{10,6},{6,2},{2,0},{1,5},{5,9},... | collective-permute-start | bytes 393224 | tf_op jit(solution)/shard_map/ppermute | solution.py:251
  15.1 2.7 %collective-permute-done.2.refs_3_ = bf16[32,2048]{1,0:T(8,128)(2,1)S(1)} collective-permute-done((bf16[32,2048]{1,0:T(8,128)(2,1)S(1)}, bf16[32,2048]{1,0:T(8,128)(2,1)S(1)}, u32[]{:S(2)}, u32[]{:S(2)}) %collective-permute-start.2) | collective-permute-done | bytes 131104 | tf_op jit(solution)/shard_map/ppermute | solution.py:251
  17.8 2.1 %collective-permute-start.3 = (bf16[32,2048]{1,0:T(8,128)(2,1)S(1)}, bf16[32,2048]{1,0:T(8,128)(2,1)S(1)}, u32[]{:S(2)}, u32[]{:S(2)}) collective-permute-start(bf16[32,2048]{1,0:T(8,128)(2,1)S(1)} %collective-permute-done.2.refs_3_), channel_id=1, source_target_pairs={{0,4},{4,8},{8,12},{12,14},{14,10},{10,6},{6,2},{2,0},{1,5},{5,9},... | collective-permute-start | bytes 393224 | tf_op jit(solution)/shard_map/ppermute | solution.py:251
  21.1 2.0 %collective-permute-start.21 = (bf16[32,4096]{1,0:T(8,128)(2,1)S(1)}, bf16[32,4096]{1,0:T(8,128)(2,1)S(1)}, u32[]{:S(2)}, u32[]{:S(2)}) collective-permute-start(bf16[32,4096]{1,0:T(8,128)(2,1)S(1)} %get-tuple-element.23.refs_0_), channel_id=1, source_target_pairs={{0,4},{4,8},{8,12},{12,14},{14,10},{10,6},{6,2},{2,0},{1,5},{5,9},... | collective-permute-start | bytes 786440 | tf_op jit(solution)/shard_map/ppermute | solution.py:251
  25.9 1.7 %collective-permute-start.10 = (bf16[32,4096]{1,0:T(8,128)(2,1)S(1)}, bf16[32,4096]{1,0:T(8,128)(2,1)S(1)}, u32[]{:S(2)}, u32[]{:S(2)}) collective-permute-start(bf16[32,4096]{1,0:T(8,128)(2,1)S(1)} %take_10240.1.refs_0_.refs_1_), channel_id=1, source_target_pairs={{0,2},{4,0},{8,4},{12,8},{14,12},{10,14},{6,10},{2,6},{1,3},{5,1},... | collective-permute-start | bytes 786440 | tf_op jit(solution)/shard_map/ppermute | solution.py:251
  33.6 2.3 %collective-permute-done.14.refs_1_ = bf16[32,4096]{1,0:T(8,128)(2,1)S(1)} collective-permute-done((bf16[32,4096]{1,0:T(8,128)(2,1)S(1)}, bf16[32,4096]{1,0:T(8,128)(2,1)S(1)}, u32[]{:S(2)}, u32[]{:S(2)}) %collective-permute-start.14) | collective-permute-done | bytes 262176 | tf_op jit(solution)/shard_map/ppermute | solution.py:251
  35.9 2.0 %collective-permute-start.7 = (bf16[32,4096]{1,0:T(8,128)(2,1)S(1)}, bf16[32,4096]{1,0:T(8,128)(2,1)S(1)}, u32[]{:S(2)}, u32[]{:S(2)}) collective-permute-start(bf16[32,4096]{1,0:T(8,128)(2,1)S(1)} %take_10240.1.refs_0_.refs_1_), channel_id=1, source_target_pairs={{0,4},{4,8},{8,12},{12,14},{14,10},{10,6},{6,2},{2,0},{1,5},{5,9},... | collective-permute-start | bytes 786440 | tf_op jit(solution)/shard_map/ppermute | solution.py:251
  38.0 3.5 %collective-permute-done.18.refs_5_ = bf16[32,4096]{1,0:T(8,128)(2,1)S(1)} collective-permute-done((bf16[32,4096]{1,0:T(8,128)(2,1)S(1)}, bf16[32,4096]{1,0:T(8,128)(2,1)S(1)}, u32[]{:S(2)}, u32[]{:S(2)}) %collective-permute-start.18) | collective-permute-done | bytes 262176 | tf_op jit(solution)/shard_map/ppermute | solution.py:251
  41.4 1.6 %collective-permute-start.15 = (bf16[32,4096]{1,0:T(8,128)(2,1)S(1)}, bf16[32,4096]{1,0:T(8,128)(2,1)}, u32[]{:S(2)}, u32[]{:S(2)}) collective-permute-start(bf16[32,4096]{1,0:T(8,128)(2,1)S(1)} %collective-permute-done.14.refs_1_), channel_id=1, source_target_pairs={{0,4},{4,8},{8,12},{12,14},{14,10},{10,6},{6,2},{2,0},{1,5},{5,9},... | collective-permute-start | bytes 786440 | tf_op jit(solution)/shard_map/ppermute | solution.py:251
  43.0 4.1 %collective-permute-done.25.refs_5_ = bf16[32,4096]{1,0:T(8,128)(2,1)} collective-permute-done((bf16[32,4096]{1,0:T(8,128)(2,1)S(1)}, bf16[32,4096]{1,0:T(8,128)(2,1)}, u32[]{:S(2)}, u32[]{:S(2)}) %collective-permute-start.25) | collective-permute-done | bytes 262176 | tf_op jit(solution)/shard_map/ppermute | solution.py:251
  50.9 1.8 %collective-permute-done.11.refs_5_.refs_6_ = bf16[32,4096]{1,0:T(8,128)(2,1)S(1)} collective-permute-done((bf16[32,4096]{1,0:T(8,128)(2,1)S(1)}, bf16[32,4096]{1,0:T(8,128)(2,1)S(1)}, u32[]{:S(2)}, u32[]{:S(2)}) %collective-permute-start.11) | collective-permute-done | bytes 262176 | tf_op jit(solution)/shard_map/ppermute | solution.py:251
  55.6 2.9 %collective-permute-done.19.refs_6_ = bf16[32,4096]{1,0:T(8,128)(2,1)} collective-permute-done((bf16[32,4096]{1,0:T(8,128)(2,1)S(1)}, bf16[32,4096]{1,0:T(8,128)(2,1)}, u32[]{:S(2)}, u32[]{:S(2)}) %collective-permute-start.19) | collective-permute-done | bytes 262176 | tf_op jit(solution)/shard_map/ppermute | solution.py:251
  58.4 1.6 %collective-permute-start.16 = (bf16[32,4096]{1,0:T(8,128)(2,1)}, bf16[32,4096]{1,0:T(8,128)(2,1)}, u32[]{:S(2)}, u32[]{:S(2)}) collective-permute-start(bf16[32,4096]{1,0:T(8,128)(2,1)} %collective-permute-done.15.refs_2_), channel_id=1, source_target_pairs={{0,4},{4,8},{8,12},{12,14},{14,10},{10,6},{6,2},{2,0},{1,5},{5,9},... | collective-permute-start | bytes 786440 | tf_op jit(solution)/shard_map/ppermute | solution.py:251
  60.0 4.0 %collective-permute-done.26.refs_6_ = bf16[32,4096]{1,0:T(8,128)(2,1)} collective-permute-done((bf16[32,4096]{1,0:T(8,128)(2,1)}, bf16[32,4096]{1,0:T(8,128)(2,1)}, u32[]{:S(2)}, u32[]{:S(2)}) %collective-permute-start.26) | collective-permute-done | bytes 262176 | tf_op jit(solution)/shard_map/ppermute | solution.py:251
  66.1 3.5 %collective-permute-done.12.refs_6_.refs_7_ = bf16[32,4096]{1,0:T(8,128)(2,1)S(1)} collective-permute-done((bf16[32,4096]{1,0:T(8,128)(2,1)S(1)}, bf16[32,4096]{1,0:T(8,128)(2,1)S(1)}, u32[]{:S(2)}, u32[]{:S(2)}) %collective-permute-start.12) | collective-permute-done | bytes 262176 | tf_op jit(solution)/shard_map/ppermute | solution.py:251
  71.4 1.6 %copy-done.5 = bf16[2,64,8192]{2,1,0:T(8,128)(2,1)S(1)} copy-done((bf16[2,64,8192]{2,1,0:T(8,128)(2,1)S(1)}, bf16[2,64,8192]{2,1,0:T(8,128)(2,1)}, u32[]{:S(2)}) %copy-start.5) | copy-done | bytes 2097176
  73.0 3.3 %expand_blocks.1.refs_0_ = bf16[8,128,512]{2,1,0:T(8,128)(2,1)} custom-call(s32[18]{0:T(128)S(1)} %dynamic-slice_bitcast_fusion.scalars, bf16[128,8192]{1,0:T(8,128)(2,1)S(1)} %bitcast.15), custom_call_target="tpu_custom_call" | custom-call | bytes 2097152 | tf_op jit(solution)/shard_map/expand_blocks/pallas_call | solution.py:54
  76.3 2.0 %copy-done = bf16[2,14336,64]{1,2,0:T(8,128)(2,1)S(1)} copy-done((bf16[2,14336,64]{1,2,0:T(8,128)(2,1)S(1)}, bf16[2,14336,64]{1,2,0:T(8,128)(2,1)}, u32[]{:S(2)}) %copy-start) | copy-done | bytes 3670040
  82.0 4.5 %chunk_0.1 = (f32[256,512]{1,0:T(8,128)S(1)}, f32[256,512]{1,0:T(8,128)S(1)}, f32[128,256]{1,0:T(8,128)S(1)}, f32[8,128]{1,0:T(8,128)}) custom-call(s32[18]{0:T(128)S(1)} %dynamic-slice_bitcast_fusion.scalars, bf16[32,2048]{1,0:T(8,128)(2,1)S(1)} %slice.15.refs_0_, bf16[32,2048]{1,0:T(8,128)(2,1)S(1)} %collective-permute-done.refs_1_, ...), custom_call_target="tpu_custom_call" | custom-call | flops 2415919104 | bytes 8126464 | tf_op jit(solution)/shard_map/chunk_0/pallas_call | solution.py:150
  90.8 5.4 %all-to-all-start = ((bf16[8,128,512]{2,1,0:T(8,128)(2,1)}), bf16[8,128,512]{2,1,0:T(8,128)(2,1)S(1)}, u32[]{:S(2)}, u32[]{:S(2)}) async-start(bf16[8,128,512]{2,1,0:T(8,128)(2,1)} %tie.1), calls=%async_computation | async-start | bytes 2097152 | tf_op jit(solution)/shard_map/all_to_all | solution.py:260
  102.1 7.1 %chunk_1.1 = (f32[256,512]{1,0:T(8,128)S(1)}, f32[256,512]{1,0:T(8,128)S(1)}, f32[128,256]{1,0:T(8,128)S(1)}, f32[8,128]{1,0:T(8,128)}) custom-call(s32[18]{0:T(128)S(1)} %dynamic-slice_bitcast_fusion.scalars, bf16[32,4096]{1,0:T(8,128)(2,1)S(1)} %copy-done.7, bf16[32,4096]{1,0:T(8,128)(2,1)S(1)} %copy-done.21, ...), custom_call_target="tpu_custom_call" | custom-call | flops 4831838208 | bytes 13893632 | tf_op jit(solution)/shard_map/chunk_1/pallas_call | solution.py:150
  109.2 7.3 %chunk_2.1 = (f32[256,512]{1,0:T(8,128)S(1)}, f32[256,512]{1,0:T(8,128)S(1)}, f32[128,256]{1,0:T(8,128)S(1)}, f32[8,128]{1,0:T(8,128)}) custom-call(s32[18]{0:T(128)S(1)} %dynamic-slice_bitcast_fusion.scalars, bf16[32,4096]{1,0:T(8,128)(2,1)S(1)} %get-tuple-element.24.refs_0_, bf16[32,4096]{1,0:T(8,128)(2,1)S(1)} %copy-done.15, ...), custom_call_target="tpu_custom_call" | custom-call | flops 4831838208 | bytes 13893632 | tf_op jit(solution)/shard_map/chunk_2/pallas_call | solution.py:150
  116.6 3.6 %last_narrow.1 = f32[128,256]{1,0:T(8,128)S(1)} custom-call(s32[18]{0:T(128)S(1)} %dynamic-slice_bitcast_fusion.scalars, bf16[32,4096]{1,0:T(8,128)(2,1)S(1)} %take_10240.1.refs_0_.refs_1_, bf16[32,4096]{1,0:T(8,128)(2,1)S(1)} %collective-permute-done.7.refs_1_.refs_2_, bf16[32,4096]{1,0:T(8,128)(2,1)S(1)} %collective-permute-done.8.refs_2_.refs_3_, ...), custom_call_target="tpu_custom_call" | custom-call | flops 536870912 | bytes 3407872 | tf_op jit(solution)/shard_map/last_narrow/pallas_call | solution.py:150
  120.3 2.1 %collective-permute-start.29 = (f32[64,256]{1,0:T(8,128)S(1)}, f32[64,256]{1,0:T(8,128)S(1)}, u32[]{:S(2)}, u32[]{:S(2)}) collective-permute-start(f32[64,256]{1,0:T(8,128)S(1)} %fusion.refs_0_), channel_id=1, source_target_pairs={{0,2},{1,3},{2,0},{3,1},{4,6},{5,7},{6,4},{7,5},{8,10},{9,11},{10,... | collective-permute-start | bytes 196616 | tf_op jit(solution)/shard_map/ppermute | solution.py:276
  122.5 4.0 %last_sent.1.refs_0_ = f32[256,512]{1,0:T(8,128)S(1)} custom-call(s32[18]{0:T(128)S(1)} %dynamic-slice_bitcast_fusion.scalars, f32[64,256]{1,0:T(8,128)S(1)} %fusion.refs_0_, bf16[32,4096]{1,0:T(8,128)(2,1)S(1)} %take_10240.1.refs_0_.refs_1_, bf16[32,4096]{1,0:T(8,128)(2,1)S(1)} %collective-permute-done.7.refs_1_.refs_2_, ...), custom_call_target="tpu_custom_call" | custom-call | flops 2147483648 | bytes 7340032 | tf_op jit(solution)/shard_map/last_sent/pallas_call | solution.py:150
  126.7 2.0 %collective-permute-start.31 = (bf16[64,256]{1,0:T(8,128)(2,1)S(1)}, bf16[64,256]{1,0:T(8,128)(2,1)S(1)}, u32[]{:S(2)}, u32[]{:S(2)}) collective-permute-start(bf16[64,256]{1,0:T(8,128)(2,1)S(1)} %add_convert_fusion), channel_id=1, source_target_pairs={{0,4},{2,6},{4,8},{6,10},{8,12},{10,14},{12,0},{14,2},{1,5},{3,7},... | collective-permute-start | bytes 98312 | tf_op jit(solution)/shard_map/ppermute | solution.py:280
  128.7 2.4 %collective-permute-start.32 = (bf16[64,256]{1,0:T(8,128)(2,1)S(1)}, bf16[64,256]{1,0:T(8,128)(2,1)S(1)}, u32[]{:S(2)}, u32[]{:S(2)}) collective-permute-start(bf16[64,256]{1,0:T(8,128)(2,1)S(1)} %add_convert_fusion), channel_id=1, source_target_pairs={{0,8},{2,10},{4,12},{6,14},{8,0},{10,2},{12,4},{14,6},{1,9},{3,11}... | collective-permute-start | bytes 98312 | tf_op jit(solution)/shard_map/ppermute | solution.py:280
  132.5 4.0 %last_kept.1.kept = f32[256,512]{1,0:T(8,128)S(1)} custom-call(s32[18]{0:T(128)S(1)} %dynamic-slice_bitcast_fusion.scalars, f32[256,512]{1,0:T(8,128)S(1)} %last_sent.1.refs_0_, bf16[32,4096]{1,0:T(8,128)(2,1)S(1)} %take_10240.1.refs_0_.refs_1_, bf16[32,4096]{1,0:T(8,128)(2,1)S(1)} %collective-permute-done.7.refs_1_.refs_2_, ...), custom_call_target="tpu_custom_call" | custom-call | flops 2147483648 | bytes 7340032 | tf_op jit(solution)/shard_map/last_kept/pallas_call | solution.py:150
  (123 shorter events, 43.9 us)
Async XLA Ops:
  0.9 6.5 %collective-permute-start = (bf16[32,2048]{1,0:T(8,128)(2,1)S(1)}, bf16[32,2048]{1,0:T(8,128)(2,1)S(1)}, u32[]{:S(2)}, u32[]{:S(2)}) collective-permute-start(bf16[32,2048]{1,0:T(8,128)(2,1)S(1)} %slice.15.refs_0_), channel_id=1, source_target_pairs={{0,4},{4,8},{8,12},{12,14},{14,10},{10,6},{6,2},{2,0},{1,5},{5,9},... | collective-permute-start | bytes 393224 | tf_op jit(solution)/shard_map/ppermute | solution.py:251
  9.2 5.6 %collective-permute-start.5 = (bf16[32,2048]{1,0:T(8,128)(2,1)S(1)}, bf16[32,2048]{1,0:T(8,128)(2,1)S(1)}, u32[]{:S(2)}, u32[]{:S(2)}) collective-permute-start(bf16[32,2048]{1,0:T(8,128)(2,1)S(1)} %collective-permute-done.4.refs_5_), channel_id=1, source_target_pairs={{0,2},{4,0},{8,4},{12,8},{14,12},{10,14},{6,10},{2,6},{1,3},{5,1},... | collective-permute-start | bytes 393224 | tf_op jit(solution)/shard_map/ppermute | solution.py:251
  14.8 9.8 %collective-permute-start.6 = (bf16[32,2048]{1,0:T(8,128)(2,1)S(1)}, bf16[32,2048]{1,0:T(8,128)(2,1)S(1)}, u32[]{:S(2)}, u32[]{:S(2)}) collective-permute-start(bf16[32,2048]{1,0:T(8,128)(2,1)S(1)} %collective-permute-done.5.refs_6_), channel_id=1, source_target_pairs={{0,2},{4,0},{8,4},{12,8},{14,12},{10,14},{6,10},{2,6},{1,3},{5,1},... | collective-permute-start | bytes 393224 | tf_op jit(solution)/shard_map/ppermute | solution.py:251
  17.8 6.8 %collective-permute-start.3 = (bf16[32,2048]{1,0:T(8,128)(2,1)S(1)}, bf16[32,2048]{1,0:T(8,128)(2,1)S(1)}, u32[]{:S(2)}, u32[]{:S(2)}) collective-permute-start(bf16[32,2048]{1,0:T(8,128)(2,1)S(1)} %collective-permute-done.2.refs_3_), channel_id=1, source_target_pairs={{0,4},{4,8},{8,12},{12,14},{14,10},{10,6},{6,2},{2,0},{1,5},{5,9},... | collective-permute-start | bytes 393224 | tf_op jit(solution)/shard_map/ppermute | solution.py:251
  21.0 9.2 %collective-permute-start.24 = (bf16[32,4096]{1,0:T(8,128)(2,1)S(1)}, bf16[32,4096]{1,0:T(8,128)(2,1)S(1)}, u32[]{:S(2)}, u32[]{:S(2)}) collective-permute-start(bf16[32,4096]{1,0:T(8,128)(2,1)S(1)} %get-tuple-element.23.refs_0_), channel_id=1, source_target_pairs={{0,2},{4,0},{8,4},{12,8},{14,12},{10,14},{6,10},{2,6},{1,3},{5,1},... | collective-permute-start | bytes 786440 | tf_op jit(solution)/shard_map/ppermute | solution.py:251
  21.1 10.4 %collective-permute-start.21 = (bf16[32,4096]{1,0:T(8,128)(2,1)S(1)}, bf16[32,4096]{1,0:T(8,128)(2,1)S(1)}, u32[]{:S(2)}, u32[]{:S(2)}) collective-permute-start(bf16[32,4096]{1,0:T(8,128)(2,1)S(1)} %get-tuple-element.23.refs_0_), channel_id=1, source_target_pairs={{0,4},{4,8},{8,12},{12,14},{14,10},{10,6},{6,2},{2,0},{1,5},{5,9},... | collective-permute-start | bytes 786440 | tf_op jit(solution)/shard_map/ppermute | solution.py:251
  23.0 12.9 %collective-permute-start.14 = (bf16[32,4096]{1,0:T(8,128)(2,1)S(1)}, bf16[32,4096]{1,0:T(8,128)(2,1)S(1)}, u32[]{:S(2)}, u32[]{:S(2)}) collective-permute-start(bf16[32,4096]{1,0:T(8,128)(2,1)S(1)} %get-tuple-element.24.refs_0_), channel_id=1, source_target_pairs={{0,4},{4,8},{8,12},{12,14},{14,10},{10,6},{6,2},{2,0},{1,5},{5,9},... | collective-permute-start | bytes 786440 | tf_op jit(solution)/shard_map/ppermute | solution.py:251
  25.9 12.0 %collective-permute-start.10 = (bf16[32,4096]{1,0:T(8,128)(2,1)S(1)}, bf16[32,4096]{1,0:T(8,128)(2,1)S(1)}, u32[]{:S(2)}, u32[]{:S(2)}) collective-permute-start(bf16[32,4096]{1,0:T(8,128)(2,1)S(1)} %take_10240.1.refs_0_.refs_1_), channel_id=1, source_target_pairs={{0,2},{4,0},{8,4},{12,8},{14,12},{10,14},{6,10},{2,6},{1,3},{5,1},... | collective-permute-start | bytes 786440 | tf_op jit(solution)/shard_map/ppermute | solution.py:251
  27.6 13.8 %collective-permute-start.18 = (bf16[32,4096]{1,0:T(8,128)(2,1)S(1)}, bf16[32,4096]{1,0:T(8,128)(2,1)S(1)}, u32[]{:S(2)}, u32[]{:S(2)}) collective-permute-start(bf16[32,4096]{1,0:T(8,128)(2,1)S(1)} %get-tuple-element.24.refs_0_), channel_id=1, source_target_pairs={{0,2},{4,0},{8,4},{12,8},{14,12},{10,14},{6,10},{2,6},{1,3},{5,1},... | collective-permute-start | bytes 786440 | tf_op jit(solution)/shard_map/ppermute | solution.py:251
  30.2 17.0 %collective-permute-start.25 = (bf16[32,4096]{1,0:T(8,128)(2,1)S(1)}, bf16[32,4096]{1,0:T(8,128)(2,1)}, u32[]{:S(2)}, u32[]{:S(2)}) collective-permute-start(bf16[32,4096]{1,0:T(8,128)(2,1)S(1)} %collective-permute-done.24.refs_4_), channel_id=1, source_target_pairs={{0,2},{4,0},{8,4},{12,8},{14,12},{10,14},{6,10},{2,6},{1,3},{5,1},... | collective-permute-start | bytes 786440 | tf_op jit(solution)/shard_map/ppermute | solution.py:251
  31.5 17.4 %collective-permute-start.22 = (bf16[32,4096]{1,0:T(8,128)(2,1)S(1)}, bf16[32,4096]{1,0:T(8,128)(2,1)}, u32[]{:S(2)}, u32[]{:S(2)}) collective-permute-start(bf16[32,4096]{1,0:T(8,128)(2,1)S(1)} %collective-permute-done.21.refs_1_), channel_id=1, source_target_pairs={{0,4},{4,8},{8,12},{12,14},{14,10},{10,6},{6,2},{2,0},{1,5},{5,9},... | collective-permute-start | bytes 786440 | tf_op jit(solution)/shard_map/ppermute | solution.py:251
  35.9 14.5 %collective-permute-start.7 = (bf16[32,4096]{1,0:T(8,128)(2,1)S(1)}, bf16[32,4096]{1,0:T(8,128)(2,1)S(1)}, u32[]{:S(2)}, u32[]{:S(2)}) collective-permute-start(bf16[32,4096]{1,0:T(8,128)(2,1)S(1)} %take_10240.1.refs_0_.refs_1_), channel_id=1, source_target_pairs={{0,4},{4,8},{8,12},{12,14},{14,10},{10,6},{6,2},{2,0},{1,5},{5,9},... | collective-permute-start | bytes 786440 | tf_op jit(solution)/shard_map/ppermute | solution.py:251
  37.9 14.8 %collective-permute-start.11 = (bf16[32,4096]{1,0:T(8,128)(2,1)S(1)}, bf16[32,4096]{1,0:T(8,128)(2,1)S(1)}, u32[]{:S(2)}, u32[]{:S(2)}) collective-permute-start(bf16[32,4096]{1,0:T(8,128)(2,1)S(1)} %collective-permute-done.10.refs_4_.refs_5_), channel_id=1, source_target_pairs={{0,2},{4,0},{8,4},{12,8},{14,12},{10,14},{6,10},{2,6},{1,3},{5,1},... | collective-permute-start | bytes 786440 | tf_op jit(solution)/shard_map/ppermute | solution.py:251
  41.4 13.0 %collective-permute-start.15 = (bf16[32,4096]{1,0:T(8,128)(2,1)S(1)}, bf16[32,4096]{1,0:T(8,128)(2,1)}, u32[]{:S(2)}, u32[]{:S(2)}) collective-permute-start(bf16[32,4096]{1,0:T(8,128)(2,1)S(1)} %collective-permute-done.14.refs_1_), channel_id=1, source_target_pairs={{0,4},{4,8},{8,12},{12,14},{14,10},{10,6},{6,2},{2,0},{1,5},{5,9},... | collective-permute-start | bytes 786440 | tf_op jit(solution)/shard_map/ppermute | solution.py:251
  47.2 11.2 %collective-permute-start.19 = (bf16[32,4096]{1,0:T(8,128)(2,1)S(1)}, bf16[32,4096]{1,0:T(8,128)(2,1)}, u32[]{:S(2)}, u32[]{:S(2)}) collective-permute-start(bf16[32,4096]{1,0:T(8,128)(2,1)S(1)} %collective-permute-done.18.refs_5_), channel_id=1, source_target_pairs={{0,2},{4,0},{8,4},{12,8},{14,12},{10,14},{6,10},{2,6},{1,3},{5,1},... | collective-permute-start | bytes 786440 | tf_op jit(solution)/shard_map/ppermute | solution.py:251
  48.9 15.1 %collective-permute-start.26 = (bf16[32,4096]{1,0:T(8,128)(2,1)}, bf16[32,4096]{1,0:T(8,128)(2,1)}, u32[]{:S(2)}, u32[]{:S(2)}) collective-permute-start(bf16[32,4096]{1,0:T(8,128)(2,1)} %collective-permute-done.25.refs_5_), channel_id=1, source_target_pairs={{0,2},{4,0},{8,4},{12,8},{14,12},{10,14},{6,10},{2,6},{1,3},{5,1},... | collective-permute-start | bytes 786440 | tf_op jit(solution)/shard_map/ppermute | solution.py:251
  50.5 14.6 %collective-permute-start.8 = (bf16[32,4096]{1,0:T(8,128)(2,1)S(1)}, bf16[32,4096]{1,0:T(8,128)(2,1)S(1)}, u32[]{:S(2)}, u32[]{:S(2)}) collective-permute-start(bf16[32,4096]{1,0:T(8,128)(2,1)S(1)} %collective-permute-done.7.refs_1_.refs_2_), channel_id=1, source_target_pairs={{0,4},{4,8},{8,12},{12,14},{14,10},{10,6},{6,2},{2,0},{1,5},{5,9},... | collective-permute-start | bytes 786440 | tf_op jit(solution)/shard_map/ppermute | solution.py:251
  52.7 16.9 %collective-permute-start.12 = (bf16[32,4096]{1,0:T(8,128)(2,1)S(1)}, bf16[32,4096]{1,0:T(8,128)(2,1)S(1)}, u32[]{:S(2)}, u32[]{:S(2)}) collective-permute-start(bf16[32,4096]{1,0:T(8,128)(2,1)S(1)} %collective-permute-done.11.refs_5_.refs_6_), channel_id=1, source_target_pairs={{0,2},{4,0},{8,4},{12,8},{14,12},{10,14},{6,10},{2,6},{1,3},{5,1},... | collective-permute-start | bytes 786440 | tf_op jit(solution)/shard_map/ppermute | solution.py:251
  54.5 41.7 %collective-permute-start.23 = (bf16[32,4096]{1,0:T(8,128)(2,1)}, bf16[32,4096]{1,0:T(8,128)(2,1)}, u32[]{:S(2)}, u32[]{:S(2)}) collective-permute-start(bf16[32,4096]{1,0:T(8,128)(2,1)} %collective-permute-done.22.refs_2_), channel_id=1, source_target_pairs={{0,4},{4,8},{8,12},{12,14},{14,10},{10,6},{6,2},{2,0},{1,5},{5,9},... | collective-permute-start | bytes 786440 | tf_op jit(solution)/shard_map/ppermute | solution.py:251
  58.4 30.4 %collective-permute-start.16 = (bf16[32,4096]{1,0:T(8,128)(2,1)}, bf16[32,4096]{1,0:T(8,128)(2,1)}, u32[]{:S(2)}, u32[]{:S(2)}) collective-permute-start(bf16[32,4096]{1,0:T(8,128)(2,1)} %collective-permute-done.15.refs_2_), channel_id=1, source_target_pairs={{0,4},{4,8},{8,12},{12,14},{14,10},{10,6},{6,2},{2,0},{1,5},{5,9},... | collective-permute-start | bytes 786440 | tf_op jit(solution)/shard_map/ppermute | solution.py:251
  64.0 32.2 %collective-permute-start.27 = (bf16[32,4096]{1,0:T(8,128)(2,1)}, bf16[32,4096]{1,0:T(8,128)(2,1)}, u32[]{:S(2)}, u32[]{:S(2)}) collective-permute-start(bf16[32,4096]{1,0:T(8,128)(2,1)} %collective-permute-done.26.refs_6_), channel_id=1, source_target_pairs={{0,2},{4,0},{8,4},{12,8},{14,12},{10,14},{6,10},{2,6},{1,3},{5,1},... | collective-permute-start | bytes 786440 | tf_op jit(solution)/shard_map/ppermute | solution.py:251
  65.0 25.3 %collective-permute-start.9 = (bf16[32,4096]{1,0:T(8,128)(2,1)S(1)}, bf16[32,4096]{1,0:T(8,128)(2,1)S(1)}, u32[]{:S(2)}, u32[]{:S(2)}) collective-permute-start(bf16[32,4096]{1,0:T(8,128)(2,1)S(1)} %collective-permute-done.8.refs_2_.refs_3_), channel_id=1, source_target_pairs={{0,4},{4,8},{8,12},{12,14},{14,10},{10,6},{6,2},{2,0},{1,5},{5,9},... | collective-permute-start | bytes 786440 | tf_op jit(solution)/shard_map/ppermute | solution.py:251
  69.5 21.3 %collective-permute-start.13 = (bf16[32,4096]{1,0:T(8,128)(2,1)S(1)}, bf16[32,4096]{1,0:T(8,128)(2,1)S(1)}, u32[]{:S(2)}, u32[]{:S(2)}) collective-permute-start(bf16[32,4096]{1,0:T(8,128)(2,1)S(1)} %collective-permute-done.12.refs_6_.refs_7_), channel_id=1, source_target_pairs={{0,2},{4,0},{8,4},{12,8},{14,12},{10,14},{6,10},{2,6},{1,3},{5,1},... | collective-permute-start | bytes 786440 | tf_op jit(solution)/shard_map/ppermute | solution.py:251
  88.8 20.4 %collective-permute-start.20 = (bf16[32,4096]{1,0:T(8,128)(2,1)}, bf16[32,4096]{1,0:T(8,128)(2,1)}, u32[]{:S(2)}, u32[]{:S(2)}) collective-permute-start(bf16[32,4096]{1,0:T(8,128)(2,1)} %collective-permute-done.19.refs_6_), channel_id=1, source_target_pairs={{0,2},{4,0},{8,4},{12,8},{14,12},{10,14},{6,10},{2,6},{1,3},{5,1},... | collective-permute-start | bytes 786440 | tf_op jit(solution)/shard_map/ppermute | solution.py:251
  90.4 18.8 %collective-permute-start.17 = (bf16[32,4096]{1,0:T(8,128)(2,1)}, bf16[32,4096]{1,0:T(8,128)(2,1)}, u32[]{:S(2)}, u32[]{:S(2)}) collective-permute-start(bf16[32,4096]{1,0:T(8,128)(2,1)} %collective-permute-done.16.refs_3_), channel_id=1, source_target_pairs={{0,4},{4,8},{8,12},{12,14},{14,10},{10,6},{6,2},{2,0},{1,5},{5,9},... | collective-permute-start | bytes 786440 | tf_op jit(solution)/shard_map/ppermute | solution.py:251
  90.8 47.3 %all-to-all-start = ((bf16[8,128,512]{2,1,0:T(8,128)(2,1)}), bf16[8,128,512]{2,1,0:T(8,128)(2,1)S(1)}, u32[]{:S(2)}, u32[]{:S(2)}) async-start(bf16[8,128,512]{2,1,0:T(8,128)(2,1)} %tie.1), calls=%async_computation | async-start | bytes 2097152 | tf_op jit(solution)/shard_map/all_to_all | solution.py:260
  120.3 6.4 %collective-permute-start.28 = (f32[64,256]{1,0:T(8,128)S(1)}, f32[64,256]{1,0:T(8,128)S(1)}, u32[]{:S(2)}, u32[]{:S(2)}) collective-permute-start(f32[64,256]{1,0:T(8,128)S(1)} %fusion.refs_0_), channel_id=1, source_target_pairs={{0,1},{1,0},{2,3},{3,2},{4,5},{5,4},{6,7},{7,6},{8,9},{9,8},{10,11... | collective-permute-start | bytes 196616 | tf_op jit(solution)/shard_map/ppermute | solution.py:276
  120.3 6.3 %collective-permute-start.29 = (f32[64,256]{1,0:T(8,128)S(1)}, f32[64,256]{1,0:T(8,128)S(1)}, u32[]{:S(2)}, u32[]{:S(2)}) collective-permute-start(f32[64,256]{1,0:T(8,128)S(1)} %fusion.refs_0_), channel_id=1, source_target_pairs={{0,2},{1,3},{2,0},{3,1},{4,6},{5,7},{6,4},{7,5},{8,10},{9,11},{10,... | collective-permute-start | bytes 196616 | tf_op jit(solution)/shard_map/ppermute | solution.py:276
  126.5 10.9 %collective-permute-start.34 = (f32[256,512]{1,0:T(8,128)S(1)}, f32[256,512]{1,0:T(8,128)S(1)}, u32[]{:S(2)}, u32[]{:S(2)}) collective-permute-start(f32[256,512]{1,0:T(8,128)S(1)} %last_sent.1.refs_0_), channel_id=1, source_target_pairs={{0,1},{1,0},{2,3},{3,2},{4,5},{5,4},{6,7},{7,6},{8,9},{9,8},{10,11... | collective-permute-start | bytes 1572872 | tf_op jit(solution)/shard_map/ppermute | solution.py:281
  126.7 10.6 %collective-permute-start.31 = (bf16[64,256]{1,0:T(8,128)(2,1)S(1)}, bf16[64,256]{1,0:T(8,128)(2,1)S(1)}, u32[]{:S(2)}, u32[]{:S(2)}) collective-permute-start(bf16[64,256]{1,0:T(8,128)(2,1)S(1)} %add_convert_fusion), channel_id=1, source_target_pairs={{0,4},{2,6},{4,8},{6,10},{8,12},{10,14},{12,0},{14,2},{1,5},{3,7},... | collective-permute-start | bytes 98312 | tf_op jit(solution)/shard_map/ppermute | solution.py:280
  128.7 8.6 %collective-permute-start.32 = (bf16[64,256]{1,0:T(8,128)(2,1)S(1)}, bf16[64,256]{1,0:T(8,128)(2,1)S(1)}, u32[]{:S(2)}, u32[]{:S(2)}) collective-permute-start(bf16[64,256]{1,0:T(8,128)(2,1)S(1)} %add_convert_fusion), channel_id=1, source_target_pairs={{0,8},{2,10},{4,12},{6,14},{8,0},{10,2},{12,4},{14,6},{1,9},{3,11}... | collective-permute-start | bytes 98312 | tf_op jit(solution)/shard_map/ppermute | solution.py:280
  131.1 6.2 %collective-permute-start.33 = (bf16[64,256]{1,0:T(8,128)(2,1)S(1)}, bf16[64,256]{1,0:T(8,128)(2,1)S(1)}, u32[]{:S(2)}, u32[]{:S(2)}) collective-permute-start(bf16[64,256]{1,0:T(8,128)(2,1)S(1)} %add_convert_fusion), channel_id=1, source_target_pairs={{0,12},{2,14},{4,0},{6,2},{8,4},{10,6},{12,8},{14,10},{1,13},{3,15... | collective-permute-start | bytes 98312 | tf_op jit(solution)/shard_map/ppermute | solution.py:280
  (36 other events, 197.8 us)

commit v7 on v6

--- a/solution.py
+++ b/solution.py
@@ -10,8 +10,9 @@
 
 F32, BF16 = jnp.float32, jnp.bfloat16
 TILE = 1024
+CHUNKS = 4
 MIB = 2**20
-MATMUL_MIB = 48
+MATMUL_MIB = 62
 
 
 def params(mib):
@@ -43,8 +44,9 @@
     )(hidden, *after)
 
 
-def split_kernel(scalars, src, dst):
+def split_kernel(scalars, src, dst, mark):
     dst[...] = src[...][None]
+    mark[...] = jnp.zeros_like(mark)
 
 
 def expand_blocks(scalars, half, expand, n, cores):
@@ -57,9 +59,9 @@
             num_scalar_prefetch=1,
             grid=(n,),
             in_specs=[pl.BlockSpec((rows, share), lambda s, t: (0, s * cores + t[half]))],
-            out_specs=pl.BlockSpec((1, rows, share), lambda s, t: (s, 0, 0)),
+            out_specs=[pl.BlockSpec((1, rows, share), lambda s, t: (s, 0, 0)), pl.BlockSpec((8, 128), lambda s, t: (0, 0))],
         ),
-        out_shape=jax.ShapeDtypeStruct((n, rows, share), BF16),
+        out_shape=[jax.ShapeDtypeStruct((n, rows, share), BF16), jax.ShapeDtypeStruct((8, 128), F32)],
         compiler_params=params(MATMUL_MIB),
         cost_estimate=pl.CostEstimate(flops=0, bytes_accessed=4 * n * rows * share, transcendentals=0),
         name="expand_blocks",
@@ -82,31 +84,30 @@
     )(array, *after)
 
 
-def matmul_kernel(n, waits, base, half, start, tiles, sides, narrow, has_acc, token, scalars, *refs):
+def matmul_kernel(n, waits, spans, half, sides, narrow, has_acc, scalars, *refs):
     refs = list(refs)[waits:]
-    pieces = [refs.pop(0) for _ in range(n)]
+    pieces = [[refs.pop(0) for _ in range(n)] for _ in spans]
     down = refs.pop(0)
     shrink = refs.pop(0)
     outs = len(sides) + narrow
     before = [refs.pop(0) for _ in range(outs)] if has_acc else []
     acc = [refs.pop(0) for _ in range(outs)]
-    if token:
-        refs.pop(0)[...] = jnp.zeros((8, 128), F32)
+    tiles = [(part, at, tile) for part, (_, _, cuts) in enumerate(spans) for at, tile in cuts]
     lefts = [refs.pop(0) for _ in tiles]
     weights = [[refs.pop(0) for _ in tiles] for _ in sides]
     ranks = [refs.pop(0) for _ in tiles] if narrow else []
     earlier = [refs.pop(0) for _ in before]
     sems, old_sems = refs
-    rows = pieces[0].shape[0]
+    rows = pieces[0][0].shape[0]
     share = down.shape[1] // 2
 
     copies = []
-    at = 0
-    for k, tile in enumerate(tiles):
+    for k, (part, at, tile) in enumerate(tiles):
+        base, start, _ = spans[part]
         group = []
         for i in range(n):
             to = pl.multiple_of(scalars[base + i] * rows, rows)
-            group.append((pieces[i].at[:, pl.ds(at, tile)], lefts[k].at[pl.ds(to, rows), :]))
+            group.append((pieces[part][i].at[:, pl.ds(at, tile)], lefts[k].at[pl.ds(to, rows), :]))
         if narrow:
             group.append((shrink.at[:, pl.ds(start + at, tile)], ranks[k]))
         for i, side in enumerate(sides):
@@ -115,7 +116,6 @@
         copies.append([pltpu.make_async_copy(*pair, sems.at[k, i]) for i, pair in enumerate(group)])
         for copy in copies[-1]:
             copy.start()
-        at += tile
     old = [pltpu.make_async_copy(a, b, old_sems.at[i]) for i, (a, b) in enumerate(zip(before, earlier))]
     for copy in old:
         copy.start()
@@ -136,33 +136,39 @@
         acc[i][...] += earlier[i][...]
 
 
-def chunk_matmul(scalars, base, half, pieces, down, shrink, acc, start, sides, narrow, label, after=(), token=False):
-    n = len(pieces)
-    rows, width = pieces[0].shape[0] * n, pieces[0].shape[1]
+def cuts_of(width):
+    first = width % TILE or TILE
+    sizes = [first // 2] * 2 if first == TILE else [first]
+    sizes += [TILE] * ((width - first) // TILE)
+    return [(sum(sizes[:i]), size) for i, size in enumerate(sizes)]
+
+
+def chunk_matmul(scalars, half, chunks, down, shrink, acc, sides, narrow, label, after=()):
+    n = len(chunks[0][0])
+    rows = chunks[0][0][0].shape[0] * n
     share = down.shape[1] // 2
     ranks = shrink.shape[0]
-    tiles = [TILE // 2] * 2 + [TILE] * (width // TILE - 1)
+    spans = [(base, start, cuts_of(pieces[0].shape[1])) for pieces, base, start in chunks]
+    sizes = [tile for _, _, cuts in spans for _, tile in cuts]
+    width = sum(sizes)
     anywhere = pl.BlockSpec(memory_space=pl.ANY)
-    args = [*after, *pieces, down, shrink, *(acc or ())]
+    args = [*after, *(piece for pieces, _, _ in chunks for piece in pieces), down, shrink, *(acc or ())]
     shapes = [(rows, share)] * len(sides) + [(ranks, rows)] * narrow
     columns = share * len(sides) + ranks * narrow
-    marks = [(8, 128)] * token
-    return pl.pallas_call(
-        functools.partial(
-            matmul_kernel, n, len(after), base, half, start, tiles, sides, narrow, acc is not None, token
-        ),
+    return pl.pallas_call(
+        functools.partial(matmul_kernel, n, len(after), spans, half, sides, narrow, acc is not None),
         grid_spec=pltpu.PrefetchScalarGridSpec(
             num_scalar_prefetch=1,
             grid=(),
             in_specs=[anywhere] * len(args),
-            out_specs=[pl.BlockSpec(memory_space=pltpu.VMEM)] * len(shapes + marks),
-            scratch_shapes=[pltpu.VMEM((rows, tile), BF16) for tile in tiles]
-            + [pltpu.VMEM((tile, share), BF16) for _ in sides for tile in tiles]
-            + [pltpu.VMEM((ranks, tile), BF16) for tile in tiles if narrow]
+            out_specs=[pl.BlockSpec(memory_space=pltpu.VMEM)] * len(shapes),
+            scratch_shapes=[pltpu.VMEM((rows, tile), BF16) for tile in sizes]
+            + [pltpu.VMEM((tile, share), BF16) for _ in sides for tile in sizes]
+            + [pltpu.VMEM((ranks, tile), BF16) for tile in sizes if narrow]
             + [pltpu.VMEM(shape, F32) for shape in shapes if acc is not None]
-            + [pltpu.SemaphoreType.DMA((len(tiles), n + 3)), pltpu.SemaphoreType.DMA((3,))],
+            + [pltpu.SemaphoreType.DMA((len(sizes), n + 3)), pltpu.SemaphoreType.DMA((3,))],
         ),
-        out_shape=[jax.ShapeDtypeStruct(shape, F32) for shape in shapes + marks],
+        out_shape=[jax.ShapeDtypeStruct(shape, F32) for shape in shapes],
         compiler_params=params(MATMUL_MIB),
         cost_estimate=pl.CostEstimate(
             flops=4 * rows * width * columns,
@@ -233,40 +239,36 @@
         slots = jnp.arange(adapter_slot.shape[0], dtype=jnp.int32)
         row_slot = jnp.sum(jnp.where(row_adapter[None, :] == slots[:, None], adapter_slot[:, None], 0), axis=0)
 
-        large = 2 * (units // (7 * TILE)) * TILE
-        widths = [units - 3 * large, large, large, large]
-
-        blocks = expand_blocks(scalars, half, expand, n, cores)
-        acc = None
-        start = 0
-        after = {}
-        for chunk, width in enumerate(widths):
-            own = take(hidden, start, width, after[chunk]) if chunk in after else hidden[:, start:start + width]
+        width = units // CHUNKS
+        blocks, mark = expand_blocks(scalars, half, expand, n, cores)
+        chunks, ends = [], []
+        for chunk in range(CHUNKS):
+            start = chunk * width
+            own = take(hidden, start, width, [mark]) if chunk == CHUNKS - 1 else hidden[:, start:start + width]
             way = chunk % 2
             pieces = [own]
-            lengths = ((long, short), (short, long))[way]
-            for length, pairs in zip(lengths, (clockwise, counter)):
+            for length, pairs in zip(((long, short), (short, long))[way], (clockwise, counter)):
                 moving = own
                 for step in range(length):
                     moving = lax.ppermute(moving, "store", pairs)
                     pieces.append(moving)
-            ends = [pieces[lengths[0]], pieces[-1]]
-            call = functools.partial(chunk_matmul, scalars, way * n, half, pieces, down, shrink_rows)
-            if chunk < len(widths) - 1:
-                *acc, token = call(acc, start, (0, 1), True, f"chunk_{chunk}", token=True)
-                if chunk == 0:
-                    after[3] = ends
-            else:
-                factors = lax.all_to_all(tie(blocks, ends), "store", 0, 0)
-                narrow, = call(acc[2:], start, (), True, "last_narrow")
-                mine = [
-                    jnp.where((row_slot == store * owned + i)[None, :], narrow[i * rank:(i + 1) * rank], 0.0)
-                    for i in range(owned)
-                ]
-                mine = sum(mine[1:], mine[0])
-                send, = call(acc[1:2], start, (1,), False, "last_sent", [mine])
-                kept, = call(acc[:1], start, (0,), False, "last_kept", [send])
-            start += width
+                ends.append(moving)
+            chunks.append((pieces, way * n, start))
+        factors = lax.all_to_all(tie(blocks, ends[:4]), "store", 0, 0)
+
+        call = functools.partial(chunk_matmul, scalars, half)
+        acc = None
+        for chunk in range(CHUNKS - 2):
+            acc = call(chunks[chunk:chunk + 1], down, shrink_rows, acc, (0, 1), True, f"chunk_{chunk}")
+        last = chunks[CHUNKS - 2:]
+        narrow, = call(last, down, shrink_rows, acc[2:], (), True, "last_narrow")
+        mine = [
+            jnp.where((row_slot == store * owned + i)[None, :], narrow[i * rank:(i + 1) * rank], 0.0)
+            for i in range(owned)
+        ]
+        mine = sum(mine[1:], mine[0])
+        send, = call(last, down, shrink_rows, acc[1:2], (1,), False, "last_sent", [mine])
+        kept, = call(last, down, shrink_rows, acc[:1], (0,), False, "last_kept", [send])
         where = [(s, t) for s in range(n) for t in range(cores)]
         whole = mine
         for ds in range(2):

time: 142 us -> 130 us (0.915)
  local copies, waits for them, and re-layouts: 26.4 us -> 5.16 us
  Pallas kernels: 35.2 us -> 51 us
  starting transfers between devices: 47.3 us -> 43.2 us
  waiting for transfers between devices: 31.6 us -> 28.4 us
    unnamed x64 -> x50, local copies, waits for them, and re-layouts: 23.6 us -> 1.9 us
    pallas_call x1, Pallas kernels: 0.03 us -> 8.06 us  [take(): pl.pallas_call(functools.partial(take_kernel, start, width), in_specs=[pl...]
    pallas_call x6 -> x5, Pallas kernels: 30.5 us -> 34.1 us  [chunk_matmul(): pl.pallas_call(functools.partial(matmul_kernel, n, len(after), spans, hal...]
    ppermute x28, waiting for transfers between devices: 31.5 us -> 28.4 us  [shards(): moving = lax.ppermute(moving, 'store', pairs)]
    pallas_call x1, Pallas kernels: 3.31 us -> 5.86 us  [expand_blocks(): pl.pallas_call(split_kernel, grid_spec=pltpu.PrefetchScalarGridSpec(num_s...]
    pallas_call x1, Pallas kernels: 1.35 us -> 2.94 us  [final(): pl.pallas_call(functools.partial(final_kernel, n, owned), in_specs=[pl.Bl...]
    all_to_all x1, starting transfers between devices: 5.38 us -> 3.87 us  [shards(): factors = lax.all_to_all(tie(blocks, ends[:4]), 'store', 0, 0)]
    ppermute x28, starting transfers between devices: 33.6 us -> 32.2 us  [shards(): moving = lax.ppermute(moving, 'store', pairs)]
  transfers between devices with their start and end apart: 36 -> 36, of which waited for: 11 -> 12; matrix products, arithmetic and copies ran while one was open for 2% -> 3% of each run, Pallas kernels for 24% -> 37%
where the time goes in v7:
time: 130 us
  Pallas kernels  51 us (39%)
  starting transfers between devices  43.2 us (33%)
  waiting for transfers between devices  28.4 us (22%)
  local copies, waits for them, and re-layouts  5.16 us (4%)
  other arithmetic  1.63 us (1%)
    pallas_call x5, Pallas kernels, chunk_matmul(): pl.pallas_call(functools.partial(matmul_kernel, n, len(after), spans, hal...  34.1 us
    ppermute x28, starting transfers between devices, shards(): moving = lax.ppermute(moving, 'store', pairs)  32.2 us
    ppermute x28, waiting for transfers between devices, shards(): moving = lax.ppermute(moving, 'store', pairs)  28.4 us
    pallas_call x1, Pallas kernels, take(): pl.pallas_call(functools.partial(take_kernel, start, width), in_specs=[pl...  8.06 us
    pallas_call x1, Pallas kernels, expand_blocks(): pl.pallas_call(split_kernel, grid_spec=pltpu.PrefetchScalarGridSpec(num_s...  5.86 us
    ppermute x3, starting transfers between devices, shards(): lax.ppermute(column, 'store', [(s, (s + ds) % n) for s in range(n)])  4.46 us
    all_to_all x1, starting transfers between devices, shards(): factors = lax.all_to_all(tie(blocks, ends[:4]), 'store', 0, 0)  3.87 us
    pallas_call x1, Pallas kernels, final(): pl.pallas_call(functools.partial(final_kernel, n, owned), in_specs=[pl.Bl...  2.94 us
  transfers between devices with their start and end apart: 36, of which 12 were waited for; matrix products, arithmetic and copies ran while one was open for 3% of the time, Pallas kernels for 37%

profile of v7, /device:TPU:0, one launch (start us, length us, event | category | flops | bytes accessed | tf_op | source)
XLA Modules:
  0.0 129.6 jit_solution(4110061236416966097)
XLA Ops:
  1.3 3.0 %collective-permute-start.25 = (bf16[32,3584]{1,0:T(8,128)(2,1)S(1)}, bf16[32,3584]{1,0:T(8,128)(2,1)}, u32[]{:S(2)}, u32[]{:S(2)}) collective-permute-start(bf16[32,3584]{1,0:T(8,128)(2,1)S(1)} %get-tuple-element.21.refs_0_), channel_id=1, source_target_pairs={{0,2},{4,0},{8,4},{12,8},{14,12},{10,14},{6,10},{2,6},{1,3},{5,1},... | collective-permute-start | bytes 688136 | tf_op jit(solution)/shard_map/ppermute | solution.py:253
  4.4 1.9 %collective-permute-start.17 = (bf16[32,3584]{1,0:T(8,128)(2,1)S(1)}, bf16[32,3584]{1,0:T(8,128)(2,1)S(1)}, u32[]{:S(2)}, u32[]{:S(2)}) collective-permute-start(bf16[32,3584]{1,0:T(8,128)(2,1)S(1)} %get-tuple-element.23.refs_0_), channel_id=1, source_target_pairs={{0,2},{4,0},{8,4},{12,8},{14,12},{10,14},{6,10},{2,6},{1,3},{5,1},... | collective-permute-start | bytes 688136 | tf_op jit(solution)/shard_map/ppermute | solution.py:253
  6.4 1.9 %collective-permute-start.4 = (bf16[32,3584]{1,0:T(8,128)(2,1)S(1)}, bf16[32,3584]{1,0:T(8,128)(2,1)S(1)}, u32[]{:S(2)}, u32[]{:S(2)}) collective-permute-start(bf16[32,3584]{1,0:T(8,128)(2,1)S(1)} %get-tuple-element.22.refs_0_.refs_1_), channel_id=1, source_target_pairs={{0,2},{4,0},{8,4},{12,8},{14,12},{10,14},{6,10},{2,6},{1,3},{5,1},... | collective-permute-start | bytes 688136 | tf_op jit(solution)/shard_map/ppermute | solution.py:253
  9.6 5.9 %expand_blocks.1 = (bf16[8,128,512]{2,1,0:T(8,128)(2,1)}, f32[8,128]{1,0:T(8,128)}) custom-call(s32[18]{0:T(128)} %dynamic-slice_bitcast_fusion.scalars, bf16[128,8192]{1,0:T(8,128)(2,1)} %bitcast.14), custom_call_target="tpu_custom_call" | custom-call | bytes 2097152 | tf_op jit(solution)/shard_map/expand_blocks/pallas_call | solution.py:56
  15.4 8.1 %take_10752.1.refs_8_.refs_9_ = bf16[32,3584]{1,0:T(8,128)(2,1)} custom-call(bf16[32,14336]{1,0:T(8,128)(2,1)} %src.1, f32[8,128]{1,0:T(8,128)} %get-tuple-element.13.refs_0_), custom_call_target="tpu_custom_call" | custom-call | bytes 458752 | tf_op jit(solution)/shard_map/take_10752/pallas_call | solution.py:35
  23.7 1.9 %collective-permute-start.10 = (bf16[32,3584]{1,0:T(8,128)(2,1)}, bf16[32,3584]{1,0:T(8,128)(2,1)S(1)}, u32[]{:S(2)}, u32[]{:S(2)}) collective-permute-start(bf16[32,3584]{1,0:T(8,128)(2,1)} %take_10752.1.refs_8_.refs_9_), channel_id=1, source_target_pairs={{0,2},{4,0},{8,4},{12,8},{14,12},{10,14},{6,10},{2,6},{1,3},{5,1},... | collective-permute-start | bytes 688136 | tf_op jit(solution)/shard_map/ppermute | solution.py:253
  25.7 1.9 %collective-permute-start.26 = (bf16[32,3584]{1,0:T(8,128)(2,1)}, bf16[32,3584]{1,0:T(8,128)(2,1)S(1)}, u32[]{:S(2)}, u32[]{:S(2)}) collective-permute-start(bf16[32,3584]{1,0:T(8,128)(2,1)} %collective-permute-done.25.refs_5_), channel_id=1, source_target_pairs={{0,2},{4,0},{8,4},{12,8},{14,12},{10,14},{6,10},{2,6},{1,3},{5,1},... | collective-permute-start | bytes 688136 | tf_op jit(solution)/shard_map/ppermute | solution.py:253
  27.8 4.3 %collective-permute-done.refs_1_.refs_2_ = bf16[32,3584]{1,0:T(8,128)(2,1)S(1)} collective-permute-done((bf16[32,3584]{1,0:T(8,128)(2,1)S(1)}, bf16[32,3584]{1,0:T(8,128)(2,1)S(1)}, u32[]{:S(2)}, u32[]{:S(2)}) %collective-permute-start) | collective-permute-done | bytes 229408 | tf_op jit(solution)/shard_map/ppermute | solution.py:253
  32.1 1.6 %collective-permute-start.18 = (bf16[32,3584]{1,0:T(8,128)(2,1)S(1)}, bf16[32,3584]{1,0:T(8,128)(2,1)S(1)}, u32[]{:S(2)}, u32[]{:S(2)}) collective-permute-start(bf16[32,3584]{1,0:T(8,128)(2,1)S(1)} %collective-permute-done.17.refs_4_), channel_id=1, source_target_pairs={{0,2},{4,0},{8,4},{12,8},{14,12},{10,14},{6,10},{2,6},{1,3},{5,1},... | collective-permute-start | bytes 688136 | tf_op jit(solution)/shard_map/ppermute | solution.py:253
  34.4 2.6 %collective-permute-done.7.refs_9_.refs_10_ = bf16[32,3584]{1,0:T(8,128)(2,1)S(1)} collective-permute-done((bf16[32,3584]{1,0:T(8,128)(2,1)}, bf16[32,3584]{1,0:T(8,128)(2,1)S(1)}, u32[]{:S(2)}, u32[]{:S(2)}) %collective-permute-start.7) | collective-permute-done | bytes 229408 | tf_op jit(solution)/shard_map/ppermute | solution.py:253
  37.0 1.6 %collective-permute-start.5 = (bf16[32,3584]{1,0:T(8,128)(2,1)S(1)}, bf16[32,3584]{1,0:T(8,128)(2,1)}, u32[]{:S(2)}, u32[]{:S(2)}) collective-permute-start(bf16[32,3584]{1,0:T(8,128)(2,1)S(1)} %collective-permute-done.4.refs_5_.refs_6_), channel_id=1, source_target_pairs={{0,2},{4,0},{8,4},{12,8},{14,12},{10,14},{6,10},{2,6},{1,3},{5,1},... | collective-permute-start | bytes 688136 | tf_op jit(solution)/shard_map/ppermute | solution.py:253
  39.3 2.6 %collective-permute-done.22.refs_2_ = bf16[32,3584]{1,0:T(8,128)(2,1)S(1)} collective-permute-done((bf16[32,3584]{1,0:T(8,128)(2,1)}, bf16[32,3584]{1,0:T(8,128)(2,1)S(1)}, u32[]{:S(2)}, u32[]{:S(2)}) %collective-permute-start.22) | collective-permute-done | bytes 229408 | tf_op jit(solution)/shard_map/ppermute | solution.py:253
  44.2 2.6 %collective-permute-done.15.refs_2_ = bf16[32,3584]{1,0:T(8,128)(2,1)S(1)} collective-permute-done((bf16[32,3584]{1,0:T(8,128)(2,1)S(1)}, bf16[32,3584]{1,0:T(8,128)(2,1)S(1)}, u32[]{:S(2)}, u32[]{:S(2)}) %collective-permute-start.15) | collective-permute-done | bytes 229408 | tf_op jit(solution)/shard_map/ppermute | solution.py:253
  46.9 1.6 %collective-permute-start.27 = (bf16[32,3584]{1,0:T(8,128)(2,1)S(1)}, bf16[32,3584]{1,0:T(8,128)(2,1)S(1)}, u32[]{:S(2)}, u32[]{:S(2)}) collective-permute-start(bf16[32,3584]{1,0:T(8,128)(2,1)S(1)} %collective-permute-done.26.refs_6_), channel_id=1, source_target_pairs={{0,2},{4,0},{8,4},{12,8},{14,12},{10,14},{6,10},{2,6},{1,3},{5,1},... | collective-permute-start | bytes 688136 | tf_op jit(solution)/shard_map/ppermute | solution.py:253
  49.3 2.5 %collective-permute-done.1.refs_2_.refs_3_ = bf16[32,3584]{1,0:T(8,128)(2,1)S(1)} collective-permute-done((bf16[32,3584]{1,0:T(8,128)(2,1)S(1)}, bf16[32,3584]{1,0:T(8,128)(2,1)S(1)}, u32[]{:S(2)}, u32[]{:S(2)}) %collective-permute-start.1) | collective-permute-done | bytes 229408 | tf_op jit(solution)/shard_map/ppermute | solution.py:253
  54.1 2.7 %collective-permute-done.8.refs_10_.refs_11_ = bf16[32,3584]{1,0:T(8,128)(2,1)} collective-permute-done((bf16[32,3584]{1,0:T(8,128)(2,1)S(1)}, bf16[32,3584]{1,0:T(8,128)(2,1)}, u32[]{:S(2)}, u32[]{:S(2)}) %collective-permute-start.8) | collective-permute-done | bytes 229408 | tf_op jit(solution)/shard_map/ppermute | solution.py:253
  57.0 1.9 %collective-permute-start.12 = (bf16[32,3584]{1,0:T(8,128)(2,1)S(1)}, bf16[32,3584]{1,0:T(8,128)(2,1)}, u32[]{:S(2)}, u32[]{:S(2)}) collective-permute-start(bf16[32,3584]{1,0:T(8,128)(2,1)S(1)} %collective-permute-done.11.refs_13_.refs_14_), channel_id=1, source_target_pairs={{0,2},{4,0},{8,4},{12,8},{14,12},{10,14},{6,10},{2,6},{1,3},{5,1},... | collective-permute-start | bytes 688136 | tf_op jit(solution)/shard_map/ppermute | solution.py:253
  58.9 2.8 %collective-permute-done.23.refs_3_ = bf16[32,3584]{1,0:T(8,128)(2,1)} collective-permute-done((bf16[32,3584]{1,0:T(8,128)(2,1)S(1)}, bf16[32,3584]{1,0:T(8,128)(2,1)}, u32[]{:S(2)}, u32[]{:S(2)}) %collective-permute-start.23) | collective-permute-done | bytes 229408 | tf_op jit(solution)/shard_map/ppermute | solution.py:253
  62.0 1.9 %collective-permute-start.20 = (bf16[32,3584]{1,0:T(8,128)(2,1)}, bf16[32,3584]{1,0:T(8,128)(2,1)S(1)}, u32[]{:S(2)}, u32[]{:S(2)}) collective-permute-start(bf16[32,3584]{1,0:T(8,128)(2,1)} %collective-permute-done.19.refs_6_), channel_id=1, source_target_pairs={{0,2},{4,0},{8,4},{12,8},{14,12},{10,14},{6,10},{2,6},{1,3},{5,1},... | collective-permute-start | bytes 688136 | tf_op jit(solution)/shard_map/ppermute | solution.py:253
  64.8 1.7 %collective-permute-done.16.refs_3_ = bf16[32,3584]{1,0:T(8,128)(2,1)S(1)} collective-permute-done((bf16[32,3584]{1,0:T(8,128)(2,1)S(1)}, bf16[32,3584]{1,0:T(8,128)(2,1)S(1)}, u32[]{:S(2)}, u32[]{:S(2)}) %collective-permute-start.16) | collective-permute-done | bytes 229408 | tf_op jit(solution)/shard_map/ppermute | solution.py:253
  68.1 3.4 %collective-permute-done.2.refs_3_.refs_4_ = bf16[32,3584]{1,0:T(8,128)(2,1)} collective-permute-done((bf16[32,3584]{1,0:T(8,128)(2,1)S(1)}, bf16[32,3584]{1,0:T(8,128)(2,1)}, u32[]{:S(2)}, u32[]{:S(2)}) %collective-permute-start.2) | collective-permute-done | bytes 229408 | tf_op jit(solution)/shard_map/ppermute | solution.py:253
  71.7 2.0 %collective-permute-start.3 = (bf16[32,3584]{1,0:T(8,128)(2,1)}, bf16[32,3584]{1,0:T(8,128)(2,1)}, u32[]{:S(2)}, u32[]{:S(2)}) collective-permute-start(bf16[32,3584]{1,0:T(8,128)(2,1)} %collective-permute-done.2.refs_3_.refs_4_), channel_id=1, source_target_pairs={{0,4},{4,8},{8,12},{12,14},{14,10},{10,6},{6,2},{2,0},{1,5},{5,9},... | collective-permute-start | bytes 688136 | tf_op jit(solution)/shard_map/ppermute | solution.py:253
  73.6 2.7 %collective-permute-done.24.refs_4_.refs_1_ = bf16[32,3584]{1,0:T(8,128)(2,1)S(1)} collective-permute-done((bf16[32,3584]{1,0:T(8,128)(2,1)}, bf16[32,3584]{1,0:T(8,128)(2,1)S(1)}, u32[]{:S(2)}, u32[]{:S(2)}) %collective-permute-start.24) | collective-permute-done | bytes 229408 | tf_op jit(solution)/shard_map/ppermute | solution.py:253
  78.6 3.9 %all-to-all-start = ((bf16[8,128,512]{2,1,0:T(8,128)(2,1)}), bf16[8,128,512]{2,1,0:T(8,128)(2,1)S(1)}, u32[]{:S(2)}, u32[]{:S(2)}) async-start(bf16[8,128,512]{2,1,0:T(8,128)(2,1)} %tie.1), calls=%async_computation | async-start | bytes 2097152 | tf_op jit(solution)/shard_map/all_to_all | solution.py:257
  82.5 6.7 %chunk_0.1 = (f32[256,512]{1,0:T(8,128)}, f32[256,512]{1,0:T(8,128)}, f32[128,256]{1,0:T(8,128)}) custom-call(s32[18]{0:T(128)} %dynamic-slice_bitcast_fusion.scalars, bf16[32,3584]{1,0:T(8,128)(2,1)} %copy-done.14, bf16[32,3584]{1,0:T(8,128)(2,1)} %collective-permute-done.21.refs_1_, bf16[32,3584]{1,0:T(8,128)(2,1)} %copy-done.21, ...), custom_call_target="tpu_custom_call" | custom-call | flops 4227858432 | bytes 12451840 | tf_op jit(solution)/shard_map/chunk_0/pallas_call | solution.py:158
  89.2 7.4 %chunk_1.1 = (f32[256,512]{1,0:T(8,128)}, f32[256,512]{1,0:T(8,128)}, f32[128,256]{1,0:T(8,128)}) custom-call(s32[18]{0:T(128)} %dynamic-slice_bitcast_fusion.scalars, bf16[32,3584]{1,0:T(8,128)(2,1)} %copy-done.13, bf16[32,3584]{1,0:T(8,128)(2,1)} %copy-done.18, bf16[32,3584]{1,0:T(8,128)(2,1)} %copy-done.22, bf16[32,3584]{1,0:T(8,128)(2,1)} %copy-done.10, ...), custom_call_target="tpu_custom_call" | custom-call | flops 4227858432 | bytes 12451840 | tf_op jit(solution)/shard_map/chunk_1/pallas_call | solution.py:158
  96.6 5.9 %last_narrow.1 = f32[128,256]{1,0:T(8,128)} custom-call(s32[18]{0:T(128)} %dynamic-slice_bitcast_fusion.scalars, bf16[32,3584]{1,0:T(8,128)(2,1)} %copy-done.1, bf16[32,3584]{1,0:T(8,128)(2,1)} %copy-done.3, bf16[32,3584]{1,0:T(8,128)(2,1)} %copy-done.6, bf16[32,3584]{1,0:T(8,128)(2,1)} %collective-permute-done.2.refs_3_.refs_4_, ...), custom_call_target="tpu_custom_call" | custom-call | flops 939524096 | bytes 5767168 | tf_op jit(solution)/shard_map/last_narrow/pallas_call | solution.py:158
  103.5 2.1 %collective-permute-start.29 = (f32[64,256]{1,0:T(8,128)S(1)}, f32[64,256]{1,0:T(8,128)S(1)}, u32[]{:S(2)}, u32[]{:S(2)}) collective-permute-start(f32[64,256]{1,0:T(8,128)S(1)} %fusion.refs_0_), channel_id=1, source_target_pairs={{0,2},{1,3},{2,0},{3,1},{4,6},{5,7},{6,4},{7,5},{8,10},{9,11},{10,... | collective-permute-start | bytes 196616 | tf_op jit(solution)/shard_map/ppermute | solution.py:278
  105.6 7.2 %last_sent.1.refs_0_ = f32[256,512]{1,0:T(8,128)} custom-call(s32[18]{0:T(128)} %dynamic-slice_bitcast_fusion.scalars, f32[64,256]{1,0:T(8,128)} %copy-done.16, bf16[32,3584]{1,0:T(8,128)(2,1)} %copy-done.1, bf16[32,3584]{1,0:T(8,128)(2,1)} %copy-done.3, bf16[32,3584]{1,0:T(8,128)(2,1)} %copy-done.6, ...), custom_call_target="tpu_custom_call" | custom-call | flops 3758096384 | bytes 12058624 | tf_op jit(solution)/shard_map/last_sent/pallas_call | solution.py:158
  113.4 3.3 %collective-permute-start.33 = (bf16[64,256]{1,0:T(8,128)(2,1)S(1)}, bf16[64,256]{1,0:T(8,128)(2,1)S(1)}, u32[]{:S(2)}, u32[]{:S(2)}) collective-permute-start(bf16[64,256]{1,0:T(8,128)(2,1)S(1)} %add_convert_fusion), channel_id=1, source_target_pairs={{0,12},{2,14},{4,0},{6,2},{8,4},{10,6},{12,8},{14,10},{1,13},{3,15... | collective-permute-start | bytes 98312 | tf_op jit(solution)/shard_map/ppermute | solution.py:282
  117.8 7.0 %last_kept.1.kept = f32[256,512]{1,0:T(8,128)} custom-call(s32[18]{0:T(128)} %dynamic-slice_bitcast_fusion.scalars, f32[256,512]{1,0:T(8,128)} %last_sent.1.refs_0_, bf16[32,3584]{1,0:T(8,128)(2,1)} %copy-done.1, bf16[32,3584]{1,0:T(8,128)(2,1)} %copy-done.3, bf16[32,3584]{1,0:T(8,128)(2,1)} %copy-done.6, ...), custom_call_target="tpu_custom_call" | custom-call | flops 3758096384 | bytes 12058624 | tf_op jit(solution)/shard_map/last_kept/pallas_call | solution.py:158
  126.7 2.9 %expand_and_add.1 = bf16[256,512]{1,0:T(8,128)(2,1)} custom-call(bf16[64,256]{1,0:T(8,128)(2,1)} %add_add_fusion.shrunk, s32[256,1]{1,0:T(8,128)} %copy.10.slot, bf16[1024,512]{1,0:T(8,128)(2,1)} %bitcast.13, f32[256,512]{1,0:T(8,128)} %last_kept.1.kept, f32[256,512]{1,0:T(8,128)} %copy-done.15), custom_call_target="tpu_custom_call" | custom-call | flops 268435456 | bytes 2359296 | tf_op jit(solution)/shard_map/expand_and_add/pallas_call | solution.py:199
  (107 shorter events, 19.9 us)
Async XLA Ops:
  1.3 22.2 %collective-permute-start.25 = (bf16[32,3584]{1,0:T(8,128)(2,1)S(1)}, bf16[32,3584]{1,0:T(8,128)(2,1)}, u32[]{:S(2)}, u32[]{:S(2)}) collective-permute-start(bf16[32,3584]{1,0:T(8,128)(2,1)S(1)} %get-tuple-element.21.refs_0_), channel_id=1, source_target_pairs={{0,2},{4,0},{8,4},{12,8},{14,12},{10,14},{6,10},{2,6},{1,3},{5,1},... | collective-permute-start | bytes 688136 | tf_op jit(solution)/shard_map/ppermute | solution.py:253
  4.3 19.4 %collective-permute-start.21 = (bf16[32,3584]{1,0:T(8,128)(2,1)S(1)}, bf16[32,3584]{1,0:T(8,128)(2,1)}, u32[]{:S(2)}, u32[]{:S(2)}) collective-permute-start(bf16[32,3584]{1,0:T(8,128)(2,1)S(1)} %get-tuple-element.21.refs_0_), channel_id=1, source_target_pairs={{0,4},{4,8},{8,12},{12,14},{14,10},{10,6},{6,2},{2,0},{1,5},{5,9},... | collective-permute-start | bytes 688136 | tf_op jit(solution)/shard_map/ppermute | solution.py:253
  4.4 21.2 %collective-permute-start.17 = (bf16[32,3584]{1,0:T(8,128)(2,1)S(1)}, bf16[32,3584]{1,0:T(8,128)(2,1)S(1)}, u32[]{:S(2)}, u32[]{:S(2)}) collective-permute-start(bf16[32,3584]{1,0:T(8,128)(2,1)S(1)} %get-tuple-element.23.refs_0_), channel_id=1, source_target_pairs={{0,2},{4,0},{8,4},{12,8},{14,12},{10,14},{6,10},{2,6},{1,3},{5,1},... | collective-permute-start | bytes 688136 | tf_op jit(solution)/shard_map/ppermute | solution.py:253
  6.3 19.4 %collective-permute-start.14 = (bf16[32,3584]{1,0:T(8,128)(2,1)S(1)}, bf16[32,3584]{1,0:T(8,128)(2,1)S(1)}, u32[]{:S(2)}, u32[]{:S(2)}) collective-permute-start(bf16[32,3584]{1,0:T(8,128)(2,1)S(1)} %get-tuple-element.23.refs_0_), channel_id=1, source_target_pairs={{0,4},{4,8},{8,12},{12,14},{14,10},{10,6},{6,2},{2,0},{1,5},{5,9},... | collective-permute-start | bytes 688136 | tf_op jit(solution)/shard_map/ppermute | solution.py:253
  6.4 21.2 %collective-permute-start.4 = (bf16[32,3584]{1,0:T(8,128)(2,1)S(1)}, bf16[32,3584]{1,0:T(8,128)(2,1)S(1)}, u32[]{:S(2)}, u32[]{:S(2)}) collective-permute-start(bf16[32,3584]{1,0:T(8,128)(2,1)S(1)} %get-tuple-element.22.refs_0_.refs_1_), channel_id=1, source_target_pairs={{0,2},{4,0},{8,4},{12,8},{14,12},{10,14},{6,10},{2,6},{1,3},{5,1},... | collective-permute-start | bytes 688136 | tf_op jit(solution)/shard_map/ppermute | solution.py:253
  23.7 10.0 %collective-permute-start.10 = (bf16[32,3584]{1,0:T(8,128)(2,1)}, bf16[32,3584]{1,0:T(8,128)(2,1)S(1)}, u32[]{:S(2)}, u32[]{:S(2)}) collective-permute-start(bf16[32,3584]{1,0:T(8,128)(2,1)} %take_10752.1.refs_8_.refs_9_), channel_id=1, source_target_pairs={{0,2},{4,0},{8,4},{12,8},{14,12},{10,14},{6,10},{2,6},{1,3},{5,1},... | collective-permute-start | bytes 688136 | tf_op jit(solution)/shard_map/ppermute | solution.py:253
  25.6 11.4 %collective-permute-start.7 = (bf16[32,3584]{1,0:T(8,128)(2,1)}, bf16[32,3584]{1,0:T(8,128)(2,1)S(1)}, u32[]{:S(2)}, u32[]{:S(2)}) collective-permute-start(bf16[32,3584]{1,0:T(8,128)(2,1)} %take_10752.1.refs_8_.refs_9_), channel_id=1, source_target_pairs={{0,4},{4,8},{8,12},{12,14},{14,10},{10,6},{6,2},{2,0},{1,5},{5,9},... | collective-permute-start | bytes 688136 | tf_op jit(solution)/shard_map/ppermute | solution.py:253
  25.7 12.9 %collective-permute-start.26 = (bf16[32,3584]{1,0:T(8,128)(2,1)}, bf16[32,3584]{1,0:T(8,128)(2,1)S(1)}, u32[]{:S(2)}, u32[]{:S(2)}) collective-permute-start(bf16[32,3584]{1,0:T(8,128)(2,1)} %collective-permute-done.25.refs_5_), channel_id=1, source_target_pairs={{0,2},{4,0},{8,4},{12,8},{14,12},{10,14},{6,10},{2,6},{1,3},{5,1},... | collective-permute-start | bytes 688136 | tf_op jit(solution)/shard_map/ppermute | solution.py:253
  27.6 14.3 %collective-permute-start.22 = (bf16[32,3584]{1,0:T(8,128)(2,1)}, bf16[32,3584]{1,0:T(8,128)(2,1)S(1)}, u32[]{:S(2)}, u32[]{:S(2)}) collective-permute-start(bf16[32,3584]{1,0:T(8,128)(2,1)} %collective-permute-done.21.refs_1_), channel_id=1, source_target_pairs={{0,4},{4,8},{8,12},{12,14},{14,10},{10,6},{6,2},{2,0},{1,5},{5,9},... | collective-permute-start | bytes 688136 | tf_op jit(solution)/shard_map/ppermute | solution.py:253
  32.1 11.4 %collective-permute-start.18 = (bf16[32,3584]{1,0:T(8,128)(2,1)S(1)}, bf16[32,3584]{1,0:T(8,128)(2,1)S(1)}, u32[]{:S(2)}, u32[]{:S(2)}) collective-permute-start(bf16[32,3584]{1,0:T(8,128)(2,1)S(1)} %collective-permute-done.17.refs_4_), channel_id=1, source_target_pairs={{0,2},{4,0},{8,4},{12,8},{14,12},{10,14},{6,10},{2,6},{1,3},{5,1},... | collective-permute-start | bytes 688136 | tf_op jit(solution)/shard_map/ppermute | solution.py:253
  33.7 13.2 %collective-permute-start.15 = (bf16[32,3584]{1,0:T(8,128)(2,1)S(1)}, bf16[32,3584]{1,0:T(8,128)(2,1)S(1)}, u32[]{:S(2)}, u32[]{:S(2)}) collective-permute-start(bf16[32,3584]{1,0:T(8,128)(2,1)S(1)} %collective-permute-done.14.refs_1_), channel_id=1, source_target_pairs={{0,4},{4,8},{8,12},{12,14},{14,10},{10,6},{6,2},{2,0},{1,5},{5,9},... | collective-permute-start | bytes 688136 | tf_op jit(solution)/shard_map/ppermute | solution.py:253
  37.0 11.4 %collective-permute-start.5 = (bf16[32,3584]{1,0:T(8,128)(2,1)S(1)}, bf16[32,3584]{1,0:T(8,128)(2,1)}, u32[]{:S(2)}, u32[]{:S(2)}) collective-permute-start(bf16[32,3584]{1,0:T(8,128)(2,1)S(1)} %collective-permute-done.4.refs_5_.refs_6_), channel_id=1, source_target_pairs={{0,2},{4,0},{8,4},{12,8},{14,12},{10,14},{6,10},{2,6},{1,3},{5,1},... | collective-permute-start | bytes 688136 | tf_op jit(solution)/shard_map/ppermute | solution.py:253
  38.6 13.2 %collective-permute-start.1 = (bf16[32,3584]{1,0:T(8,128)(2,1)S(1)}, bf16[32,3584]{1,0:T(8,128)(2,1)S(1)}, u32[]{:S(2)}, u32[]{:S(2)}) collective-permute-start(bf16[32,3584]{1,0:T(8,128)(2,1)S(1)} %collective-permute-done.refs_1_.refs_2_), channel_id=1, source_target_pairs={{0,4},{4,8},{8,12},{12,14},{14,10},{10,6},{6,2},{2,0},{1,5},{5,9},... | collective-permute-start | bytes 688136 | tf_op jit(solution)/shard_map/ppermute | solution.py:253
  41.9 11.4 %collective-permute-start.11 = (bf16[32,3584]{1,0:T(8,128)(2,1)S(1)}, bf16[32,3584]{1,0:T(8,128)(2,1)S(1)}, u32[]{:S(2)}, u32[]{:S(2)}) collective-permute-start(bf16[32,3584]{1,0:T(8,128)(2,1)S(1)} %collective-permute-done.10.refs_12_.refs_13_), channel_id=1, source_target_pairs={{0,2},{4,0},{8,4},{12,8},{14,12},{10,14},{6,10},{2,6},{1,3},{5,1},... | collective-permute-start | bytes 688136 | tf_op jit(solution)/shard_map/ppermute | solution.py:253
  43.5 13.3 %collective-permute-start.8 = (bf16[32,3584]{1,0:T(8,128)(2,1)S(1)}, bf16[32,3584]{1,0:T(8,128)(2,1)}, u32[]{:S(2)}, u32[]{:S(2)}) collective-permute-start(bf16[32,3584]{1,0:T(8,128)(2,1)S(1)} %collective-permute-done.7.refs_9_.refs_10_), channel_id=1, source_target_pairs={{0,4},{4,8},{8,12},{12,14},{14,10},{10,6},{6,2},{2,0},{1,5},{5,9},... | collective-permute-start | bytes 688136 | tf_op jit(solution)/shard_map/ppermute | solution.py:253
  46.9 10.2 %collective-permute-start.27 = (bf16[32,3584]{1,0:T(8,128)(2,1)S(1)}, bf16[32,3584]{1,0:T(8,128)(2,1)S(1)}, u32[]{:S(2)}, u32[]{:S(2)}) collective-permute-start(bf16[32,3584]{1,0:T(8,128)(2,1)S(1)} %collective-permute-done.26.refs_6_), channel_id=1, source_target_pairs={{0,2},{4,0},{8,4},{12,8},{14,12},{10,14},{6,10},{2,6},{1,3},{5,1},... | collective-permute-start | bytes 688136 | tf_op jit(solution)/shard_map/ppermute | solution.py:253
  48.4 13.3 %collective-permute-start.23 = (bf16[32,3584]{1,0:T(8,128)(2,1)S(1)}, bf16[32,3584]{1,0:T(8,128)(2,1)}, u32[]{:S(2)}, u32[]{:S(2)}) collective-permute-start(bf16[32,3584]{1,0:T(8,128)(2,1)S(1)} %collective-permute-done.22.refs_2_), channel_id=1, source_target_pairs={{0,4},{4,8},{8,12},{12,14},{14,10},{10,6},{6,2},{2,0},{1,5},{5,9},... | collective-permute-start | bytes 688136 | tf_op jit(solution)/shard_map/ppermute | solution.py:253
  51.8 10.3 %collective-permute-start.19 = (bf16[32,3584]{1,0:T(8,128)(2,1)S(1)}, bf16[32,3584]{1,0:T(8,128)(2,1)}, u32[]{:S(2)}, u32[]{:S(2)}) collective-permute-start(bf16[32,3584]{1,0:T(8,128)(2,1)S(1)} %collective-permute-done.18.refs_5_), channel_id=1, source_target_pairs={{0,2},{4,0},{8,4},{12,8},{14,12},{10,14},{6,10},{2,6},{1,3},{5,1},... | collective-permute-start | bytes 688136 | tf_op jit(solution)/shard_map/ppermute | solution.py:253
  53.4 13.1 %collective-permute-start.16 = (bf16[32,3584]{1,0:T(8,128)(2,1)S(1)}, bf16[32,3584]{1,0:T(8,128)(2,1)S(1)}, u32[]{:S(2)}, u32[]{:S(2)}) collective-permute-start(bf16[32,3584]{1,0:T(8,128)(2,1)S(1)} %collective-permute-done.15.refs_2_), channel_id=1, source_target_pairs={{0,4},{4,8},{8,12},{12,14},{14,10},{10,6},{6,2},{2,0},{1,5},{5,9},... | collective-permute-start | bytes 688136 | tf_op jit(solution)/shard_map/ppermute | solution.py:253
  56.8 14.7 %collective-permute-start.2 = (bf16[32,3584]{1,0:T(8,128)(2,1)S(1)}, bf16[32,3584]{1,0:T(8,128)(2,1)}, u32[]{:S(2)}, u32[]{:S(2)}) collective-permute-start(bf16[32,3584]{1,0:T(8,128)(2,1)S(1)} %collective-permute-done.1.refs_2_.refs_3_), channel_id=1, source_target_pairs={{0,4},{4,8},{8,12},{12,14},{14,10},{10,6},{6,2},{2,0},{1,5},{5,9},... | collective-permute-start | bytes 688136 | tf_op jit(solution)/shard_map/ppermute | solution.py:253
  57.0 14.6 %collective-permute-start.12 = (bf16[32,3584]{1,0:T(8,128)(2,1)S(1)}, bf16[32,3584]{1,0:T(8,128)(2,1)}, u32[]{:S(2)}, u32[]{:S(2)}) collective-permute-start(bf16[32,3584]{1,0:T(8,128)(2,1)S(1)} %collective-permute-done.11.refs_13_.refs_14_), channel_id=1, source_target_pairs={{0,2},{4,0},{8,4},{12,8},{14,12},{10,14},{6,10},{2,6},{1,3},{5,1},... | collective-permute-start | bytes 688136 | tf_op jit(solution)/shard_map/ppermute | solution.py:253
  61.7 14.6 %collective-permute-start.24 = (bf16[32,3584]{1,0:T(8,128)(2,1)}, bf16[32,3584]{1,0:T(8,128)(2,1)S(1)}, u32[]{:S(2)}, u32[]{:S(2)}) collective-permute-start(bf16[32,3584]{1,0:T(8,128)(2,1)} %collective-permute-done.23.refs_3_), channel_id=1, source_target_pairs={{0,4},{4,8},{8,12},{12,14},{14,10},{10,6},{6,2},{2,0},{1,5},{5,9},... | collective-permute-start | bytes 688136 | tf_op jit(solution)/shard_map/ppermute | solution.py:253
  62.0 15.9 %collective-permute-start.20 = (bf16[32,3584]{1,0:T(8,128)(2,1)}, bf16[32,3584]{1,0:T(8,128)(2,1)S(1)}, u32[]{:S(2)}, u32[]{:S(2)}) collective-permute-start(bf16[32,3584]{1,0:T(8,128)(2,1)} %collective-permute-done.19.refs_6_), channel_id=1, source_target_pairs={{0,2},{4,0},{8,4},{12,8},{14,12},{10,14},{6,10},{2,6},{1,3},{5,1},... | collective-permute-start | bytes 688136 | tf_op jit(solution)/shard_map/ppermute | solution.py:253
  66.5 30.1 %collective-permute-start.6 = (bf16[32,3584]{1,0:T(8,128)(2,1)}, bf16[32,3584]{1,0:T(8,128)(2,1)}, u32[]{:S(2)}, u32[]{:S(2)}) collective-permute-start(bf16[32,3584]{1,0:T(8,128)(2,1)} %collective-permute-done.5.refs_6_.refs_7_), channel_id=1, source_target_pairs={{0,2},{4,0},{8,4},{12,8},{14,12},{10,14},{6,10},{2,6},{1,3},{5,1},... | collective-permute-start | bytes 688136 | tf_op jit(solution)/shard_map/ppermute | solution.py:253
  71.5 25.1 %collective-permute-start.9 = (bf16[32,3584]{1,0:T(8,128)(2,1)}, bf16[32,3584]{1,0:T(8,128)(2,1)}, u32[]{:S(2)}, u32[]{:S(2)}) collective-permute-start(bf16[32,3584]{1,0:T(8,128)(2,1)} %collective-permute-done.8.refs_10_.refs_11_), channel_id=1, source_target_pairs={{0,4},{4,8},{8,12},{12,14},{14,10},{10,6},{6,2},{2,0},{1,5},{5,9},... | collective-permute-start | bytes 688136 | tf_op jit(solution)/shard_map/ppermute | solution.py:253
  71.7 25.0 %collective-permute-start.3 = (bf16[32,3584]{1,0:T(8,128)(2,1)}, bf16[32,3584]{1,0:T(8,128)(2,1)}, u32[]{:S(2)}, u32[]{:S(2)}) collective-permute-start(bf16[32,3584]{1,0:T(8,128)(2,1)} %collective-permute-done.2.refs_3_.refs_4_), channel_id=1, source_target_pairs={{0,4},{4,8},{8,12},{12,14},{14,10},{10,6},{6,2},{2,0},{1,5},{5,9},... | collective-permute-start | bytes 688136 | tf_op jit(solution)/shard_map/ppermute | solution.py:253
  76.3 20.3 %collective-permute-start.13 = (bf16[32,3584]{1,0:T(8,128)(2,1)}, bf16[32,3584]{1,0:T(8,128)(2,1)}, u32[]{:S(2)}, u32[]{:S(2)}) collective-permute-start(bf16[32,3584]{1,0:T(8,128)(2,1)} %collective-permute-done.12.refs_14_.refs_15_), channel_id=1, source_target_pairs={{0,2},{4,0},{8,4},{12,8},{14,12},{10,14},{6,10},{2,6},{1,3},{5,1},... | collective-permute-start | bytes 688136 | tf_op jit(solution)/shard_map/ppermute | solution.py:253
  78.6 46.9 %all-to-all-start = ((bf16[8,128,512]{2,1,0:T(8,128)(2,1)}), bf16[8,128,512]{2,1,0:T(8,128)(2,1)S(1)}, u32[]{:S(2)}, u32[]{:S(2)}) async-start(bf16[8,128,512]{2,1,0:T(8,128)(2,1)} %tie.1), calls=%async_computation | async-start | bytes 2097152 | tf_op jit(solution)/shard_map/all_to_all | solution.py:257
  103.4 9.9 %collective-permute-start.30 = (f32[64,256]{1,0:T(8,128)S(1)}, f32[64,256]{1,0:T(8,128)S(1)}, u32[]{:S(2)}, u32[]{:S(2)}) collective-permute-start(f32[64,256]{1,0:T(8,128)S(1)} %fusion.refs_0_), channel_id=1, source_target_pairs={{0,3},{1,2},{2,1},{3,0},{4,7},{5,6},{6,5},{7,4},{8,11},{9,10},{10,... | collective-permute-start | bytes 196616 | tf_op jit(solution)/shard_map/ppermute | solution.py:278
  103.5 9.8 %collective-permute-start.29 = (f32[64,256]{1,0:T(8,128)S(1)}, f32[64,256]{1,0:T(8,128)S(1)}, u32[]{:S(2)}, u32[]{:S(2)}) collective-permute-start(f32[64,256]{1,0:T(8,128)S(1)} %fusion.refs_0_), channel_id=1, source_target_pairs={{0,2},{1,3},{2,0},{3,1},{4,6},{5,7},{6,4},{7,5},{8,10},{9,11},{10,... | collective-permute-start | bytes 196616 | tf_op jit(solution)/shard_map/ppermute | solution.py:278
  112.8 12.7 %collective-permute-start.34 = (f32[256,512]{1,0:T(8,128)}, f32[256,512]{1,0:T(8,128)S(1)}, u32[]{:S(2)}, u32[]{:S(2)}) collective-permute-start(f32[256,512]{1,0:T(8,128)} %last_sent.1.refs_0_), channel_id=1, source_target_pairs={{0,1},{1,0},{2,3},{3,2},{4,5},{5,4},{6,7},{7,6},{8,9},{9,8},{10,11... | collective-permute-start | bytes 1572872 | tf_op jit(solution)/shard_map/ppermute | solution.py:283
  113.4 11.5 %collective-permute-start.33 = (bf16[64,256]{1,0:T(8,128)(2,1)S(1)}, bf16[64,256]{1,0:T(8,128)(2,1)S(1)}, u32[]{:S(2)}, u32[]{:S(2)}) collective-permute-start(bf16[64,256]{1,0:T(8,128)(2,1)S(1)} %add_convert_fusion), channel_id=1, source_target_pairs={{0,12},{2,14},{4,0},{6,2},{8,4},{10,6},{12,8},{14,10},{1,13},{3,15... | collective-permute-start | bytes 98312 | tf_op jit(solution)/shard_map/ppermute | solution.py:282
  (29 other events, 803.7 us)

commit v8 on v7

--- a/solution.py
+++ b/solution.py
@@ -9,8 +9,7 @@
 from jax.sharding import PartitionSpec as P
 
 F32, BF16 = jnp.float32, jnp.bfloat16
-TILE = 1024
-CHUNKS = 4
+TILE = 2048
 MIB = 2**20
 MATMUL_MIB = 62
 
@@ -21,27 +20,6 @@
 
 def ring_order(n):
     return list(range(0, n, 2)) + list(range(1, n, 2))[::-1]
-
-
-def take_kernel(start, width, src, *refs):
-    *_, dst, sem = refs
-    copy = pltpu.make_async_copy(src.at[:, pl.ds(start, width)], dst, sem)
-    copy.start()
-    copy.wait()
-
-
-def take(hidden, start, width, after):
-    rows = hidden.shape[0]
-    return pl.pallas_call(
-        functools.partial(take_kernel, start, width),
-        in_specs=[pl.BlockSpec(memory_space=pl.ANY)] * (1 + len(after)),
-        out_specs=pl.BlockSpec(memory_space=pl.ANY),
-        scratch_shapes=[pltpu.SemaphoreType.DMA],
-        out_shape=jax.ShapeDtypeStruct((rows, width), BF16),
-        compiler_params=params(MATMUL_MIB),
-        cost_estimate=pl.CostEstimate(flops=0, bytes_accessed=4 * rows * width, transcendentals=0),
-        name=f"take_{start}",
-    )(hidden, *after)
 
 
 def split_kernel(scalars, src, dst, mark):
@@ -79,12 +57,12 @@
         out_specs=pl.BlockSpec(memory_space=pl.ANY),
         out_shape=jax.ShapeDtypeStruct(array.shape, array.dtype),
         input_output_aliases={0: 0},
-        compiler_params=params(MATMUL_MIB),
+        compiler_params=params(1),
         name="tie",
     )(array, *after)
 
 
-def matmul_kernel(n, waits, spans, half, sides, narrow, has_acc, scalars, *refs):
+def matmul_kernel(n, waits, spans, half, sides, narrow, has_acc, token, scalars, *refs):
     refs = list(refs)[waits:]
     pieces = [[refs.pop(0) for _ in range(n)] for _ in spans]
     down = refs.pop(0)
@@ -92,6 +70,8 @@
     outs = len(sides) + narrow
     before = [refs.pop(0) for _ in range(outs)] if has_acc else []
     acc = [refs.pop(0) for _ in range(outs)]
+    if token:
+        refs.pop(0)[...] = jnp.zeros((8, 128), F32)
     tiles = [(part, at, tile) for part, (_, _, cuts) in enumerate(spans) for at, tile in cuts]
     lefts = [refs.pop(0) for _ in tiles]
     weights = [[refs.pop(0) for _ in tiles] for _ in sides]
@@ -136,39 +116,39 @@
         acc[i][...] += earlier[i][...]
 
 
-def cuts_of(width):
-    first = width % TILE or TILE
-    sizes = [first // 2] * 2 if first == TILE else [first]
-    sizes += [TILE] * ((width - first) // TILE)
+def cuts_of(width, most):
+    count = -(-width // most)
+    sizes = [width - most * (count - 1)] + [most] * (count - 1)
     return [(sum(sizes[:i]), size) for i, size in enumerate(sizes)]
 
 
-def chunk_matmul(scalars, half, chunks, down, shrink, acc, sides, narrow, label, after=()):
+def chunk_matmul(scalars, half, chunks, down, shrink, acc, sides, narrow, label, after=(), token=False):
     n = len(chunks[0][0])
     rows = chunks[0][0][0].shape[0] * n
     share = down.shape[1] // 2
     ranks = shrink.shape[0]
-    spans = [(base, start, cuts_of(pieces[0].shape[1])) for pieces, base, start in chunks]
+    spans = [(base, start, cuts_of(pieces[0].shape[1], TILE if sides else 2 * TILE)) for pieces, base, start in chunks]
     sizes = [tile for _, _, cuts in spans for _, tile in cuts]
     width = sum(sizes)
     anywhere = pl.BlockSpec(memory_space=pl.ANY)
     args = [*after, *(piece for pieces, _, _ in chunks for piece in pieces), down, shrink, *(acc or ())]
     shapes = [(rows, share)] * len(sides) + [(ranks, rows)] * narrow
+    marks = [(8, 128)] * token
     columns = share * len(sides) + ranks * narrow
     return pl.pallas_call(
-        functools.partial(matmul_kernel, n, len(after), spans, half, sides, narrow, acc is not None),
+        functools.partial(matmul_kernel, n, len(after), spans, half, sides, narrow, acc is not None, token),
         grid_spec=pltpu.PrefetchScalarGridSpec(
             num_scalar_prefetch=1,
             grid=(),
             in_specs=[anywhere] * len(args),
-            out_specs=[pl.BlockSpec(memory_space=pltpu.VMEM)] * len(shapes),
+            out_specs=[pl.BlockSpec(memory_space=pltpu.VMEM)] * len(shapes + marks),
             scratch_shapes=[pltpu.VMEM((rows, tile), BF16) for tile in sizes]
             + [pltpu.VMEM((tile, share), BF16) for _ in sides for tile in sizes]
             + [pltpu.VMEM((ranks, tile), BF16) for tile in sizes if narrow]
             + [pltpu.VMEM(shape, F32) for shape in shapes if acc is not None]
             + [pltpu.SemaphoreType.DMA((len(sizes), n + 3)), pltpu.SemaphoreType.DMA((3,))],
         ),
-        out_shape=[jax.ShapeDtypeStruct(shape, F32) for shape in shapes],
+        out_shape=[jax.ShapeDtypeStruct(shape, F32) for shape in shapes + marks],
         compiler_params=params(MATMUL_MIB),
         cost_estimate=pl.CostEstimate(
             flops=4 * rows * width * columns,
@@ -239,28 +219,34 @@
         slots = jnp.arange(adapter_slot.shape[0], dtype=jnp.int32)
         row_slot = jnp.sum(jnp.where(row_adapter[None, :] == slots[:, None], adapter_slot[:, None], 0), axis=0)
 
-        width = units // CHUNKS
-        blocks, mark = expand_blocks(scalars, half, expand, n, cores)
-        chunks, ends = [], []
-        for chunk in range(CHUNKS):
-            start = chunk * width
-            own = take(hidden, start, width, [mark]) if chunk == CHUNKS - 1 else hidden[:, start:start + width]
+        small = 3 * units // 14
+        widths = [small, units // 2 - small, units // 2 - small, small]
+        starts = [sum(widths[:chunk]) for chunk in range(4)]
+
+        def ring(chunk, own, held=None):
             way = chunk % 2
             pieces = [own]
-            for length, pairs in zip(((long, short), (short, long))[way], (clockwise, counter)):
+            for turn, length in enumerate(((long, short), (short, long))[way]):
                 moving = own
-                for step in range(length):
-                    moving = lax.ppermute(moving, "store", pairs)
+                for step in range(1, length + 1):
+                    moving = lax.ppermute(moving, "store", (clockwise, counter)[turn])
+                    if held and turn == 0 and step == held[0]:
+                        moving = tie(moving, held[1:])
                     pieces.append(moving)
-                ends.append(moving)
-            chunks.append((pieces, way * n, start))
-        factors = lax.all_to_all(tie(blocks, ends[:4]), "store", 0, 0)
+            ends = [pieces[((long, short), (short, long))[way][0]], pieces[-1]]
+            return (pieces, way * n, starts[chunk]), ends
 
         call = functools.partial(chunk_matmul, scalars, half)
-        acc = None
-        for chunk in range(CHUNKS - 2):
-            acc = call(chunks[chunk:chunk + 1], down, shrink_rows, acc, (0, 1), True, f"chunk_{chunk}")
-        last = chunks[CHUNKS - 2:]
+        own = [hidden[:, at:at + width] for at, width in zip(starts, widths)]
+        blocks, mark = expand_blocks(scalars, half, expand, n, cores)
+        chunk_0, ends_0 = ring(0, own[0], (2, mark))
+        chunk_1, ends_1 = ring(1, own[1])
+        *acc, token = call([chunk_0], down, shrink_rows, None, (0, 1), True, "chunk_0", token=True)
+        chunk_2, ends_2 = ring(2, tie(own[2], ends_0), (1, token))
+        *acc, token = call([chunk_1], down, shrink_rows, acc, (0, 1), True, "chunk_1", token=True)
+        chunk_3, ends_3 = ring(3, tie(own[3], ends_1), (1, token))
+        factors = lax.all_to_all(tie(blocks, ends_2), "store", 0, 0)
+        last = [chunk_2, chunk_3]
         narrow, = call(last, down, shrink_rows, acc[2:], (), True, "last_narrow")
         mine = [
             jnp.where((row_slot == store * owned + i)[None, :], narrow[i * rank:(i + 1) * rank], 0.0)

time: 130 us -> 146 us (1.12)
  waiting for transfers between devices: 28.4 us -> 41 us
  starting transfers between devices: 43.2 us -> 50.3 us
  Pallas kernels: 51 us -> 44 us
  local copies, waits for them, and re-layouts: 5.16 us -> 7.83 us
    ppermute x28, waiting for transfers between devices: 28.4 us -> 41 us  [ring(): moving = lax.ppermute(moving, 'store', (clockwise, counter)[turn])]
    pallas_call x1 -> x0, Pallas kernels: 8.06 us -> none  [take(): pl.pallas_call(functools.partial(take_kernel, start, width), in_specs=[pl...]
    ppermute x3, starting transfers between devices: 4.46 us -> 10.9 us  [shards(): lax.ppermute(column, 'store', [(s, (s + ds) % n) for s in range(n)])]
    all_to_all x1, starting transfers between devices: 3.87 us -> 6.47 us  [shards(): factors = lax.all_to_all(tie(blocks, ends_2), 'store', 0, 0)]
    ppermute x28, starting transfers between devices: 32.2 us -> 30.2 us  [ring(): moving = lax.ppermute(moving, 'store', (clockwise, counter)[turn])]
    unnamed x50 -> x66, local copies, waits for them, and re-layouts: 1.9 us -> 3.65 us
  transfers between devices with their start and end apart: 36 -> 36, of which waited for: 12 -> 9; matrix products, arithmetic and copies ran while one was open for 3% -> 3% of each run, Pallas kernels for 37% -> 28%
where the time goes in v8:
time: 146 us; the launch traced here: 145 us
  starting transfers between devices  50.3 us (34%)
  Pallas kernels  44 us (30%)
  waiting for transfers between devices  41 us (28%)
  local copies, waits for them, and re-layouts  7.83 us (5%)
  other arithmetic  1.62 us (1%)
    ppermute x28, waiting for transfers between devices, ring(): moving = lax.ppermute(moving, 'store', (clockwise, counter)[turn])  41 us
    pallas_call x5, Pallas kernels, chunk_matmul(): pl.pallas_call(functools.partial(matmul_kernel, n, len(after), spans, hal...  35.2 us
    ppermute x28, starting transfers between devices, ring(): moving = lax.ppermute(moving, 'store', (clockwise, counter)[turn])  30.2 us
    ppermute x3, starting transfers between devices, shards(): lax.ppermute(column, 'store', [(s, (s + ds) % n) for s in range(n)])  10.9 us
    all_to_all x1, starting transfers between devices, shards(): factors = lax.all_to_all(tie(blocks, ends_2), 'store', 0, 0)  6.47 us
    pallas_call x1, Pallas kernels, expand_blocks(): pl.pallas_call(split_kernel, grid_spec=pltpu.PrefetchScalarGridSpec(num_s...  5.86 us
    unnamed x66, local copies, waits for them, and re-layouts  3.65 us
    pallas_call x1, Pallas kernels, final(): pl.pallas_call(functools.partial(final_kernel, n, owned), in_specs=[pl.Bl...  2.94 us
  transfers between devices with their start and end apart: 36, of which 9 were waited for; matrix products, arithmetic and copies ran while one was open for 3% of the time, Pallas kernels for 28%

profile of v8, /device:TPU:0, one launch (start us, length us, event | category | flops | bytes accessed | tf_op | source)
XLA Modules:
  0.0 145.1 jit_solution(16160723359183317142)
XLA Ops:
  1.1 3.1 %collective-permute-start = (bf16[32,3072]{1,0:T(8,128)(2,1)S(1)}, bf16[32,3072]{1,0:T(8,128)(2,1)S(1)}, u32[]{:S(2)}, u32[]{:S(2)}) collective-permute-start(bf16[32,3072]{1,0:T(8,128)(2,1)S(1)} %get-tuple-element.28.refs_0_), channel_id=1, source_target_pairs={{0,4},{4,8},{8,12},{12,14},{14,10},{10,6},{6,2},{2,0},{1,5},{5,9},... | collective-permute-start | bytes 589832 | tf_op jit(solution)/shard_map/ppermute | solution.py:232
  4.1 4.8 %collective-permute-done.refs_1_ = bf16[32,3072]{1,0:T(8,128)(2,1)S(1)} collective-permute-done((bf16[32,3072]{1,0:T(8,128)(2,1)S(1)}, bf16[32,3072]{1,0:T(8,128)(2,1)S(1)}, u32[]{:S(2)}, u32[]{:S(2)}) %collective-permute-start) | collective-permute-done | bytes 196640 | tf_op jit(solution)/shard_map/ppermute | solution.py:232
  9.0 1.8 %collective-permute-start.1 = (bf16[32,3072]{1,0:T(8,128)(2,1)S(1)}, bf16[32,3072]{1,0:T(8,128)(2,1)S(1)}, u32[]{:S(2)}, u32[]{:S(2)}) collective-permute-start(bf16[32,3072]{1,0:T(8,128)(2,1)S(1)} %collective-permute-done.refs_1_), channel_id=1, source_target_pairs={{0,4},{4,8},{8,12},{12,14},{14,10},{10,6},{6,2},{2,0},{1,5},{5,9},... | collective-permute-start | bytes 589832 | tf_op jit(solution)/shard_map/ppermute | solution.py:232
  13.4 5.9 %expand_blocks.1 = (bf16[8,128,512]{2,1,0:T(8,128)(2,1)}, f32[8,128]{1,0:T(8,128)}) custom-call(s32[18]{0:T(128)} %dynamic-slice_bitcast_fusion.scalars, bf16[128,8192]{1,0:T(8,128)(2,1)} %bitcast.13), custom_call_target="tpu_custom_call" | custom-call | bytes 2097152 | tf_op jit(solution)/shard_map/expand_blocks/pallas_call | solution.py:34
  19.3 1.8 %collective-permute-start.5 = (bf16[32,3072]{1,0:T(8,128)(2,1)S(1)}, bf16[32,3072]{1,0:T(8,128)(2,1)S(1)}, u32[]{:S(2)}, u32[]{:S(2)}) collective-permute-start(bf16[32,3072]{1,0:T(8,128)(2,1)S(1)} %collective-permute-done.4.refs_5_), channel_id=1, source_target_pairs={{0,2},{4,0},{8,4},{12,8},{14,12},{10,14},{6,10},{2,6},{1,3},{5,1},... | collective-permute-start | bytes 589832 | tf_op jit(solution)/shard_map/ppermute | solution.py:232
  22.0 1.8 %collective-permute-start.14 = (bf16[32,4096]{1,0:T(8,128)(2,1)S(1)}, bf16[32,4096]{1,0:T(8,128)(2,1)S(1)}, u32[]{:S(2)}, u32[]{:S(2)}) collective-permute-start(bf16[32,4096]{1,0:T(8,128)(2,1)S(1)} %get-tuple-element.25.refs_0_), channel_id=1, source_target_pairs={{0,4},{4,8},{8,12},{12,14},{14,10},{10,6},{6,2},{2,0},{1,5},{5,9},... | collective-permute-start | bytes 786440 | tf_op jit(solution)/shard_map/ppermute | solution.py:232
  24.0 2.3 %collective-permute-done.5.refs_6_ = bf16[32,3072]{1,0:T(8,128)(2,1)S(1)} collective-permute-done((bf16[32,3072]{1,0:T(8,128)(2,1)S(1)}, bf16[32,3072]{1,0:T(8,128)(2,1)S(1)}, u32[]{:S(2)}, u32[]{:S(2)}) %collective-permute-start.5) | collective-permute-done | bytes 196640 | tf_op jit(solution)/shard_map/ppermute | solution.py:232
  26.3 2.5 %collective-permute-start.6 = (bf16[32,3072]{1,0:T(8,128)(2,1)S(1)}, bf16[32,3072]{1,0:T(8,128)(2,1)S(1)}, u32[]{:S(2)}, u32[]{:S(2)}) collective-permute-start(bf16[32,3072]{1,0:T(8,128)(2,1)S(1)} %collective-permute-done.5.refs_6_), channel_id=1, source_target_pairs={{0,2},{4,0},{8,4},{12,8},{14,12},{10,14},{6,10},{2,6},{1,3},{5,1},... | collective-permute-start | bytes 589832 | tf_op jit(solution)/shard_map/ppermute | solution.py:232
  29.8 5.3 %collective-permute-done.14.refs_1_ = bf16[32,4096]{1,0:T(8,128)(2,1)S(1)} collective-permute-done((bf16[32,4096]{1,0:T(8,128)(2,1)S(1)}, bf16[32,4096]{1,0:T(8,128)(2,1)S(1)}, u32[]{:S(2)}, u32[]{:S(2)}) %collective-permute-start.14) | collective-permute-done | bytes 262176 | tf_op jit(solution)/shard_map/ppermute | solution.py:232
  35.5 1.7 %collective-permute-start.19 = (bf16[32,4096]{1,0:T(8,128)(2,1)}, bf16[32,4096]{1,0:T(8,128)(2,1)}, u32[]{:S(2)}, u32[]{:S(2)}) collective-permute-start(bf16[32,4096]{1,0:T(8,128)(2,1)} %collective-permute-done.18.refs_5_), channel_id=1, source_target_pairs={{0,2},{4,0},{8,4},{12,8},{14,12},{10,14},{6,10},{2,6},{1,3},{5,1},... | collective-permute-start | bytes 786440 | tf_op jit(solution)/shard_map/ppermute | solution.py:232
  37.2 2.2 %collective-permute-done.3.refs_1_.refs_4_ = bf16[32,3072]{1,0:T(8,128)(2,1)S(1)} collective-permute-done((bf16[32,3072]{1,0:T(8,128)(2,1)S(1)}, bf16[32,3072]{1,0:T(8,128)(2,1)S(1)}, u32[]{:S(2)}, u32[]{:S(2)}) %collective-permute-start.3) | collective-permute-done | bytes 196640 | tf_op jit(solution)/shard_map/ppermute | solution.py:232
  39.8 1.7 %collective-permute-start.11 = (bf16[32,4096]{1,0:T(8,128)(2,1)S(1)}, bf16[32,4096]{1,0:T(8,128)(2,1)S(1)}, u32[]{:S(2)}, u32[]{:S(2)}) collective-permute-start(bf16[32,4096]{1,0:T(8,128)(2,1)S(1)} %tie.7.refs_0_.refs_1_), channel_id=1, source_target_pairs={{0,2},{4,0},{8,4},{12,8},{14,12},{10,14},{6,10},{2,6},{1,3},{5,1},... | collective-permute-start | bytes 786440 | tf_op jit(solution)/shard_map/ppermute | solution.py:232
  41.5 7.0 %chunk_0.1 = (f32[256,512]{1,0:T(8,128)}, f32[256,512]{1,0:T(8,128)}, f32[128,256]{1,0:T(8,128)}, f32[8,128]{1,0:T(8,128)}) custom-call(s32[18]{0:T(128)} %dynamic-slice_bitcast_fusion.scalars, bf16[32,3072]{1,0:T(8,128)(2,1)} %copy-done.22, bf16[32,3072]{1,0:T(8,128)(2,1)} %copy-done.27, bf16[32,3072]{1,0:T(8,128)(2,1)} %copy-done.10, ...), custom_call_target="tpu_custom_call" | custom-call | flops 3623878656 | bytes 11010048 | tf_op jit(solution)/shard_map/chunk_0/pallas_call | solution.py:138
  49.5 1.8 %collective-permute-start.16 = (bf16[32,4096]{1,0:T(8,128)(2,1)}, bf16[32,4096]{1,0:T(8,128)(2,1)S(1)}, u32[]{:S(2)}, u32[]{:S(2)}) collective-permute-start(bf16[32,4096]{1,0:T(8,128)(2,1)} %collective-permute-done.15.refs_2_), channel_id=1, source_target_pairs={{0,4},{4,8},{8,12},{12,14},{14,10},{10,6},{6,2},{2,0},{1,5},{5,9},... | collective-permute-start | bytes 786440 | tf_op jit(solution)/shard_map/ppermute | solution.py:232
  51.6 1.7 %collective-permute-start.12 = (bf16[32,4096]{1,0:T(8,128)(2,1)S(1)}, bf16[32,4096]{1,0:T(8,128)(2,1)}, u32[]{:S(2)}, u32[]{:S(2)}) collective-permute-start(bf16[32,4096]{1,0:T(8,128)(2,1)S(1)} %collective-permute-done.11.refs_5_.refs_6_), channel_id=1, source_target_pairs={{0,2},{4,0},{8,4},{12,8},{14,12},{10,14},{6,10},{2,6},{1,3},{5,1},... | collective-permute-start | bytes 786440 | tf_op jit(solution)/shard_map/ppermute | solution.py:232
  53.3 5.2 %collective-permute-done.8.refs_2_.refs_3_ = bf16[32,4096]{1,0:T(8,128)(2,1)S(1)} collective-permute-done((bf16[32,4096]{1,0:T(8,128)(2,1)S(1)}, bf16[32,4096]{1,0:T(8,128)(2,1)S(1)}, u32[]{:S(2)}, u32[]{:S(2)}) %collective-permute-start.8) | collective-permute-done | bytes 262176 | tf_op jit(solution)/shard_map/ppermute | solution.py:232
  58.8 5.3 %collective-permute-done.16.refs_1_.refs_3_ = bf16[32,4096]{1,0:T(8,128)(2,1)S(1)} collective-permute-done((bf16[32,4096]{1,0:T(8,128)(2,1)}, bf16[32,4096]{1,0:T(8,128)(2,1)S(1)}, u32[]{:S(2)}, u32[]{:S(2)}) %collective-permute-start.16) | collective-permute-done | bytes 262176 | tf_op jit(solution)/shard_map/ppermute | solution.py:232
  64.1 1.6 %collective-permute-start.24 = (bf16[32,3072]{1,0:T(8,128)(2,1)S(1)}, bf16[32,3072]{1,0:T(8,128)(2,1)}, u32[]{:S(2)}, u32[]{:S(2)}) collective-permute-start(bf16[32,3072]{1,0:T(8,128)(2,1)S(1)} %tie.9.refs_8_.refs_9_), channel_id=1, source_target_pairs={{0,2},{4,0},{8,4},{12,8},{14,12},{10,14},{6,10},{2,6},{1,3},{5,1},... | collective-permute-start | bytes 589832 | tf_op jit(solution)/shard_map/ppermute | solution.py:232
  66.2 5.9 %collective-permute-done.24.refs_12_.refs_13_ = bf16[32,3072]{1,0:T(8,128)(2,1)} collective-permute-done((bf16[32,3072]{1,0:T(8,128)(2,1)S(1)}, bf16[32,3072]{1,0:T(8,128)(2,1)}, u32[]{:S(2)}, u32[]{:S(2)}) %collective-permute-start.24) | collective-permute-done | bytes 196640 | tf_op jit(solution)/shard_map/ppermute | solution.py:232
  73.7 1.6 %collective-permute-start.13 = (bf16[32,4096]{1,0:T(8,128)(2,1)}, bf16[32,4096]{1,0:T(8,128)(2,1)S(1)}, u32[]{:S(2)}, u32[]{:S(2)}) collective-permute-start(bf16[32,4096]{1,0:T(8,128)(2,1)} %collective-permute-done.12.refs_6_.refs_7_), channel_id=1, source_target_pairs={{0,2},{4,0},{8,4},{12,8},{14,12},{10,14},{6,10},{2,6},{1,3},{5,1},... | collective-permute-start | bytes 786440 | tf_op jit(solution)/shard_map/ppermute | solution.py:232
  75.7 8.5 %chunk_1.1 = (f32[256,512]{1,0:T(8,128)}, f32[256,512]{1,0:T(8,128)}, f32[128,256]{1,0:T(8,128)}, f32[8,128]{1,0:T(8,128)}) custom-call(s32[18]{0:T(128)} %dynamic-slice_bitcast_fusion.scalars, bf16[32,4096]{1,0:T(8,128)(2,1)} %copy-done.21, bf16[32,4096]{1,0:T(8,128)(2,1)} %copy-done.25, bf16[32,4096]{1,0:T(8,128)(2,1)} %collective-permute-done.15.refs_2_, ...), custom_call_target="tpu_custom_call" | custom-call | flops 4831838208 | bytes 13893632 | tf_op jit(solution)/shard_map/chunk_1/pallas_call | solution.py:138
  85.4 1.6 %collective-permute-start.26 = (bf16[32,3072]{1,0:T(8,128)(2,1)}, bf16[32,3072]{1,0:T(8,128)(2,1)S(1)}, u32[]{:S(2)}, u32[]{:S(2)}) collective-permute-start(bf16[32,3072]{1,0:T(8,128)(2,1)} %collective-permute-done.25.refs_13_.refs_14_), channel_id=1, source_target_pairs={{0,2},{4,0},{8,4},{12,8},{14,12},{10,14},{6,10},{2,6},{1,3},{5,1},... | collective-permute-start | bytes 589832 | tf_op jit(solution)/shard_map/ppermute | solution.py:232
  87.0 6.5 %all-to-all-start = ((bf16[8,128,512]{2,1,0:T(8,128)(2,1)}), bf16[8,128,512]{2,1,0:T(8,128)(2,1)}, u32[]{:S(2)}, u32[]{:S(2)}) async-start(bf16[8,128,512]{2,1,0:T(8,128)(2,1)} %tie.11), calls=%async_computation | async-start | bytes 2097152 | tf_op jit(solution)/shard_map/all_to_all | solution.py:248
  94.4 2.0 %collective-permute-start.23 = (bf16[32,3072]{1,0:T(8,128)(2,1)S(1)}, bf16[32,3072]{1,0:T(8,128)(2,1)S(1)}, u32[]{:S(2)}, u32[]{:S(2)}) collective-permute-start(bf16[32,3072]{1,0:T(8,128)(2,1)S(1)} %collective-permute-done.22.refs_10_.refs_11_), channel_id=1, source_target_pairs={{0,4},{4,8},{8,12},{12,14},{14,10},{10,6},{6,2},{2,0},{1,5},{5,9},... | collective-permute-start | bytes 589832 | tf_op jit(solution)/shard_map/ppermute | solution.py:232
  96.5 9.2 %collective-permute-done.23.refs_11_.refs_12_ = bf16[32,3072]{1,0:T(8,128)(2,1)S(1)} collective-permute-done((bf16[32,3072]{1,0:T(8,128)(2,1)S(1)}, bf16[32,3072]{1,0:T(8,128)(2,1)S(1)}, u32[]{:S(2)}, u32[]{:S(2)}) %collective-permute-start.23) | collective-permute-done | bytes 196640 | tf_op jit(solution)/shard_map/ppermute | solution.py:232
  106.5 5.5 %last_narrow.1 = f32[128,256]{1,0:T(8,128)} custom-call(s32[18]{0:T(128)} %dynamic-slice_bitcast_fusion.scalars, bf16[32,4096]{1,0:T(8,128)(2,1)} %copy-done, bf16[32,4096]{1,0:T(8,128)(2,1)} %copy-done.4, bf16[32,4096]{1,0:T(8,128)(2,1)} %copy-done.15, bf16[32,4096]{1,0:T(8,128)(2,1)} %collective-permute-done.9.refs_3_.refs_4_, bf16[32,4096]{1,0:T(8,128)(2,1)} %copy-done.3, ...), custom_call_target="tpu_custom_call" | custom-call | flops 939524096 | bytes 5767168 | tf_op jit(solution)/shard_map/last_narrow/pallas_call | solution.py:138
  113.0 2.3 %collective-permute-start.29 = (f32[64,256]{1,0:T(8,128)S(1)}, f32[64,256]{1,0:T(8,128)S(1)}, u32[]{:S(2)}, u32[]{:S(2)}) collective-permute-start(f32[64,256]{1,0:T(8,128)S(1)} %fusion.refs_0_), channel_id=1, source_target_pairs={{0,2},{1,3},{2,0},{3,1},{4,6},{5,7},{6,4},{7,5},{8,10},{9,11},{10,... | collective-permute-start | bytes 196616 | tf_op jit(solution)/shard_map/ppermute | solution.py:264
  115.4 7.2 %last_sent.1.refs_0_ = f32[256,512]{1,0:T(8,128)} custom-call(s32[18]{0:T(128)} %dynamic-slice_bitcast_fusion.scalars, f32[64,256]{1,0:T(8,128)} %copy-done.26, bf16[32,4096]{1,0:T(8,128)(2,1)} %copy-done, bf16[32,4096]{1,0:T(8,128)(2,1)} %copy-done.4, bf16[32,4096]{1,0:T(8,128)(2,1)} %copy-done.15, bf16[32,4096]{1,0:T(8,128)(2,1)} %collective-permute-done.9.refs_3_.refs_4_, ...), custom_call_target="tpu_custom_call" | custom-call | flops 3758096384 | bytes 12058624 | tf_op jit(solution)/shard_map/last_sent/pallas_call | solution.py:138
  122.8 7.2 %collective-permute-start.31 = (bf16[64,256]{1,0:T(8,128)(2,1)S(1)}, bf16[64,256]{1,0:T(8,128)(2,1)S(1)}, u32[]{:S(2)}, u32[]{:S(2)}) collective-permute-start(bf16[64,256]{1,0:T(8,128)(2,1)S(1)} %add_convert_fusion), channel_id=1, source_target_pairs={{0,4},{2,6},{4,8},{6,10},{8,12},{10,14},{12,0},{14,2},{1,5},{3,7},... | collective-permute-start | bytes 98312 | tf_op jit(solution)/shard_map/ppermute | solution.py:268
  130.9 2.8 %collective-permute-start.33 = (bf16[64,256]{1,0:T(8,128)(2,1)S(1)}, bf16[64,256]{1,0:T(8,128)(2,1)S(1)}, u32[]{:S(2)}, u32[]{:S(2)}) collective-permute-start(bf16[64,256]{1,0:T(8,128)(2,1)S(1)} %add_convert_fusion), channel_id=1, source_target_pairs={{0,12},{2,14},{4,0},{6,2},{8,4},{10,6},{12,8},{14,10},{1,13},{3,15... | collective-permute-start | bytes 98312 | tf_op jit(solution)/shard_map/ppermute | solution.py:268
  133.7 7.0 %last_kept.1.kept = f32[256,512]{1,0:T(8,128)} custom-call(s32[18]{0:T(128)} %dynamic-slice_bitcast_fusion.scalars, f32[256,512]{1,0:T(8,128)} %last_sent.1.refs_0_, bf16[32,4096]{1,0:T(8,128)(2,1)} %copy-done, bf16[32,4096]{1,0:T(8,128)(2,1)} %copy-done.4, bf16[32,4096]{1,0:T(8,128)(2,1)} %copy-done.15, ...), custom_call_target="tpu_custom_call" | custom-call | flops 3758096384 | bytes 12058624 | tf_op jit(solution)/shard_map/last_kept/pallas_call | solution.py:138
  142.2 2.9 %expand_and_add.1 = bf16[256,512]{1,0:T(8,128)(2,1)} custom-call(bf16[64,256]{1,0:T(8,128)(2,1)} %add_add_fusion.shrunk, s32[256,1]{1,0:T(8,128)} %copy.15.slot, bf16[1024,512]{1,0:T(8,128)(2,1)} %bitcast.6.factors, f32[256,512]{1,0:T(8,128)} %last_kept.1.kept, f32[256,512]{1,0:T(8,128)} %copy-done.23), custom_call_target="tpu_custom_call" | custom-call | flops 268435456 | bytes 2359296 | tf_op jit(solution)/shard_map/expand_and_add/pallas_call | solution.py:179
  (128 shorter events, 17.0 us)
Async XLA Ops:
  4.1 15.1 %collective-permute-start.4 = (bf16[32,3072]{1,0:T(8,128)(2,1)S(1)}, bf16[32,3072]{1,0:T(8,128)(2,1)S(1)}, u32[]{:S(2)}, u32[]{:S(2)}) collective-permute-start(bf16[32,3072]{1,0:T(8,128)(2,1)S(1)} %get-tuple-element.28.refs_0_), channel_id=1, source_target_pairs={{0,2},{4,0},{8,4},{12,8},{14,12},{10,14},{6,10},{2,6},{1,3},{5,1},... | collective-permute-start | bytes 589832 | tf_op jit(solution)/shard_map/ppermute | solution.py:232
  9.0 12.0 %collective-permute-start.1 = (bf16[32,3072]{1,0:T(8,128)(2,1)S(1)}, bf16[32,3072]{1,0:T(8,128)(2,1)S(1)}, u32[]{:S(2)}, u32[]{:S(2)}) collective-permute-start(bf16[32,3072]{1,0:T(8,128)(2,1)S(1)} %collective-permute-done.refs_1_), channel_id=1, source_target_pairs={{0,4},{4,8},{8,12},{12,14},{14,10},{10,6},{6,2},{2,0},{1,5},{5,9},... | collective-permute-start | bytes 589832 | tf_op jit(solution)/shard_map/ppermute | solution.py:232
  11.9 11.9 %collective-permute-start.17 = (bf16[32,4096]{1,0:T(8,128)(2,1)S(1)}, bf16[32,4096]{1,0:T(8,128)(2,1)S(1)}, u32[]{:S(2)}, u32[]{:S(2)}) collective-permute-start(bf16[32,4096]{1,0:T(8,128)(2,1)S(1)} %get-tuple-element.25.refs_0_), channel_id=1, source_target_pairs={{0,2},{4,0},{8,4},{12,8},{14,12},{10,14},{6,10},{2,6},{1,3},{5,1},... | collective-permute-start | bytes 786440 | tf_op jit(solution)/shard_map/ppermute | solution.py:232
  22.0 13.2 %collective-permute-start.14 = (bf16[32,4096]{1,0:T(8,128)(2,1)S(1)}, bf16[32,4096]{1,0:T(8,128)(2,1)S(1)}, u32[]{:S(2)}, u32[]{:S(2)}) collective-permute-start(bf16[32,4096]{1,0:T(8,128)(2,1)S(1)} %get-tuple-element.25.refs_0_), channel_id=1, source_target_pairs={{0,4},{4,8},{8,12},{12,14},{14,10},{10,6},{6,2},{2,0},{1,5},{5,9},... | collective-permute-start | bytes 786440 | tf_op jit(solution)/shard_map/ppermute | solution.py:232
  23.8 11.7 %collective-permute-start.18 = (bf16[32,4096]{1,0:T(8,128)(2,1)S(1)}, bf16[32,4096]{1,0:T(8,128)(2,1)}, u32[]{:S(2)}, u32[]{:S(2)}) collective-permute-start(bf16[32,4096]{1,0:T(8,128)(2,1)S(1)} %collective-permute-done.17.refs_4_), channel_id=1, source_target_pairs={{0,2},{4,0},{8,4},{12,8},{14,12},{10,14},{6,10},{2,6},{1,3},{5,1},... | collective-permute-start | bytes 786440 | tf_op jit(solution)/shard_map/ppermute | solution.py:232
  26.3 10.9 %collective-permute-start.6 = (bf16[32,3072]{1,0:T(8,128)(2,1)S(1)}, bf16[32,3072]{1,0:T(8,128)(2,1)S(1)}, u32[]{:S(2)}, u32[]{:S(2)}) collective-permute-start(bf16[32,3072]{1,0:T(8,128)(2,1)S(1)} %collective-permute-done.5.refs_6_), channel_id=1, source_target_pairs={{0,2},{4,0},{8,4},{12,8},{14,12},{10,14},{6,10},{2,6},{1,3},{5,1},... | collective-permute-start | bytes 589832 | tf_op jit(solution)/shard_map/ppermute | solution.py:232
  29.6 9.8 %collective-permute-start.3 = (bf16[32,3072]{1,0:T(8,128)(2,1)S(1)}, bf16[32,3072]{1,0:T(8,128)(2,1)S(1)}, u32[]{:S(2)}, u32[]{:S(2)}) collective-permute-start(bf16[32,3072]{1,0:T(8,128)(2,1)S(1)} %collective-permute-done.2.refs_3_), channel_id=1, source_target_pairs={{0,4},{4,8},{8,12},{12,14},{14,10},{10,6},{6,2},{2,0},{1,5},{5,9},... | collective-permute-start | bytes 589832 | tf_op jit(solution)/shard_map/ppermute | solution.py:232
  35.2 14.3 %collective-permute-start.15 = (bf16[32,4096]{1,0:T(8,128)(2,1)S(1)}, bf16[32,4096]{1,0:T(8,128)(2,1)}, u32[]{:S(2)}, u32[]{:S(2)}) collective-permute-start(bf16[32,4096]{1,0:T(8,128)(2,1)S(1)} %collective-permute-done.14.refs_1_), channel_id=1, source_target_pairs={{0,4},{4,8},{8,12},{12,14},{14,10},{10,6},{6,2},{2,0},{1,5},{5,9},... | collective-permute-start | bytes 786440 | tf_op jit(solution)/shard_map/ppermute | solution.py:232
  35.5 15.9 %collective-permute-start.19 = (bf16[32,4096]{1,0:T(8,128)(2,1)}, bf16[32,4096]{1,0:T(8,128)(2,1)}, u32[]{:S(2)}, u32[]{:S(2)}) collective-permute-start(bf16[32,4096]{1,0:T(8,128)(2,1)} %collective-permute-done.18.refs_5_), channel_id=1, source_target_pairs={{0,2},{4,0},{8,4},{12,8},{14,12},{10,14},{6,10},{2,6},{1,3},{5,1},... | collective-permute-start | bytes 786440 | tf_op jit(solution)/shard_map/ppermute | solution.py:232
  39.4 9.1 %collective-permute-start.7 = (bf16[32,4096]{1,0:T(8,128)(2,1)S(1)}, bf16[32,4096]{1,0:T(8,128)(2,1)S(1)}, u32[]{:S(2)}, u32[]{:S(2)}) collective-permute-start(bf16[32,4096]{1,0:T(8,128)(2,1)S(1)} %tie.7.refs_0_.refs_1_), channel_id=1, source_target_pairs={{0,4},{4,8},{8,12},{12,14},{14,10},{10,6},{6,2},{2,0},{1,5},{5,9},... | collective-permute-start | bytes 786440 | tf_op jit(solution)/shard_map/ppermute | solution.py:232
  39.8 11.8 %collective-permute-start.11 = (bf16[32,4096]{1,0:T(8,128)(2,1)S(1)}, bf16[32,4096]{1,0:T(8,128)(2,1)S(1)}, u32[]{:S(2)}, u32[]{:S(2)}) collective-permute-start(bf16[32,4096]{1,0:T(8,128)(2,1)S(1)} %tie.7.refs_0_.refs_1_), channel_id=1, source_target_pairs={{0,2},{4,0},{8,4},{12,8},{14,12},{10,14},{6,10},{2,6},{1,3},{5,1},... | collective-permute-start | bytes 786440 | tf_op jit(solution)/shard_map/ppermute | solution.py:232
  49.2 9.2 %collective-permute-start.8 = (bf16[32,4096]{1,0:T(8,128)(2,1)S(1)}, bf16[32,4096]{1,0:T(8,128)(2,1)S(1)}, u32[]{:S(2)}, u32[]{:S(2)}) collective-permute-start(bf16[32,4096]{1,0:T(8,128)(2,1)S(1)} %tie.8.refs_1_.refs_2_), channel_id=1, source_target_pairs={{0,4},{4,8},{8,12},{12,14},{14,10},{10,6},{6,2},{2,0},{1,5},{5,9},... | collective-permute-start | bytes 786440 | tf_op jit(solution)/shard_map/ppermute | solution.py:232
  49.5 14.6 %collective-permute-start.16 = (bf16[32,4096]{1,0:T(8,128)(2,1)}, bf16[32,4096]{1,0:T(8,128)(2,1)S(1)}, u32[]{:S(2)}, u32[]{:S(2)}) collective-permute-start(bf16[32,4096]{1,0:T(8,128)(2,1)} %collective-permute-done.15.refs_2_), channel_id=1, source_target_pairs={{0,4},{4,8},{8,12},{12,14},{14,10},{10,6},{6,2},{2,0},{1,5},{5,9},... | collective-permute-start | bytes 786440 | tf_op jit(solution)/shard_map/ppermute | solution.py:232
  51.3 12.8 %collective-permute-start.20 = (bf16[32,4096]{1,0:T(8,128)(2,1)}, bf16[32,4096]{1,0:T(8,128)(2,1)S(1)}, u32[]{:S(2)}, u32[]{:S(2)}) collective-permute-start(bf16[32,4096]{1,0:T(8,128)(2,1)} %collective-permute-done.19.refs_6_), channel_id=1, source_target_pairs={{0,2},{4,0},{8,4},{12,8},{14,12},{10,14},{6,10},{2,6},{1,3},{5,1},... | collective-permute-start | bytes 786440 | tf_op jit(solution)/shard_map/ppermute | solution.py:232
  51.6 22.1 %collective-permute-start.12 = (bf16[32,4096]{1,0:T(8,128)(2,1)S(1)}, bf16[32,4096]{1,0:T(8,128)(2,1)}, u32[]{:S(2)}, u32[]{:S(2)}) collective-permute-start(bf16[32,4096]{1,0:T(8,128)(2,1)S(1)} %collective-permute-done.11.refs_5_.refs_6_), channel_id=1, source_target_pairs={{0,2},{4,0},{8,4},{12,8},{14,12},{10,14},{6,10},{2,6},{1,3},{5,1},... | collective-permute-start | bytes 786440 | tf_op jit(solution)/shard_map/ppermute | solution.py:232
  58.5 16.8 %collective-permute-start.9 = (bf16[32,4096]{1,0:T(8,128)(2,1)S(1)}, bf16[32,4096]{1,0:T(8,128)(2,1)}, u32[]{:S(2)}, u32[]{:S(2)}) collective-permute-start(bf16[32,4096]{1,0:T(8,128)(2,1)S(1)} %collective-permute-done.8.refs_2_.refs_3_), channel_id=1, source_target_pairs={{0,4},{4,8},{8,12},{12,14},{14,10},{10,6},{6,2},{2,0},{1,5},{5,9},... | collective-permute-start | bytes 786440 | tf_op jit(solution)/shard_map/ppermute | solution.py:232
  64.1 8.0 %collective-permute-start.24 = (bf16[32,3072]{1,0:T(8,128)(2,1)S(1)}, bf16[32,3072]{1,0:T(8,128)(2,1)}, u32[]{:S(2)}, u32[]{:S(2)}) collective-permute-start(bf16[32,3072]{1,0:T(8,128)(2,1)S(1)} %tie.9.refs_8_.refs_9_), channel_id=1, source_target_pairs={{0,2},{4,0},{8,4},{12,8},{14,12},{10,14},{6,10},{2,6},{1,3},{5,1},... | collective-permute-start | bytes 589832 | tf_op jit(solution)/shard_map/ppermute | solution.py:232
  65.8 18.5 %collective-permute-start.21 = (bf16[32,3072]{1,0:T(8,128)(2,1)S(1)}, bf16[32,3072]{1,0:T(8,128)(2,1)S(1)}, u32[]{:S(2)}, u32[]{:S(2)}) collective-permute-start(bf16[32,3072]{1,0:T(8,128)(2,1)S(1)} %tie.9.refs_8_.refs_9_), channel_id=1, source_target_pairs={{0,4},{4,8},{8,12},{12,14},{14,10},{10,6},{6,2},{2,0},{1,5},{5,9},... | collective-permute-start | bytes 589832 | tf_op jit(solution)/shard_map/ppermute | solution.py:232
  72.1 13.3 %collective-permute-start.25 = (bf16[32,3072]{1,0:T(8,128)(2,1)}, bf16[32,3072]{1,0:T(8,128)(2,1)}, u32[]{:S(2)}, u32[]{:S(2)}) collective-permute-start(bf16[32,3072]{1,0:T(8,128)(2,1)} %collective-permute-done.24.refs_12_.refs_13_), channel_id=1, source_target_pairs={{0,2},{4,0},{8,4},{12,8},{14,12},{10,14},{6,10},{2,6},{1,3},{5,1},... | collective-permute-start | bytes 589832 | tf_op jit(solution)/shard_map/ppermute | solution.py:232
  73.7 13.3 %collective-permute-start.13 = (bf16[32,4096]{1,0:T(8,128)(2,1)}, bf16[32,4096]{1,0:T(8,128)(2,1)S(1)}, u32[]{:S(2)}, u32[]{:S(2)}) collective-permute-start(bf16[32,4096]{1,0:T(8,128)(2,1)} %collective-permute-done.12.refs_6_.refs_7_), channel_id=1, source_target_pairs={{0,2},{4,0},{8,4},{12,8},{14,12},{10,14},{6,10},{2,6},{1,3},{5,1},... | collective-permute-start | bytes 786440 | tf_op jit(solution)/shard_map/ppermute | solution.py:232
  75.3 11.7 %collective-permute-start.10 = (bf16[32,4096]{1,0:T(8,128)(2,1)}, bf16[32,4096]{1,0:T(8,128)(2,1)S(1)}, u32[]{:S(2)}, u32[]{:S(2)}) collective-permute-start(bf16[32,4096]{1,0:T(8,128)(2,1)} %collective-permute-done.9.refs_3_.refs_4_), channel_id=1, source_target_pairs={{0,4},{4,8},{8,12},{12,14},{14,10},{10,6},{6,2},{2,0},{1,5},{5,9},... | collective-permute-start | bytes 786440 | tf_op jit(solution)/shard_map/ppermute | solution.py:232
  85.0 9.5 %collective-permute-start.22 = (bf16[32,3072]{1,0:T(8,128)(2,1)S(1)}, bf16[32,3072]{1,0:T(8,128)(2,1)S(1)}, u32[]{:S(2)}, u32[]{:S(2)}) collective-permute-start(bf16[32,3072]{1,0:T(8,128)(2,1)S(1)} %tie.10.refs_9_.refs_10_), channel_id=1, source_target_pairs={{0,4},{4,8},{8,12},{12,14},{14,10},{10,6},{6,2},{2,0},{1,5},{5,9},... | collective-permute-start | bytes 589832 | tf_op jit(solution)/shard_map/ppermute | solution.py:232
  85.4 11.0 %collective-permute-start.26 = (bf16[32,3072]{1,0:T(8,128)(2,1)}, bf16[32,3072]{1,0:T(8,128)(2,1)S(1)}, u32[]{:S(2)}, u32[]{:S(2)}) collective-permute-start(bf16[32,3072]{1,0:T(8,128)(2,1)} %collective-permute-done.25.refs_13_.refs_14_), channel_id=1, source_target_pairs={{0,2},{4,0},{8,4},{12,8},{14,12},{10,14},{6,10},{2,6},{1,3},{5,1},... | collective-permute-start | bytes 589832 | tf_op jit(solution)/shard_map/ppermute | solution.py:232
  87.0 54.3 %all-to-all-start = ((bf16[8,128,512]{2,1,0:T(8,128)(2,1)}), bf16[8,128,512]{2,1,0:T(8,128)(2,1)}, u32[]{:S(2)}, u32[]{:S(2)}) async-start(bf16[8,128,512]{2,1,0:T(8,128)(2,1)} %tie.11), calls=%async_computation | async-start | bytes 2097152 | tf_op jit(solution)/shard_map/all_to_all | solution.py:248
  94.4 11.3 %collective-permute-start.23 = (bf16[32,3072]{1,0:T(8,128)(2,1)S(1)}, bf16[32,3072]{1,0:T(8,128)(2,1)S(1)}, u32[]{:S(2)}, u32[]{:S(2)}) collective-permute-start(bf16[32,3072]{1,0:T(8,128)(2,1)S(1)} %collective-permute-done.22.refs_10_.refs_11_), channel_id=1, source_target_pairs={{0,4},{4,8},{8,12},{12,14},{14,10},{10,6},{6,2},{2,0},{1,5},{5,9},... | collective-permute-start | bytes 589832 | tf_op jit(solution)/shard_map/ppermute | solution.py:232
  96.5 9.3 %collective-permute-start.27 = (bf16[32,3072]{1,0:T(8,128)(2,1)S(1)}, bf16[32,3072]{1,0:T(8,128)(2,1)S(1)}, u32[]{:S(2)}, u32[]{:S(2)}) collective-permute-start(bf16[32,3072]{1,0:T(8,128)(2,1)S(1)} %collective-permute-done.26.refs_14_.refs_15_), channel_id=1, source_target_pairs={{0,2},{4,0},{8,4},{12,8},{14,12},{10,14},{6,10},{2,6},{1,3},{5,1},... | collective-permute-start | bytes 589832 | tf_op jit(solution)/shard_map/ppermute | solution.py:232
  112.9 9.8 %collective-permute-start.28 = (f32[64,256]{1,0:T(8,128)S(1)}, f32[64,256]{1,0:T(8,128)S(1)}, u32[]{:S(2)}, u32[]{:S(2)}) collective-permute-start(f32[64,256]{1,0:T(8,128)S(1)} %fusion.refs_0_), channel_id=1, source_target_pairs={{0,1},{1,0},{2,3},{3,2},{4,5},{5,4},{6,7},{7,6},{8,9},{9,8},{10,11... | collective-permute-start | bytes 196616 | tf_op jit(solution)/shard_map/ppermute | solution.py:264
  113.0 9.7 %collective-permute-start.29 = (f32[64,256]{1,0:T(8,128)S(1)}, f32[64,256]{1,0:T(8,128)S(1)}, u32[]{:S(2)}, u32[]{:S(2)}) collective-permute-start(f32[64,256]{1,0:T(8,128)S(1)} %fusion.refs_0_), channel_id=1, source_target_pairs={{0,2},{1,3},{2,0},{3,1},{4,6},{5,7},{6,4},{7,5},{8,10},{9,11},{10,... | collective-permute-start | bytes 196616 | tf_op jit(solution)/shard_map/ppermute | solution.py:264
  122.5 18.8 %collective-permute-start.34 = (f32[256,512]{1,0:T(8,128)}, f32[256,512]{1,0:T(8,128)S(1)}, u32[]{:S(2)}, u32[]{:S(2)}) collective-permute-start(f32[256,512]{1,0:T(8,128)} %last_sent.1.refs_0_), channel_id=1, source_target_pairs={{0,1},{1,0},{2,3},{3,2},{4,5},{5,4},{6,7},{7,6},{8,9},{9,8},{10,11... | collective-permute-start | bytes 1572872 | tf_op jit(solution)/shard_map/ppermute | solution.py:269
  122.8 17.9 %collective-permute-start.31 = (bf16[64,256]{1,0:T(8,128)(2,1)S(1)}, bf16[64,256]{1,0:T(8,128)(2,1)S(1)}, u32[]{:S(2)}, u32[]{:S(2)}) collective-permute-start(bf16[64,256]{1,0:T(8,128)(2,1)S(1)} %add_convert_fusion), channel_id=1, source_target_pairs={{0,4},{2,6},{4,8},{6,10},{8,12},{10,14},{12,0},{14,2},{1,5},{3,7},... | collective-permute-start | bytes 98312 | tf_op jit(solution)/shard_map/ppermute | solution.py:268
  130.0 10.7 %collective-permute-start.32 = (bf16[64,256]{1,0:T(8,128)(2,1)S(1)}, bf16[64,256]{1,0:T(8,128)(2,1)S(1)}, u32[]{:S(2)}, u32[]{:S(2)}) collective-permute-start(bf16[64,256]{1,0:T(8,128)(2,1)S(1)} %add_convert_fusion), channel_id=1, source_target_pairs={{0,8},{2,10},{4,12},{6,14},{8,0},{10,2},{12,4},{14,6},{1,9},{3,11}... | collective-permute-start | bytes 98312 | tf_op jit(solution)/shard_map/ppermute | solution.py:268
  130.9 9.9 %collective-permute-start.33 = (bf16[64,256]{1,0:T(8,128)(2,1)S(1)}, bf16[64,256]{1,0:T(8,128)(2,1)S(1)}, u32[]{:S(2)}, u32[]{:S(2)}) collective-permute-start(bf16[64,256]{1,0:T(8,128)(2,1)S(1)} %add_convert_fusion), channel_id=1, source_target_pairs={{0,12},{2,14},{4,0},{6,2},{8,4},{10,6},{12,8},{14,10},{1,13},{3,15... | collective-permute-start | bytes 98312 | tf_op jit(solution)/shard_map/ppermute | solution.py:268
  (37 other events, 451.8 us)

commit v9 on v7

--- a/solution.py
+++ b/solution.py
@@ -12,7 +12,7 @@
 TILE = 1024
 CHUNKS = 4
 MIB = 2**20
-MATMUL_MIB = 62
+MATMUL_MIB = 28
 
 
 def params(mib):
@@ -21,27 +21,6 @@
 
 def ring_order(n):
     return list(range(0, n, 2)) + list(range(1, n, 2))[::-1]
-
-
-def take_kernel(start, width, src, *refs):
-    *_, dst, sem = refs
-    copy = pltpu.make_async_copy(src.at[:, pl.ds(start, width)], dst, sem)
-    copy.start()
-    copy.wait()
-
-
-def take(hidden, start, width, after):
-    rows = hidden.shape[0]
-    return pl.pallas_call(
-        functools.partial(take_kernel, start, width),
-        in_specs=[pl.BlockSpec(memory_space=pl.ANY)] * (1 + len(after)),
-        out_specs=pl.BlockSpec(memory_space=pl.ANY),
-        scratch_shapes=[pltpu.SemaphoreType.DMA],
-        out_shape=jax.ShapeDtypeStruct((rows, width), BF16),
-        compiler_params=params(MATMUL_MIB),
-        cost_estimate=pl.CostEstimate(flops=0, bytes_accessed=4 * rows * width, transcendentals=0),
-        name=f"take_{start}",
-    )(hidden, *after)
 
 
 def split_kernel(scalars, src, dst, mark):
@@ -62,7 +41,7 @@
             out_specs=[pl.BlockSpec((1, rows, share), lambda s, t: (s, 0, 0)), pl.BlockSpec((8, 128), lambda s, t: (0, 0))],
         ),
         out_shape=[jax.ShapeDtypeStruct((n, rows, share), BF16), jax.ShapeDtypeStruct((8, 128), F32)],
-        compiler_params=params(MATMUL_MIB),
+        compiler_params=params(4),
         cost_estimate=pl.CostEstimate(flops=0, bytes_accessed=4 * n * rows * share, transcendentals=0),
         name="expand_blocks",
     )(scalars, expand.reshape(rows, width))
@@ -79,7 +58,7 @@
         out_specs=pl.BlockSpec(memory_space=pl.ANY),
         out_shape=jax.ShapeDtypeStruct(array.shape, array.dtype),
         input_output_aliases={0: 0},
-        compiler_params=params(MATMUL_MIB),
+        compiler_params=params(1),
         name="tie",
     )(array, *after)
 
@@ -202,7 +181,7 @@
         out_specs=pl.BlockSpec(memory_space=pltpu.VMEM),
         scratch_shapes=[pltpu.VMEM((rows, n * wide), BF16)],
         out_shape=jax.ShapeDtypeStruct((rows, share), BF16),
-        compiler_params=params(MATMUL_MIB),
+        compiler_params=params(8),
         cost_estimate=pl.CostEstimate(
             flops=2 * rows * share * n * wide,
             bytes_accessed=2 * n * wide * share + 10 * rows * share,
@@ -244,7 +223,9 @@
         chunks, ends = [], []
         for chunk in range(CHUNKS):
             start = chunk * width
-            own = take(hidden, start, width, [mark]) if chunk == CHUNKS - 1 else hidden[:, start:start + width]
+            own = hidden[:, start:start + width]
+            if chunk == CHUNKS - 1:
+                own = tie(own, [mark])
             way = chunk % 2
             pieces = [own]
             for length, pairs in zip(((long, short), (short, long))[way], (clockwise, counter)):
@@ -257,10 +238,8 @@
         factors = lax.all_to_all(tie(blocks, ends[:4]), "store", 0, 0)
 
         call = functools.partial(chunk_matmul, scalars, half)
-        acc = None
-        for chunk in range(CHUNKS - 2):
-            acc = call(chunks[chunk:chunk + 1], down, shrink_rows, acc, (0, 1), True, f"chunk_{chunk}")
-        last = chunks[CHUNKS - 2:]
+        first, last = chunks[:CHUNKS // 2], chunks[CHUNKS // 2:]
+        acc = call(first, down, shrink_rows, None, (0, 1), True, "first_chunks")
         narrow, = call(last, down, shrink_rows, acc[2:], (), True, "last_narrow")
         mine = [
             jnp.where((row_slot == store * owned + i)[None, :], narrow[i * rank:(i + 1) * rank], 0.0)

time: 130 us -> 126 us (0.969)
  local copies, waits for them, and re-layouts: 5.16 us -> 27.2 us
  Pallas kernels: 51 us -> 30.7 us
  waiting for transfers between devices: 28.4 us -> 14.9 us
  starting transfers between devices: 43.2 us -> 52 us
  other arithmetic: 1.63 us -> 0.15 us
    unnamed x50 -> x74, local copies, waits for them, and re-layouts: 1.9 us -> 25.1 us
    ppermute x28, waiting for transfers between devices: 28.4 us -> 14.9 us  [shards(): moving = lax.ppermute(moving, 'store', pairs)]
    pallas_call x1 -> x0, Pallas kernels: 8.06 us -> none  [take(): pl.pallas_call(functools.partial(take_kernel, start, width), in_specs=[pl...]
    pallas_call x5 -> x4, Pallas kernels: 34.1 us -> 26.1 us  [chunk_matmul(): pl.pallas_call(functools.partial(matmul_kernel, n, len(after), spans, hal...]
    ppermute x28, starting transfers between devices: 32.2 us -> 39.9 us  [shards(): moving = lax.ppermute(moving, 'store', pairs)]
    pallas_call x1, Pallas kernels: 5.86 us -> 3.32 us  [expand_blocks(): pl.pallas_call(split_kernel, grid_spec=pltpu.PrefetchScalarGridSpec(num_s...]
    pallas_call x1, Pallas kernels: 2.94 us -> 1.35 us  [final(): pl.pallas_call(functools.partial(final_kernel, n, owned), in_specs=[pl.Bl...]
  transfers between devices with their start and end apart: 36 -> 36, of which waited for: 12 -> 9; matrix products, arithmetic and copies ran while one was open for 3% -> 1% of each run, Pallas kernels for 37% -> 23%
where the time goes in v9:
time: 126 us; the launch traced here: 125 us
  starting transfers between devices  52 us (41%)
  Pallas kernels  30.7 us (24%)
  local copies, waits for them, and re-layouts  27.2 us (22%)
  waiting for transfers between devices  14.9 us (12%)
    ppermute x28, starting transfers between devices, shards(): moving = lax.ppermute(moving, 'store', pairs)  39.9 us
    pallas_call x4, Pallas kernels, chunk_matmul(): pl.pallas_call(functools.partial(matmul_kernel, n, len(after), spans, hal...  26.1 us
    unnamed x74, local copies, waits for them, and re-layouts  25.1 us
    ppermute x28, waiting for transfers between devices, shards(): moving = lax.ppermute(moving, 'store', pairs)  14.9 us
    all_to_all x1, starting transfers between devices, shards(): factors = lax.all_to_all(tie(blocks, ends[:4]), 'store', 0, 0)  4.88 us
    ppermute x3, starting transfers between devices, shards(): lax.ppermute(column, 'store', [(s, (s + ds) % n) for s in range(n)])  4.44 us
    pallas_call x1, Pallas kernels, expand_blocks(): pl.pallas_call(split_kernel, grid_spec=pltpu.PrefetchScalarGridSpec(num_s...  3.32 us
  transfers between devices with their start and end apart: 36, of which 9 were waited for; matrix products, arithmetic and copies ran while one was open for 1% of the time, Pallas kernels for 23%

profile of v9, /device:TPU:0, one launch (start us, length us, event | category | flops | bytes accessed | tf_op | source)
XLA Modules:
  0.0 125.3 jit_solution(6907310320836416828)
XLA Ops:
  1.4 3.0 %collective-permute-start.24 = (bf16[32,3584]{1,0:T(8,128)(2,1)S(1)}, bf16[32,3584]{1,0:T(8,128)(2,1)S(1)}, u32[]{:S(2)}, u32[]{:S(2)}) collective-permute-start(bf16[32,3584]{1,0:T(8,128)(2,1)S(1)} %get-tuple-element.15.refs_8_), channel_id=1, source_target_pairs={{0,2},{4,0},{8,4},{12,8},{14,12},{10,14},{6,10},{2,6},{1,3},{5,1},... | collective-permute-start | bytes 688136 | tf_op jit(solution)/shard_map/ppermute | solution.py:234
  4.5 1.9 %collective-permute-start.18 = (bf16[32,3584]{1,0:T(8,128)(2,1)S(1)}, bf16[32,3584]{1,0:T(8,128)(2,1)S(1)}, u32[]{:S(2)}, u32[]{:S(2)}) collective-permute-start(bf16[32,3584]{1,0:T(8,128)(2,1)S(1)} %get-tuple-element.18.refs_0_), channel_id=1, source_target_pairs={{0,2},{4,0},{8,4},{12,8},{14,12},{10,14},{6,10},{2,6},{1,3},{5,1},... | collective-permute-start | bytes 688136 | tf_op jit(solution)/shard_map/ppermute | solution.py:234
  6.6 1.9 %collective-permute-start.4 = (bf16[32,3584]{1,0:T(8,128)(2,1)S(1)}, bf16[32,3584]{1,0:T(8,128)(2,1)S(1)}, u32[]{:S(2)}, u32[]{:S(2)}) collective-permute-start(bf16[32,3584]{1,0:T(8,128)(2,1)S(1)} %get-tuple-element.17.refs_0_.refs_1_), channel_id=1, source_target_pairs={{0,2},{4,0},{8,4},{12,8},{14,12},{10,14},{6,10},{2,6},{1,3},{5,1},... | collective-permute-start | bytes 688136 | tf_op jit(solution)/shard_map/ppermute | solution.py:234
  9.2 1.6 %copy-done.2 = bf16[2,64,8192]{2,1,0:T(8,128)(2,1)S(1)} copy-done((bf16[2,64,8192]{2,1,0:T(8,128)(2,1)S(1)}, bf16[2,64,8192]{2,1,0:T(8,128)(2,1)}, u32[]{:S(2)}) %copy-start.2) | copy-done | bytes 2097176
  10.7 3.3 %expand_blocks.1 = (bf16[8,128,512]{2,1,0:T(8,128)(2,1)}, f32[8,128]{1,0:T(8,128)S(1)}) custom-call(s32[18]{0:T(128)S(1)} %dynamic-slice_bitcast_fusion.scalars, bf16[128,8192]{1,0:T(8,128)(2,1)S(1)} %bitcast.13), custom_call_target="tpu_custom_call" | custom-call | bytes 2097152 | tf_op jit(solution)/shard_map/expand_blocks/pallas_call | solution.py:35
  14.2 1.9 %collective-permute-start.10 = (bf16[32,3584]{1,0:T(8,128)(2,1)S(1)}, bf16[32,3584]{1,0:T(8,128)(2,1)S(1)}, u32[]{:S(2)}, u32[]{:S(2)}) collective-permute-start(bf16[32,3584]{1,0:T(8,128)(2,1)S(1)} %tie.2.refs_8_.refs_9_), channel_id=1, source_target_pairs={{0,2},{4,0},{8,4},{12,8},{14,12},{10,14},{6,10},{2,6},{1,3},{5,1},... | collective-permute-start | bytes 688136 | tf_op jit(solution)/shard_map/ppermute | solution.py:234
  16.1 1.8 %collective-permute-start.7 = (bf16[32,3584]{1,0:T(8,128)(2,1)S(1)}, bf16[32,3584]{1,0:T(8,128)(2,1)S(1)}, u32[]{:S(2)}, u32[]{:S(2)}) collective-permute-start(bf16[32,3584]{1,0:T(8,128)(2,1)S(1)} %tie.2.refs_8_.refs_9_), channel_id=1, source_target_pairs={{0,4},{4,8},{8,12},{12,14},{14,10},{10,6},{6,2},{2,0},{1,5},{5,9},... | collective-permute-start | bytes 688136 | tf_op jit(solution)/shard_map/ppermute | solution.py:234
  20.7 2.1 %collective-permute-start.22 = (bf16[32,3584]{1,0:T(8,128)(2,1)S(1)}, bf16[32,3584]{1,0:T(8,128)(2,1)S(1)}, u32[]{:S(2)}, u32[]{:S(2)}) collective-permute-start(bf16[32,3584]{1,0:T(8,128)(2,1)S(1)} %collective-permute-done.21.refs_9_), channel_id=1, source_target_pairs={{0,4},{4,8},{8,12},{12,14},{14,10},{10,6},{6,2},{2,0},{1,5},{5,9},... | collective-permute-start | bytes 688136 | tf_op jit(solution)/shard_map/ppermute | solution.py:234
  25.6 2.1 %collective-permute-start.15 = (bf16[32,3584]{1,0:T(8,128)(2,1)S(1)}, bf16[32,3584]{1,0:T(8,128)(2,1)S(1)}, u32[]{:S(2)}, u32[]{:S(2)}) collective-permute-start(bf16[32,3584]{1,0:T(8,128)(2,1)S(1)} %collective-permute-done.14.refs_1_), channel_id=1, source_target_pairs={{0,4},{4,8},{8,12},{12,14},{14,10},{10,6},{6,2},{2,0},{1,5},{5,9},... | collective-permute-start | bytes 688136 | tf_op jit(solution)/shard_map/ppermute | solution.py:234
  29.1 1.5 %collective-permute-done.25.refs_13_ = bf16[32,3584]{1,0:T(8,128)(2,1)S(1)} collective-permute-done((bf16[32,3584]{1,0:T(8,128)(2,1)S(1)}, bf16[32,3584]{1,0:T(8,128)(2,1)S(1)}, u32[]{:S(2)}, u32[]{:S(2)}) %collective-permute-start.25) | collective-permute-done | bytes 229408 | tf_op jit(solution)/shard_map/ppermute | solution.py:234
  30.6 2.1 %collective-permute-start.1 = (bf16[32,3584]{1,0:T(8,128)(2,1)S(1)}, bf16[32,3584]{1,0:T(8,128)(2,1)S(1)}, u32[]{:S(2)}, u32[]{:S(2)}) collective-permute-start(bf16[32,3584]{1,0:T(8,128)(2,1)S(1)} %collective-permute-done.refs_1_.refs_2_), channel_id=1, source_target_pairs={{0,4},{4,8},{8,12},{12,14},{14,10},{10,6},{6,2},{2,0},{1,5},{5,9},... | collective-permute-start | bytes 688136 | tf_op jit(solution)/shard_map/ppermute | solution.py:234
  34.0 1.6 %collective-permute-done.19.refs_6_ = bf16[32,3584]{1,0:T(8,128)(2,1)} collective-permute-done((bf16[32,3584]{1,0:T(8,128)(2,1)S(1)}, bf16[32,3584]{1,0:T(8,128)(2,1)}, u32[]{:S(2)}, u32[]{:S(2)}) %collective-permute-start.19) | collective-permute-done | bytes 229408 | tf_op jit(solution)/shard_map/ppermute | solution.py:234
  35.6 2.1 %collective-permute-start.8 = (bf16[32,3584]{1,0:T(8,128)(2,1)S(1)}, bf16[32,3584]{1,0:T(8,128)(2,1)S(1)}, u32[]{:S(2)}, u32[]{:S(2)}) collective-permute-start(bf16[32,3584]{1,0:T(8,128)(2,1)S(1)} %collective-permute-done.7.refs_9_.refs_10_), channel_id=1, source_target_pairs={{0,4},{4,8},{8,12},{12,14},{14,10},{10,6},{6,2},{2,0},{1,5},{5,9},... | collective-permute-start | bytes 688136 | tf_op jit(solution)/shard_map/ppermute | solution.py:234
  40.4 2.1 %collective-permute-start.23 = (bf16[32,3584]{1,0:T(8,128)(2,1)S(1)}, bf16[32,3584]{1,0:T(8,128)(2,1)S(1)}, u32[]{:S(2)}, u32[]{:S(2)}) collective-permute-start(bf16[32,3584]{1,0:T(8,128)(2,1)S(1)} %collective-permute-done.22.refs_10_), channel_id=1, source_target_pairs={{0,4},{4,8},{8,12},{12,14},{14,10},{10,6},{6,2},{2,0},{1,5},{5,9},... | collective-permute-start | bytes 688136 | tf_op jit(solution)/shard_map/ppermute | solution.py:234
  43.1 1.6 %collective-permute-start.16 = (bf16[32,3584]{1,0:T(8,128)(2,1)S(1)}, bf16[32,3584]{1,0:T(8,128)(2,1)}, u32[]{:S(2)}, u32[]{:S(2)}) collective-permute-start(bf16[32,3584]{1,0:T(8,128)(2,1)S(1)} %collective-permute-done.15.refs_2_), channel_id=1, source_target_pairs={{0,4},{4,8},{8,12},{12,14},{14,10},{10,6},{6,2},{2,0},{1,5},{5,9},... | collective-permute-start | bytes 688136 | tf_op jit(solution)/shard_map/ppermute | solution.py:234
  45.4 1.9 %collective-permute-start.20 = (bf16[32,3584]{1,0:T(8,128)(2,1)}, bf16[32,3584]{1,0:T(8,128)(2,1)S(1)}, u32[]{:S(2)}, u32[]{:S(2)}) collective-permute-start(bf16[32,3584]{1,0:T(8,128)(2,1)} %collective-permute-done.19.refs_6_), channel_id=1, source_target_pairs={{0,2},{4,0},{8,4},{12,8},{14,12},{10,14},{6,10},{2,6},{1,3},{5,1},... | collective-permute-start | bytes 688136 | tf_op jit(solution)/shard_map/ppermute | solution.py:234
  47.4 2.9 %collective-permute-done.26.refs_14_ = bf16[32,3584]{1,0:T(8,128)(2,1)} collective-permute-done((bf16[32,3584]{1,0:T(8,128)(2,1)S(1)}, bf16[32,3584]{1,0:T(8,128)(2,1)}, u32[]{:S(2)}, u32[]{:S(2)}) %collective-permute-start.26) | collective-permute-done | bytes 229408 | tf_op jit(solution)/shard_map/ppermute | solution.py:234
  50.3 2.0 %collective-permute-start.12 = (bf16[32,3584]{1,0:T(8,128)(2,1)S(1)}, bf16[32,3584]{1,0:T(8,128)(2,1)}, u32[]{:S(2)}, u32[]{:S(2)}) collective-permute-start(bf16[32,3584]{1,0:T(8,128)(2,1)S(1)} %collective-permute-done.11.refs_13_.refs_14_), channel_id=1, source_target_pairs={{0,2},{4,0},{8,4},{12,8},{14,12},{10,14},{6,10},{2,6},{1,3},{5,1},... | collective-permute-start | bytes 688136 | tf_op jit(solution)/shard_map/ppermute | solution.py:234
  52.3 1.6 %collective-permute-start.27 = (bf16[32,3584]{1,0:T(8,128)(2,1)}, bf16[32,3584]{1,0:T(8,128)(2,1)S(1)}, u32[]{:S(2)}, u32[]{:S(2)}) collective-permute-start(bf16[32,3584]{1,0:T(8,128)(2,1)} %collective-permute-done.26.refs_14_), channel_id=1, source_target_pairs={{0,2},{4,0},{8,4},{12,8},{14,12},{10,14},{6,10},{2,6},{1,3},{5,1},... | collective-permute-start | bytes 688136 | tf_op jit(solution)/shard_map/ppermute | solution.py:234
  53.9 3.2 %collective-permute-done.16.refs_3_ = bf16[32,3584]{1,0:T(8,128)(2,1)} collective-permute-done((bf16[32,3584]{1,0:T(8,128)(2,1)S(1)}, bf16[32,3584]{1,0:T(8,128)(2,1)}, u32[]{:S(2)}, u32[]{:S(2)}) %collective-permute-start.16) | collective-permute-done | bytes 229408 | tf_op jit(solution)/shard_map/ppermute | solution.py:234
  57.6 1.8 %collective-permute-start.6 = (bf16[32,3584]{1,0:T(8,128)(2,1)S(1)}, bf16[32,3584]{1,0:T(8,128)(2,1)}, u32[]{:S(2)}, u32[]{:S(2)}) collective-permute-start(bf16[32,3584]{1,0:T(8,128)(2,1)S(1)} %collective-permute-done.5.refs_6_.refs_7_), channel_id=1, source_target_pairs={{0,2},{4,0},{8,4},{12,8},{14,12},{10,14},{6,10},{2,6},{1,3},{5,1},... | collective-permute-start | bytes 688136 | tf_op jit(solution)/shard_map/ppermute | solution.py:234
  59.5 2.6 %collective-permute-done.2.refs_3_.refs_4_ = bf16[32,3584]{1,0:T(8,128)(2,1)} collective-permute-done((bf16[32,3584]{1,0:T(8,128)(2,1)S(1)}, bf16[32,3584]{1,0:T(8,128)(2,1)}, u32[]{:S(2)}, u32[]{:S(2)}) %collective-permute-start.2) | collective-permute-done | bytes 229408 | tf_op jit(solution)/shard_map/ppermute | solution.py:234
  62.3 1.8 %collective-permute-start.3 = (bf16[32,3584]{1,0:T(8,128)(2,1)}, bf16[32,3584]{1,0:T(8,128)(2,1)}, u32[]{:S(2)}, u32[]{:S(2)}) collective-permute-start(bf16[32,3584]{1,0:T(8,128)(2,1)} %collective-permute-done.2.refs_3_.refs_4_), channel_id=1, source_target_pairs={{0,4},{4,8},{8,12},{12,14},{14,10},{10,6},{6,2},{2,0},{1,5},{5,9},... | collective-permute-start | bytes 688136 | tf_op jit(solution)/shard_map/ppermute | solution.py:234
  65.0 2.0 %collective-permute-start.13 = (bf16[32,3584]{1,0:T(8,128)(2,1)}, bf16[32,3584]{1,0:T(8,128)(2,1)}, u32[]{:S(2)}, u32[]{:S(2)}) collective-permute-start(bf16[32,3584]{1,0:T(8,128)(2,1)} %collective-permute-done.12.refs_14_.refs_15_), channel_id=1, source_target_pairs={{0,2},{4,0},{8,4},{12,8},{14,12},{10,14},{6,10},{2,6},{1,3},{5,1},... | collective-permute-start | bytes 688136 | tf_op jit(solution)/shard_map/ppermute | solution.py:234
  67.7 4.9 %all-to-all-start = ((bf16[8,128,512]{2,1,0:T(8,128)(2,1)}), bf16[8,128,512]{2,1,0:T(8,128)(2,1)S(1)}, u32[]{:S(2)}, u32[]{:S(2)}) async-start(bf16[8,128,512]{2,1,0:T(8,128)(2,1)} %tie.3), calls=%async_computation | async-start | bytes 2097152 | tf_op jit(solution)/shard_map/all_to_all | solution.py:238
  72.5 2.0 %copy-done = bf16[2,14336,64]{1,2,0:T(8,128)(2,1)S(1)} copy-done((bf16[2,14336,64]{1,2,0:T(8,128)(2,1)S(1)}, bf16[2,14336,64]{1,2,0:T(8,128)(2,1)}, u32[]{:S(2)}) %copy-start) | copy-done | bytes 3670040
  86.8 9.6 %first_chunks.1 = (f32[256,512]{1,0:T(8,128)S(1)}, f32[256,512]{1,0:T(8,128)S(1)}, f32[128,256]{1,0:T(8,128)S(1)}) custom-call(s32[18]{0:T(128)S(1)} %dynamic-slice_bitcast_fusion.scalars, bf16[32,3584]{1,0:T(8,128)(2,1)S(1)} %copy-done.18, bf16[32,3584]{1,0:T(8,128)(2,1)S(1)} %copy-done.28, bf16[32,3584]{1,0:T(8,128)(2,1)S(1)} %copy-done.34, ...), custom_call_target="tpu_custom_call" | custom-call | flops 8455716864 | bytes 22544384 | tf_op jit(solution)/shard_map/first_chunks/pallas_call | solution.py:137
  96.4 5.3 %last_narrow.1 = f32[128,256]{1,0:T(8,128)S(1)} custom-call(s32[18]{0:T(128)S(1)} %dynamic-slice_bitcast_fusion.scalars, bf16[32,3584]{1,0:T(8,128)(2,1)S(1)} %get-tuple-element.17.refs_0_.refs_1_, bf16[32,3584]{1,0:T(8,128)(2,1)S(1)} %collective-permute-done.refs_1_.refs_2_, bf16[32,3584]{1,0:T(8,128)(2,1)S(1)} %collective-permute-done.1.refs_2_.refs_3_, ...), custom_call_target="tpu_custom_call" | custom-call | flops 939524096 | bytes 5767168 | tf_op jit(solution)/shard_map/last_narrow/pallas_call | solution.py:137
  101.8 2.1 %collective-permute-start.29 = (f32[64,256]{1,0:T(8,128)S(1)}, f32[64,256]{1,0:T(8,128)S(1)}, u32[]{:S(2)}, u32[]{:S(2)}) collective-permute-start(f32[64,256]{1,0:T(8,128)S(1)} %fusion.refs_0_), channel_id=1, source_target_pairs={{0,2},{1,3},{2,0},{3,1},{4,6},{5,7},{6,4},{7,5},{8,10},{9,11},{10,... | collective-permute-start | bytes 196616 | tf_op jit(solution)/shard_map/ppermute | solution.py:257
  103.9 5.6 %last_sent.1.refs_0_ = f32[256,512]{1,0:T(8,128)S(1)} custom-call(s32[18]{0:T(128)S(1)} %dynamic-slice_bitcast_fusion.scalars, f32[64,256]{1,0:T(8,128)S(1)} %fusion.refs_0_, bf16[32,3584]{1,0:T(8,128)(2,1)S(1)} %get-tuple-element.17.refs_0_.refs_1_, bf16[32,3584]{1,0:T(8,128)(2,1)S(1)} %collective-permute-done.refs_1_.refs_2_, ...), custom_call_target="tpu_custom_call" | custom-call | flops 3758096384 | bytes 12058624 | tf_op jit(solution)/shard_map/last_sent/pallas_call | solution.py:137
  110.1 3.3 %collective-permute-start.33 = (bf16[64,256]{1,0:T(8,128)(2,1)S(1)}, bf16[64,256]{1,0:T(8,128)(2,1)S(1)}, u32[]{:S(2)}, u32[]{:S(2)}) collective-permute-start(bf16[64,256]{1,0:T(8,128)(2,1)S(1)} %add_convert_fusion), channel_id=1, source_target_pairs={{0,12},{2,14},{4,0},{6,2},{8,4},{10,6},{12,8},{14,10},{1,13},{3,15... | collective-permute-start | bytes 98312 | tf_op jit(solution)/shard_map/ppermute | solution.py:261
  116.4 5.6 %last_kept.1.kept = f32[256,512]{1,0:T(8,128)S(1)} custom-call(s32[18]{0:T(128)S(1)} %dynamic-slice_bitcast_fusion.scalars, f32[256,512]{1,0:T(8,128)S(1)} %last_sent.1.refs_0_, bf16[32,3584]{1,0:T(8,128)(2,1)S(1)} %get-tuple-element.17.refs_0_.refs_1_, bf16[32,3584]{1,0:T(8,128)(2,1)S(1)} %collective-permute-done.refs_1_.refs_2_, ...), custom_call_target="tpu_custom_call" | custom-call | flops 3758096384 | bytes 12058624 | tf_op jit(solution)/shard_map/last_kept/pallas_call | solution.py:137
  (130 shorter events, 36.5 us)
Async XLA Ops:
  1.4 12.7 %collective-permute-start.24 = (bf16[32,3584]{1,0:T(8,128)(2,1)S(1)}, bf16[32,3584]{1,0:T(8,128)(2,1)S(1)}, u32[]{:S(2)}, u32[]{:S(2)}) collective-permute-start(bf16[32,3584]{1,0:T(8,128)(2,1)S(1)} %get-tuple-element.15.refs_8_), channel_id=1, source_target_pairs={{0,2},{4,0},{8,4},{12,8},{14,12},{10,14},{6,10},{2,6},{1,3},{5,1},... | collective-permute-start | bytes 688136 | tf_op jit(solution)/shard_map/ppermute | solution.py:234
  4.4 9.8 %collective-permute-start.21 = (bf16[32,3584]{1,0:T(8,128)(2,1)S(1)}, bf16[32,3584]{1,0:T(8,128)(2,1)S(1)}, u32[]{:S(2)}, u32[]{:S(2)}) collective-permute-start(bf16[32,3584]{1,0:T(8,128)(2,1)S(1)} %get-tuple-element.15.refs_8_), channel_id=1, source_target_pairs={{0,4},{4,8},{8,12},{12,14},{14,10},{10,6},{6,2},{2,0},{1,5},{5,9},... | collective-permute-start | bytes 688136 | tf_op jit(solution)/shard_map/ppermute | solution.py:234
  4.5 11.6 %collective-permute-start.18 = (bf16[32,3584]{1,0:T(8,128)(2,1)S(1)}, bf16[32,3584]{1,0:T(8,128)(2,1)S(1)}, u32[]{:S(2)}, u32[]{:S(2)}) collective-permute-start(bf16[32,3584]{1,0:T(8,128)(2,1)S(1)} %get-tuple-element.18.refs_0_), channel_id=1, source_target_pairs={{0,2},{4,0},{8,4},{12,8},{14,12},{10,14},{6,10},{2,6},{1,3},{5,1},... | collective-permute-start | bytes 688136 | tf_op jit(solution)/shard_map/ppermute | solution.py:234
  6.4 11.4 %collective-permute-start.14 = (bf16[32,3584]{1,0:T(8,128)(2,1)S(1)}, bf16[32,3584]{1,0:T(8,128)(2,1)S(1)}, u32[]{:S(2)}, u32[]{:S(2)}) collective-permute-start(bf16[32,3584]{1,0:T(8,128)(2,1)S(1)} %get-tuple-element.18.refs_0_), channel_id=1, source_target_pairs={{0,4},{4,8},{8,12},{12,14},{14,10},{10,6},{6,2},{2,0},{1,5},{5,9},... | collective-permute-start | bytes 688136 | tf_op jit(solution)/shard_map/ppermute | solution.py:234
  6.6 14.2 %collective-permute-start.4 = (bf16[32,3584]{1,0:T(8,128)(2,1)S(1)}, bf16[32,3584]{1,0:T(8,128)(2,1)S(1)}, u32[]{:S(2)}, u32[]{:S(2)}) collective-permute-start(bf16[32,3584]{1,0:T(8,128)(2,1)S(1)} %get-tuple-element.17.refs_0_.refs_1_), channel_id=1, source_target_pairs={{0,2},{4,0},{8,4},{12,8},{14,12},{10,14},{6,10},{2,6},{1,3},{5,1},... | collective-permute-start | bytes 688136 | tf_op jit(solution)/shard_map/ppermute | solution.py:234
  14.1 9.4 %collective-permute-start = (bf16[32,3584]{1,0:T(8,128)(2,1)S(1)}, bf16[32,3584]{1,0:T(8,128)(2,1)S(1)}, u32[]{:S(2)}, u32[]{:S(2)}) collective-permute-start(bf16[32,3584]{1,0:T(8,128)(2,1)S(1)} %get-tuple-element.17.refs_0_.refs_1_), channel_id=1, source_target_pairs={{0,4},{4,8},{8,12},{12,14},{14,10},{10,6},{6,2},{2,0},{1,5},{5,9},... | collective-permute-start | bytes 688136 | tf_op jit(solution)/shard_map/ppermute | solution.py:234
  14.2 11.4 %collective-permute-start.10 = (bf16[32,3584]{1,0:T(8,128)(2,1)S(1)}, bf16[32,3584]{1,0:T(8,128)(2,1)S(1)}, u32[]{:S(2)}, u32[]{:S(2)}) collective-permute-start(bf16[32,3584]{1,0:T(8,128)(2,1)S(1)} %tie.2.refs_8_.refs_9_), channel_id=1, source_target_pairs={{0,2},{4,0},{8,4},{12,8},{14,12},{10,14},{6,10},{2,6},{1,3},{5,1},... | collective-permute-start | bytes 688136 | tf_op jit(solution)/shard_map/ppermute | solution.py:234
  16.1 12.3 %collective-permute-start.7 = (bf16[32,3584]{1,0:T(8,128)(2,1)S(1)}, bf16[32,3584]{1,0:T(8,128)(2,1)S(1)}, u32[]{:S(2)}, u32[]{:S(2)}) collective-permute-start(bf16[32,3584]{1,0:T(8,128)(2,1)S(1)} %tie.2.refs_8_.refs_9_), channel_id=1, source_target_pairs={{0,4},{4,8},{8,12},{12,14},{14,10},{10,6},{6,2},{2,0},{1,5},{5,9},... | collective-permute-start | bytes 688136 | tf_op jit(solution)/shard_map/ppermute | solution.py:234
  17.9 12.7 %collective-permute-start.25 = (bf16[32,3584]{1,0:T(8,128)(2,1)S(1)}, bf16[32,3584]{1,0:T(8,128)(2,1)S(1)}, u32[]{:S(2)}, u32[]{:S(2)}) collective-permute-start(bf16[32,3584]{1,0:T(8,128)(2,1)S(1)} %collective-permute-done.24.refs_12_), channel_id=1, source_target_pairs={{0,2},{4,0},{8,4},{12,8},{14,12},{10,14},{6,10},{2,6},{1,3},{5,1},... | collective-permute-start | bytes 688136 | tf_op jit(solution)/shard_map/ppermute | solution.py:234
  20.7 11.9 %collective-permute-start.22 = (bf16[32,3584]{1,0:T(8,128)(2,1)S(1)}, bf16[32,3584]{1,0:T(8,128)(2,1)S(1)}, u32[]{:S(2)}, u32[]{:S(2)}) collective-permute-start(bf16[32,3584]{1,0:T(8,128)(2,1)S(1)} %collective-permute-done.21.refs_9_), channel_id=1, source_target_pairs={{0,4},{4,8},{8,12},{12,14},{14,10},{10,6},{6,2},{2,0},{1,5},{5,9},... | collective-permute-start | bytes 688136 | tf_op jit(solution)/shard_map/ppermute | solution.py:234
  23.5 12.1 %collective-permute-start.19 = (bf16[32,3584]{1,0:T(8,128)(2,1)S(1)}, bf16[32,3584]{1,0:T(8,128)(2,1)}, u32[]{:S(2)}, u32[]{:S(2)}) collective-permute-start(bf16[32,3584]{1,0:T(8,128)(2,1)S(1)} %collective-permute-done.18.refs_5_), channel_id=1, source_target_pairs={{0,2},{4,0},{8,4},{12,8},{14,12},{10,14},{6,10},{2,6},{1,3},{5,1},... | collective-permute-start | bytes 688136 | tf_op jit(solution)/shard_map/ppermute | solution.py:234
  25.6 12.0 %collective-permute-start.15 = (bf16[32,3584]{1,0:T(8,128)(2,1)S(1)}, bf16[32,3584]{1,0:T(8,128)(2,1)S(1)}, u32[]{:S(2)}, u32[]{:S(2)}) collective-permute-start(bf16[32,3584]{1,0:T(8,128)(2,1)S(1)} %collective-permute-done.14.refs_1_), channel_id=1, source_target_pairs={{0,4},{4,8},{8,12},{12,14},{14,10},{10,6},{6,2},{2,0},{1,5},{5,9},... | collective-permute-start | bytes 688136 | tf_op jit(solution)/shard_map/ppermute | solution.py:234
  28.4 12.0 %collective-permute-start.5 = (bf16[32,3584]{1,0:T(8,128)(2,1)S(1)}, bf16[32,3584]{1,0:T(8,128)(2,1)S(1)}, u32[]{:S(2)}, u32[]{:S(2)}) collective-permute-start(bf16[32,3584]{1,0:T(8,128)(2,1)S(1)} %collective-permute-done.4.refs_5_.refs_6_), channel_id=1, source_target_pairs={{0,2},{4,0},{8,4},{12,8},{14,12},{10,14},{6,10},{2,6},{1,3},{5,1},... | collective-permute-start | bytes 688136 | tf_op jit(solution)/shard_map/ppermute | solution.py:234
  30.6 12.6 %collective-permute-start.1 = (bf16[32,3584]{1,0:T(8,128)(2,1)S(1)}, bf16[32,3584]{1,0:T(8,128)(2,1)S(1)}, u32[]{:S(2)}, u32[]{:S(2)}) collective-permute-start(bf16[32,3584]{1,0:T(8,128)(2,1)S(1)} %collective-permute-done.refs_1_.refs_2_), channel_id=1, source_target_pairs={{0,4},{4,8},{8,12},{12,14},{14,10},{10,6},{6,2},{2,0},{1,5},{5,9},... | collective-permute-start | bytes 688136 | tf_op jit(solution)/shard_map/ppermute | solution.py:234
  32.6 12.8 %collective-permute-start.11 = (bf16[32,3584]{1,0:T(8,128)(2,1)S(1)}, bf16[32,3584]{1,0:T(8,128)(2,1)S(1)}, u32[]{:S(2)}, u32[]{:S(2)}) collective-permute-start(bf16[32,3584]{1,0:T(8,128)(2,1)S(1)} %collective-permute-done.10.refs_12_.refs_13_), channel_id=1, source_target_pairs={{0,2},{4,0},{8,4},{12,8},{14,12},{10,14},{6,10},{2,6},{1,3},{5,1},... | collective-permute-start | bytes 688136 | tf_op jit(solution)/shard_map/ppermute | solution.py:234
  35.6 11.7 %collective-permute-start.8 = (bf16[32,3584]{1,0:T(8,128)(2,1)S(1)}, bf16[32,3584]{1,0:T(8,128)(2,1)S(1)}, u32[]{:S(2)}, u32[]{:S(2)}) collective-permute-start(bf16[32,3584]{1,0:T(8,128)(2,1)S(1)} %collective-permute-done.7.refs_9_.refs_10_), channel_id=1, source_target_pairs={{0,4},{4,8},{8,12},{12,14},{14,10},{10,6},{6,2},{2,0},{1,5},{5,9},... | collective-permute-start | bytes 688136 | tf_op jit(solution)/shard_map/ppermute | solution.py:234
  37.6 12.7 %collective-permute-start.26 = (bf16[32,3584]{1,0:T(8,128)(2,1)S(1)}, bf16[32,3584]{1,0:T(8,128)(2,1)}, u32[]{:S(2)}, u32[]{:S(2)}) collective-permute-start(bf16[32,3584]{1,0:T(8,128)(2,1)S(1)} %collective-permute-done.25.refs_13_), channel_id=1, source_target_pairs={{0,2},{4,0},{8,4},{12,8},{14,12},{10,14},{6,10},{2,6},{1,3},{5,1},... | collective-permute-start | bytes 688136 | tf_op jit(solution)/shard_map/ppermute | solution.py:234
  40.4 11.9 %collective-permute-start.23 = (bf16[32,3584]{1,0:T(8,128)(2,1)S(1)}, bf16[32,3584]{1,0:T(8,128)(2,1)S(1)}, u32[]{:S(2)}, u32[]{:S(2)}) collective-permute-start(bf16[32,3584]{1,0:T(8,128)(2,1)S(1)} %collective-permute-done.22.refs_10_), channel_id=1, source_target_pairs={{0,4},{4,8},{8,12},{12,14},{14,10},{10,6},{6,2},{2,0},{1,5},{5,9},... | collective-permute-start | bytes 688136 | tf_op jit(solution)/shard_map/ppermute | solution.py:234
  43.1 14.0 %collective-permute-start.16 = (bf16[32,3584]{1,0:T(8,128)(2,1)S(1)}, bf16[32,3584]{1,0:T(8,128)(2,1)}, u32[]{:S(2)}, u32[]{:S(2)}) collective-permute-start(bf16[32,3584]{1,0:T(8,128)(2,1)S(1)} %collective-permute-done.15.refs_2_), channel_id=1, source_target_pairs={{0,4},{4,8},{8,12},{12,14},{14,10},{10,6},{6,2},{2,0},{1,5},{5,9},... | collective-permute-start | bytes 688136 | tf_op jit(solution)/shard_map/ppermute | solution.py:234
  45.4 12.2 %collective-permute-start.20 = (bf16[32,3584]{1,0:T(8,128)(2,1)}, bf16[32,3584]{1,0:T(8,128)(2,1)S(1)}, u32[]{:S(2)}, u32[]{:S(2)}) collective-permute-start(bf16[32,3584]{1,0:T(8,128)(2,1)} %collective-permute-done.19.refs_6_), channel_id=1, source_target_pairs={{0,2},{4,0},{8,4},{12,8},{14,12},{10,14},{6,10},{2,6},{1,3},{5,1},... | collective-permute-start | bytes 688136 | tf_op jit(solution)/shard_map/ppermute | solution.py:234
  47.3 14.7 %collective-permute-start.2 = (bf16[32,3584]{1,0:T(8,128)(2,1)S(1)}, bf16[32,3584]{1,0:T(8,128)(2,1)}, u32[]{:S(2)}, u32[]{:S(2)}) collective-permute-start(bf16[32,3584]{1,0:T(8,128)(2,1)S(1)} %collective-permute-done.1.refs_2_.refs_3_), channel_id=1, source_target_pairs={{0,4},{4,8},{8,12},{12,14},{14,10},{10,6},{6,2},{2,0},{1,5},{5,9},... | collective-permute-start | bytes 688136 | tf_op jit(solution)/shard_map/ppermute | solution.py:234
  50.3 12.0 %collective-permute-start.12 = (bf16[32,3584]{1,0:T(8,128)(2,1)S(1)}, bf16[32,3584]{1,0:T(8,128)(2,1)}, u32[]{:S(2)}, u32[]{:S(2)}) collective-permute-start(bf16[32,3584]{1,0:T(8,128)(2,1)S(1)} %collective-permute-done.11.refs_13_.refs_14_), channel_id=1, source_target_pairs={{0,2},{4,0},{8,4},{12,8},{14,12},{10,14},{6,10},{2,6},{1,3},{5,1},... | collective-permute-start | bytes 688136 | tf_op jit(solution)/shard_map/ppermute | solution.py:234
  52.3 12.6 %collective-permute-start.27 = (bf16[32,3584]{1,0:T(8,128)(2,1)}, bf16[32,3584]{1,0:T(8,128)(2,1)S(1)}, u32[]{:S(2)}, u32[]{:S(2)}) collective-permute-start(bf16[32,3584]{1,0:T(8,128)(2,1)} %collective-permute-done.26.refs_14_), channel_id=1, source_target_pairs={{0,2},{4,0},{8,4},{12,8},{14,12},{10,14},{6,10},{2,6},{1,3},{5,1},... | collective-permute-start | bytes 688136 | tf_op jit(solution)/shard_map/ppermute | solution.py:234
  57.1 9.8 %collective-permute-start.17 = (bf16[32,3584]{1,0:T(8,128)(2,1)}, bf16[32,3584]{1,0:T(8,128)(2,1)S(1)}, u32[]{:S(2)}, u32[]{:S(2)}) collective-permute-start(bf16[32,3584]{1,0:T(8,128)(2,1)} %collective-permute-done.16.refs_3_), channel_id=1, source_target_pairs={{0,4},{4,8},{8,12},{12,14},{14,10},{10,6},{6,2},{2,0},{1,5},{5,9},... | collective-permute-start | bytes 688136 | tf_op jit(solution)/shard_map/ppermute | solution.py:234
  57.6 38.7 %collective-permute-start.6 = (bf16[32,3584]{1,0:T(8,128)(2,1)S(1)}, bf16[32,3584]{1,0:T(8,128)(2,1)}, u32[]{:S(2)}, u32[]{:S(2)}) collective-permute-start(bf16[32,3584]{1,0:T(8,128)(2,1)S(1)} %collective-permute-done.5.refs_6_.refs_7_), channel_id=1, source_target_pairs={{0,2},{4,0},{8,4},{12,8},{14,12},{10,14},{6,10},{2,6},{1,3},{5,1},... | collective-permute-start | bytes 688136 | tf_op jit(solution)/shard_map/ppermute | solution.py:234
  62.0 34.3 %collective-permute-start.9 = (bf16[32,3584]{1,0:T(8,128)(2,1)S(1)}, bf16[32,3584]{1,0:T(8,128)(2,1)}, u32[]{:S(2)}, u32[]{:S(2)}) collective-permute-start(bf16[32,3584]{1,0:T(8,128)(2,1)S(1)} %collective-permute-done.8.refs_10_.refs_11_), channel_id=1, source_target_pairs={{0,4},{4,8},{8,12},{12,14},{14,10},{10,6},{6,2},{2,0},{1,5},{5,9},... | collective-permute-start | bytes 688136 | tf_op jit(solution)/shard_map/ppermute | solution.py:234
  62.3 34.1 %collective-permute-start.3 = (bf16[32,3584]{1,0:T(8,128)(2,1)}, bf16[32,3584]{1,0:T(8,128)(2,1)}, u32[]{:S(2)}, u32[]{:S(2)}) collective-permute-start(bf16[32,3584]{1,0:T(8,128)(2,1)} %collective-permute-done.2.refs_3_.refs_4_), channel_id=1, source_target_pairs={{0,4},{4,8},{8,12},{12,14},{14,10},{10,6},{6,2},{2,0},{1,5},{5,9},... | collective-permute-start | bytes 688136 | tf_op jit(solution)/shard_map/ppermute | solution.py:234
  65.0 31.4 %collective-permute-start.13 = (bf16[32,3584]{1,0:T(8,128)(2,1)}, bf16[32,3584]{1,0:T(8,128)(2,1)}, u32[]{:S(2)}, u32[]{:S(2)}) collective-permute-start(bf16[32,3584]{1,0:T(8,128)(2,1)} %collective-permute-done.12.refs_14_.refs_15_), channel_id=1, source_target_pairs={{0,2},{4,0},{8,4},{12,8},{14,12},{10,14},{6,10},{2,6},{1,3},{5,1},... | collective-permute-start | bytes 688136 | tf_op jit(solution)/shard_map/ppermute | solution.py:234
  67.7 55.3 %all-to-all-start = ((bf16[8,128,512]{2,1,0:T(8,128)(2,1)}), bf16[8,128,512]{2,1,0:T(8,128)(2,1)S(1)}, u32[]{:S(2)}, u32[]{:S(2)}) async-start(bf16[8,128,512]{2,1,0:T(8,128)(2,1)} %tie.3), calls=%async_computation | async-start | bytes 2097152 | tf_op jit(solution)/shard_map/all_to_all | solution.py:238
  109.5 12.6 %collective-permute-start.34 = (f32[256,512]{1,0:T(8,128)S(1)}, f32[256,512]{1,0:T(8,128)S(1)}, u32[]{:S(2)}, u32[]{:S(2)}) collective-permute-start(f32[256,512]{1,0:T(8,128)S(1)} %last_sent.1.refs_0_), channel_id=1, source_target_pairs={{0,1},{1,0},{2,3},{3,2},{4,5},{5,4},{6,7},{7,6},{8,9},{9,8},{10,11... | collective-permute-start | bytes 1572872 | tf_op jit(solution)/shard_map/ppermute | solution.py:262
  110.1 12.0 %collective-permute-start.33 = (bf16[64,256]{1,0:T(8,128)(2,1)S(1)}, bf16[64,256]{1,0:T(8,128)(2,1)S(1)}, u32[]{:S(2)}, u32[]{:S(2)}) collective-permute-start(bf16[64,256]{1,0:T(8,128)(2,1)S(1)} %add_convert_fusion), channel_id=1, source_target_pairs={{0,12},{2,14},{4,0},{6,2},{8,4},{10,6},{12,8},{14,10},{1,13},{3,15... | collective-permute-start | bytes 98312 | tf_op jit(solution)/shard_map/ppermute | solution.py:261
  113.5 8.7 %collective-permute-start.31 = (bf16[64,256]{1,0:T(8,128)(2,1)S(1)}, bf16[64,256]{1,0:T(8,128)(2,1)S(1)}, u32[]{:S(2)}, u32[]{:S(2)}) collective-permute-start(bf16[64,256]{1,0:T(8,128)(2,1)S(1)} %add_convert_fusion), channel_id=1, source_target_pairs={{0,4},{2,6},{4,8},{6,10},{8,12},{10,14},{12,0},{14,2},{1,5},{3,7},... | collective-permute-start | bytes 98312 | tf_op jit(solution)/shard_map/ppermute | solution.py:261
  (41 other events, 386.0 us)

commit v10 on v9

--- a/solution.py
+++ b/solution.py
@@ -17,6 +17,9 @@
 
 def params(mib):
     return pltpu.CompilerParams(vmem_limit_bytes=mib * MIB)
+
+
+placed = pltpu.with_memory_space_constraint
 
 
 def ring_order(n):
@@ -131,7 +134,8 @@
     sizes = [tile for _, _, cuts in spans for _, tile in cuts]
     width = sum(sizes)
     anywhere = pl.BlockSpec(memory_space=pl.ANY)
-    args = [*after, *(piece for pieces, _, _ in chunks for piece in pieces), down, shrink, *(acc or ())]
+    held = [placed(piece, pltpu.VMEM) for pieces, _, _ in chunks for piece in pieces]
+    args = [*after, *held, placed(down, pltpu.HBM), placed(shrink, pltpu.HBM), *(acc or ())]
     shapes = [(rows, share)] * len(sides) + [(ranks, rows)] * narrow
     columns = share * len(sides) + ranks * narrow
     return pl.pallas_call(
@@ -240,14 +244,13 @@
         call = functools.partial(chunk_matmul, scalars, half)
         first, last = chunks[:CHUNKS // 2], chunks[CHUNKS // 2:]
         acc = call(first, down, shrink_rows, None, (0, 1), True, "first_chunks")
-        narrow, = call(last, down, shrink_rows, acc[2:], (), True, "last_narrow")
+        send, narrow = call(last, down, shrink_rows, acc[1:], (1,), True, "last_sent")
         mine = [
             jnp.where((row_slot == store * owned + i)[None, :], narrow[i * rank:(i + 1) * rank], 0.0)
             for i in range(owned)
         ]
         mine = sum(mine[1:], mine[0])
-        send, = call(last, down, shrink_rows, acc[1:2], (1,), False, "last_sent", [mine])
-        kept, = call(last, down, shrink_rows, acc[:1], (0,), False, "last_kept", [send])
+        kept, = call(last, down, shrink_rows, acc[:1], (0,), False, "last_kept", [mine])
         where = [(s, t) for s in range(n) for t in range(cores)]
         whole = mine
         for ds in range(2):

time: 126 us -> 128 us (1.016)
  Pallas kernels: 30.7 us -> 27.1 us
  waiting for transfers between devices: 14.9 us -> 17.6 us
    pallas_call x4 -> x3, Pallas kernels: 26.1 us -> 22.4 us  [chunk_matmul(): pl.pallas_call(functools.partial(matmul_kernel, n, len(after), spans, hal...]
    ppermute x3, waiting for transfers between devices: 0.01 us -> 2.61 us  [shards(): whole = whole + lax.ppermute(mine, ('store', 'tensor'), pairs)]
    unnamed x74 -> x82, local copies, waits for them, and re-layouts: 25.1 us -> 25.8 us
  transfers between devices with their start and end apart: 36 -> 36, of which waited for: 9 -> 11; matrix products, arithmetic and copies ran while one was open for 1% -> 1% of each run, Pallas kernels for 23% -> 20%
where the time goes in v10:
time: 128 us; the launch traced here: 127 us
  starting transfers between devices  52.9 us (41%)
  local copies, waits for them, and re-layouts  27.9 us (22%)
  Pallas kernels  27.1 us (21%)
  waiting for transfers between devices  17.6 us (14%)
    ppermute x28, starting transfers between devices, shards(): moving = lax.ppermute(moving, 'store', pairs)  40 us
    unnamed x82, local copies, waits for them, and re-layouts  25.8 us
    pallas_call x3, Pallas kernels, chunk_matmul(): pl.pallas_call(functools.partial(matmul_kernel, n, len(after), spans, hal...  22.4 us
    ppermute x28, waiting for transfers between devices, shards(): moving = lax.ppermute(moving, 'store', pairs)  15 us
    ppermute x3, starting transfers between devices, shards(): lax.ppermute(column, 'store', [(s, (s + ds) % n) for s in range(n)])  5.37 us
    all_to_all x1, starting transfers between devices, shards(): factors = lax.all_to_all(tie(blocks, ends[:4]), 'store', 0, 0)  4.88 us
    pallas_call x1, Pallas kernels, expand_blocks(): pl.pallas_call(split_kernel, grid_spec=pltpu.PrefetchScalarGridSpec(num_s...  3.36 us
    ppermute x3, waiting for transfers between devices, shards(): whole = whole + lax.ppermute(mine, ('store', 'tensor'), pairs)  2.61 us
  transfers between devices with their start and end apart: 36, of which 11 were waited for; matrix products, arithmetic and copies ran while one was open for 1% of the time, Pallas kernels for 20%

profile of v10, /device:TPU:0, one launch (start us, length us, event | category | flops | bytes accessed | tf_op | source)
XLA Modules:
  0.0 126.9 jit_solution(6823774545063467521)
XLA Ops:
  1.4 3.0 %collective-permute-start.24 = (bf16[32,3584]{1,0:T(8,128)(2,1)S(1)}, bf16[32,3584]{1,0:T(8,128)(2,1)S(1)}, u32[]{:S(2)}, u32[]{:S(2)}) collective-permute-start(bf16[32,3584]{1,0:T(8,128)(2,1)S(1)} %get-tuple-element.19.refs_8_), channel_id=1, source_target_pairs={{0,2},{4,0},{8,4},{12,8},{14,12},{10,14},{6,10},{2,6},{1,3},{5,1},... | collective-permute-start | bytes 688136 | tf_op jit(solution)/shard_map/ppermute | solution.py:238
  4.5 1.9 %collective-permute-start.18 = (bf16[32,3584]{1,0:T(8,128)(2,1)S(1)}, bf16[32,3584]{1,0:T(8,128)(2,1)S(1)}, u32[]{:S(2)}, u32[]{:S(2)}) collective-permute-start(bf16[32,3584]{1,0:T(8,128)(2,1)S(1)} %get-tuple-element.22.refs_0_), channel_id=1, source_target_pairs={{0,2},{4,0},{8,4},{12,8},{14,12},{10,14},{6,10},{2,6},{1,3},{5,1},... | collective-permute-start | bytes 688136 | tf_op jit(solution)/shard_map/ppermute | solution.py:238
  6.6 1.9 %collective-permute-start.4 = (bf16[32,3584]{1,0:T(8,128)(2,1)S(1)}, bf16[32,3584]{1,0:T(8,128)(2,1)S(1)}, u32[]{:S(2)}, u32[]{:S(2)}) collective-permute-start(bf16[32,3584]{1,0:T(8,128)(2,1)S(1)} %get-tuple-element.21.refs_0_.refs_1_), channel_id=1, source_target_pairs={{0,2},{4,0},{8,4},{12,8},{14,12},{10,14},{6,10},{2,6},{1,3},{5,1},... | collective-permute-start | bytes 688136 | tf_op jit(solution)/shard_map/ppermute | solution.py:238
  9.2 1.6 %copy-done = bf16[2,64,8192]{2,1,0:T(8,128)(2,1)S(1)} copy-done((bf16[2,64,8192]{2,1,0:T(8,128)(2,1)S(1)}, bf16[2,64,8192]{2,1,0:T(8,128)(2,1)}, u32[]{:S(2)}) %copy-start) | copy-done | bytes 2097176
  10.7 3.4 %expand_blocks.1 = (bf16[8,128,512]{2,1,0:T(8,128)(2,1)}, f32[8,128]{1,0:T(8,128)S(1)}) custom-call(s32[18]{0:T(128)S(1)} %dynamic-slice_bitcast_fusion.scalars, bf16[128,8192]{1,0:T(8,128)(2,1)S(1)} %bitcast.9), custom_call_target="tpu_custom_call" | custom-call | bytes 2097152 | tf_op jit(solution)/shard_map/expand_blocks/pallas_call | solution.py:38
  14.2 1.9 %collective-permute-start.10 = (bf16[32,3584]{1,0:T(8,128)(2,1)S(1)}, bf16[32,3584]{1,0:T(8,128)(2,1)S(1)}, u32[]{:S(2)}, u32[]{:S(2)}) collective-permute-start(bf16[32,3584]{1,0:T(8,128)(2,1)S(1)} %tie.2.refs_8_.refs_9_), channel_id=1, source_target_pairs={{0,2},{4,0},{8,4},{12,8},{14,12},{10,14},{6,10},{2,6},{1,3},{5,1},... | collective-permute-start | bytes 688136 | tf_op jit(solution)/shard_map/ppermute | solution.py:238
  16.1 1.7 %collective-permute-start.7 = (bf16[32,3584]{1,0:T(8,128)(2,1)S(1)}, bf16[32,3584]{1,0:T(8,128)(2,1)S(1)}, u32[]{:S(2)}, u32[]{:S(2)}) collective-permute-start(bf16[32,3584]{1,0:T(8,128)(2,1)S(1)} %tie.2.refs_8_.refs_9_), channel_id=1, source_target_pairs={{0,4},{4,8},{8,12},{12,14},{14,10},{10,6},{6,2},{2,0},{1,5},{5,9},... | collective-permute-start | bytes 688136 | tf_op jit(solution)/shard_map/ppermute | solution.py:238
  20.7 2.1 %collective-permute-start.22 = (bf16[32,3584]{1,0:T(8,128)(2,1)S(1)}, bf16[32,3584]{1,0:T(8,128)(2,1)S(1)}, u32[]{:S(2)}, u32[]{:S(2)}) collective-permute-start(bf16[32,3584]{1,0:T(8,128)(2,1)S(1)} %collective-permute-done.21.refs_9_), channel_id=1, source_target_pairs={{0,4},{4,8},{8,12},{12,14},{14,10},{10,6},{6,2},{2,0},{1,5},{5,9},... | collective-permute-start | bytes 688136 | tf_op jit(solution)/shard_map/ppermute | solution.py:238
  25.6 2.1 %collective-permute-start.15 = (bf16[32,3584]{1,0:T(8,128)(2,1)S(1)}, bf16[32,3584]{1,0:T(8,128)(2,1)S(1)}, u32[]{:S(2)}, u32[]{:S(2)}) collective-permute-start(bf16[32,3584]{1,0:T(8,128)(2,1)S(1)} %collective-permute-done.14.refs_1_), channel_id=1, source_target_pairs={{0,4},{4,8},{8,12},{12,14},{14,10},{10,6},{6,2},{2,0},{1,5},{5,9},... | collective-permute-start | bytes 688136 | tf_op jit(solution)/shard_map/ppermute | solution.py:238
  29.1 1.4 %collective-permute-done.25.refs_13_ = bf16[32,3584]{1,0:T(8,128)(2,1)S(1)} collective-permute-done((bf16[32,3584]{1,0:T(8,128)(2,1)S(1)}, bf16[32,3584]{1,0:T(8,128)(2,1)S(1)}, u32[]{:S(2)}, u32[]{:S(2)}) %collective-permute-start.25) | collective-permute-done | bytes 229408 | tf_op jit(solution)/shard_map/ppermute | solution.py:238
  30.6 2.1 %collective-permute-start.1 = (bf16[32,3584]{1,0:T(8,128)(2,1)S(1)}, bf16[32,3584]{1,0:T(8,128)(2,1)S(1)}, u32[]{:S(2)}, u32[]{:S(2)}) collective-permute-start(bf16[32,3584]{1,0:T(8,128)(2,1)S(1)} %collective-permute-done.refs_1_.refs_2_), channel_id=1, source_target_pairs={{0,4},{4,8},{8,12},{12,14},{14,10},{10,6},{6,2},{2,0},{1,5},{5,9},... | collective-permute-start | bytes 688136 | tf_op jit(solution)/shard_map/ppermute | solution.py:238
  32.6 1.4 %collective-permute-start.11 = (bf16[32,3584]{1,0:T(8,128)(2,1)S(1)}, bf16[32,3584]{1,0:T(8,128)(2,1)S(1)}, u32[]{:S(2)}, u32[]{:S(2)}) collective-permute-start(bf16[32,3584]{1,0:T(8,128)(2,1)S(1)} %collective-permute-done.10.refs_12_.refs_13_), channel_id=1, source_target_pairs={{0,2},{4,0},{8,4},{12,8},{14,12},{10,14},{6,10},{2,6},{1,3},{5,1},... | collective-permute-start | bytes 688136 | tf_op jit(solution)/shard_map/ppermute | solution.py:238
  34.1 1.5 %collective-permute-done.19.refs_6_ = bf16[32,3584]{1,0:T(8,128)(2,1)} collective-permute-done((bf16[32,3584]{1,0:T(8,128)(2,1)S(1)}, bf16[32,3584]{1,0:T(8,128)(2,1)}, u32[]{:S(2)}, u32[]{:S(2)}) %collective-permute-start.19) | collective-permute-done | bytes 229408 | tf_op jit(solution)/shard_map/ppermute | solution.py:238
  35.6 2.1 %collective-permute-start.8 = (bf16[32,3584]{1,0:T(8,128)(2,1)S(1)}, bf16[32,3584]{1,0:T(8,128)(2,1)S(1)}, u32[]{:S(2)}, u32[]{:S(2)}) collective-permute-start(bf16[32,3584]{1,0:T(8,128)(2,1)S(1)} %collective-permute-done.7.refs_9_.refs_10_), channel_id=1, source_target_pairs={{0,4},{4,8},{8,12},{12,14},{14,10},{10,6},{6,2},{2,0},{1,5},{5,9},... | collective-permute-start | bytes 688136 | tf_op jit(solution)/shard_map/ppermute | solution.py:238
  40.4 2.1 %collective-permute-start.23 = (bf16[32,3584]{1,0:T(8,128)(2,1)S(1)}, bf16[32,3584]{1,0:T(8,128)(2,1)S(1)}, u32[]{:S(2)}, u32[]{:S(2)}) collective-permute-start(bf16[32,3584]{1,0:T(8,128)(2,1)S(1)} %collective-permute-done.22.refs_10_), channel_id=1, source_target_pairs={{0,4},{4,8},{8,12},{12,14},{14,10},{10,6},{6,2},{2,0},{1,5},{5,9},... | collective-permute-start | bytes 688136 | tf_op jit(solution)/shard_map/ppermute | solution.py:238
  43.2 1.6 %collective-permute-start.16 = (bf16[32,3584]{1,0:T(8,128)(2,1)S(1)}, bf16[32,3584]{1,0:T(8,128)(2,1)}, u32[]{:S(2)}, u32[]{:S(2)}) collective-permute-start(bf16[32,3584]{1,0:T(8,128)(2,1)S(1)} %collective-permute-done.15.refs_2_), channel_id=1, source_target_pairs={{0,4},{4,8},{8,12},{12,14},{14,10},{10,6},{6,2},{2,0},{1,5},{5,9},... | collective-permute-start | bytes 688136 | tf_op jit(solution)/shard_map/ppermute | solution.py:238
  45.4 1.9 %collective-permute-start.20 = (bf16[32,3584]{1,0:T(8,128)(2,1)}, bf16[32,3584]{1,0:T(8,128)(2,1)S(1)}, u32[]{:S(2)}, u32[]{:S(2)}) collective-permute-start(bf16[32,3584]{1,0:T(8,128)(2,1)} %collective-permute-done.19.refs_6_), channel_id=1, source_target_pairs={{0,2},{4,0},{8,4},{12,8},{14,12},{10,14},{6,10},{2,6},{1,3},{5,1},... | collective-permute-start | bytes 688136 | tf_op jit(solution)/shard_map/ppermute | solution.py:238
  47.5 2.9 %collective-permute-done.26.refs_14_ = bf16[32,3584]{1,0:T(8,128)(2,1)} collective-permute-done((bf16[32,3584]{1,0:T(8,128)(2,1)S(1)}, bf16[32,3584]{1,0:T(8,128)(2,1)}, u32[]{:S(2)}, u32[]{:S(2)}) %collective-permute-start.26) | collective-permute-done | bytes 229408 | tf_op jit(solution)/shard_map/ppermute | solution.py:238
  50.3 2.0 %collective-permute-start.12 = (bf16[32,3584]{1,0:T(8,128)(2,1)S(1)}, bf16[32,3584]{1,0:T(8,128)(2,1)}, u32[]{:S(2)}, u32[]{:S(2)}) collective-permute-start(bf16[32,3584]{1,0:T(8,128)(2,1)S(1)} %collective-permute-done.11.refs_13_.refs_14_), channel_id=1, source_target_pairs={{0,2},{4,0},{8,4},{12,8},{14,12},{10,14},{6,10},{2,6},{1,3},{5,1},... | collective-permute-start | bytes 688136 | tf_op jit(solution)/shard_map/ppermute | solution.py:238
  52.3 1.6 %collective-permute-start.27 = (bf16[32,3584]{1,0:T(8,128)(2,1)}, bf16[32,3584]{1,0:T(8,128)(2,1)S(1)}, u32[]{:S(2)}, u32[]{:S(2)}) collective-permute-start(bf16[32,3584]{1,0:T(8,128)(2,1)} %collective-permute-done.26.refs_14_), channel_id=1, source_target_pairs={{0,2},{4,0},{8,4},{12,8},{14,12},{10,14},{6,10},{2,6},{1,3},{5,1},... | collective-permute-start | bytes 688136 | tf_op jit(solution)/shard_map/ppermute | solution.py:238
  53.9 3.2 %collective-permute-done.16.refs_3_ = bf16[32,3584]{1,0:T(8,128)(2,1)} collective-permute-done((bf16[32,3584]{1,0:T(8,128)(2,1)S(1)}, bf16[32,3584]{1,0:T(8,128)(2,1)}, u32[]{:S(2)}, u32[]{:S(2)}) %collective-permute-start.16) | collective-permute-done | bytes 229408 | tf_op jit(solution)/shard_map/ppermute | solution.py:238
  57.5 1.9 %collective-permute-start.6 = (bf16[32,3584]{1,0:T(8,128)(2,1)S(1)}, bf16[32,3584]{1,0:T(8,128)(2,1)}, u32[]{:S(2)}, u32[]{:S(2)}) collective-permute-start(bf16[32,3584]{1,0:T(8,128)(2,1)S(1)} %collective-permute-done.5.refs_6_.refs_7_), channel_id=1, source_target_pairs={{0,2},{4,0},{8,4},{12,8},{14,12},{10,14},{6,10},{2,6},{1,3},{5,1},... | collective-permute-start | bytes 688136 | tf_op jit(solution)/shard_map/ppermute | solution.py:238
  59.4 2.7 %collective-permute-done.2.refs_3_.refs_4_ = bf16[32,3584]{1,0:T(8,128)(2,1)} collective-permute-done((bf16[32,3584]{1,0:T(8,128)(2,1)S(1)}, bf16[32,3584]{1,0:T(8,128)(2,1)}, u32[]{:S(2)}, u32[]{:S(2)}) %collective-permute-start.2) | collective-permute-done | bytes 229408 | tf_op jit(solution)/shard_map/ppermute | solution.py:238
  62.3 1.9 %collective-permute-start.3 = (bf16[32,3584]{1,0:T(8,128)(2,1)}, bf16[32,3584]{1,0:T(8,128)(2,1)}, u32[]{:S(2)}, u32[]{:S(2)}) collective-permute-start(bf16[32,3584]{1,0:T(8,128)(2,1)} %collective-permute-done.2.refs_3_.refs_4_), channel_id=1, source_target_pairs={{0,4},{4,8},{8,12},{12,14},{14,10},{10,6},{6,2},{2,0},{1,5},{5,9},... | collective-permute-start | bytes 688136 | tf_op jit(solution)/shard_map/ppermute | solution.py:238
  65.0 2.0 %collective-permute-start.13 = (bf16[32,3584]{1,0:T(8,128)(2,1)}, bf16[32,3584]{1,0:T(8,128)(2,1)}, u32[]{:S(2)}, u32[]{:S(2)}) collective-permute-start(bf16[32,3584]{1,0:T(8,128)(2,1)} %collective-permute-done.12.refs_14_.refs_15_), channel_id=1, source_target_pairs={{0,2},{4,0},{8,4},{12,8},{14,12},{10,14},{6,10},{2,6},{1,3},{5,1},... | collective-permute-start | bytes 688136 | tf_op jit(solution)/shard_map/ppermute | solution.py:238
  67.7 4.9 %all-to-all-start = ((bf16[8,128,512]{2,1,0:T(8,128)(2,1)}), bf16[8,128,512]{2,1,0:T(8,128)(2,1)S(1)}, u32[]{:S(2)}, u32[]{:S(2)}) async-start(bf16[8,128,512]{2,1,0:T(8,128)(2,1)} %tie.3), calls=%async_computation | async-start | bytes 2097152 | tf_op jit(solution)/shard_map/all_to_all | solution.py:242
  84.8 9.5 %first_chunks.1 = (f32[256,512]{1,0:T(8,128)S(1)}, f32[256,512]{1,0:T(8,128)S(1)}, f32[128,256]{1,0:T(8,128)S(1)}) custom-call(s32[18]{0:T(128)S(1)} %dynamic-slice_bitcast_fusion.scalars, bf16[32,3584]{1,0:T(8,128)(2,1)S(1)} %copy-done.16, bf16[32,3584]{1,0:T(8,128)(2,1)S(1)} %copy-done.31, bf16[32,3584]{1,0:T(8,128)(2,1)S(1)} %copy-done.37, ...), custom_call_target="tpu_custom_call" | custom-call | flops 8455716864 | bytes 22544384 | tf_op jit(solution)/shard_map/first_chunks/pallas_call | solution.py:141
  95.1 7.3 %last_sent.1 = (f32[256,512]{1,0:T(8,128)S(1)}, f32[128,256]{1,0:T(8,128)S(1)}) custom-call(s32[18]{0:T(128)S(1)} %dynamic-slice_bitcast_fusion.scalars, bf16[32,3584]{1,0:T(8,128)(2,1)S(1)} %get-tuple-element.21.refs_0_.refs_1_, bf16[32,3584]{1,0:T(8,128)(2,1)S(1)} %collective-permute-done.refs_1_.refs_2_, ...), custom_call_target="tpu_custom_call" | custom-call | flops 4697620480 | bytes 14155776 | tf_op jit(solution)/shard_map/last_sent/pallas_call | solution.py:141
  102.5 2.1 %collective-permute-start.29 = (f32[64,256]{1,0:T(8,128)S(1)}, f32[64,256]{1,0:T(8,128)S(1)}, u32[]{:S(2)}, u32[]{:S(2)}) collective-permute-start(f32[64,256]{1,0:T(8,128)S(1)} %select_add_fusion.refs_0_), channel_id=1, source_target_pairs={{0,2},{1,3},{2,0},{3,1},{4,6},{5,7},{6,4},{7,5},{8,10},{9,11},{10,... | collective-permute-start | bytes 196616 | tf_op jit(solution)/shard_map/ppermute | solution.py:260
  106.4 1.6 %collective-permute-done.29 = f32[64,256]{1,0:T(8,128)S(1)} collective-permute-done((f32[64,256]{1,0:T(8,128)S(1)}, f32[64,256]{1,0:T(8,128)S(1)}, u32[]{:S(2)}, u32[]{:S(2)}) %collective-permute-start.29) | collective-permute-done | bytes 65568 | tf_op jit(solution)/shard_map/ppermute | solution.py:260
  108.8 4.2 %collective-permute-start.33 = (bf16[64,256]{1,0:T(8,128)(2,1)S(1)}, bf16[64,256]{1,0:T(8,128)(2,1)S(1)}, u32[]{:S(2)}, u32[]{:S(2)}) collective-permute-start(bf16[64,256]{1,0:T(8,128)(2,1)S(1)} %add_convert_fusion), channel_id=1, source_target_pairs={{0,12},{2,14},{4,0},{6,2},{8,4},{10,6},{12,8},{14,10},{1,13},{3,15... | collective-permute-start | bytes 98312 | tf_op jit(solution)/shard_map/ppermute | solution.py:264
  118.0 5.6 %last_kept.1.kept = f32[256,512]{1,0:T(8,128)S(1)} custom-call(s32[18]{0:T(128)S(1)} %dynamic-slice_bitcast_fusion.scalars, f32[64,256]{1,0:T(8,128)S(1)} %copy-done.23, bf16[32,3584]{1,0:T(8,128)(2,1)S(1)} %get-tuple-element.21.refs_0_.refs_1_, bf16[32,3584]{1,0:T(8,128)(2,1)S(1)} %collective-permute-done.refs_1_.refs_2_, ...), custom_call_target="tpu_custom_call" | custom-call | flops 3758096384 | bytes 12058624 | tf_op jit(solution)/shard_map/last_kept/pallas_call | solution.py:141
  (137 shorter events, 39.8 us)
Async XLA Ops:
  1.4 12.7 %collective-permute-start.24 = (bf16[32,3584]{1,0:T(8,128)(2,1)S(1)}, bf16[32,3584]{1,0:T(8,128)(2,1)S(1)}, u32[]{:S(2)}, u32[]{:S(2)}) collective-permute-start(bf16[32,3584]{1,0:T(8,128)(2,1)S(1)} %get-tuple-element.19.refs_8_), channel_id=1, source_target_pairs={{0,2},{4,0},{8,4},{12,8},{14,12},{10,14},{6,10},{2,6},{1,3},{5,1},... | collective-permute-start | bytes 688136 | tf_op jit(solution)/shard_map/ppermute | solution.py:238
  4.4 9.8 %collective-permute-start.21 = (bf16[32,3584]{1,0:T(8,128)(2,1)S(1)}, bf16[32,3584]{1,0:T(8,128)(2,1)S(1)}, u32[]{:S(2)}, u32[]{:S(2)}) collective-permute-start(bf16[32,3584]{1,0:T(8,128)(2,1)S(1)} %get-tuple-element.19.refs_8_), channel_id=1, source_target_pairs={{0,4},{4,8},{8,12},{12,14},{14,10},{10,6},{6,2},{2,0},{1,5},{5,9},... | collective-permute-start | bytes 688136 | tf_op jit(solution)/shard_map/ppermute | solution.py:238
  4.5 11.6 %collective-permute-start.18 = (bf16[32,3584]{1,0:T(8,128)(2,1)S(1)}, bf16[32,3584]{1,0:T(8,128)(2,1)S(1)}, u32[]{:S(2)}, u32[]{:S(2)}) collective-permute-start(bf16[32,3584]{1,0:T(8,128)(2,1)S(1)} %get-tuple-element.22.refs_0_), channel_id=1, source_target_pairs={{0,2},{4,0},{8,4},{12,8},{14,12},{10,14},{6,10},{2,6},{1,3},{5,1},... | collective-permute-start | bytes 688136 | tf_op jit(solution)/shard_map/ppermute | solution.py:238
  6.4 11.4 %collective-permute-start.14 = (bf16[32,3584]{1,0:T(8,128)(2,1)S(1)}, bf16[32,3584]{1,0:T(8,128)(2,1)S(1)}, u32[]{:S(2)}, u32[]{:S(2)}) collective-permute-start(bf16[32,3584]{1,0:T(8,128)(2,1)S(1)} %get-tuple-element.22.refs_0_), channel_id=1, source_target_pairs={{0,4},{4,8},{8,12},{12,14},{14,10},{10,6},{6,2},{2,0},{1,5},{5,9},... | collective-permute-start | bytes 688136 | tf_op jit(solution)/shard_map/ppermute | solution.py:238
  6.6 14.2 %collective-permute-start.4 = (bf16[32,3584]{1,0:T(8,128)(2,1)S(1)}, bf16[32,3584]{1,0:T(8,128)(2,1)S(1)}, u32[]{:S(2)}, u32[]{:S(2)}) collective-permute-start(bf16[32,3584]{1,0:T(8,128)(2,1)S(1)} %get-tuple-element.21.refs_0_.refs_1_), channel_id=1, source_target_pairs={{0,2},{4,0},{8,4},{12,8},{14,12},{10,14},{6,10},{2,6},{1,3},{5,1},... | collective-permute-start | bytes 688136 | tf_op jit(solution)/shard_map/ppermute | solution.py:238
  14.2 11.4 %collective-permute-start.10 = (bf16[32,3584]{1,0:T(8,128)(2,1)S(1)}, bf16[32,3584]{1,0:T(8,128)(2,1)S(1)}, u32[]{:S(2)}, u32[]{:S(2)}) collective-permute-start(bf16[32,3584]{1,0:T(8,128)(2,1)S(1)} %tie.2.refs_8_.refs_9_), channel_id=1, source_target_pairs={{0,2},{4,0},{8,4},{12,8},{14,12},{10,14},{6,10},{2,6},{1,3},{5,1},... | collective-permute-start | bytes 688136 | tf_op jit(solution)/shard_map/ppermute | solution.py:238
  16.1 12.3 %collective-permute-start.7 = (bf16[32,3584]{1,0:T(8,128)(2,1)S(1)}, bf16[32,3584]{1,0:T(8,128)(2,1)S(1)}, u32[]{:S(2)}, u32[]{:S(2)}) collective-permute-start(bf16[32,3584]{1,0:T(8,128)(2,1)S(1)} %tie.2.refs_8_.refs_9_), channel_id=1, source_target_pairs={{0,4},{4,8},{8,12},{12,14},{14,10},{10,6},{6,2},{2,0},{1,5},{5,9},... | collective-permute-start | bytes 688136 | tf_op jit(solution)/shard_map/ppermute | solution.py:238
  17.9 12.7 %collective-permute-start.25 = (bf16[32,3584]{1,0:T(8,128)(2,1)S(1)}, bf16[32,3584]{1,0:T(8,128)(2,1)S(1)}, u32[]{:S(2)}, u32[]{:S(2)}) collective-permute-start(bf16[32,3584]{1,0:T(8,128)(2,1)S(1)} %collective-permute-done.24.refs_12_), channel_id=1, source_target_pairs={{0,2},{4,0},{8,4},{12,8},{14,12},{10,14},{6,10},{2,6},{1,3},{5,1},... | collective-permute-start | bytes 688136 | tf_op jit(solution)/shard_map/ppermute | solution.py:238
  20.7 11.9 %collective-permute-start.22 = (bf16[32,3584]{1,0:T(8,128)(2,1)S(1)}, bf16[32,3584]{1,0:T(8,128)(2,1)S(1)}, u32[]{:S(2)}, u32[]{:S(2)}) collective-permute-start(bf16[32,3584]{1,0:T(8,128)(2,1)S(1)} %collective-permute-done.21.refs_9_), channel_id=1, source_target_pairs={{0,4},{4,8},{8,12},{12,14},{14,10},{10,6},{6,2},{2,0},{1,5},{5,9},... | collective-permute-start | bytes 688136 | tf_op jit(solution)/shard_map/ppermute | solution.py:238
  23.5 12.1 %collective-permute-start.19 = (bf16[32,3584]{1,0:T(8,128)(2,1)S(1)}, bf16[32,3584]{1,0:T(8,128)(2,1)}, u32[]{:S(2)}, u32[]{:S(2)}) collective-permute-start(bf16[32,3584]{1,0:T(8,128)(2,1)S(1)} %collective-permute-done.18.refs_5_), channel_id=1, source_target_pairs={{0,2},{4,0},{8,4},{12,8},{14,12},{10,14},{6,10},{2,6},{1,3},{5,1},... | collective-permute-start | bytes 688136 | tf_op jit(solution)/shard_map/ppermute | solution.py:238
  25.6 12.0 %collective-permute-start.15 = (bf16[32,3584]{1,0:T(8,128)(2,1)S(1)}, bf16[32,3584]{1,0:T(8,128)(2,1)S(1)}, u32[]{:S(2)}, u32[]{:S(2)}) collective-permute-start(bf16[32,3584]{1,0:T(8,128)(2,1)S(1)} %collective-permute-done.14.refs_1_), channel_id=1, source_target_pairs={{0,4},{4,8},{8,12},{12,14},{14,10},{10,6},{6,2},{2,0},{1,5},{5,9},... | collective-permute-start | bytes 688136 | tf_op jit(solution)/shard_map/ppermute | solution.py:238
  28.4 12.0 %collective-permute-start.5 = (bf16[32,3584]{1,0:T(8,128)(2,1)S(1)}, bf16[32,3584]{1,0:T(8,128)(2,1)S(1)}, u32[]{:S(2)}, u32[]{:S(2)}) collective-permute-start(bf16[32,3584]{1,0:T(8,128)(2,1)S(1)} %collective-permute-done.4.refs_5_.refs_6_), channel_id=1, source_target_pairs={{0,2},{4,0},{8,4},{12,8},{14,12},{10,14},{6,10},{2,6},{1,3},{5,1},... | collective-permute-start | bytes 688136 | tf_op jit(solution)/shard_map/ppermute | solution.py:238
  30.6 12.6 %collective-permute-start.1 = (bf16[32,3584]{1,0:T(8,128)(2,1)S(1)}, bf16[32,3584]{1,0:T(8,128)(2,1)S(1)}, u32[]{:S(2)}, u32[]{:S(2)}) collective-permute-start(bf16[32,3584]{1,0:T(8,128)(2,1)S(1)} %collective-permute-done.refs_1_.refs_2_), channel_id=1, source_target_pairs={{0,4},{4,8},{8,12},{12,14},{14,10},{10,6},{6,2},{2,0},{1,5},{5,9},... | collective-permute-start | bytes 688136 | tf_op jit(solution)/shard_map/ppermute | solution.py:238
  32.6 12.8 %collective-permute-start.11 = (bf16[32,3584]{1,0:T(8,128)(2,1)S(1)}, bf16[32,3584]{1,0:T(8,128)(2,1)S(1)}, u32[]{:S(2)}, u32[]{:S(2)}) collective-permute-start(bf16[32,3584]{1,0:T(8,128)(2,1)S(1)} %collective-permute-done.10.refs_12_.refs_13_), channel_id=1, source_target_pairs={{0,2},{4,0},{8,4},{12,8},{14,12},{10,14},{6,10},{2,6},{1,3},{5,1},... | collective-permute-start | bytes 688136 | tf_op jit(solution)/shard_map/ppermute | solution.py:238
  35.6 11.7 %collective-permute-start.8 = (bf16[32,3584]{1,0:T(8,128)(2,1)S(1)}, bf16[32,3584]{1,0:T(8,128)(2,1)S(1)}, u32[]{:S(2)}, u32[]{:S(2)}) collective-permute-start(bf16[32,3584]{1,0:T(8,128)(2,1)S(1)} %collective-permute-done.7.refs_9_.refs_10_), channel_id=1, source_target_pairs={{0,4},{4,8},{8,12},{12,14},{14,10},{10,6},{6,2},{2,0},{1,5},{5,9},... | collective-permute-start | bytes 688136 | tf_op jit(solution)/shard_map/ppermute | solution.py:238
  37.6 12.7 %collective-permute-start.26 = (bf16[32,3584]{1,0:T(8,128)(2,1)S(1)}, bf16[32,3584]{1,0:T(8,128)(2,1)}, u32[]{:S(2)}, u32[]{:S(2)}) collective-permute-start(bf16[32,3584]{1,0:T(8,128)(2,1)S(1)} %collective-permute-done.25.refs_13_), channel_id=1, source_target_pairs={{0,2},{4,0},{8,4},{12,8},{14,12},{10,14},{6,10},{2,6},{1,3},{5,1},... | collective-permute-start | bytes 688136 | tf_op jit(solution)/shard_map/ppermute | solution.py:238
  40.4 11.9 %collective-permute-start.23 = (bf16[32,3584]{1,0:T(8,128)(2,1)S(1)}, bf16[32,3584]{1,0:T(8,128)(2,1)S(1)}, u32[]{:S(2)}, u32[]{:S(2)}) collective-permute-start(bf16[32,3584]{1,0:T(8,128)(2,1)S(1)} %collective-permute-done.22.refs_10_), channel_id=1, source_target_pairs={{0,4},{4,8},{8,12},{12,14},{14,10},{10,6},{6,2},{2,0},{1,5},{5,9},... | collective-permute-start | bytes 688136 | tf_op jit(solution)/shard_map/ppermute | solution.py:238
  43.2 14.0 %collective-permute-start.16 = (bf16[32,3584]{1,0:T(8,128)(2,1)S(1)}, bf16[32,3584]{1,0:T(8,128)(2,1)}, u32[]{:S(2)}, u32[]{:S(2)}) collective-permute-start(bf16[32,3584]{1,0:T(8,128)(2,1)S(1)} %collective-permute-done.15.refs_2_), channel_id=1, source_target_pairs={{0,4},{4,8},{8,12},{12,14},{14,10},{10,6},{6,2},{2,0},{1,5},{5,9},... | collective-permute-start | bytes 688136 | tf_op jit(solution)/shard_map/ppermute | solution.py:238
  45.4 12.0 %collective-permute-start.20 = (bf16[32,3584]{1,0:T(8,128)(2,1)}, bf16[32,3584]{1,0:T(8,128)(2,1)S(1)}, u32[]{:S(2)}, u32[]{:S(2)}) collective-permute-start(bf16[32,3584]{1,0:T(8,128)(2,1)} %collective-permute-done.19.refs_6_), channel_id=1, source_target_pairs={{0,2},{4,0},{8,4},{12,8},{14,12},{10,14},{6,10},{2,6},{1,3},{5,1},... | collective-permute-start | bytes 688136 | tf_op jit(solution)/shard_map/ppermute | solution.py:238
  47.3 14.8 %collective-permute-start.2 = (bf16[32,3584]{1,0:T(8,128)(2,1)S(1)}, bf16[32,3584]{1,0:T(8,128)(2,1)}, u32[]{:S(2)}, u32[]{:S(2)}) collective-permute-start(bf16[32,3584]{1,0:T(8,128)(2,1)S(1)} %collective-permute-done.1.refs_2_.refs_3_), channel_id=1, source_target_pairs={{0,4},{4,8},{8,12},{12,14},{14,10},{10,6},{6,2},{2,0},{1,5},{5,9},... | collective-permute-start | bytes 688136 | tf_op jit(solution)/shard_map/ppermute | solution.py:238
  50.3 12.0 %collective-permute-start.12 = (bf16[32,3584]{1,0:T(8,128)(2,1)S(1)}, bf16[32,3584]{1,0:T(8,128)(2,1)}, u32[]{:S(2)}, u32[]{:S(2)}) collective-permute-start(bf16[32,3584]{1,0:T(8,128)(2,1)S(1)} %collective-permute-done.11.refs_13_.refs_14_), channel_id=1, source_target_pairs={{0,2},{4,0},{8,4},{12,8},{14,12},{10,14},{6,10},{2,6},{1,3},{5,1},... | collective-permute-start | bytes 688136 | tf_op jit(solution)/shard_map/ppermute | solution.py:238
  52.3 12.6 %collective-permute-start.27 = (bf16[32,3584]{1,0:T(8,128)(2,1)}, bf16[32,3584]{1,0:T(8,128)(2,1)S(1)}, u32[]{:S(2)}, u32[]{:S(2)}) collective-permute-start(bf16[32,3584]{1,0:T(8,128)(2,1)} %collective-permute-done.26.refs_14_), channel_id=1, source_target_pairs={{0,2},{4,0},{8,4},{12,8},{14,12},{10,14},{6,10},{2,6},{1,3},{5,1},... | collective-permute-start | bytes 688136 | tf_op jit(solution)/shard_map/ppermute | solution.py:238
  57.2 9.8 %collective-permute-start.17 = (bf16[32,3584]{1,0:T(8,128)(2,1)}, bf16[32,3584]{1,0:T(8,128)(2,1)S(1)}, u32[]{:S(2)}, u32[]{:S(2)}) collective-permute-start(bf16[32,3584]{1,0:T(8,128)(2,1)} %collective-permute-done.16.refs_3_), channel_id=1, source_target_pairs={{0,4},{4,8},{8,12},{12,14},{14,10},{10,6},{6,2},{2,0},{1,5},{5,9},... | collective-permute-start | bytes 688136 | tf_op jit(solution)/shard_map/ppermute | solution.py:238
  57.5 37.5 %collective-permute-start.6 = (bf16[32,3584]{1,0:T(8,128)(2,1)S(1)}, bf16[32,3584]{1,0:T(8,128)(2,1)}, u32[]{:S(2)}, u32[]{:S(2)}) collective-permute-start(bf16[32,3584]{1,0:T(8,128)(2,1)S(1)} %collective-permute-done.5.refs_6_.refs_7_), channel_id=1, source_target_pairs={{0,2},{4,0},{8,4},{12,8},{14,12},{10,14},{6,10},{2,6},{1,3},{5,1},... | collective-permute-start | bytes 688136 | tf_op jit(solution)/shard_map/ppermute | solution.py:238
  62.1 33.0 %collective-permute-start.9 = (bf16[32,3584]{1,0:T(8,128)(2,1)S(1)}, bf16[32,3584]{1,0:T(8,128)(2,1)}, u32[]{:S(2)}, u32[]{:S(2)}) collective-permute-start(bf16[32,3584]{1,0:T(8,128)(2,1)S(1)} %collective-permute-done.8.refs_10_.refs_11_), channel_id=1, source_target_pairs={{0,4},{4,8},{8,12},{12,14},{14,10},{10,6},{6,2},{2,0},{1,5},{5,9},... | collective-permute-start | bytes 688136 | tf_op jit(solution)/shard_map/ppermute | solution.py:238
  62.3 32.8 %collective-permute-start.3 = (bf16[32,3584]{1,0:T(8,128)(2,1)}, bf16[32,3584]{1,0:T(8,128)(2,1)}, u32[]{:S(2)}, u32[]{:S(2)}) collective-permute-start(bf16[32,3584]{1,0:T(8,128)(2,1)} %collective-permute-done.2.refs_3_.refs_4_), channel_id=1, source_target_pairs={{0,4},{4,8},{8,12},{12,14},{14,10},{10,6},{6,2},{2,0},{1,5},{5,9},... | collective-permute-start | bytes 688136 | tf_op jit(solution)/shard_map/ppermute | solution.py:238
  65.0 30.1 %collective-permute-start.13 = (bf16[32,3584]{1,0:T(8,128)(2,1)}, bf16[32,3584]{1,0:T(8,128)(2,1)}, u32[]{:S(2)}, u32[]{:S(2)}) collective-permute-start(bf16[32,3584]{1,0:T(8,128)(2,1)} %collective-permute-done.12.refs_14_.refs_15_), channel_id=1, source_target_pairs={{0,2},{4,0},{8,4},{12,8},{14,12},{10,14},{6,10},{2,6},{1,3},{5,1},... | collective-permute-start | bytes 688136 | tf_op jit(solution)/shard_map/ppermute | solution.py:238
  67.7 56.8 %all-to-all-start = ((bf16[8,128,512]{2,1,0:T(8,128)(2,1)}), bf16[8,128,512]{2,1,0:T(8,128)(2,1)S(1)}, u32[]{:S(2)}, u32[]{:S(2)}) async-start(bf16[8,128,512]{2,1,0:T(8,128)(2,1)} %tie.3), calls=%async_computation | async-start | bytes 2097152 | tf_op jit(solution)/shard_map/all_to_all | solution.py:242
  104.8 18.9 %collective-permute-start.34 = (f32[256,512]{1,0:T(8,128)}, f32[256,512]{1,0:T(8,128)S(1)}, u32[]{:S(2)}, u32[]{:S(2)}) collective-permute-start(f32[256,512]{1,0:T(8,128)} %copy-done.38), channel_id=1, source_target_pairs={{0,1},{1,0},{2,3},{3,2},{4,5},{5,4},{6,7},{7,6},{8,9},{9,8},{10,11... | collective-permute-start | bytes 1572872 | tf_op jit(solution)/shard_map/ppermute | solution.py:265
  108.8 14.8 %collective-permute-start.33 = (bf16[64,256]{1,0:T(8,128)(2,1)S(1)}, bf16[64,256]{1,0:T(8,128)(2,1)S(1)}, u32[]{:S(2)}, u32[]{:S(2)}) collective-permute-start(bf16[64,256]{1,0:T(8,128)(2,1)S(1)} %add_convert_fusion), channel_id=1, source_target_pairs={{0,12},{2,14},{4,0},{6,2},{8,4},{10,6},{12,8},{14,10},{1,13},{3,15... | collective-permute-start | bytes 98312 | tf_op jit(solution)/shard_map/ppermute | solution.py:264
  113.1 10.5 %collective-permute-start.32 = (bf16[64,256]{1,0:T(8,128)(2,1)S(1)}, bf16[64,256]{1,0:T(8,128)(2,1)S(1)}, u32[]{:S(2)}, u32[]{:S(2)}) collective-permute-start(bf16[64,256]{1,0:T(8,128)(2,1)S(1)} %add_convert_fusion), channel_id=1, source_target_pairs={{0,8},{2,10},{4,12},{6,14},{8,0},{10,2},{12,4},{14,6},{1,9},{3,11}... | collective-permute-start | bytes 98312 | tf_op jit(solution)/shard_map/ppermute | solution.py:264
  113.1 10.6 %collective-permute-start.31 = (bf16[64,256]{1,0:T(8,128)(2,1)S(1)}, bf16[64,256]{1,0:T(8,128)(2,1)S(1)}, u32[]{:S(2)}, u32[]{:S(2)}) collective-permute-start(bf16[64,256]{1,0:T(8,128)(2,1)S(1)} %add_convert_fusion), channel_id=1, source_target_pairs={{0,4},{2,6},{4,8},{6,10},{8,12},{10,14},{12,0},{14,2},{1,5},{3,7},... | collective-permute-start | bytes 98312 | tf_op jit(solution)/shard_map/ppermute | solution.py:264
  (45 other events, 366.4 us)

commit v11 on v9

--- a/solution.py
+++ b/solution.py
@@ -17,6 +17,10 @@
 
 def params(mib):
     return pltpu.CompilerParams(vmem_limit_bytes=mib * MIB)
+
+
+def in_hbm(array):
+    return pltpu.with_memory_space_constraint(array, pltpu.HBM)
 
 
 def ring_order(n):
@@ -131,7 +135,13 @@
     sizes = [tile for _, _, cuts in spans for _, tile in cuts]
     width = sum(sizes)
     anywhere = pl.BlockSpec(memory_space=pl.ANY)
-    args = [*after, *(piece for pieces, _, _ in chunks for piece in pieces), down, shrink, *(acc or ())]
+    held = [
+        piece if i in late else in_hbm(piece)
+        for pieces, base, _ in chunks
+        for late in [(3, 4, n - 1) if base == 0 else (3, n - 2, n - 1)]
+        for i, piece in enumerate(pieces)
+    ]
+    args = [*after, *held, in_hbm(down), in_hbm(shrink), *(acc or ())]
     shapes = [(rows, share)] * len(sides) + [(ranks, rows)] * narrow
     columns = share * len(sides) + ranks * narrow
     return pl.pallas_call(

time: 126 us -> 113 us (0.90)
  local copies, waits for them, and re-layouts: 27.2 us -> 9.83 us
  waiting for transfers between devices: 14.9 us -> 17.3 us
  starting transfers between devices: 52 us -> 53.7 us
    unnamed x74 -> x56, local copies, waits for them, and re-layouts: 25.1 us -> 7.64 us
    ppermute x28, waiting for transfers between devices: 14.9 us -> 17.3 us  [shards(): moving = lax.ppermute(moving, 'store', pairs)]
    ppermute x28, starting transfers between devices: 39.9 us -> 41.7 us  [shards(): moving = lax.ppermute(moving, 'store', pairs)]
  transfers between devices with their start and end apart: 36 -> 36, of which waited for: 9 -> 10; matrix products, arithmetic and copies ran while one was open for 1% -> 1% of each run, Pallas kernels for 23% -> 26%
where the time goes in v11:
time: 113 us; the launch traced here: 112 us
  starting transfers between devices  53.7 us (48%)
  Pallas kernels  30.9 us (27%)
  waiting for transfers between devices  17.3 us (15%)
  local copies, waits for them, and re-layouts  9.83 us (9%)
    ppermute x28, starting transfers between devices, shards(): moving = lax.ppermute(moving, 'store', pairs)  41.7 us
    pallas_call x4, Pallas kernels, chunk_matmul(): pl.pallas_call(functools.partial(matmul_kernel, n, len(after), spans, hal...  26.2 us
    ppermute x28, waiting for transfers between devices, shards(): moving = lax.ppermute(moving, 'store', pairs)  17.3 us
    unnamed x56, local copies, waits for them, and re-layouts  7.64 us
    all_to_all x1, starting transfers between devices, shards(): factors = lax.all_to_all(tie(blocks, ends[:4]), 'store', 0, 0)  4.88 us
    ppermute x3, starting transfers between devices, shards(): lax.ppermute(column, 'store', [(s, (s + ds) % n) for s in range(n)])  4.44 us
    pallas_call x1, Pallas kernels, expand_blocks(): pl.pallas_call(split_kernel, grid_spec=pltpu.PrefetchScalarGridSpec(num_s...  3.32 us
  transfers between devices with their start and end apart: 36, of which 10 were waited for; matrix products, arithmetic and copies ran while one was open for 1% of the time, Pallas kernels for 26%

profile of v11, /device:TPU:0, one launch (start us, length us, event | category | flops | bytes accessed | tf_op | source)
XLA Modules:
  0.0 112.1 jit_solution(18127532764245672140)
XLA Ops:
  1.4 3.0 %collective-permute-start.24 = (bf16[32,3584]{1,0:T(8,128)(2,1)S(1)}, bf16[32,3584]{1,0:T(8,128)(2,1)S(1)}, u32[]{:S(2)}, u32[]{:S(2)}) collective-permute-start(bf16[32,3584]{1,0:T(8,128)(2,1)S(1)} %get-tuple-element.15.refs_8_), channel_id=1, source_target_pairs={{0,2},{4,0},{8,4},{12,8},{14,12},{10,14},{6,10},{2,6},{1,3},{5,1},... | collective-permute-start | bytes 688136 | tf_op jit(solution)/shard_map/ppermute | solution.py:244
  4.5 1.9 %collective-permute-start.18 = (bf16[32,3584]{1,0:T(8,128)(2,1)S(1)}, bf16[32,3584]{1,0:T(8,128)(2,1)S(1)}, u32[]{:S(2)}, u32[]{:S(2)}) collective-permute-start(bf16[32,3584]{1,0:T(8,128)(2,1)S(1)} %get-tuple-element.18.refs_0_), channel_id=1, source_target_pairs={{0,2},{4,0},{8,4},{12,8},{14,12},{10,14},{6,10},{2,6},{1,3},{5,1},... | collective-permute-start | bytes 688136 | tf_op jit(solution)/shard_map/ppermute | solution.py:244
  6.6 1.9 %collective-permute-start.4 = (bf16[32,3584]{1,0:T(8,128)(2,1)S(1)}, bf16[32,3584]{1,0:T(8,128)(2,1)S(1)}, u32[]{:S(2)}, u32[]{:S(2)}) collective-permute-start(bf16[32,3584]{1,0:T(8,128)(2,1)S(1)} %get-tuple-element.17.refs_0_.refs_1_), channel_id=1, source_target_pairs={{0,2},{4,0},{8,4},{12,8},{14,12},{10,14},{6,10},{2,6},{1,3},{5,1},... | collective-permute-start | bytes 688136 | tf_op jit(solution)/shard_map/ppermute | solution.py:244
  9.2 1.6 %copy-done.1 = bf16[2,64,8192]{2,1,0:T(8,128)(2,1)S(1)} copy-done((bf16[2,64,8192]{2,1,0:T(8,128)(2,1)S(1)}, bf16[2,64,8192]{2,1,0:T(8,128)(2,1)}, u32[]{:S(2)}) %copy-start.1) | copy-done | bytes 2097176
  10.8 3.3 %expand_blocks.1 = (bf16[8,128,512]{2,1,0:T(8,128)(2,1)}, f32[8,128]{1,0:T(8,128)S(1)}) custom-call(s32[18]{0:T(128)S(1)} %dynamic-slice_bitcast_fusion.scalars, bf16[128,8192]{1,0:T(8,128)(2,1)S(1)} %bitcast.9), custom_call_target="tpu_custom_call" | custom-call | bytes 2097152 | tf_op jit(solution)/shard_map/expand_blocks/pallas_call | solution.py:39
  14.3 2.0 %collective-permute-start.10 = (bf16[32,3584]{1,0:T(8,128)(2,1)S(1)}, bf16[32,3584]{1,0:T(8,128)(2,1)S(1)}, u32[]{:S(2)}, u32[]{:S(2)}) collective-permute-start(bf16[32,3584]{1,0:T(8,128)(2,1)S(1)} %tie.2.refs_8_.refs_9_), channel_id=1, source_target_pairs={{0,2},{4,0},{8,4},{12,8},{14,12},{10,14},{6,10},{2,6},{1,3},{5,1},... | collective-permute-start | bytes 688136 | tf_op jit(solution)/shard_map/ppermute | solution.py:244
  16.2 1.7 %collective-permute-start.7 = (bf16[32,3584]{1,0:T(8,128)(2,1)S(1)}, bf16[32,3584]{1,0:T(8,128)(2,1)S(1)}, u32[]{:S(2)}, u32[]{:S(2)}) collective-permute-start(bf16[32,3584]{1,0:T(8,128)(2,1)S(1)} %tie.2.refs_8_.refs_9_), channel_id=1, source_target_pairs={{0,4},{4,8},{8,12},{12,14},{14,10},{10,6},{6,2},{2,0},{1,5},{5,9},... | collective-permute-start | bytes 688136 | tf_op jit(solution)/shard_map/ppermute | solution.py:244
  19.1 1.6 %collective-permute-done.4.refs_5_.refs_6_ = bf16[32,3584]{1,0:T(8,128)(2,1)S(1)} collective-permute-done((bf16[32,3584]{1,0:T(8,128)(2,1)S(1)}, bf16[32,3584]{1,0:T(8,128)(2,1)S(1)}, u32[]{:S(2)}, u32[]{:S(2)}) %collective-permute-start.4) | collective-permute-done | bytes 229408 | tf_op jit(solution)/shard_map/ppermute | solution.py:244
  20.7 2.1 %collective-permute-start.22 = (bf16[32,3584]{1,0:T(8,128)(2,1)S(1)}, bf16[32,3584]{1,0:T(8,128)(2,1)S(1)}, u32[]{:S(2)}, u32[]{:S(2)}) collective-permute-start(bf16[32,3584]{1,0:T(8,128)(2,1)S(1)} %collective-permute-done.21.refs_9_), channel_id=1, source_target_pairs={{0,4},{4,8},{8,12},{12,14},{14,10},{10,6},{6,2},{2,0},{1,5},{5,9},... | collective-permute-start | bytes 688136 | tf_op jit(solution)/shard_map/ppermute | solution.py:244
  25.7 2.1 %collective-permute-start.15 = (bf16[32,3584]{1,0:T(8,128)(2,1)S(1)}, bf16[32,3584]{1,0:T(8,128)(2,1)S(1)}, u32[]{:S(2)}, u32[]{:S(2)}) collective-permute-start(bf16[32,3584]{1,0:T(8,128)(2,1)S(1)} %collective-permute-done.14.refs_1_), channel_id=1, source_target_pairs={{0,4},{4,8},{8,12},{12,14},{14,10},{10,6},{6,2},{2,0},{1,5},{5,9},... | collective-permute-start | bytes 688136 | tf_op jit(solution)/shard_map/ppermute | solution.py:244
  30.6 2.1 %collective-permute-start.1 = (bf16[32,3584]{1,0:T(8,128)(2,1)S(1)}, bf16[32,3584]{1,0:T(8,128)(2,1)S(1)}, u32[]{:S(2)}, u32[]{:S(2)}) collective-permute-start(bf16[32,3584]{1,0:T(8,128)(2,1)S(1)} %collective-permute-done.refs_1_.refs_2_), channel_id=1, source_target_pairs={{0,4},{4,8},{8,12},{12,14},{14,10},{10,6},{6,2},{2,0},{1,5},{5,9},... | collective-permute-start | bytes 688136 | tf_op jit(solution)/shard_map/ppermute | solution.py:244
  34.1 1.5 %collective-permute-done.19.refs_6_ = bf16[32,3584]{1,0:T(8,128)(2,1)} collective-permute-done((bf16[32,3584]{1,0:T(8,128)(2,1)S(1)}, bf16[32,3584]{1,0:T(8,128)(2,1)}, u32[]{:S(2)}, u32[]{:S(2)}) %collective-permute-start.19) | collective-permute-done | bytes 229408 | tf_op jit(solution)/shard_map/ppermute | solution.py:244
  35.6 2.1 %collective-permute-start.8 = (bf16[32,3584]{1,0:T(8,128)(2,1)S(1)}, bf16[32,3584]{1,0:T(8,128)(2,1)}, u32[]{:S(2)}, u32[]{:S(2)}) collective-permute-start(bf16[32,3584]{1,0:T(8,128)(2,1)S(1)} %collective-permute-done.7.refs_9_.refs_10_), channel_id=1, source_target_pairs={{0,4},{4,8},{8,12},{12,14},{14,10},{10,6},{6,2},{2,0},{1,5},{5,9},... | collective-permute-start | bytes 688136 | tf_op jit(solution)/shard_map/ppermute | solution.py:244
  39.0 1.5 %collective-permute-done.5.refs_6_.refs_7_ = bf16[32,3584]{1,0:T(8,128)(2,1)} collective-permute-done((bf16[32,3584]{1,0:T(8,128)(2,1)S(1)}, bf16[32,3584]{1,0:T(8,128)(2,1)}, u32[]{:S(2)}, u32[]{:S(2)}) %collective-permute-start.5) | collective-permute-done | bytes 229408 | tf_op jit(solution)/shard_map/ppermute | solution.py:244
  40.5 2.1 %collective-permute-start.23 = (bf16[32,3584]{1,0:T(8,128)(2,1)S(1)}, bf16[32,3584]{1,0:T(8,128)(2,1)S(1)}, u32[]{:S(2)}, u32[]{:S(2)}) collective-permute-start(bf16[32,3584]{1,0:T(8,128)(2,1)S(1)} %collective-permute-done.22.refs_10_), channel_id=1, source_target_pairs={{0,4},{4,8},{8,12},{12,14},{14,10},{10,6},{6,2},{2,0},{1,5},{5,9},... | collective-permute-start | bytes 688136 | tf_op jit(solution)/shard_map/ppermute | solution.py:244
  42.6 1.6 %collective-permute-start.16 = (bf16[32,3584]{1,0:T(8,128)(2,1)S(1)}, bf16[32,3584]{1,0:T(8,128)(2,1)S(1)}, u32[]{:S(2)}, u32[]{:S(2)}) collective-permute-start(bf16[32,3584]{1,0:T(8,128)(2,1)S(1)} %collective-permute-done.15.refs_2_), channel_id=1, source_target_pairs={{0,4},{4,8},{8,12},{12,14},{14,10},{10,6},{6,2},{2,0},{1,5},{5,9},... | collective-permute-start | bytes 688136 | tf_op jit(solution)/shard_map/ppermute | solution.py:244
  45.3 2.0 %collective-permute-start.20 = (bf16[32,3584]{1,0:T(8,128)(2,1)}, bf16[32,3584]{1,0:T(8,128)(2,1)S(1)}, u32[]{:S(2)}, u32[]{:S(2)}) collective-permute-start(bf16[32,3584]{1,0:T(8,128)(2,1)} %collective-permute-done.19.refs_6_), channel_id=1, source_target_pairs={{0,2},{4,0},{8,4},{12,8},{14,12},{10,14},{6,10},{2,6},{1,3},{5,1},... | collective-permute-start | bytes 688136 | tf_op jit(solution)/shard_map/ppermute | solution.py:244
  47.5 2.7 %collective-permute-done.26.refs_14_ = bf16[32,3584]{1,0:T(8,128)(2,1)S(1)} collective-permute-done((bf16[32,3584]{1,0:T(8,128)(2,1)S(1)}, bf16[32,3584]{1,0:T(8,128)(2,1)S(1)}, u32[]{:S(2)}, u32[]{:S(2)}) %collective-permute-start.26) | collective-permute-done | bytes 229408 | tf_op jit(solution)/shard_map/ppermute | solution.py:244
  50.2 2.0 %collective-permute-start.12 = (bf16[32,3584]{1,0:T(8,128)(2,1)S(1)}, bf16[32,3584]{1,0:T(8,128)(2,1)S(1)}, u32[]{:S(2)}, u32[]{:S(2)}) collective-permute-start(bf16[32,3584]{1,0:T(8,128)(2,1)S(1)} %collective-permute-done.11.refs_13_.refs_14_), channel_id=1, source_target_pairs={{0,2},{4,0},{8,4},{12,8},{14,12},{10,14},{6,10},{2,6},{1,3},{5,1},... | collective-permute-start | bytes 688136 | tf_op jit(solution)/shard_map/ppermute | solution.py:244
  52.2 1.6 %collective-permute-start.27 = (bf16[32,3584]{1,0:T(8,128)(2,1)S(1)}, bf16[32,3584]{1,0:T(8,128)(2,1)S(1)}, u32[]{:S(2)}, u32[]{:S(2)}) collective-permute-start(bf16[32,3584]{1,0:T(8,128)(2,1)S(1)} %collective-permute-done.26.refs_14_), channel_id=1, source_target_pairs={{0,2},{4,0},{8,4},{12,8},{14,12},{10,14},{6,10},{2,6},{1,3},{5,1},... | collective-permute-start | bytes 688136 | tf_op jit(solution)/shard_map/ppermute | solution.py:244
  54.5 2.6 %collective-permute-done.16.refs_3_ = bf16[32,3584]{1,0:T(8,128)(2,1)S(1)} collective-permute-done((bf16[32,3584]{1,0:T(8,128)(2,1)S(1)}, bf16[32,3584]{1,0:T(8,128)(2,1)S(1)}, u32[]{:S(2)}, u32[]{:S(2)}) %collective-permute-start.16) | collective-permute-done | bytes 229408 | tf_op jit(solution)/shard_map/ppermute | solution.py:244
  57.5 1.9 %collective-permute-start.6 = (bf16[32,3584]{1,0:T(8,128)(2,1)}, bf16[32,3584]{1,0:T(8,128)(2,1)S(1)}, u32[]{:S(2)}, u32[]{:S(2)}) collective-permute-start(bf16[32,3584]{1,0:T(8,128)(2,1)} %collective-permute-done.5.refs_6_.refs_7_), channel_id=1, source_target_pairs={{0,2},{4,0},{8,4},{12,8},{14,12},{10,14},{6,10},{2,6},{1,3},{5,1},... | collective-permute-start | bytes 688136 | tf_op jit(solution)/shard_map/ppermute | solution.py:244
  59.5 2.6 %collective-permute-done.2.refs_3_.refs_4_ = bf16[32,3584]{1,0:T(8,128)(2,1)S(1)} collective-permute-done((bf16[32,3584]{1,0:T(8,128)(2,1)S(1)}, bf16[32,3584]{1,0:T(8,128)(2,1)S(1)}, u32[]{:S(2)}, u32[]{:S(2)}) %collective-permute-start.2) | collective-permute-done | bytes 229408 | tf_op jit(solution)/shard_map/ppermute | solution.py:244
  62.2 1.9 %collective-permute-start.3 = (bf16[32,3584]{1,0:T(8,128)(2,1)S(1)}, bf16[32,3584]{1,0:T(8,128)(2,1)S(1)}, u32[]{:S(2)}, u32[]{:S(2)}) collective-permute-start(bf16[32,3584]{1,0:T(8,128)(2,1)S(1)} %collective-permute-done.2.refs_3_.refs_4_), channel_id=1, source_target_pairs={{0,4},{4,8},{8,12},{12,14},{14,10},{10,6},{6,2},{2,0},{1,5},{5,9},... | collective-permute-start | bytes 688136 | tf_op jit(solution)/shard_map/ppermute | solution.py:244
  65.0 2.0 %collective-permute-start.13 = (bf16[32,3584]{1,0:T(8,128)(2,1)S(1)}, bf16[32,3584]{1,0:T(8,128)(2,1)S(1)}, u32[]{:S(2)}, u32[]{:S(2)}) collective-permute-start(bf16[32,3584]{1,0:T(8,128)(2,1)S(1)} %collective-permute-done.12.refs_14_.refs_15_), channel_id=1, source_target_pairs={{0,2},{4,0},{8,4},{12,8},{14,12},{10,14},{6,10},{2,6},{1,3},{5,1},... | collective-permute-start | bytes 688136 | tf_op jit(solution)/shard_map/ppermute | solution.py:244
  67.7 4.9 %all-to-all-start = ((bf16[8,128,512]{2,1,0:T(8,128)(2,1)}), bf16[8,128,512]{2,1,0:T(8,128)(2,1)S(1)}, u32[]{:S(2)}, u32[]{:S(2)}) async-start(bf16[8,128,512]{2,1,0:T(8,128)(2,1)} %tie.3), calls=%async_computation | async-start | bytes 2097152 | tf_op jit(solution)/shard_map/all_to_all | solution.py:248
  75.4 9.5 %first_chunks.1 = (f32[256,512]{1,0:T(8,128)S(1)}, f32[256,512]{1,0:T(8,128)S(1)}, f32[128,256]{1,0:T(8,128)S(1)}) custom-call(s32[18]{0:T(128)S(1)} %dynamic-slice_bitcast_fusion.scalars, bf16[32,3584]{1,0:T(8,128)(2,1)} %copy-done.18, bf16[32,3584]{1,0:T(8,128)(2,1)} %copy-done.22, bf16[32,3584]{1,0:T(8,128)(2,1)} %copy-done.25, ...), custom_call_target="tpu_custom_call" | custom-call | flops 8455716864 | bytes 22544384 | tf_op jit(solution)/shard_map/first_chunks/pallas_call | solution.py:147
  84.9 5.0 %last_narrow.1 = f32[128,256]{1,0:T(8,128)S(1)} custom-call(s32[18]{0:T(128)S(1)} %dynamic-slice_bitcast_fusion.scalars, bf16[32,3584]{1,0:T(8,128)(2,1)} %copy-done.10, bf16[32,3584]{1,0:T(8,128)(2,1)} %copy-done.12, bf16[32,3584]{1,0:T(8,128)(2,1)} %copy-done.15, bf16[32,3584]{1,0:T(8,128)(2,1)S(1)} %collective-permute-done.2.refs_3_.refs_4_, ...), custom_call_target="tpu_custom_call" | custom-call | flops 939524096 | bytes 5767168 | tf_op jit(solution)/shard_map/last_narrow/pallas_call | solution.py:147
  90.1 2.1 %collective-permute-start.29 = (f32[64,256]{1,0:T(8,128)S(1)}, f32[64,256]{1,0:T(8,128)S(1)}, u32[]{:S(2)}, u32[]{:S(2)}) collective-permute-start(f32[64,256]{1,0:T(8,128)S(1)} %fusion.refs_0_), channel_id=1, source_target_pairs={{0,2},{1,3},{2,0},{3,1},{4,6},{5,7},{6,4},{7,5},{8,10},{9,11},{10,... | collective-permute-start | bytes 196616 | tf_op jit(solution)/shard_map/ppermute | solution.py:267
  92.2 5.8 %last_sent.1.refs_0_ = f32[256,512]{1,0:T(8,128)S(1)} custom-call(s32[18]{0:T(128)S(1)} %dynamic-slice_bitcast_fusion.scalars, f32[64,256]{1,0:T(8,128)S(1)} %fusion.refs_0_, bf16[32,3584]{1,0:T(8,128)(2,1)} %copy-done.10, bf16[32,3584]{1,0:T(8,128)(2,1)} %copy-done.12, bf16[32,3584]{1,0:T(8,128)(2,1)} %copy-done.15, ...), custom_call_target="tpu_custom_call" | custom-call | flops 3758096384 | bytes 12058624 | tf_op jit(solution)/shard_map/last_sent/pallas_call | solution.py:147
  98.6 3.3 %collective-permute-start.33 = (bf16[64,256]{1,0:T(8,128)(2,1)S(1)}, bf16[64,256]{1,0:T(8,128)(2,1)S(1)}, u32[]{:S(2)}, u32[]{:S(2)}) collective-permute-start(bf16[64,256]{1,0:T(8,128)(2,1)S(1)} %add_convert_fusion), channel_id=1, source_target_pairs={{0,12},{2,14},{4,0},{6,2},{8,4},{10,6},{12,8},{14,10},{1,13},{3,15... | collective-permute-start | bytes 98312 | tf_op jit(solution)/shard_map/ppermute | solution.py:271
  103.1 5.8 %last_kept.1.kept = f32[256,512]{1,0:T(8,128)S(1)} custom-call(s32[18]{0:T(128)S(1)} %dynamic-slice_bitcast_fusion.scalars, f32[256,512]{1,0:T(8,128)S(1)} %last_sent.1.refs_0_, bf16[32,3584]{1,0:T(8,128)(2,1)} %copy-done.10, bf16[32,3584]{1,0:T(8,128)(2,1)} %copy-done.12, bf16[32,3584]{1,0:T(8,128)(2,1)} %copy-done.15, ...), custom_call_target="tpu_custom_call" | custom-call | flops 3758096384 | bytes 12058624 | tf_op jit(solution)/shard_map/last_kept/pallas_call | solution.py:147
  (112 shorter events, 24.3 us)
Async XLA Ops:
  1.4 12.7 %collective-permute-start.24 = (bf16[32,3584]{1,0:T(8,128)(2,1)S(1)}, bf16[32,3584]{1,0:T(8,128)(2,1)S(1)}, u32[]{:S(2)}, u32[]{:S(2)}) collective-permute-start(bf16[32,3584]{1,0:T(8,128)(2,1)S(1)} %get-tuple-element.15.refs_8_), channel_id=1, source_target_pairs={{0,2},{4,0},{8,4},{12,8},{14,12},{10,14},{6,10},{2,6},{1,3},{5,1},... | collective-permute-start | bytes 688136 | tf_op jit(solution)/shard_map/ppermute | solution.py:244
  4.4 9.9 %collective-permute-start.21 = (bf16[32,3584]{1,0:T(8,128)(2,1)S(1)}, bf16[32,3584]{1,0:T(8,128)(2,1)S(1)}, u32[]{:S(2)}, u32[]{:S(2)}) collective-permute-start(bf16[32,3584]{1,0:T(8,128)(2,1)S(1)} %get-tuple-element.15.refs_8_), channel_id=1, source_target_pairs={{0,4},{4,8},{8,12},{12,14},{14,10},{10,6},{6,2},{2,0},{1,5},{5,9},... | collective-permute-start | bytes 688136 | tf_op jit(solution)/shard_map/ppermute | solution.py:244
  4.5 11.7 %collective-permute-start.18 = (bf16[32,3584]{1,0:T(8,128)(2,1)S(1)}, bf16[32,3584]{1,0:T(8,128)(2,1)S(1)}, u32[]{:S(2)}, u32[]{:S(2)}) collective-permute-start(bf16[32,3584]{1,0:T(8,128)(2,1)S(1)} %get-tuple-element.18.refs_0_), channel_id=1, source_target_pairs={{0,2},{4,0},{8,4},{12,8},{14,12},{10,14},{6,10},{2,6},{1,3},{5,1},... | collective-permute-start | bytes 688136 | tf_op jit(solution)/shard_map/ppermute | solution.py:244
  6.4 11.4 %collective-permute-start.14 = (bf16[32,3584]{1,0:T(8,128)(2,1)S(1)}, bf16[32,3584]{1,0:T(8,128)(2,1)S(1)}, u32[]{:S(2)}, u32[]{:S(2)}) collective-permute-start(bf16[32,3584]{1,0:T(8,128)(2,1)S(1)} %get-tuple-element.18.refs_0_), channel_id=1, source_target_pairs={{0,4},{4,8},{8,12},{12,14},{14,10},{10,6},{6,2},{2,0},{1,5},{5,9},... | collective-permute-start | bytes 688136 | tf_op jit(solution)/shard_map/ppermute | solution.py:244
  6.6 14.2 %collective-permute-start.4 = (bf16[32,3584]{1,0:T(8,128)(2,1)S(1)}, bf16[32,3584]{1,0:T(8,128)(2,1)S(1)}, u32[]{:S(2)}, u32[]{:S(2)}) collective-permute-start(bf16[32,3584]{1,0:T(8,128)(2,1)S(1)} %get-tuple-element.17.refs_0_.refs_1_), channel_id=1, source_target_pairs={{0,2},{4,0},{8,4},{12,8},{14,12},{10,14},{6,10},{2,6},{1,3},{5,1},... | collective-permute-start | bytes 688136 | tf_op jit(solution)/shard_map/ppermute | solution.py:244
  14.1 8.7 %collective-permute-start = (bf16[32,3584]{1,0:T(8,128)(2,1)S(1)}, bf16[32,3584]{1,0:T(8,128)(2,1)S(1)}, u32[]{:S(2)}, u32[]{:S(2)}) collective-permute-start(bf16[32,3584]{1,0:T(8,128)(2,1)S(1)} %get-tuple-element.17.refs_0_.refs_1_), channel_id=1, source_target_pairs={{0,4},{4,8},{8,12},{12,14},{14,10},{10,6},{6,2},{2,0},{1,5},{5,9},... | collective-permute-start | bytes 688136 | tf_op jit(solution)/shard_map/ppermute | solution.py:244
  14.3 11.4 %collective-permute-start.10 = (bf16[32,3584]{1,0:T(8,128)(2,1)S(1)}, bf16[32,3584]{1,0:T(8,128)(2,1)S(1)}, u32[]{:S(2)}, u32[]{:S(2)}) collective-permute-start(bf16[32,3584]{1,0:T(8,128)(2,1)S(1)} %tie.2.refs_8_.refs_9_), channel_id=1, source_target_pairs={{0,2},{4,0},{8,4},{12,8},{14,12},{10,14},{6,10},{2,6},{1,3},{5,1},... | collective-permute-start | bytes 688136 | tf_op jit(solution)/shard_map/ppermute | solution.py:244
  16.2 11.5 %collective-permute-start.7 = (bf16[32,3584]{1,0:T(8,128)(2,1)S(1)}, bf16[32,3584]{1,0:T(8,128)(2,1)S(1)}, u32[]{:S(2)}, u32[]{:S(2)}) collective-permute-start(bf16[32,3584]{1,0:T(8,128)(2,1)S(1)} %tie.2.refs_8_.refs_9_), channel_id=1, source_target_pairs={{0,4},{4,8},{8,12},{12,14},{14,10},{10,6},{6,2},{2,0},{1,5},{5,9},... | collective-permute-start | bytes 688136 | tf_op jit(solution)/shard_map/ppermute | solution.py:244
  17.9 12.7 %collective-permute-start.25 = (bf16[32,3584]{1,0:T(8,128)(2,1)S(1)}, bf16[32,3584]{1,0:T(8,128)(2,1)S(1)}, u32[]{:S(2)}, u32[]{:S(2)}) collective-permute-start(bf16[32,3584]{1,0:T(8,128)(2,1)S(1)} %collective-permute-done.24.refs_12_), channel_id=1, source_target_pairs={{0,2},{4,0},{8,4},{12,8},{14,12},{10,14},{6,10},{2,6},{1,3},{5,1},... | collective-permute-start | bytes 688136 | tf_op jit(solution)/shard_map/ppermute | solution.py:244
  20.7 11.9 %collective-permute-start.22 = (bf16[32,3584]{1,0:T(8,128)(2,1)S(1)}, bf16[32,3584]{1,0:T(8,128)(2,1)S(1)}, u32[]{:S(2)}, u32[]{:S(2)}) collective-permute-start(bf16[32,3584]{1,0:T(8,128)(2,1)S(1)} %collective-permute-done.21.refs_9_), channel_id=1, source_target_pairs={{0,4},{4,8},{8,12},{12,14},{14,10},{10,6},{6,2},{2,0},{1,5},{5,9},... | collective-permute-start | bytes 688136 | tf_op jit(solution)/shard_map/ppermute | solution.py:244
  22.8 12.8 %collective-permute-start.19 = (bf16[32,3584]{1,0:T(8,128)(2,1)S(1)}, bf16[32,3584]{1,0:T(8,128)(2,1)}, u32[]{:S(2)}, u32[]{:S(2)}) collective-permute-start(bf16[32,3584]{1,0:T(8,128)(2,1)S(1)} %collective-permute-done.18.refs_5_), channel_id=1, source_target_pairs={{0,2},{4,0},{8,4},{12,8},{14,12},{10,14},{6,10},{2,6},{1,3},{5,1},... | collective-permute-start | bytes 688136 | tf_op jit(solution)/shard_map/ppermute | solution.py:244
  25.7 12.0 %collective-permute-start.15 = (bf16[32,3584]{1,0:T(8,128)(2,1)S(1)}, bf16[32,3584]{1,0:T(8,128)(2,1)S(1)}, u32[]{:S(2)}, u32[]{:S(2)}) collective-permute-start(bf16[32,3584]{1,0:T(8,128)(2,1)S(1)} %collective-permute-done.14.refs_1_), channel_id=1, source_target_pairs={{0,4},{4,8},{8,12},{12,14},{14,10},{10,6},{6,2},{2,0},{1,5},{5,9},... | collective-permute-start | bytes 688136 | tf_op jit(solution)/shard_map/ppermute | solution.py:244
  27.7 12.8 %collective-permute-start.5 = (bf16[32,3584]{1,0:T(8,128)(2,1)S(1)}, bf16[32,3584]{1,0:T(8,128)(2,1)}, u32[]{:S(2)}, u32[]{:S(2)}) collective-permute-start(bf16[32,3584]{1,0:T(8,128)(2,1)S(1)} %collective-permute-done.4.refs_5_.refs_6_), channel_id=1, source_target_pairs={{0,2},{4,0},{8,4},{12,8},{14,12},{10,14},{6,10},{2,6},{1,3},{5,1},... | collective-permute-start | bytes 688136 | tf_op jit(solution)/shard_map/ppermute | solution.py:244
  30.6 12.0 %collective-permute-start.1 = (bf16[32,3584]{1,0:T(8,128)(2,1)S(1)}, bf16[32,3584]{1,0:T(8,128)(2,1)S(1)}, u32[]{:S(2)}, u32[]{:S(2)}) collective-permute-start(bf16[32,3584]{1,0:T(8,128)(2,1)S(1)} %collective-permute-done.refs_1_.refs_2_), channel_id=1, source_target_pairs={{0,4},{4,8},{8,12},{12,14},{14,10},{10,6},{6,2},{2,0},{1,5},{5,9},... | collective-permute-start | bytes 688136 | tf_op jit(solution)/shard_map/ppermute | solution.py:244
  32.6 12.7 %collective-permute-start.11 = (bf16[32,3584]{1,0:T(8,128)(2,1)S(1)}, bf16[32,3584]{1,0:T(8,128)(2,1)S(1)}, u32[]{:S(2)}, u32[]{:S(2)}) collective-permute-start(bf16[32,3584]{1,0:T(8,128)(2,1)S(1)} %collective-permute-done.10.refs_12_.refs_13_), channel_id=1, source_target_pairs={{0,2},{4,0},{8,4},{12,8},{14,12},{10,14},{6,10},{2,6},{1,3},{5,1},... | collective-permute-start | bytes 688136 | tf_op jit(solution)/shard_map/ppermute | solution.py:244
  35.6 11.8 %collective-permute-start.8 = (bf16[32,3584]{1,0:T(8,128)(2,1)S(1)}, bf16[32,3584]{1,0:T(8,128)(2,1)}, u32[]{:S(2)}, u32[]{:S(2)}) collective-permute-start(bf16[32,3584]{1,0:T(8,128)(2,1)S(1)} %collective-permute-done.7.refs_9_.refs_10_), channel_id=1, source_target_pairs={{0,4},{4,8},{8,12},{12,14},{14,10},{10,6},{6,2},{2,0},{1,5},{5,9},... | collective-permute-start | bytes 688136 | tf_op jit(solution)/shard_map/ppermute | solution.py:244
  37.7 12.6 %collective-permute-start.26 = (bf16[32,3584]{1,0:T(8,128)(2,1)S(1)}, bf16[32,3584]{1,0:T(8,128)(2,1)S(1)}, u32[]{:S(2)}, u32[]{:S(2)}) collective-permute-start(bf16[32,3584]{1,0:T(8,128)(2,1)S(1)} %collective-permute-done.25.refs_13_), channel_id=1, source_target_pairs={{0,2},{4,0},{8,4},{12,8},{14,12},{10,14},{6,10},{2,6},{1,3},{5,1},... | collective-permute-start | bytes 688136 | tf_op jit(solution)/shard_map/ppermute | solution.py:244
  40.5 11.7 %collective-permute-start.23 = (bf16[32,3584]{1,0:T(8,128)(2,1)S(1)}, bf16[32,3584]{1,0:T(8,128)(2,1)S(1)}, u32[]{:S(2)}, u32[]{:S(2)}) collective-permute-start(bf16[32,3584]{1,0:T(8,128)(2,1)S(1)} %collective-permute-done.22.refs_10_), channel_id=1, source_target_pairs={{0,4},{4,8},{8,12},{12,14},{14,10},{10,6},{6,2},{2,0},{1,5},{5,9},... | collective-permute-start | bytes 688136 | tf_op jit(solution)/shard_map/ppermute | solution.py:244
  42.6 14.5 %collective-permute-start.16 = (bf16[32,3584]{1,0:T(8,128)(2,1)S(1)}, bf16[32,3584]{1,0:T(8,128)(2,1)S(1)}, u32[]{:S(2)}, u32[]{:S(2)}) collective-permute-start(bf16[32,3584]{1,0:T(8,128)(2,1)S(1)} %collective-permute-done.15.refs_2_), channel_id=1, source_target_pairs={{0,4},{4,8},{8,12},{12,14},{14,10},{10,6},{6,2},{2,0},{1,5},{5,9},... | collective-permute-start | bytes 688136 | tf_op jit(solution)/shard_map/ppermute | solution.py:244
  45.3 12.2 %collective-permute-start.20 = (bf16[32,3584]{1,0:T(8,128)(2,1)}, bf16[32,3584]{1,0:T(8,128)(2,1)S(1)}, u32[]{:S(2)}, u32[]{:S(2)}) collective-permute-start(bf16[32,3584]{1,0:T(8,128)(2,1)} %collective-permute-done.19.refs_6_), channel_id=1, source_target_pairs={{0,2},{4,0},{8,4},{12,8},{14,12},{10,14},{6,10},{2,6},{1,3},{5,1},... | collective-permute-start | bytes 688136 | tf_op jit(solution)/shard_map/ppermute | solution.py:244
  47.4 14.6 %collective-permute-start.2 = (bf16[32,3584]{1,0:T(8,128)(2,1)S(1)}, bf16[32,3584]{1,0:T(8,128)(2,1)S(1)}, u32[]{:S(2)}, u32[]{:S(2)}) collective-permute-start(bf16[32,3584]{1,0:T(8,128)(2,1)S(1)} %collective-permute-done.1.refs_2_.refs_3_), channel_id=1, source_target_pairs={{0,4},{4,8},{8,12},{12,14},{14,10},{10,6},{6,2},{2,0},{1,5},{5,9},... | collective-permute-start | bytes 688136 | tf_op jit(solution)/shard_map/ppermute | solution.py:244
  50.2 12.0 %collective-permute-start.12 = (bf16[32,3584]{1,0:T(8,128)(2,1)S(1)}, bf16[32,3584]{1,0:T(8,128)(2,1)S(1)}, u32[]{:S(2)}, u32[]{:S(2)}) collective-permute-start(bf16[32,3584]{1,0:T(8,128)(2,1)S(1)} %collective-permute-done.11.refs_13_.refs_14_), channel_id=1, source_target_pairs={{0,2},{4,0},{8,4},{12,8},{14,12},{10,14},{6,10},{2,6},{1,3},{5,1},... | collective-permute-start | bytes 688136 | tf_op jit(solution)/shard_map/ppermute | solution.py:244
  52.2 12.7 %collective-permute-start.27 = (bf16[32,3584]{1,0:T(8,128)(2,1)S(1)}, bf16[32,3584]{1,0:T(8,128)(2,1)S(1)}, u32[]{:S(2)}, u32[]{:S(2)}) collective-permute-start(bf16[32,3584]{1,0:T(8,128)(2,1)S(1)} %collective-permute-done.26.refs_14_), channel_id=1, source_target_pairs={{0,2},{4,0},{8,4},{12,8},{14,12},{10,14},{6,10},{2,6},{1,3},{5,1},... | collective-permute-start | bytes 688136 | tf_op jit(solution)/shard_map/ppermute | solution.py:244
  57.1 9.9 %collective-permute-start.17 = (bf16[32,3584]{1,0:T(8,128)(2,1)S(1)}, bf16[32,3584]{1,0:T(8,128)(2,1)S(1)}, u32[]{:S(2)}, u32[]{:S(2)}) collective-permute-start(bf16[32,3584]{1,0:T(8,128)(2,1)S(1)} %collective-permute-done.16.refs_3_), channel_id=1, source_target_pairs={{0,4},{4,8},{8,12},{12,14},{14,10},{10,6},{6,2},{2,0},{1,5},{5,9},... | collective-permute-start | bytes 688136 | tf_op jit(solution)/shard_map/ppermute | solution.py:244
  57.5 27.3 %collective-permute-start.6 = (bf16[32,3584]{1,0:T(8,128)(2,1)}, bf16[32,3584]{1,0:T(8,128)(2,1)S(1)}, u32[]{:S(2)}, u32[]{:S(2)}) collective-permute-start(bf16[32,3584]{1,0:T(8,128)(2,1)} %collective-permute-done.5.refs_6_.refs_7_), channel_id=1, source_target_pairs={{0,2},{4,0},{8,4},{12,8},{14,12},{10,14},{6,10},{2,6},{1,3},{5,1},... | collective-permute-start | bytes 688136 | tf_op jit(solution)/shard_map/ppermute | solution.py:244
  62.0 22.9 %collective-permute-start.9 = (bf16[32,3584]{1,0:T(8,128)(2,1)}, bf16[32,3584]{1,0:T(8,128)(2,1)S(1)}, u32[]{:S(2)}, u32[]{:S(2)}) collective-permute-start(bf16[32,3584]{1,0:T(8,128)(2,1)} %collective-permute-done.8.refs_10_.refs_11_), channel_id=1, source_target_pairs={{0,4},{4,8},{8,12},{12,14},{14,10},{10,6},{6,2},{2,0},{1,5},{5,9},... | collective-permute-start | bytes 688136 | tf_op jit(solution)/shard_map/ppermute | solution.py:244
  62.2 22.7 %collective-permute-start.3 = (bf16[32,3584]{1,0:T(8,128)(2,1)S(1)}, bf16[32,3584]{1,0:T(8,128)(2,1)S(1)}, u32[]{:S(2)}, u32[]{:S(2)}) collective-permute-start(bf16[32,3584]{1,0:T(8,128)(2,1)S(1)} %collective-permute-done.2.refs_3_.refs_4_), channel_id=1, source_target_pairs={{0,4},{4,8},{8,12},{12,14},{14,10},{10,6},{6,2},{2,0},{1,5},{5,9},... | collective-permute-start | bytes 688136 | tf_op jit(solution)/shard_map/ppermute | solution.py:244
  65.0 19.9 %collective-permute-start.13 = (bf16[32,3584]{1,0:T(8,128)(2,1)S(1)}, bf16[32,3584]{1,0:T(8,128)(2,1)S(1)}, u32[]{:S(2)}, u32[]{:S(2)}) collective-permute-start(bf16[32,3584]{1,0:T(8,128)(2,1)S(1)} %collective-permute-done.12.refs_14_.refs_15_), channel_id=1, source_target_pairs={{0,2},{4,0},{8,4},{12,8},{14,12},{10,14},{6,10},{2,6},{1,3},{5,1},... | collective-permute-start | bytes 688136 | tf_op jit(solution)/shard_map/ppermute | solution.py:244
  67.7 42.1 %all-to-all-start = ((bf16[8,128,512]{2,1,0:T(8,128)(2,1)}), bf16[8,128,512]{2,1,0:T(8,128)(2,1)S(1)}, u32[]{:S(2)}, u32[]{:S(2)}) async-start(bf16[8,128,512]{2,1,0:T(8,128)(2,1)} %tie.3), calls=%async_computation | async-start | bytes 2097152 | tf_op jit(solution)/shard_map/all_to_all | solution.py:248
  90.0 8.6 %collective-permute-start.30 = (f32[64,256]{1,0:T(8,128)S(1)}, f32[64,256]{1,0:T(8,128)S(1)}, u32[]{:S(2)}, u32[]{:S(2)}) collective-permute-start(f32[64,256]{1,0:T(8,128)S(1)} %fusion.refs_0_), channel_id=1, source_target_pairs={{0,3},{1,2},{2,1},{3,0},{4,7},{5,6},{6,5},{7,4},{8,11},{9,10},{10,... | collective-permute-start | bytes 196616 | tf_op jit(solution)/shard_map/ppermute | solution.py:267
  98.0 10.9 %collective-permute-start.34 = (f32[256,512]{1,0:T(8,128)S(1)}, f32[256,512]{1,0:T(8,128)S(1)}, u32[]{:S(2)}, u32[]{:S(2)}) collective-permute-start(f32[256,512]{1,0:T(8,128)S(1)} %last_sent.1.refs_0_), channel_id=1, source_target_pairs={{0,1},{1,0},{2,3},{3,2},{4,5},{5,4},{6,7},{7,6},{8,9},{9,8},{10,11... | collective-permute-start | bytes 1572872 | tf_op jit(solution)/shard_map/ppermute | solution.py:272
  98.6 10.3 %collective-permute-start.33 = (bf16[64,256]{1,0:T(8,128)(2,1)S(1)}, bf16[64,256]{1,0:T(8,128)(2,1)S(1)}, u32[]{:S(2)}, u32[]{:S(2)}) collective-permute-start(bf16[64,256]{1,0:T(8,128)(2,1)S(1)} %add_convert_fusion), channel_id=1, source_target_pairs={{0,12},{2,14},{4,0},{6,2},{8,4},{10,6},{12,8},{14,10},{1,13},{3,15... | collective-permute-start | bytes 98312 | tf_op jit(solution)/shard_map/ppermute | solution.py:271
  (32 other events, 652.7 us)

commit v12 on v11

--- a/solution.py
+++ b/solution.py
@@ -67,7 +67,7 @@
     )(array, *after)
 
 
-def matmul_kernel(n, waits, spans, half, sides, narrow, has_acc, scalars, *refs):
+def matmul_kernel(n, waits, spans, half, sides, narrow, has_acc, token, scalars, *refs):
     refs = list(refs)[waits:]
     pieces = [[refs.pop(0) for _ in range(n)] for _ in spans]
     down = refs.pop(0)
@@ -75,6 +75,8 @@
     outs = len(sides) + narrow
     before = [refs.pop(0) for _ in range(outs)] if has_acc else []
     acc = [refs.pop(0) for _ in range(outs)]
+    if token:
+        refs.pop(0)[...] = jnp.zeros((8, 128), F32)
     tiles = [(part, at, tile) for part, (_, _, cuts) in enumerate(spans) for at, tile in cuts]
     lefts = [refs.pop(0) for _ in tiles]
     weights = [[refs.pop(0) for _ in tiles] for _ in sides]
@@ -126,7 +128,7 @@
     return [(sum(sizes[:i]), size) for i, size in enumerate(sizes)]
 
 
-def chunk_matmul(scalars, half, chunks, down, shrink, acc, sides, narrow, label, after=()):
+def chunk_matmul(scalars, half, recent, chunks, down, shrink, acc, sides, narrow, label, after=(), token=False):
     n = len(chunks[0][0])
     rows = chunks[0][0][0].shape[0] * n
     share = down.shape[1] // 2
@@ -138,26 +140,27 @@
     held = [
         piece if i in late else in_hbm(piece)
         for pieces, base, _ in chunks
-        for late in [(3, 4, n - 1) if base == 0 else (3, n - 2, n - 1)]
+        for late in [recent[base > 0]]
         for i, piece in enumerate(pieces)
     ]
     args = [*after, *held, in_hbm(down), in_hbm(shrink), *(acc or ())]
     shapes = [(rows, share)] * len(sides) + [(ranks, rows)] * narrow
+    marks = [(8, 128)] * token
     columns = share * len(sides) + ranks * narrow
     return pl.pallas_call(
-        functools.partial(matmul_kernel, n, len(after), spans, half, sides, narrow, acc is not None),
+        functools.partial(matmul_kernel, n, len(after), spans, half, sides, narrow, acc is not None, token),
         grid_spec=pltpu.PrefetchScalarGridSpec(
             num_scalar_prefetch=1,
             grid=(),
             in_specs=[anywhere] * len(args),
-            out_specs=[pl.BlockSpec(memory_space=pltpu.VMEM)] * len(shapes),
+            out_specs=[pl.BlockSpec(memory_space=pltpu.VMEM)] * len(shapes + marks),
             scratch_shapes=[pltpu.VMEM((rows, tile), BF16) for tile in sizes]
             + [pltpu.VMEM((tile, share), BF16) for _ in sides for tile in sizes]
             + [pltpu.VMEM((ranks, tile), BF16) for tile in sizes if narrow]
             + [pltpu.VMEM(shape, F32) for shape in shapes if acc is not None]
             + [pltpu.SemaphoreType.DMA((len(sizes), n + 3)), pltpu.SemaphoreType.DMA((3,))],
         ),
-        out_shape=[jax.ShapeDtypeStruct(shape, F32) for shape in shapes],
+        out_shape=[jax.ShapeDtypeStruct(shape, F32) for shape in shapes + marks],
         compiler_params=params(MATMUL_MIB),
         cost_estimate=pl.CostEstimate(
             flops=4 * rows * width * columns,
@@ -230,26 +233,37 @@
 
         width = units // CHUNKS
         blocks, mark = expand_blocks(scalars, half, expand, n, cores)
-        chunks, ends = [], []
-        for chunk in range(CHUNKS):
-            start = chunk * width
-            own = hidden[:, start:start + width]
-            if chunk == CHUNKS - 1:
-                own = tie(own, [mark])
-            way = chunk % 2
+
+        def ring(chunk, own, holds):
             pieces = [own]
-            for length, pairs in zip(((long, short), (short, long))[way], (clockwise, counter)):
+            for way, length in enumerate(lengths[chunk % 2]):
                 moving = own
-                for step in range(length):
-                    moving = lax.ppermute(moving, "store", pairs)
+                for step in range(1, length + 1):
+                    moving = lax.ppermute(moving, "store", (clockwise, counter)[way])
+                    if (way, step) in holds:
+                        moving = tie(moving, holds[way, step])
                     pieces.append(moving)
-                ends.append(moving)
-            chunks.append((pieces, way * n, start))
-        factors = lax.all_to_all(tie(blocks, ends[:4]), "store", 0, 0)
-
+            return pieces, chunk % 2 * n, chunk * width
+
+        def arrived(chunk, step):
+            pieces, base, _ = chunk
+            return [pieces[step], pieces[lengths[base > 0][0] + step]]
+
+        lengths = ((long, short), (short, long))
+        own = [hidden[:, chunk * width:(chunk + 1) * width] for chunk in range(CHUNKS)]
+        own[-1] = tie(own[-1], [mark])
+        first = [ring(chunk, own[chunk], {}) for chunk in range(2)]
         call = functools.partial(chunk_matmul, scalars, half)
-        first, last = chunks[:CHUNKS // 2], chunks[CHUNKS // 2:]
-        acc = call(first, down, shrink_rows, None, (0, 1), True, "first_chunks")
+        *acc, token = call(((long,), (n - 1,)), first, down, shrink_rows, None, (0, 1), True, "first_chunks", token=True)
+        last = []
+        for chunk in range(2):
+            before = arrived(first[chunk], short)
+            holds = {(0, 1): before, (1, 1): before, (chunk, short): [token]}
+            last.append(ring(chunk + 2, own[chunk + 2], holds))
+        ready = arrived(last[0], short) + arrived(last[1], short)
+        factors = lax.all_to_all(tie(blocks, ready), "store", 0, 0)
+        recent = ((short, long, n - 1), (short, n - 2, n - 1))
+        call = functools.partial(call, recent)
         narrow, = call(last, down, shrink_rows, acc[2:], (), True, "last_narrow")
         mine = [
             jnp.where((row_slot == store * owned + i)[None, :], narrow[i * rank:(i + 1) * rank], 0.0)

time: 113 us -> 134 us (1.19)
  waiting for transfers between devices: 17.3 us -> 41.5 us
  starting transfers between devices: 53.7 us -> 51.8 us
    ppermute x28, waiting for transfers between devices: 17.3 us -> 41.5 us  [ring(): moving = lax.ppermute(moving, 'store', (clockwise, counter)[way])]
    ppermute x28, starting transfers between devices: 41.7 us -> 34.1 us  [ring(): moving = lax.ppermute(moving, 'store', (clockwise, counter)[way])]
    ppermute x3, starting transfers between devices: 4.44 us -> 11.7 us  [shards(): lax.ppermute(column, 'store', [(s, (s + ds) % n) for s in range(n)])]
    unnamed x56 -> x68, local copies, waits for them, and re-layouts: 7.64 us -> 6.1 us
  transfers between devices with their start and end apart: 36 -> 36, of which waited for: 10 -> 16; matrix products, arithmetic and copies ran while one was open for 1% -> 1% of each run, Pallas kernels for 26% -> 22%
where the time goes in v12:
time: 134 us
  starting transfers between devices  51.8 us (39%)
  waiting for transfers between devices  41.5 us (31%)
  Pallas kernels  31 us (23%)
  local copies, waits for them, and re-layouts  8.92 us (7%)
    ppermute x28, waiting for transfers between devices, ring(): moving = lax.ppermute(moving, 'store', (clockwise, counter)[way])  41.5 us
    ppermute x28, starting transfers between devices, ring(): moving = lax.ppermute(moving, 'store', (clockwise, counter)[way])  34.1 us
    pallas_call x4, Pallas kernels, chunk_matmul(): pl.pallas_call(functools.partial(matmul_kernel, n, len(after), spans, hal...  26.3 us
    ppermute x3, starting transfers between devices, shards(): lax.ppermute(column, 'store', [(s, (s + ds) % n) for s in range(n)])  11.7 us
    unnamed x68, local copies, waits for them, and re-layouts  6.1 us
    all_to_all x1, starting transfers between devices, shards(): factors = lax.all_to_all(tie(blocks, ready), 'store', 0, 0)  3.56 us
    pallas_call x1, Pallas kernels, expand_blocks(): pl.pallas_call(split_kernel, grid_spec=pltpu.PrefetchScalarGridSpec(num_s...  3.36 us
  transfers between devices with their start and end apart: 36, of which 16 were waited for; matrix products, arithmetic and copies ran while one was open for 1% of the time, Pallas kernels for 22%

profile of v12, /device:TPU:0, one launch (start us, length us, event | category | flops | bytes accessed | tf_op | source)
XLA Modules:
  0.0 133.7 jit_solution(16431930888305986286)
XLA Ops:
  1.4 3.0 %collective-permute-start.13 = (bf16[32,3584]{1,0:T(8,128)(2,1)S(1)}, bf16[32,3584]{1,0:T(8,128)(2,1)S(1)}, u32[]{:S(2)}, u32[]{:S(2)}) collective-permute-start(bf16[32,3584]{1,0:T(8,128)(2,1)S(1)} %get-tuple-element.20.refs_8_), channel_id=1, source_target_pairs={{0,2},{4,0},{8,4},{12,8},{14,12},{10,14},{6,10},{2,6},{1,3},{5,1},... | collective-permute-start | bytes 688136 | tf_op jit(solution)/shard_map/ppermute | solution.py:242
  4.5 2.0 %collective-permute-start.1 = (bf16[32,3584]{1,0:T(8,128)(2,1)S(1)}, bf16[32,3584]{1,0:T(8,128)(2,1)S(1)}, u32[]{:S(2)}, u32[]{:S(2)}) collective-permute-start(bf16[32,3584]{1,0:T(8,128)(2,1)S(1)} %get-tuple-element.18.refs_0_), channel_id=1, source_target_pairs={{0,4},{4,8},{8,12},{12,14},{14,10},{10,6},{6,2},{2,0},{1,5},{5,9},... | collective-permute-start | bytes 688136 | tf_op jit(solution)/shard_map/ppermute | solution.py:242
  7.2 1.6 %copy-done.5 = bf16[2,64,8192]{2,1,0:T(8,128)(2,1)S(1)} copy-done((bf16[2,64,8192]{2,1,0:T(8,128)(2,1)S(1)}, bf16[2,64,8192]{2,1,0:T(8,128)(2,1)}, u32[]{:S(2)}) %copy-start.5) | copy-done | bytes 2097176
  8.8 3.4 %expand_blocks.1 = (bf16[8,128,512]{2,1,0:T(8,128)(2,1)}, f32[8,128]{1,0:T(8,128)S(1)}) custom-call(s32[18]{0:T(128)S(1)} %dynamic-slice_bitcast_fusion.scalars, bf16[128,8192]{1,0:T(8,128)(2,1)S(1)} %bitcast.9), custom_call_target="tpu_custom_call" | custom-call | bytes 2097152 | tf_op jit(solution)/shard_map/expand_blocks/pallas_call | solution.py:39
  12.2 1.9 %collective-permute-start.24 = (bf16[32,3584]{1,0:T(8,128)(2,1)S(1)}, bf16[32,3584]{1,0:T(8,128)(2,1)S(1)}, u32[]{:S(2)}, u32[]{:S(2)}) collective-permute-start(bf16[32,3584]{1,0:T(8,128)(2,1)S(1)} %tie.11.refs_8_.refs_9_), channel_id=1, source_target_pairs={{0,2},{4,0},{8,4},{12,8},{14,12},{10,14},{6,10},{2,6},{1,3},{5,1},... | collective-permute-start | bytes 688136 | tf_op jit(solution)/shard_map/ppermute | solution.py:242
  14.1 1.6 %collective-permute-start.14 = (bf16[32,3584]{1,0:T(8,128)(2,1)S(1)}, bf16[32,3584]{1,0:T(8,128)(2,1)S(1)}, u32[]{:S(2)}, u32[]{:S(2)}) collective-permute-start(bf16[32,3584]{1,0:T(8,128)(2,1)S(1)} %collective-permute-done.13.refs_12_), channel_id=1, source_target_pairs={{0,2},{4,0},{8,4},{12,8},{14,12},{10,14},{6,10},{2,6},{1,3},{5,1},... | collective-permute-start | bytes 688136 | tf_op jit(solution)/shard_map/ppermute | solution.py:242
  18.4 2.3 %collective-permute-done.24.refs_0_ = bf16[32,3584]{1,0:T(8,128)(2,1)S(1)} collective-permute-done((bf16[32,3584]{1,0:T(8,128)(2,1)S(1)}, bf16[32,3584]{1,0:T(8,128)(2,1)S(1)}, u32[]{:S(2)}, u32[]{:S(2)}) %collective-permute-start.24) | collective-permute-done | bytes 229408 | tf_op jit(solution)/shard_map/ppermute | solution.py:242
  20.7 2.1 %collective-permute-start = (bf16[32,3584]{1,0:T(8,128)(2,1)S(1)}, bf16[32,3584]{1,0:T(8,128)(2,1)S(1)}, u32[]{:S(2)}, u32[]{:S(2)}) collective-permute-start(bf16[32,3584]{1,0:T(8,128)(2,1)S(1)} %get-tuple-element.19.refs_0_.refs_1_), channel_id=1, source_target_pairs={{0,4},{4,8},{8,12},{12,14},{14,10},{10,6},{6,2},{2,0},{1,5},{5,9},... | collective-permute-start | bytes 688136 | tf_op jit(solution)/shard_map/ppermute | solution.py:242
  22.8 2.9 %collective-permute-done.14.refs_13_ = bf16[32,3584]{1,0:T(8,128)(2,1)S(1)} collective-permute-done((bf16[32,3584]{1,0:T(8,128)(2,1)S(1)}, bf16[32,3584]{1,0:T(8,128)(2,1)S(1)}, u32[]{:S(2)}, u32[]{:S(2)}) %collective-permute-start.14) | collective-permute-done | bytes 229408 | tf_op jit(solution)/shard_map/ppermute | solution.py:242
  25.6 2.0 %collective-permute-start.15 = (bf16[32,3584]{1,0:T(8,128)(2,1)S(1)}, bf16[32,3584]{1,0:T(8,128)(2,1)S(1)}, u32[]{:S(2)}, u32[]{:S(2)}) collective-permute-start(bf16[32,3584]{1,0:T(8,128)(2,1)S(1)} %collective-permute-done.14.refs_13_), channel_id=1, source_target_pairs={{0,2},{4,0},{8,4},{12,8},{14,12},{10,14},{6,10},{2,6},{1,3},{5,1},... | collective-permute-start | bytes 688136 | tf_op jit(solution)/shard_map/ppermute | solution.py:242
  30.5 2.0 %collective-permute-start.6 = (bf16[32,3584]{1,0:T(8,128)(2,1)S(1)}, bf16[32,3584]{1,0:T(8,128)(2,1)S(1)}, u32[]{:S(2)}, u32[]{:S(2)}) collective-permute-start(bf16[32,3584]{1,0:T(8,128)(2,1)S(1)} %collective-permute-done.5.refs_6_), channel_id=1, source_target_pairs={{0,2},{4,0},{8,4},{12,8},{14,12},{10,14},{6,10},{2,6},{1,3},{5,1},... | collective-permute-start | bytes 688136 | tf_op jit(solution)/shard_map/ppermute | solution.py:242
  35.5 2.0 %collective-permute-start.18 = (bf16[32,3584]{1,0:T(8,128)(2,1)S(1)}, bf16[32,3584]{1,0:T(8,128)(2,1)S(1)}, u32[]{:S(2)}, u32[]{:S(2)}) collective-permute-start(bf16[32,3584]{1,0:T(8,128)(2,1)S(1)} %get-tuple-element.19.refs_0_.refs_1_), channel_id=1, source_target_pairs={{0,2},{4,0},{8,4},{12,8},{14,12},{10,14},{6,10},{2,6},{1,3},{5,1},... | collective-permute-start | bytes 688136 | tf_op jit(solution)/shard_map/ppermute | solution.py:242
  39.0 1.6 %collective-permute-start.16 = (bf16[32,3584]{1,0:T(8,128)(2,1)S(1)}, bf16[32,3584]{1,0:T(8,128)(2,1)S(1)}, u32[]{:S(2)}, u32[]{:S(2)}) collective-permute-start(bf16[32,3584]{1,0:T(8,128)(2,1)S(1)} %collective-permute-done.15.refs_14_.refs_2_), channel_id=1, source_target_pairs={{0,2},{4,0},{8,4},{12,8},{14,12},{10,14},{6,10},{2,6},{1,3},{5,1},... | collective-permute-start | bytes 688136 | tf_op jit(solution)/shard_map/ppermute | solution.py:242
  40.6 3.3 %collective-permute-done.3.refs_1_.refs_3_ = bf16[32,3584]{1,0:T(8,128)(2,1)S(1)} collective-permute-done((bf16[32,3584]{1,0:T(8,128)(2,1)S(1)}, bf16[32,3584]{1,0:T(8,128)(2,1)S(1)}, u32[]{:S(2)}, u32[]{:S(2)}) %collective-permute-start.3) | collective-permute-done | bytes 229408 | tf_op jit(solution)/shard_map/ppermute | solution.py:242
  43.9 1.6 %collective-permute-start.25 = (bf16[32,3584]{1,0:T(8,128)(2,1)S(1)}, bf16[32,3584]{1,0:T(8,128)(2,1)S(1)}, u32[]{:S(2)}, u32[]{:S(2)}) collective-permute-start(bf16[32,3584]{1,0:T(8,128)(2,1)S(1)} %tie.13.refs_12_.refs_13_), channel_id=1, source_target_pairs={{0,2},{4,0},{8,4},{12,8},{14,12},{10,14},{6,10},{2,6},{1,3},{5,1},... | collective-permute-start | bytes 688136 | tf_op jit(solution)/shard_map/ppermute | solution.py:242
  46.0 2.8 %collective-permute-done.21.refs_0_ = bf16[32,3584]{1,0:T(8,128)(2,1)S(1)} collective-permute-done((bf16[32,3584]{1,0:T(8,128)(2,1)S(1)}, bf16[32,3584]{1,0:T(8,128)(2,1)S(1)}, u32[]{:S(2)}, u32[]{:S(2)}) %collective-permute-start.21) | collective-permute-done | bytes 229408 | tf_op jit(solution)/shard_map/ppermute | solution.py:242
  49.3 1.6 %collective-permute-start.19 = (bf16[32,3584]{1,0:T(8,128)(2,1)S(1)}, bf16[32,3584]{1,0:T(8,128)(2,1)S(1)}, u32[]{:S(2)}, u32[]{:S(2)}) collective-permute-start(bf16[32,3584]{1,0:T(8,128)(2,1)S(1)} %tie.10.refs_5_.refs_6_), channel_id=1, source_target_pairs={{0,2},{4,0},{8,4},{12,8},{14,12},{10,14},{6,10},{2,6},{1,3},{5,1},... | collective-permute-start | bytes 688136 | tf_op jit(solution)/shard_map/ppermute | solution.py:242
  52.3 2.9 %collective-permute-done.25.refs_13_.refs_14_ = bf16[32,3584]{1,0:T(8,128)(2,1)S(1)} collective-permute-done((bf16[32,3584]{1,0:T(8,128)(2,1)S(1)}, bf16[32,3584]{1,0:T(8,128)(2,1)S(1)}, u32[]{:S(2)}, u32[]{:S(2)}) %collective-permute-start.25) | collective-permute-done | bytes 229408 | tf_op jit(solution)/shard_map/ppermute | solution.py:242
  55.1 2.0 %collective-permute-start.26 = (bf16[32,3584]{1,0:T(8,128)(2,1)S(1)}, bf16[32,3584]{1,0:T(8,128)(2,1)S(1)}, u32[]{:S(2)}, u32[]{:S(2)}) collective-permute-start(bf16[32,3584]{1,0:T(8,128)(2,1)S(1)} %collective-permute-done.25.refs_13_.refs_14_), channel_id=1, source_target_pairs={{0,2},{4,0},{8,4},{12,8},{14,12},{10,14},{6,10},{2,6},{1,3},{5,1},... | collective-permute-start | bytes 688136 | tf_op jit(solution)/shard_map/ppermute | solution.py:242
  57.3 1.7 %collective-permute-done.22.refs_10_.refs_11_ = bf16[32,3584]{1,0:T(8,128)(2,1)S(1)} collective-permute-done((bf16[32,3584]{1,0:T(8,128)(2,1)S(1)}, bf16[32,3584]{1,0:T(8,128)(2,1)S(1)}, u32[]{:S(2)}, u32[]{:S(2)}) %collective-permute-start.22) | collective-permute-done | bytes 229408 | tf_op jit(solution)/shard_map/ppermute | solution.py:242
  60.0 2.0 %collective-permute-start.20 = (bf16[32,3584]{1,0:T(8,128)(2,1)S(1)}, bf16[32,3584]{1,0:T(8,128)(2,1)S(1)}, u32[]{:S(2)}, u32[]{:S(2)}) collective-permute-start(bf16[32,3584]{1,0:T(8,128)(2,1)S(1)} %collective-permute-done.19.refs_6_.refs_7_), channel_id=1, source_target_pairs={{0,2},{4,0},{8,4},{12,8},{14,12},{10,14},{6,10},{2,6},{1,3},{5,1},... | collective-permute-start | bytes 688136 | tf_op jit(solution)/shard_map/ppermute | solution.py:242
  62.0 1.9 %collective-permute-done.9.refs_4_ = bf16[32,3584]{1,0:T(8,128)(2,1)S(1)} collective-permute-done((bf16[32,3584]{1,0:T(8,128)(2,1)S(1)}, bf16[32,3584]{1,0:T(8,128)(2,1)S(1)}, u32[]{:S(2)}, u32[]{:S(2)}) %collective-permute-start.9) | collective-permute-done | bytes 229408 | tf_op jit(solution)/shard_map/ppermute | solution.py:242
  64.0 9.6 %first_chunks.1 = (f32[256,512]{1,0:T(8,128)S(1)}, f32[256,512]{1,0:T(8,128)S(1)}, f32[128,256]{1,0:T(8,128)S(1)}, f32[8,128]{1,0:T(8,128)S(1)}) custom-call(s32[18]{0:T(128)S(1)} %dynamic-slice_bitcast_fusion.scalars, bf16[32,3584]{1,0:T(8,128)(2,1)} %copy-done.22, bf16[32,3584]{1,0:T(8,128)(2,1)} %copy-done.26, bf16[32,3584]{1,0:T(8,128)(2,1)} %copy-done.30, ...), custom_call_target="tpu_custom_call" | custom-call | flops 8455716864 | bytes 22544384 | tf_op jit(solution)/shard_map/first_chunks/pallas_call | solution.py:150
  74.5 3.6 %all-to-all-start = ((bf16[8,128,512]{2,1,0:T(8,128)(2,1)}), bf16[8,128,512]{2,1,0:T(8,128)(2,1)S(1)}, u32[]{:S(2)}, u32[]{:S(2)}) async-start(bf16[8,128,512]{2,1,0:T(8,128)(2,1)} %tie.15), calls=%async_computation | async-start | bytes 2097152 | tf_op jit(solution)/shard_map/all_to_all | solution.py:264
  78.1 1.9 %collective-permute-start.27 = (bf16[32,3584]{1,0:T(8,128)(2,1)S(1)}, bf16[32,3584]{1,0:T(8,128)(2,1)S(1)}, u32[]{:S(2)}, u32[]{:S(2)}) collective-permute-start(bf16[32,3584]{1,0:T(8,128)(2,1)S(1)} %tie.14.refs_14_.refs_4_.refs_15_), channel_id=1, source_target_pairs={{0,2},{4,0},{8,4},{12,8},{14,12},{10,14},{6,10},{2,6},{1,3},{5,1},... | collective-permute-start | bytes 688136 | tf_op jit(solution)/shard_map/ppermute | solution.py:242
  81.0 15.8 %collective-permute-done.27.refs_15_.refs_16_ = bf16[32,3584]{1,0:T(8,128)(2,1)S(1)} collective-permute-done((bf16[32,3584]{1,0:T(8,128)(2,1)S(1)}, bf16[32,3584]{1,0:T(8,128)(2,1)S(1)}, u32[]{:S(2)}, u32[]{:S(2)}) %collective-permute-start.27) | collective-permute-done | bytes 229408 | tf_op jit(solution)/shard_map/ppermute | solution.py:242
  98.7 5.0 %last_narrow.1 = f32[128,256]{1,0:T(8,128)S(1)} custom-call(s32[18]{0:T(128)S(1)} %dynamic-slice_bitcast_fusion.scalars, bf16[32,3584]{1,0:T(8,128)(2,1)} %copy-done.17, bf16[32,3584]{1,0:T(8,128)(2,1)} %copy-done.2, bf16[32,3584]{1,0:T(8,128)(2,1)} %copy-done.19, bf16[32,3584]{1,0:T(8,128)(2,1)S(1)} %tie.9.refs_3_.refs_1_.refs_4_, ...), custom_call_target="tpu_custom_call" | custom-call | flops 939524096 | bytes 5767168 | tf_op jit(solution)/shard_map/last_narrow/pallas_call | solution.py:150
  103.8 1.7 %collective-permute-start.29 = (f32[64,256]{1,0:T(8,128)S(1)}, f32[64,256]{1,0:T(8,128)S(1)}, u32[]{:S(2)}, u32[]{:S(2)}) collective-permute-start(f32[64,256]{1,0:T(8,128)S(1)} %fusion.refs_0_), channel_id=1, source_target_pairs={{0,2},{1,3},{2,0},{3,1},{4,6},{5,7},{6,4},{7,5},{8,10},{9,11},{10,... | collective-permute-start | bytes 196616 | tf_op jit(solution)/shard_map/ppermute | solution.py:281
  105.7 5.8 %last_sent.1.refs_0_ = f32[256,512]{1,0:T(8,128)S(1)} custom-call(s32[18]{0:T(128)S(1)} %dynamic-slice_bitcast_fusion.scalars, f32[64,256]{1,0:T(8,128)S(1)} %fusion.refs_0_, bf16[32,3584]{1,0:T(8,128)(2,1)} %copy-done.17, bf16[32,3584]{1,0:T(8,128)(2,1)} %copy-done.2, bf16[32,3584]{1,0:T(8,128)(2,1)} %copy-done.19, ...), custom_call_target="tpu_custom_call" | custom-call | flops 3758096384 | bytes 12058624 | tf_op jit(solution)/shard_map/last_sent/pallas_call | solution.py:150
  112.0 9.0 %collective-permute-start.31 = (bf16[64,256]{1,0:T(8,128)(2,1)S(1)}, bf16[64,256]{1,0:T(8,128)(2,1)S(1)}, u32[]{:S(2)}, u32[]{:S(2)}) collective-permute-start(bf16[64,256]{1,0:T(8,128)(2,1)S(1)} %add_convert_fusion), channel_id=1, source_target_pairs={{0,4},{2,6},{4,8},{6,10},{8,12},{10,14},{12,0},{14,2},{1,5},{3,7},... | collective-permute-start | bytes 98312 | tf_op jit(solution)/shard_map/ppermute | solution.py:285
  120.9 2.8 %collective-permute-start.33 = (bf16[64,256]{1,0:T(8,128)(2,1)S(1)}, bf16[64,256]{1,0:T(8,128)(2,1)S(1)}, u32[]{:S(2)}, u32[]{:S(2)}) collective-permute-start(bf16[64,256]{1,0:T(8,128)(2,1)S(1)} %add_convert_fusion), channel_id=1, source_target_pairs={{0,12},{2,14},{4,0},{6,2},{8,4},{10,6},{12,8},{14,10},{1,13},{3,15... | collective-permute-start | bytes 98312 | tf_op jit(solution)/shard_map/ppermute | solution.py:285
  123.7 5.8 %last_kept.1.kept = f32[256,512]{1,0:T(8,128)S(1)} custom-call(s32[18]{0:T(128)S(1)} %dynamic-slice_bitcast_fusion.scalars, f32[256,512]{1,0:T(8,128)S(1)} %last_sent.1.refs_0_, bf16[32,3584]{1,0:T(8,128)(2,1)} %copy-done.17, bf16[32,3584]{1,0:T(8,128)(2,1)} %copy-done.2, bf16[32,3584]{1,0:T(8,128)(2,1)} %copy-done.19, ...), custom_call_target="tpu_custom_call" | custom-call | flops 3758096384 | bytes 12058624 | tf_op jit(solution)/shard_map/last_kept/pallas_call | solution.py:150
  (130 shorter events, 24.4 us)
Async XLA Ops:
  1.4 12.7 %collective-permute-start.13 = (bf16[32,3584]{1,0:T(8,128)(2,1)S(1)}, bf16[32,3584]{1,0:T(8,128)(2,1)S(1)}, u32[]{:S(2)}, u32[]{:S(2)}) collective-permute-start(bf16[32,3584]{1,0:T(8,128)(2,1)S(1)} %get-tuple-element.20.refs_8_), channel_id=1, source_target_pairs={{0,2},{4,0},{8,4},{12,8},{14,12},{10,14},{6,10},{2,6},{1,3},{5,1},... | collective-permute-start | bytes 688136 | tf_op jit(solution)/shard_map/ppermute | solution.py:242
  4.4 11.3 %collective-permute-start.10 = (bf16[32,3584]{1,0:T(8,128)(2,1)S(1)}, bf16[32,3584]{1,0:T(8,128)(2,1)S(1)}, u32[]{:S(2)}, u32[]{:S(2)}) collective-permute-start(bf16[32,3584]{1,0:T(8,128)(2,1)S(1)} %get-tuple-element.20.refs_8_), channel_id=1, source_target_pairs={{0,4},{4,8},{8,12},{12,14},{14,10},{10,6},{6,2},{2,0},{1,5},{5,9},... | collective-permute-start | bytes 688136 | tf_op jit(solution)/shard_map/ppermute | solution.py:242
  4.5 11.9 %collective-permute-start.1 = (bf16[32,3584]{1,0:T(8,128)(2,1)S(1)}, bf16[32,3584]{1,0:T(8,128)(2,1)S(1)}, u32[]{:S(2)}, u32[]{:S(2)}) collective-permute-start(bf16[32,3584]{1,0:T(8,128)(2,1)S(1)} %get-tuple-element.18.refs_0_), channel_id=1, source_target_pairs={{0,4},{4,8},{8,12},{12,14},{14,10},{10,6},{6,2},{2,0},{1,5},{5,9},... | collective-permute-start | bytes 688136 | tf_op jit(solution)/shard_map/ppermute | solution.py:242
  6.5 10.6 %collective-permute-start.4 = (bf16[32,3584]{1,0:T(8,128)(2,1)S(1)}, bf16[32,3584]{1,0:T(8,128)(2,1)S(1)}, u32[]{:S(2)}, u32[]{:S(2)}) collective-permute-start(bf16[32,3584]{1,0:T(8,128)(2,1)S(1)} %get-tuple-element.18.refs_0_), channel_id=1, source_target_pairs={{0,2},{4,0},{8,4},{12,8},{14,12},{10,14},{6,10},{2,6},{1,3},{5,1},... | collective-permute-start | bytes 688136 | tf_op jit(solution)/shard_map/ppermute | solution.py:242
  14.1 11.5 %collective-permute-start.14 = (bf16[32,3584]{1,0:T(8,128)(2,1)S(1)}, bf16[32,3584]{1,0:T(8,128)(2,1)S(1)}, u32[]{:S(2)}, u32[]{:S(2)}) collective-permute-start(bf16[32,3584]{1,0:T(8,128)(2,1)S(1)} %collective-permute-done.13.refs_12_), channel_id=1, source_target_pairs={{0,2},{4,0},{8,4},{12,8},{14,12},{10,14},{6,10},{2,6},{1,3},{5,1},... | collective-permute-start | bytes 688136 | tf_op jit(solution)/shard_map/ppermute | solution.py:242
  15.7 12.0 %collective-permute-start.11 = (bf16[32,3584]{1,0:T(8,128)(2,1)S(1)}, bf16[32,3584]{1,0:T(8,128)(2,1)S(1)}, u32[]{:S(2)}, u32[]{:S(2)}) collective-permute-start(bf16[32,3584]{1,0:T(8,128)(2,1)S(1)} %collective-permute-done.10.refs_9_), channel_id=1, source_target_pairs={{0,4},{4,8},{8,12},{12,14},{14,10},{10,6},{6,2},{2,0},{1,5},{5,9},... | collective-permute-start | bytes 688136 | tf_op jit(solution)/shard_map/ppermute | solution.py:242
  16.4 12.8 %collective-permute-start.2 = (bf16[32,3584]{1,0:T(8,128)(2,1)S(1)}, bf16[32,3584]{1,0:T(8,128)(2,1)S(1)}, u32[]{:S(2)}, u32[]{:S(2)}) collective-permute-start(bf16[32,3584]{1,0:T(8,128)(2,1)S(1)} %collective-permute-done.1.refs_1_), channel_id=1, source_target_pairs={{0,4},{4,8},{8,12},{12,14},{14,10},{10,6},{6,2},{2,0},{1,5},{5,9},... | collective-permute-start | bytes 688136 | tf_op jit(solution)/shard_map/ppermute | solution.py:242
  17.1 13.5 %collective-permute-start.5 = (bf16[32,3584]{1,0:T(8,128)(2,1)S(1)}, bf16[32,3584]{1,0:T(8,128)(2,1)S(1)}, u32[]{:S(2)}, u32[]{:S(2)}) collective-permute-start(bf16[32,3584]{1,0:T(8,128)(2,1)S(1)} %collective-permute-done.4.refs_5_), channel_id=1, source_target_pairs={{0,2},{4,0},{8,4},{12,8},{14,12},{10,14},{6,10},{2,6},{1,3},{5,1},... | collective-permute-start | bytes 688136 | tf_op jit(solution)/shard_map/ppermute | solution.py:242
  20.7 13.3 %collective-permute-start = (bf16[32,3584]{1,0:T(8,128)(2,1)S(1)}, bf16[32,3584]{1,0:T(8,128)(2,1)S(1)}, u32[]{:S(2)}, u32[]{:S(2)}) collective-permute-start(bf16[32,3584]{1,0:T(8,128)(2,1)S(1)} %get-tuple-element.19.refs_0_.refs_1_), channel_id=1, source_target_pairs={{0,4},{4,8},{8,12},{12,14},{14,10},{10,6},{6,2},{2,0},{1,5},{5,9},... | collective-permute-start | bytes 688136 | tf_op jit(solution)/shard_map/ppermute | solution.py:242
  25.6 9.8 %collective-permute-start.15 = (bf16[32,3584]{1,0:T(8,128)(2,1)S(1)}, bf16[32,3584]{1,0:T(8,128)(2,1)S(1)}, u32[]{:S(2)}, u32[]{:S(2)}) collective-permute-start(bf16[32,3584]{1,0:T(8,128)(2,1)S(1)} %collective-permute-done.14.refs_13_), channel_id=1, source_target_pairs={{0,2},{4,0},{8,4},{12,8},{14,12},{10,14},{6,10},{2,6},{1,3},{5,1},... | collective-permute-start | bytes 688136 | tf_op jit(solution)/shard_map/ppermute | solution.py:242
  27.6 11.3 %collective-permute-start.12 = (bf16[32,3584]{1,0:T(8,128)(2,1)S(1)}, bf16[32,3584]{1,0:T(8,128)(2,1)S(1)}, u32[]{:S(2)}, u32[]{:S(2)}) collective-permute-start(bf16[32,3584]{1,0:T(8,128)(2,1)S(1)} %collective-permute-done.11.refs_10_), channel_id=1, source_target_pairs={{0,4},{4,8},{8,12},{12,14},{14,10},{10,6},{6,2},{2,0},{1,5},{5,9},... | collective-permute-start | bytes 688136 | tf_op jit(solution)/shard_map/ppermute | solution.py:242
  29.1 14.7 %collective-permute-start.3 = (bf16[32,3584]{1,0:T(8,128)(2,1)S(1)}, bf16[32,3584]{1,0:T(8,128)(2,1)S(1)}, u32[]{:S(2)}, u32[]{:S(2)}) collective-permute-start(bf16[32,3584]{1,0:T(8,128)(2,1)S(1)} %collective-permute-done.2.refs_2_), channel_id=1, source_target_pairs={{0,4},{4,8},{8,12},{12,14},{14,10},{10,6},{6,2},{2,0},{1,5},{5,9},... | collective-permute-start | bytes 688136 | tf_op jit(solution)/shard_map/ppermute | solution.py:242
  30.5 14.9 %collective-permute-start.6 = (bf16[32,3584]{1,0:T(8,128)(2,1)S(1)}, bf16[32,3584]{1,0:T(8,128)(2,1)S(1)}, u32[]{:S(2)}, u32[]{:S(2)}) collective-permute-start(bf16[32,3584]{1,0:T(8,128)(2,1)S(1)} %collective-permute-done.5.refs_6_), channel_id=1, source_target_pairs={{0,2},{4,0},{8,4},{12,8},{14,12},{10,14},{6,10},{2,6},{1,3},{5,1},... | collective-permute-start | bytes 688136 | tf_op jit(solution)/shard_map/ppermute | solution.py:242
  34.1 14.7 %collective-permute-start.21 = (bf16[32,3584]{1,0:T(8,128)(2,1)S(1)}, bf16[32,3584]{1,0:T(8,128)(2,1)S(1)}, u32[]{:S(2)}, u32[]{:S(2)}) collective-permute-start(bf16[32,3584]{1,0:T(8,128)(2,1)S(1)} %tie.11.refs_8_.refs_9_), channel_id=1, source_target_pairs={{0,4},{4,8},{8,12},{12,14},{14,10},{10,6},{6,2},{2,0},{1,5},{5,9},... | collective-permute-start | bytes 688136 | tf_op jit(solution)/shard_map/ppermute | solution.py:242
  35.5 13.8 %collective-permute-start.18 = (bf16[32,3584]{1,0:T(8,128)(2,1)S(1)}, bf16[32,3584]{1,0:T(8,128)(2,1)S(1)}, u32[]{:S(2)}, u32[]{:S(2)}) collective-permute-start(bf16[32,3584]{1,0:T(8,128)(2,1)S(1)} %get-tuple-element.19.refs_0_.refs_1_), channel_id=1, source_target_pairs={{0,2},{4,0},{8,4},{12,8},{14,12},{10,14},{6,10},{2,6},{1,3},{5,1},... | collective-permute-start | bytes 688136 | tf_op jit(solution)/shard_map/ppermute | solution.py:242
  39.0 11.9 %collective-permute-start.16 = (bf16[32,3584]{1,0:T(8,128)(2,1)S(1)}, bf16[32,3584]{1,0:T(8,128)(2,1)S(1)}, u32[]{:S(2)}, u32[]{:S(2)}) collective-permute-start(bf16[32,3584]{1,0:T(8,128)(2,1)S(1)} %collective-permute-done.15.refs_14_.refs_2_), channel_id=1, source_target_pairs={{0,2},{4,0},{8,4},{12,8},{14,12},{10,14},{6,10},{2,6},{1,3},{5,1},... | collective-permute-start | bytes 688136 | tf_op jit(solution)/shard_map/ppermute | solution.py:242
  43.9 11.2 %collective-permute-start.25 = (bf16[32,3584]{1,0:T(8,128)(2,1)S(1)}, bf16[32,3584]{1,0:T(8,128)(2,1)S(1)}, u32[]{:S(2)}, u32[]{:S(2)}) collective-permute-start(bf16[32,3584]{1,0:T(8,128)(2,1)S(1)} %tie.13.refs_12_.refs_13_), channel_id=1, source_target_pairs={{0,2},{4,0},{8,4},{12,8},{14,12},{10,14},{6,10},{2,6},{1,3},{5,1},... | collective-permute-start | bytes 688136 | tf_op jit(solution)/shard_map/ppermute | solution.py:242
  45.5 11.7 %collective-permute-start.7 = (bf16[32,3584]{1,0:T(8,128)(2,1)S(1)}, bf16[32,3584]{1,0:T(8,128)(2,1)S(1)}, u32[]{:S(2)}, u32[]{:S(2)}) collective-permute-start(bf16[32,3584]{1,0:T(8,128)(2,1)S(1)} %tie.8.refs_1_.refs_2_), channel_id=1, source_target_pairs={{0,4},{4,8},{8,12},{12,14},{14,10},{10,6},{6,2},{2,0},{1,5},{5,9},... | collective-permute-start | bytes 688136 | tf_op jit(solution)/shard_map/ppermute | solution.py:242
  48.8 10.2 %collective-permute-start.22 = (bf16[32,3584]{1,0:T(8,128)(2,1)S(1)}, bf16[32,3584]{1,0:T(8,128)(2,1)S(1)}, u32[]{:S(2)}, u32[]{:S(2)}) collective-permute-start(bf16[32,3584]{1,0:T(8,128)(2,1)S(1)} %tie.12.refs_9_.refs_10_), channel_id=1, source_target_pairs={{0,4},{4,8},{8,12},{12,14},{14,10},{10,6},{6,2},{2,0},{1,5},{5,9},... | collective-permute-start | bytes 688136 | tf_op jit(solution)/shard_map/ppermute | solution.py:242
  49.3 10.8 %collective-permute-start.19 = (bf16[32,3584]{1,0:T(8,128)(2,1)S(1)}, bf16[32,3584]{1,0:T(8,128)(2,1)S(1)}, u32[]{:S(2)}, u32[]{:S(2)}) collective-permute-start(bf16[32,3584]{1,0:T(8,128)(2,1)S(1)} %tie.10.refs_5_.refs_6_), channel_id=1, source_target_pairs={{0,2},{4,0},{8,4},{12,8},{14,12},{10,14},{6,10},{2,6},{1,3},{5,1},... | collective-permute-start | bytes 688136 | tf_op jit(solution)/shard_map/ppermute | solution.py:242
  50.8 13.1 %collective-permute-start.9 = (bf16[32,3584]{1,0:T(8,128)(2,1)S(1)}, bf16[32,3584]{1,0:T(8,128)(2,1)S(1)}, u32[]{:S(2)}, u32[]{:S(2)}) collective-permute-start(bf16[32,3584]{1,0:T(8,128)(2,1)S(1)} %collective-permute-done.3.refs_1_.refs_3_), channel_id=1, source_target_pairs={{0,4},{4,8},{8,12},{12,14},{14,10},{10,6},{6,2},{2,0},{1,5},{5,9},... | collective-permute-start | bytes 688136 | tf_op jit(solution)/shard_map/ppermute | solution.py:242
  55.1 18.6 %collective-permute-start.26 = (bf16[32,3584]{1,0:T(8,128)(2,1)S(1)}, bf16[32,3584]{1,0:T(8,128)(2,1)S(1)}, u32[]{:S(2)}, u32[]{:S(2)}) collective-permute-start(bf16[32,3584]{1,0:T(8,128)(2,1)S(1)} %collective-permute-done.25.refs_13_.refs_14_), channel_id=1, source_target_pairs={{0,2},{4,0},{8,4},{12,8},{14,12},{10,14},{6,10},{2,6},{1,3},{5,1},... | collective-permute-start | bytes 688136 | tf_op jit(solution)/shard_map/ppermute | solution.py:242
  57.1 16.6 %collective-permute-start.8 = (bf16[32,3584]{1,0:T(8,128)(2,1)S(1)}, bf16[32,3584]{1,0:T(8,128)(2,1)S(1)}, u32[]{:S(2)}, u32[]{:S(2)}) collective-permute-start(bf16[32,3584]{1,0:T(8,128)(2,1)S(1)} %collective-permute-done.7.refs_2_.refs_3_), channel_id=1, source_target_pairs={{0,4},{4,8},{8,12},{12,14},{14,10},{10,6},{6,2},{2,0},{1,5},{5,9},... | collective-permute-start | bytes 688136 | tf_op jit(solution)/shard_map/ppermute | solution.py:242
  59.0 14.8 %collective-permute-start.23 = (bf16[32,3584]{1,0:T(8,128)(2,1)S(1)}, bf16[32,3584]{1,0:T(8,128)(2,1)S(1)}, u32[]{:S(2)}, u32[]{:S(2)}) collective-permute-start(bf16[32,3584]{1,0:T(8,128)(2,1)S(1)} %collective-permute-done.22.refs_10_.refs_11_), channel_id=1, source_target_pairs={{0,4},{4,8},{8,12},{12,14},{14,10},{10,6},{6,2},{2,0},{1,5},{5,9},... | collective-permute-start | bytes 688136 | tf_op jit(solution)/shard_map/ppermute | solution.py:242
  60.0 13.7 %collective-permute-start.20 = (bf16[32,3584]{1,0:T(8,128)(2,1)S(1)}, bf16[32,3584]{1,0:T(8,128)(2,1)S(1)}, u32[]{:S(2)}, u32[]{:S(2)}) collective-permute-start(bf16[32,3584]{1,0:T(8,128)(2,1)S(1)} %collective-permute-done.19.refs_6_.refs_7_), channel_id=1, source_target_pairs={{0,2},{4,0},{8,4},{12,8},{14,12},{10,14},{6,10},{2,6},{1,3},{5,1},... | collective-permute-start | bytes 688136 | tf_op jit(solution)/shard_map/ppermute | solution.py:242
  74.5 55.9 %all-to-all-start = ((bf16[8,128,512]{2,1,0:T(8,128)(2,1)}), bf16[8,128,512]{2,1,0:T(8,128)(2,1)S(1)}, u32[]{:S(2)}, u32[]{:S(2)}) async-start(bf16[8,128,512]{2,1,0:T(8,128)(2,1)} %tie.15), calls=%async_computation | async-start | bytes 2097152 | tf_op jit(solution)/shard_map/all_to_all | solution.py:264
  78.1 18.8 %collective-permute-start.27 = (bf16[32,3584]{1,0:T(8,128)(2,1)S(1)}, bf16[32,3584]{1,0:T(8,128)(2,1)S(1)}, u32[]{:S(2)}, u32[]{:S(2)}) collective-permute-start(bf16[32,3584]{1,0:T(8,128)(2,1)S(1)} %tie.14.refs_14_.refs_4_.refs_15_), channel_id=1, source_target_pairs={{0,2},{4,0},{8,4},{12,8},{14,12},{10,14},{6,10},{2,6},{1,3},{5,1},... | collective-permute-start | bytes 688136 | tf_op jit(solution)/shard_map/ppermute | solution.py:242
  80.0 17.8 %collective-permute-start.17 = (bf16[32,3584]{1,0:T(8,128)(2,1)S(1)}, bf16[32,3584]{1,0:T(8,128)(2,1)S(1)}, u32[]{:S(2)}, u32[]{:S(2)}) collective-permute-start(bf16[32,3584]{1,0:T(8,128)(2,1)S(1)} %tie.9.refs_3_.refs_1_.refs_4_), channel_id=1, source_target_pairs={{0,4},{4,8},{8,12},{12,14},{14,10},{10,6},{6,2},{2,0},{1,5},{5,9},... | collective-permute-start | bytes 688136 | tf_op jit(solution)/shard_map/ppermute | solution.py:242
  111.5 18.1 %collective-permute-start.34 = (f32[256,512]{1,0:T(8,128)S(1)}, f32[256,512]{1,0:T(8,128)S(1)}, u32[]{:S(2)}, u32[]{:S(2)}) collective-permute-start(f32[256,512]{1,0:T(8,128)S(1)} %last_sent.1.refs_0_), channel_id=1, source_target_pairs={{0,1},{1,0},{2,3},{3,2},{4,5},{5,4},{6,7},{7,6},{8,9},{9,8},{10,11... | collective-permute-start | bytes 1572872 | tf_op jit(solution)/shard_map/ppermute | solution.py:286
  112.0 17.6 %collective-permute-start.31 = (bf16[64,256]{1,0:T(8,128)(2,1)S(1)}, bf16[64,256]{1,0:T(8,128)(2,1)S(1)}, u32[]{:S(2)}, u32[]{:S(2)}) collective-permute-start(bf16[64,256]{1,0:T(8,128)(2,1)S(1)} %add_convert_fusion), channel_id=1, source_target_pairs={{0,4},{2,6},{4,8},{6,10},{8,12},{10,14},{12,0},{14,2},{1,5},{3,7},... | collective-permute-start | bytes 98312 | tf_op jit(solution)/shard_map/ppermute | solution.py:285
  120.9 8.6 %collective-permute-start.32 = (bf16[64,256]{1,0:T(8,128)(2,1)S(1)}, bf16[64,256]{1,0:T(8,128)(2,1)S(1)}, u32[]{:S(2)}, u32[]{:S(2)}) collective-permute-start(bf16[64,256]{1,0:T(8,128)(2,1)S(1)} %add_convert_fusion), channel_id=1, source_target_pairs={{0,8},{2,10},{4,12},{6,14},{8,0},{10,2},{12,4},{14,6},{1,9},{3,11}... | collective-permute-start | bytes 98312 | tf_op jit(solution)/shard_map/ppermute | solution.py:285
  120.9 8.6 %collective-permute-start.33 = (bf16[64,256]{1,0:T(8,128)(2,1)S(1)}, bf16[64,256]{1,0:T(8,128)(2,1)S(1)}, u32[]{:S(2)}, u32[]{:S(2)}) collective-permute-start(bf16[64,256]{1,0:T(8,128)(2,1)S(1)} %add_convert_fusion), channel_id=1, source_target_pairs={{0,12},{2,14},{4,0},{6,2},{8,4},{10,6},{12,8},{14,10},{1,13},{3,15... | collective-permute-start | bytes 98312 | tf_op jit(solution)/shard_map/ppermute | solution.py:285
  (38 other events, 762.5 us)

commit v13 on v11

--- a/solution.py
+++ b/solution.py
@@ -12,7 +12,6 @@
 TILE = 1024
 CHUNKS = 4
 MIB = 2**20
-MATMUL_MIB = 28
 
 
 def params(mib):
@@ -131,19 +130,19 @@
     rows = chunks[0][0][0].shape[0] * n
     share = down.shape[1] // 2
     ranks = shrink.shape[0]
-    spans = [(base, start, cuts_of(pieces[0].shape[1])) for pieces, base, start in chunks]
+    spans = [(base, start, cuts_of(pieces[0].shape[1])) for pieces, base, start, _ in chunks]
     sizes = [tile for _, _, cuts in spans for _, tile in cuts]
     width = sum(sizes)
     anywhere = pl.BlockSpec(memory_space=pl.ANY)
     held = [
         piece if i in late else in_hbm(piece)
-        for pieces, base, _ in chunks
-        for late in [(3, 4, n - 1) if base == 0 else (3, n - 2, n - 1)]
+        for pieces, _, _, late in chunks
         for i, piece in enumerate(pieces)
     ]
     args = [*after, *held, in_hbm(down), in_hbm(shrink), *(acc or ())]
     shapes = [(rows, share)] * len(sides) + [(ranks, rows)] * narrow
     columns = share * len(sides) + ranks * narrow
+    needed = 2 * width * (rows + columns) + (4 + 4 * (acc is not None)) * rows * columns
     return pl.pallas_call(
         functools.partial(matmul_kernel, n, len(after), spans, half, sides, narrow, acc is not None),
         grid_spec=pltpu.PrefetchScalarGridSpec(
@@ -158,7 +157,7 @@
             + [pltpu.SemaphoreType.DMA((len(sizes), n + 3)), pltpu.SemaphoreType.DMA((3,))],
         ),
         out_shape=[jax.ShapeDtypeStruct(shape, F32) for shape in shapes],
-        compiler_params=params(MATMUL_MIB),
+        compiler_params=params(-(-needed // MIB) + 4),
         cost_estimate=pl.CostEstimate(
             flops=4 * rows * width * columns,
             bytes_accessed=2 * width * (columns + rows) + 8 * rows * columns,
@@ -244,20 +243,19 @@
                     moving = lax.ppermute(moving, "store", pairs)
                     pieces.append(moving)
                 ends.append(moving)
-            chunks.append((pieces, way * n, start))
-        factors = lax.all_to_all(tie(blocks, ends[:4]), "store", 0, 0)
+            late = ((long,), (n - 1,)) if chunk < 2 else ((short, long, n - 1), (short, n - 2, n - 1))
+            chunks.append((pieces, way * n, start, late[way]))
+        factors = lax.all_to_all(tie(blocks, [ends[0], ends[3]]), "store", 0, 0)
 
         call = functools.partial(chunk_matmul, scalars, half)
         first, last = chunks[:CHUNKS // 2], chunks[CHUNKS // 2:]
-        acc = call(first, down, shrink_rows, None, (0, 1), True, "first_chunks")
-        narrow, = call(last, down, shrink_rows, acc[2:], (), True, "last_narrow")
+        send, narrow = call(chunks, down, shrink_rows, None, (1,), True, "narrow_and_sent")
         mine = [
             jnp.where((row_slot == store * owned + i)[None, :], narrow[i * rank:(i + 1) * rank], 0.0)
             for i in range(owned)
         ]
         mine = sum(mine[1:], mine[0])
-        send, = call(last, down, shrink_rows, acc[1:2], (1,), False, "last_sent", [mine])
-        kept, = call(last, down, shrink_rows, acc[:1], (0,), False, "last_kept", [send])
+        kept = call(first, down, shrink_rows, None, (0,), False, "kept_first", [mine])
         where = [(s, t) for s in range(n) for t in range(cores)]
         whole = mine
         for ds in range(2):
@@ -266,6 +264,7 @@
                     pairs = [(s * cores + t, (s ^ ds) * cores + (t + dt) % cores) for s, t in where]
                     whole = whole + lax.ppermute(mine, ("store", "tensor"), pairs)
         column = whole.astype(BF16)
+        kept, = call(last, down, shrink_rows, kept, (0,), False, "kept_last", [column])
         shrunk = column
         for ds in range(2, n, 2):
             shrunk = shrunk + lax.ppermute(column, "store", [(s, (s + ds) % n) for s in range(n)])

time: 113 us -> 121 us (1.071)
  waiting for transfers between devices: 17.3 us -> 28.6 us
  local copies, waits for them, and re-layouts: 9.83 us -> 5.73 us
  starting transfers between devices: 53.7 us -> 56.7 us
  Pallas kernels: 30.9 us -> 29.1 us
    ppermute x28, waiting for transfers between devices: 17.3 us -> 28.6 us  [shards(): moving = lax.ppermute(moving, 'store', pairs)]
    unnamed x56 -> x48, local copies, waits for them, and re-layouts: 7.64 us -> 3.5 us
    ppermute x3, starting transfers between devices: 4.44 us -> 7.51 us  [shards(): lax.ppermute(column, 'store', [(s, (s + ds) % n) for s in range(n)])]
    pallas_call x4 -> x3, Pallas kernels: 26.2 us -> 24.4 us  [chunk_matmul(): pl.pallas_call(functools.partial(matmul_kernel, n, len(after), spans, hal...]
    all_to_all x1, starting transfers between devices: 4.88 us -> 6.32 us  [shards(): factors = lax.all_to_all(tie(blocks, [ends[0], ends[3]]), 'store', 0, 0)]
  transfers between devices with their start and end apart: 36 -> 36, of which waited for: 10 -> 14; matrix products, arithmetic and copies ran while one was open for 1% -> 0% of each run, Pallas kernels for 26% -> 20%
where the time goes in v13:
time: 121 us
  starting transfers between devices  56.7 us (47%)
  Pallas kernels  29.1 us (24%)
  waiting for transfers between devices  28.6 us (24%)
  local copies, waits for them, and re-layouts  5.73 us (5%)
    ppermute x28, starting transfers between devices, shards(): moving = lax.ppermute(moving, 'store', pairs)  40.6 us
    ppermute x28, waiting for transfers between devices, shards(): moving = lax.ppermute(moving, 'store', pairs)  28.6 us
    pallas_call x3, Pallas kernels, chunk_matmul(): pl.pallas_call(functools.partial(matmul_kernel, n, len(after), spans, hal...  24.4 us
    ppermute x3, starting transfers between devices, shards(): lax.ppermute(column, 'store', [(s, (s + ds) % n) for s in range(n)])  7.51 us
    all_to_all x1, starting transfers between devices, shards(): factors = lax.all_to_all(tie(blocks, [ends[0], ends[3]]), 'store', 0, 0)  6.32 us
    unnamed x48, local copies, waits for them, and re-layouts  3.5 us
    pallas_call x1, Pallas kernels, expand_blocks(): pl.pallas_call(split_kernel, grid_spec=pltpu.PrefetchScalarGridSpec(num_s...  3.36 us
  transfers between devices with their start and end apart: 36, of which 14 were waited for; matrix products, arithmetic and copies ran while one was open for 0% of the time, Pallas kernels for 20%

profile of v13, /device:TPU:0, one launch (start us, length us, event | category | flops | bytes accessed | tf_op | source)
XLA Modules:
  0.0 120.7 jit_solution(16860190298759726933)
XLA Ops:
  2.1 1.6 %copy-done.1 = bf16[2,64,8192]{2,1,0:T(8,128)(2,1)S(1)} copy-done((bf16[2,64,8192]{2,1,0:T(8,128)(2,1)S(1)}, bf16[2,64,8192]{2,1,0:T(8,128)(2,1)}, u32[]{:S(2)}) %copy-start.1) | copy-done | bytes 2097176
  3.7 3.4 %expand_blocks.1 = (bf16[8,128,512]{2,1,0:T(8,128)(2,1)}, f32[8,128]{1,0:T(8,128)S(1)}) custom-call(s32[18]{0:T(128)S(1)} %dynamic-slice_bitcast_fusion.scalars, bf16[128,8192]{1,0:T(8,128)(2,1)S(1)} %bitcast.9), custom_call_target="tpu_custom_call" | custom-call | bytes 2097152 | tf_op jit(solution)/shard_map/expand_blocks/pallas_call | solution.py:38
  7.1 3.0 %collective-permute-start.24 = (bf16[32,3584]{1,0:T(8,128)(2,1)S(1)}, bf16[32,3584]{1,0:T(8,128)(2,1)S(1)}, u32[]{:S(2)}, u32[]{:S(2)}) collective-permute-start(bf16[32,3584]{1,0:T(8,128)(2,1)S(1)} %tie.2.refs_24_.refs_9_), channel_id=1, source_target_pairs={{0,2},{4,0},{8,4},{12,8},{14,12},{10,14},{6,10},{2,6},{1,3},{5,1},... | collective-permute-start | bytes 688136 | tf_op jit(solution)/shard_map/ppermute | solution.py:243
  10.1 2.0 %collective-permute-start.10 = (bf16[32,3584]{1,0:T(8,128)(2,1)S(1)}, bf16[32,3584]{1,0:T(8,128)(2,1)S(1)}, u32[]{:S(2)}, u32[]{:S(2)}) collective-permute-start(bf16[32,3584]{1,0:T(8,128)(2,1)S(1)} %get-tuple-element.14.refs_8_.refs_9_), channel_id=1, source_target_pairs={{0,2},{4,0},{8,4},{12,8},{14,12},{10,14},{6,10},{2,6},{1,3},{5,1},... | collective-permute-start | bytes 688136 | tf_op jit(solution)/shard_map/ppermute | solution.py:243
  12.1 2.0 %collective-permute-start.14 = (bf16[32,3584]{1,0:T(8,128)(2,1)S(1)}, bf16[32,3584]{1,0:T(8,128)(2,1)S(1)}, u32[]{:S(2)}, u32[]{:S(2)}) collective-permute-start(bf16[32,3584]{1,0:T(8,128)(2,1)S(1)} %get-tuple-element.16.refs_16_.refs_1_), channel_id=1, source_target_pairs={{0,4},{4,8},{8,12},{12,14},{14,10},{10,6},{6,2},{2,0},{1,5},{5,9},... | collective-permute-start | bytes 688136 | tf_op jit(solution)/shard_map/ppermute | solution.py:243
  14.2 2.4 %collective-permute-done.24.refs_28_.refs_13_ = bf16[32,3584]{1,0:T(8,128)(2,1)S(1)} collective-permute-done((bf16[32,3584]{1,0:T(8,128)(2,1)S(1)}, bf16[32,3584]{1,0:T(8,128)(2,1)S(1)}, u32[]{:S(2)}, u32[]{:S(2)}) %collective-permute-start.24) | collective-permute-done | bytes 229408 | tf_op jit(solution)/shard_map/ppermute | solution.py:243
  16.5 2.0 %collective-permute-start.18 = (bf16[32,3584]{1,0:T(8,128)(2,1)S(1)}, bf16[32,3584]{1,0:T(8,128)(2,1)S(1)}, u32[]{:S(2)}, u32[]{:S(2)}) collective-permute-start(bf16[32,3584]{1,0:T(8,128)(2,1)S(1)} %get-tuple-element.16.refs_16_.refs_1_), channel_id=1, source_target_pairs={{0,2},{4,0},{8,4},{12,8},{14,12},{10,14},{6,10},{2,6},{1,3},{5,1},... | collective-permute-start | bytes 688136 | tf_op jit(solution)/shard_map/ppermute | solution.py:243
  21.5 2.1 %collective-permute-start.7 = (bf16[32,3584]{1,0:T(8,128)(2,1)S(1)}, bf16[32,3584]{1,0:T(8,128)(2,1)S(1)}, u32[]{:S(2)}, u32[]{:S(2)}) collective-permute-start(bf16[32,3584]{1,0:T(8,128)(2,1)S(1)} %get-tuple-element.14.refs_8_.refs_9_), channel_id=1, source_target_pairs={{0,4},{4,8},{8,12},{12,14},{14,10},{10,6},{6,2},{2,0},{1,5},{5,9},... | collective-permute-start | bytes 688136 | tf_op jit(solution)/shard_map/ppermute | solution.py:243
  25.1 3.3 %collective-permute-done.14.refs_17_.refs_2_ = bf16[32,3584]{1,0:T(8,128)(2,1)S(1)} collective-permute-done((bf16[32,3584]{1,0:T(8,128)(2,1)S(1)}, bf16[32,3584]{1,0:T(8,128)(2,1)S(1)}, u32[]{:S(2)}, u32[]{:S(2)}) %collective-permute-start.14) | collective-permute-done | bytes 229408 | tf_op jit(solution)/shard_map/ppermute | solution.py:243
  28.4 2.0 %collective-permute-start.11 = (bf16[32,3584]{1,0:T(8,128)(2,1)S(1)}, bf16[32,3584]{1,0:T(8,128)(2,1)S(1)}, u32[]{:S(2)}, u32[]{:S(2)}) collective-permute-start(bf16[32,3584]{1,0:T(8,128)(2,1)S(1)} %collective-permute-done.10.refs_12_.refs_13_), channel_id=1, source_target_pairs={{0,2},{4,0},{8,4},{12,8},{14,12},{10,14},{6,10},{2,6},{1,3},{5,1},... | collective-permute-start | bytes 688136 | tf_op jit(solution)/shard_map/ppermute | solution.py:243
  31.3 2.1 %collective-permute-start.1 = (bf16[32,3584]{1,0:T(8,128)(2,1)S(1)}, bf16[32,3584]{1,0:T(8,128)(2,1)S(1)}, u32[]{:S(2)}, u32[]{:S(2)}) collective-permute-start(bf16[32,3584]{1,0:T(8,128)(2,1)S(1)} %collective-permute-done.refs_1_.refs_2_), channel_id=1, source_target_pairs={{0,4},{4,8},{8,12},{12,14},{14,10},{10,6},{6,2},{2,0},{1,5},{5,9},... | collective-permute-start | bytes 688136 | tf_op jit(solution)/shard_map/ppermute | solution.py:243
  36.2 2.0 %collective-permute-start.19 = (bf16[32,3584]{1,0:T(8,128)(2,1)S(1)}, bf16[32,3584]{1,0:T(8,128)(2,1)}, u32[]{:S(2)}, u32[]{:S(2)}) collective-permute-start(bf16[32,3584]{1,0:T(8,128)(2,1)S(1)} %collective-permute-done.18.refs_21_.refs_6_), channel_id=1, source_target_pairs={{0,2},{4,0},{8,4},{12,8},{14,12},{10,14},{6,10},{2,6},{1,3},{5,1},... | collective-permute-start | bytes 688136 | tf_op jit(solution)/shard_map/ppermute | solution.py:243
  41.1 2.1 %collective-permute-start.8 = (bf16[32,3584]{1,0:T(8,128)(2,1)S(1)}, bf16[32,3584]{1,0:T(8,128)(2,1)}, u32[]{:S(2)}, u32[]{:S(2)}) collective-permute-start(bf16[32,3584]{1,0:T(8,128)(2,1)S(1)} %collective-permute-done.7.refs_9_.refs_10_), channel_id=1, source_target_pairs={{0,4},{4,8},{8,12},{12,14},{14,10},{10,6},{6,2},{2,0},{1,5},{5,9},... | collective-permute-start | bytes 688136 | tf_op jit(solution)/shard_map/ppermute | solution.py:243
  44.7 3.3 %collective-permute-done.15.refs_18_.refs_3_ = bf16[32,3584]{1,0:T(8,128)(2,1)S(1)} collective-permute-done((bf16[32,3584]{1,0:T(8,128)(2,1)S(1)}, bf16[32,3584]{1,0:T(8,128)(2,1)S(1)}, u32[]{:S(2)}, u32[]{:S(2)}) %collective-permute-start.15) | collective-permute-done | bytes 229408 | tf_op jit(solution)/shard_map/ppermute | solution.py:243
  48.1 2.0 %collective-permute-start.26 = (bf16[32,3584]{1,0:T(8,128)(2,1)S(1)}, bf16[32,3584]{1,0:T(8,128)(2,1)S(1)}, u32[]{:S(2)}, u32[]{:S(2)}) collective-permute-start(bf16[32,3584]{1,0:T(8,128)(2,1)S(1)} %collective-permute-done.25.refs_29_.refs_14_), channel_id=1, source_target_pairs={{0,2},{4,0},{8,4},{12,8},{14,12},{10,14},{6,10},{2,6},{1,3},{5,1},... | collective-permute-start | bytes 688136 | tf_op jit(solution)/shard_map/ppermute | solution.py:243
  51.0 2.1 %collective-permute-start.23 = (bf16[32,3584]{1,0:T(8,128)(2,1)S(1)}, bf16[32,3584]{1,0:T(8,128)(2,1)S(1)}, u32[]{:S(2)}, u32[]{:S(2)}) collective-permute-start(bf16[32,3584]{1,0:T(8,128)(2,1)S(1)} %collective-permute-done.22.refs_26_.refs_11_), channel_id=1, source_target_pairs={{0,4},{4,8},{8,12},{12,14},{14,10},{10,6},{6,2},{2,0},{1,5},{5,9},... | collective-permute-start | bytes 688136 | tf_op jit(solution)/shard_map/ppermute | solution.py:243
  53.1 1.6 %collective-permute-start.16 = (bf16[32,3584]{1,0:T(8,128)(2,1)S(1)}, bf16[32,3584]{1,0:T(8,128)(2,1)S(1)}, u32[]{:S(2)}, u32[]{:S(2)}) collective-permute-start(bf16[32,3584]{1,0:T(8,128)(2,1)S(1)} %collective-permute-done.15.refs_18_.refs_3_), channel_id=1, source_target_pairs={{0,4},{4,8},{8,12},{12,14},{14,10},{10,6},{6,2},{2,0},{1,5},{5,9},... | collective-permute-start | bytes 688136 | tf_op jit(solution)/shard_map/ppermute | solution.py:243
  55.9 2.0 %collective-permute-start.13 = (bf16[32,3584]{1,0:T(8,128)(2,1)S(1)}, bf16[32,3584]{1,0:T(8,128)(2,1)S(1)}, u32[]{:S(2)}, u32[]{:S(2)}) collective-permute-start(bf16[32,3584]{1,0:T(8,128)(2,1)S(1)} %collective-permute-done.12.refs_14_.refs_15_), channel_id=1, source_target_pairs={{0,2},{4,0},{8,4},{12,8},{14,12},{10,14},{6,10},{2,6},{1,3},{5,1},... | collective-permute-start | bytes 688136 | tf_op jit(solution)/shard_map/ppermute | solution.py:243
  58.0 2.8 %collective-permute-done.26.refs_30_.refs_15_ = bf16[32,3584]{1,0:T(8,128)(2,1)S(1)} collective-permute-done((bf16[32,3584]{1,0:T(8,128)(2,1)S(1)}, bf16[32,3584]{1,0:T(8,128)(2,1)S(1)}, u32[]{:S(2)}, u32[]{:S(2)}) %collective-permute-start.26) | collective-permute-done | bytes 229408 | tf_op jit(solution)/shard_map/ppermute | solution.py:243
  60.8 2.0 %collective-permute-start.20 = (bf16[32,3584]{1,0:T(8,128)(2,1)}, bf16[32,3584]{1,0:T(8,128)(2,1)S(1)}, u32[]{:S(2)}, u32[]{:S(2)}) collective-permute-start(bf16[32,3584]{1,0:T(8,128)(2,1)} %collective-permute-done.19.refs_22_.refs_7_), channel_id=1, source_target_pairs={{0,2},{4,0},{8,4},{12,8},{14,12},{10,14},{6,10},{2,6},{1,3},{5,1},... | collective-permute-start | bytes 688136 | tf_op jit(solution)/shard_map/ppermute | solution.py:243
  64.4 3.3 %collective-permute-done.16.refs_19_.refs_4_ = bf16[32,3584]{1,0:T(8,128)(2,1)S(1)} collective-permute-done((bf16[32,3584]{1,0:T(8,128)(2,1)S(1)}, bf16[32,3584]{1,0:T(8,128)(2,1)S(1)}, u32[]{:S(2)}, u32[]{:S(2)}) %collective-permute-start.16) | collective-permute-done | bytes 229408 | tf_op jit(solution)/shard_map/ppermute | solution.py:243
  67.8 2.0 %collective-permute-start.27 = (bf16[32,3584]{1,0:T(8,128)(2,1)S(1)}, bf16[32,3584]{1,0:T(8,128)(2,1)S(1)}, u32[]{:S(2)}, u32[]{:S(2)}) collective-permute-start(bf16[32,3584]{1,0:T(8,128)(2,1)S(1)} %collective-permute-done.26.refs_30_.refs_15_), channel_id=1, source_target_pairs={{0,2},{4,0},{8,4},{12,8},{14,12},{10,14},{6,10},{2,6},{1,3},{5,1},... | collective-permute-start | bytes 688136 | tf_op jit(solution)/shard_map/ppermute | solution.py:243
  69.8 2.9 %collective-permute-done.3.refs_4_.refs_1_.refs_5_ = bf16[32,3584]{1,0:T(8,128)(2,1)S(1)} collective-permute-done((bf16[32,3584]{1,0:T(8,128)(2,1)S(1)}, bf16[32,3584]{1,0:T(8,128)(2,1)S(1)}, u32[]{:S(2)}, u32[]{:S(2)}) %collective-permute-start.3) | collective-permute-done | bytes 229408 | tf_op jit(solution)/shard_map/ppermute | solution.py:243
  73.1 6.3 %all-to-all-start = ((bf16[8,128,512]{2,1,0:T(8,128)(2,1)}), bf16[8,128,512]{2,1,0:T(8,128)(2,1)S(1)}, u32[]{:S(2)}, u32[]{:S(2)}) async-start(bf16[8,128,512]{2,1,0:T(8,128)(2,1)} %tie.3), calls=%async_computation | async-start | bytes 2097152 | tf_op jit(solution)/shard_map/all_to_all | solution.py:248
  79.4 1.9 %collective-permute-done.27.refs_31_.refs_16_ = bf16[32,3584]{1,0:T(8,128)(2,1)S(1)} collective-permute-done((bf16[32,3584]{1,0:T(8,128)(2,1)S(1)}, bf16[32,3584]{1,0:T(8,128)(2,1)S(1)}, u32[]{:S(2)}, u32[]{:S(2)}) %collective-permute-start.27) | collective-permute-done | bytes 229408 | tf_op jit(solution)/shard_map/ppermute | solution.py:243
  81.4 1.7 %collective-permute-done.17.refs_20_.refs_5_ = bf16[32,3584]{1,0:T(8,128)(2,1)S(1)} collective-permute-done((bf16[32,3584]{1,0:T(8,128)(2,1)S(1)}, bf16[32,3584]{1,0:T(8,128)(2,1)S(1)}, u32[]{:S(2)}, u32[]{:S(2)}) %collective-permute-start.17) | collective-permute-done | bytes 229408 | tf_op jit(solution)/shard_map/ppermute | solution.py:243
  83.0 12.6 %narrow_and_sent.1 = (f32[256,512]{1,0:T(8,128)S(1)}, f32[128,256]{1,0:T(8,128)S(1)}) custom-call(s32[18]{0:T(128)S(1)} %dynamic-slice_bitcast_fusion.scalars, bf16[32,3584]{1,0:T(8,128)(2,1)} %copy-done.5, bf16[32,3584]{1,0:T(8,128)(2,1)} %copy-done.8, bf16[32,3584]{1,0:T(8,128)(2,1)} %copy-done.12, bf16[32,3584]{1,0:T(8,128)(2,1)} %copy-done.14, ...), custom_call_target="tpu_custom_call" | custom-call | flops 9395240960 | bytes 27000832 | tf_op jit(solution)/shard_map/narrow_and_sent/pallas_call | solution.py:146
  95.8 2.1 %collective-permute-start.29 = (f32[64,256]{1,0:T(8,128)S(1)}, f32[64,256]{1,0:T(8,128)S(1)}, u32[]{:S(2)}, u32[]{:S(2)}) collective-permute-start(f32[64,256]{1,0:T(8,128)S(1)} %select_add_fusion.refs_0_), channel_id=1, source_target_pairs={{0,2},{1,3},{2,0},{3,1},{4,6},{5,7},{6,4},{7,5},{8,10},{9,11},{10,... | collective-permute-start | bytes 196616 | tf_op jit(solution)/shard_map/ppermute | solution.py:265
  98.0 6.0 %kept_first.1.refs_19_ = f32[256,512]{1,0:T(8,128)S(1)} custom-call(s32[18]{0:T(128)S(1)} %dynamic-slice_bitcast_fusion.scalars, f32[64,256]{1,0:T(8,128)S(1)} %select_add_fusion.refs_0_, bf16[32,3584]{1,0:T(8,128)(2,1)} %copy-done.5, bf16[32,3584]{1,0:T(8,128)(2,1)} %copy-done.8, bf16[32,3584]{1,0:T(8,128)(2,1)} %copy-done.12, bf16[32,3584]{1,0:T(8,128)(2,1)} %copy-done.14, ...), custom_call_target="tpu_custom_call" | custom-call | flops 3758096384 | bytes 12058624 | tf_op jit(solution)/shard_map/kept_first/pallas_call | solution.py:146
  104.1 2.2 %collective-permute-start.31 = (bf16[64,256]{1,0:T(8,128)(2,1)S(1)}, bf16[64,256]{1,0:T(8,128)(2,1)S(1)}, u32[]{:S(2)}, u32[]{:S(2)}) collective-permute-start(bf16[64,256]{1,0:T(8,128)(2,1)S(1)} %add_convert_fusion.refs_0_), channel_id=1, source_target_pairs={{0,4},{2,6},{4,8},{6,10},{8,12},{10,14},{12,0},{14,2},{1,5},{3,7},... | collective-permute-start | bytes 98312 | tf_op jit(solution)/shard_map/ppermute | solution.py:270
  106.2 4.4 %collective-permute-start.32 = (bf16[64,256]{1,0:T(8,128)(2,1)S(1)}, bf16[64,256]{1,0:T(8,128)(2,1)S(1)}, u32[]{:S(2)}, u32[]{:S(2)}) collective-permute-start(bf16[64,256]{1,0:T(8,128)(2,1)S(1)} %add_convert_fusion.refs_0_), channel_id=1, source_target_pairs={{0,8},{2,10},{4,12},{6,14},{8,0},{10,2},{12,4},{14,6},{1,9},{3,11}... | collective-permute-start | bytes 98312 | tf_op jit(solution)/shard_map/ppermute | solution.py:270
  111.6 5.8 %kept_last.1.kept = f32[256,512]{1,0:T(8,128)S(1)} custom-call(s32[18]{0:T(128)S(1)} %dynamic-slice_bitcast_fusion.scalars, bf16[64,256]{1,0:T(8,128)(2,1)S(1)} %add_convert_fusion.refs_0_, bf16[32,3584]{1,0:T(8,128)(2,1)} %copy-done.6, bf16[32,3584]{1,0:T(8,128)(2,1)} %copy-done.17, bf16[32,3584]{1,0:T(8,128)(2,1)} %copy-done.21, ...), custom_call_target="tpu_custom_call" | custom-call | flops 3758096384 | bytes 12058624 | tf_op jit(solution)/shard_map/kept_last/pallas_call | solution.py:146
  (103 shorter events, 23.6 us)
Async XLA Ops:
  7.1 9.5 %collective-permute-start.24 = (bf16[32,3584]{1,0:T(8,128)(2,1)S(1)}, bf16[32,3584]{1,0:T(8,128)(2,1)S(1)}, u32[]{:S(2)}, u32[]{:S(2)}) collective-permute-start(bf16[32,3584]{1,0:T(8,128)(2,1)S(1)} %tie.2.refs_24_.refs_9_), channel_id=1, source_target_pairs={{0,2},{4,0},{8,4},{12,8},{14,12},{10,14},{6,10},{2,6},{1,3},{5,1},... | collective-permute-start | bytes 688136 | tf_op jit(solution)/shard_map/ppermute | solution.py:243
  10.1 8.5 %collective-permute-start.21 = (bf16[32,3584]{1,0:T(8,128)(2,1)S(1)}, bf16[32,3584]{1,0:T(8,128)(2,1)S(1)}, u32[]{:S(2)}, u32[]{:S(2)}) collective-permute-start(bf16[32,3584]{1,0:T(8,128)(2,1)S(1)} %tie.2.refs_24_.refs_9_), channel_id=1, source_target_pairs={{0,4},{4,8},{8,12},{12,14},{14,10},{10,6},{6,2},{2,0},{1,5},{5,9},... | collective-permute-start | bytes 688136 | tf_op jit(solution)/shard_map/ppermute | solution.py:243
  10.1 11.3 %collective-permute-start.10 = (bf16[32,3584]{1,0:T(8,128)(2,1)S(1)}, bf16[32,3584]{1,0:T(8,128)(2,1)S(1)}, u32[]{:S(2)}, u32[]{:S(2)}) collective-permute-start(bf16[32,3584]{1,0:T(8,128)(2,1)S(1)} %get-tuple-element.14.refs_8_.refs_9_), channel_id=1, source_target_pairs={{0,2},{4,0},{8,4},{12,8},{14,12},{10,14},{6,10},{2,6},{1,3},{5,1},... | collective-permute-start | bytes 688136 | tf_op jit(solution)/shard_map/ppermute | solution.py:243
  12.1 11.4 %collective-permute-start = (bf16[32,3584]{1,0:T(8,128)(2,1)S(1)}, bf16[32,3584]{1,0:T(8,128)(2,1)S(1)}, u32[]{:S(2)}, u32[]{:S(2)}) collective-permute-start(bf16[32,3584]{1,0:T(8,128)(2,1)S(1)} %get-tuple-element.15.refs_0_.refs_1_), channel_id=1, source_target_pairs={{0,4},{4,8},{8,12},{12,14},{14,10},{10,6},{6,2},{2,0},{1,5},{5,9},... | collective-permute-start | bytes 688136 | tf_op jit(solution)/shard_map/ppermute | solution.py:243
  12.1 16.3 %collective-permute-start.14 = (bf16[32,3584]{1,0:T(8,128)(2,1)S(1)}, bf16[32,3584]{1,0:T(8,128)(2,1)S(1)}, u32[]{:S(2)}, u32[]{:S(2)}) collective-permute-start(bf16[32,3584]{1,0:T(8,128)(2,1)S(1)} %get-tuple-element.16.refs_16_.refs_1_), channel_id=1, source_target_pairs={{0,4},{4,8},{8,12},{12,14},{14,10},{10,6},{6,2},{2,0},{1,5},{5,9},... | collective-permute-start | bytes 688136 | tf_op jit(solution)/shard_map/ppermute | solution.py:243
  16.5 11.9 %collective-permute-start.18 = (bf16[32,3584]{1,0:T(8,128)(2,1)S(1)}, bf16[32,3584]{1,0:T(8,128)(2,1)S(1)}, u32[]{:S(2)}, u32[]{:S(2)}) collective-permute-start(bf16[32,3584]{1,0:T(8,128)(2,1)S(1)} %get-tuple-element.16.refs_16_.refs_1_), channel_id=1, source_target_pairs={{0,2},{4,0},{8,4},{12,8},{14,12},{10,14},{6,10},{2,6},{1,3},{5,1},... | collective-permute-start | bytes 688136 | tf_op jit(solution)/shard_map/ppermute | solution.py:243
  18.6 12.7 %collective-permute-start.4 = (bf16[32,3584]{1,0:T(8,128)(2,1)S(1)}, bf16[32,3584]{1,0:T(8,128)(2,1)S(1)}, u32[]{:S(2)}, u32[]{:S(2)}) collective-permute-start(bf16[32,3584]{1,0:T(8,128)(2,1)S(1)} %get-tuple-element.15.refs_0_.refs_1_), channel_id=1, source_target_pairs={{0,2},{4,0},{8,4},{12,8},{14,12},{10,14},{6,10},{2,6},{1,3},{5,1},... | collective-permute-start | bytes 688136 | tf_op jit(solution)/shard_map/ppermute | solution.py:243
  21.5 11.9 %collective-permute-start.7 = (bf16[32,3584]{1,0:T(8,128)(2,1)S(1)}, bf16[32,3584]{1,0:T(8,128)(2,1)S(1)}, u32[]{:S(2)}, u32[]{:S(2)}) collective-permute-start(bf16[32,3584]{1,0:T(8,128)(2,1)S(1)} %get-tuple-element.14.refs_8_.refs_9_), channel_id=1, source_target_pairs={{0,4},{4,8},{8,12},{12,14},{14,10},{10,6},{6,2},{2,0},{1,5},{5,9},... | collective-permute-start | bytes 688136 | tf_op jit(solution)/shard_map/ppermute | solution.py:243
  23.5 12.7 %collective-permute-start.25 = (bf16[32,3584]{1,0:T(8,128)(2,1)S(1)}, bf16[32,3584]{1,0:T(8,128)(2,1)S(1)}, u32[]{:S(2)}, u32[]{:S(2)}) collective-permute-start(bf16[32,3584]{1,0:T(8,128)(2,1)S(1)} %collective-permute-done.24.refs_28_.refs_13_), channel_id=1, source_target_pairs={{0,2},{4,0},{8,4},{12,8},{14,12},{10,14},{6,10},{2,6},{1,3},{5,1},... | collective-permute-start | bytes 688136 | tf_op jit(solution)/shard_map/ppermute | solution.py:243
  28.4 9.8 %collective-permute-start.22 = (bf16[32,3584]{1,0:T(8,128)(2,1)S(1)}, bf16[32,3584]{1,0:T(8,128)(2,1)S(1)}, u32[]{:S(2)}, u32[]{:S(2)}) collective-permute-start(bf16[32,3584]{1,0:T(8,128)(2,1)S(1)} %collective-permute-done.21.refs_25_.refs_10_), channel_id=1, source_target_pairs={{0,4},{4,8},{8,12},{12,14},{14,10},{10,6},{6,2},{2,0},{1,5},{5,9},... | collective-permute-start | bytes 688136 | tf_op jit(solution)/shard_map/ppermute | solution.py:243
  28.4 12.7 %collective-permute-start.11 = (bf16[32,3584]{1,0:T(8,128)(2,1)S(1)}, bf16[32,3584]{1,0:T(8,128)(2,1)S(1)}, u32[]{:S(2)}, u32[]{:S(2)}) collective-permute-start(bf16[32,3584]{1,0:T(8,128)(2,1)S(1)} %collective-permute-done.10.refs_12_.refs_13_), channel_id=1, source_target_pairs={{0,2},{4,0},{8,4},{12,8},{14,12},{10,14},{6,10},{2,6},{1,3},{5,1},... | collective-permute-start | bytes 688136 | tf_op jit(solution)/shard_map/ppermute | solution.py:243
  31.3 11.9 %collective-permute-start.1 = (bf16[32,3584]{1,0:T(8,128)(2,1)S(1)}, bf16[32,3584]{1,0:T(8,128)(2,1)S(1)}, u32[]{:S(2)}, u32[]{:S(2)}) collective-permute-start(bf16[32,3584]{1,0:T(8,128)(2,1)S(1)} %collective-permute-done.refs_1_.refs_2_), channel_id=1, source_target_pairs={{0,4},{4,8},{8,12},{12,14},{14,10},{10,6},{6,2},{2,0},{1,5},{5,9},... | collective-permute-start | bytes 688136 | tf_op jit(solution)/shard_map/ppermute | solution.py:243
  33.4 14.7 %collective-permute-start.15 = (bf16[32,3584]{1,0:T(8,128)(2,1)S(1)}, bf16[32,3584]{1,0:T(8,128)(2,1)S(1)}, u32[]{:S(2)}, u32[]{:S(2)}) collective-permute-start(bf16[32,3584]{1,0:T(8,128)(2,1)S(1)} %collective-permute-done.14.refs_17_.refs_2_), channel_id=1, source_target_pairs={{0,4},{4,8},{8,12},{12,14},{14,10},{10,6},{6,2},{2,0},{1,5},{5,9},... | collective-permute-start | bytes 688136 | tf_op jit(solution)/shard_map/ppermute | solution.py:243
  36.2 11.9 %collective-permute-start.19 = (bf16[32,3584]{1,0:T(8,128)(2,1)S(1)}, bf16[32,3584]{1,0:T(8,128)(2,1)}, u32[]{:S(2)}, u32[]{:S(2)}) collective-permute-start(bf16[32,3584]{1,0:T(8,128)(2,1)S(1)} %collective-permute-done.18.refs_21_.refs_6_), channel_id=1, source_target_pairs={{0,2},{4,0},{8,4},{12,8},{14,12},{10,14},{6,10},{2,6},{1,3},{5,1},... | collective-permute-start | bytes 688136 | tf_op jit(solution)/shard_map/ppermute | solution.py:243
  38.2 12.8 %collective-permute-start.5 = (bf16[32,3584]{1,0:T(8,128)(2,1)S(1)}, bf16[32,3584]{1,0:T(8,128)(2,1)}, u32[]{:S(2)}, u32[]{:S(2)}) collective-permute-start(bf16[32,3584]{1,0:T(8,128)(2,1)S(1)} %collective-permute-done.4.refs_5_.refs_6_), channel_id=1, source_target_pairs={{0,2},{4,0},{8,4},{12,8},{14,12},{10,14},{6,10},{2,6},{1,3},{5,1},... | collective-permute-start | bytes 688136 | tf_op jit(solution)/shard_map/ppermute | solution.py:243
  41.1 12.0 %collective-permute-start.8 = (bf16[32,3584]{1,0:T(8,128)(2,1)S(1)}, bf16[32,3584]{1,0:T(8,128)(2,1)}, u32[]{:S(2)}, u32[]{:S(2)}) collective-permute-start(bf16[32,3584]{1,0:T(8,128)(2,1)S(1)} %collective-permute-done.7.refs_9_.refs_10_), channel_id=1, source_target_pairs={{0,4},{4,8},{8,12},{12,14},{14,10},{10,6},{6,2},{2,0},{1,5},{5,9},... | collective-permute-start | bytes 688136 | tf_op jit(solution)/shard_map/ppermute | solution.py:243
  43.2 12.7 %collective-permute-start.12 = (bf16[32,3584]{1,0:T(8,128)(2,1)S(1)}, bf16[32,3584]{1,0:T(8,128)(2,1)S(1)}, u32[]{:S(2)}, u32[]{:S(2)}) collective-permute-start(bf16[32,3584]{1,0:T(8,128)(2,1)S(1)} %collective-permute-done.11.refs_13_.refs_14_), channel_id=1, source_target_pairs={{0,2},{4,0},{8,4},{12,8},{14,12},{10,14},{6,10},{2,6},{1,3},{5,1},... | collective-permute-start | bytes 688136 | tf_op jit(solution)/shard_map/ppermute | solution.py:243
  48.1 9.8 %collective-permute-start.2 = (bf16[32,3584]{1,0:T(8,128)(2,1)S(1)}, bf16[32,3584]{1,0:T(8,128)(2,1)S(1)}, u32[]{:S(2)}, u32[]{:S(2)}) collective-permute-start(bf16[32,3584]{1,0:T(8,128)(2,1)S(1)} %collective-permute-done.1.refs_2_.refs_3_), channel_id=1, source_target_pairs={{0,4},{4,8},{8,12},{12,14},{14,10},{10,6},{6,2},{2,0},{1,5},{5,9},... | collective-permute-start | bytes 688136 | tf_op jit(solution)/shard_map/ppermute | solution.py:243
  48.1 12.7 %collective-permute-start.26 = (bf16[32,3584]{1,0:T(8,128)(2,1)S(1)}, bf16[32,3584]{1,0:T(8,128)(2,1)S(1)}, u32[]{:S(2)}, u32[]{:S(2)}) collective-permute-start(bf16[32,3584]{1,0:T(8,128)(2,1)S(1)} %collective-permute-done.25.refs_29_.refs_14_), channel_id=1, source_target_pairs={{0,2},{4,0},{8,4},{12,8},{14,12},{10,14},{6,10},{2,6},{1,3},{5,1},... | collective-permute-start | bytes 688136 | tf_op jit(solution)/shard_map/ppermute | solution.py:243
  51.0 11.8 %collective-permute-start.23 = (bf16[32,3584]{1,0:T(8,128)(2,1)S(1)}, bf16[32,3584]{1,0:T(8,128)(2,1)S(1)}, u32[]{:S(2)}, u32[]{:S(2)}) collective-permute-start(bf16[32,3584]{1,0:T(8,128)(2,1)S(1)} %collective-permute-done.22.refs_26_.refs_11_), channel_id=1, source_target_pairs={{0,4},{4,8},{8,12},{12,14},{14,10},{10,6},{6,2},{2,0},{1,5},{5,9},... | collective-permute-start | bytes 688136 | tf_op jit(solution)/shard_map/ppermute | solution.py:243
  53.1 14.6 %collective-permute-start.16 = (bf16[32,3584]{1,0:T(8,128)(2,1)S(1)}, bf16[32,3584]{1,0:T(8,128)(2,1)S(1)}, u32[]{:S(2)}, u32[]{:S(2)}) collective-permute-start(bf16[32,3584]{1,0:T(8,128)(2,1)S(1)} %collective-permute-done.15.refs_18_.refs_3_), channel_id=1, source_target_pairs={{0,4},{4,8},{8,12},{12,14},{14,10},{10,6},{6,2},{2,0},{1,5},{5,9},... | collective-permute-start | bytes 688136 | tf_op jit(solution)/shard_map/ppermute | solution.py:243
  55.9 11.9 %collective-permute-start.13 = (bf16[32,3584]{1,0:T(8,128)(2,1)S(1)}, bf16[32,3584]{1,0:T(8,128)(2,1)S(1)}, u32[]{:S(2)}, u32[]{:S(2)}) collective-permute-start(bf16[32,3584]{1,0:T(8,128)(2,1)S(1)} %collective-permute-done.12.refs_14_.refs_15_), channel_id=1, source_target_pairs={{0,2},{4,0},{8,4},{12,8},{14,12},{10,14},{6,10},{2,6},{1,3},{5,1},... | collective-permute-start | bytes 688136 | tf_op jit(solution)/shard_map/ppermute | solution.py:243
  57.9 14.7 %collective-permute-start.3 = (bf16[32,3584]{1,0:T(8,128)(2,1)S(1)}, bf16[32,3584]{1,0:T(8,128)(2,1)S(1)}, u32[]{:S(2)}, u32[]{:S(2)}) collective-permute-start(bf16[32,3584]{1,0:T(8,128)(2,1)S(1)} %collective-permute-done.2.refs_3_.refs_4_), channel_id=1, source_target_pairs={{0,4},{4,8},{8,12},{12,14},{14,10},{10,6},{6,2},{2,0},{1,5},{5,9},... | collective-permute-start | bytes 688136 | tf_op jit(solution)/shard_map/ppermute | solution.py:243
  60.8 18.6 %collective-permute-start.20 = (bf16[32,3584]{1,0:T(8,128)(2,1)}, bf16[32,3584]{1,0:T(8,128)(2,1)S(1)}, u32[]{:S(2)}, u32[]{:S(2)}) collective-permute-start(bf16[32,3584]{1,0:T(8,128)(2,1)} %collective-permute-done.19.refs_22_.refs_7_), channel_id=1, source_target_pairs={{0,2},{4,0},{8,4},{12,8},{14,12},{10,14},{6,10},{2,6},{1,3},{5,1},... | collective-permute-start | bytes 688136 | tf_op jit(solution)/shard_map/ppermute | solution.py:243
  62.8 16.6 %collective-permute-start.6 = (bf16[32,3584]{1,0:T(8,128)(2,1)}, bf16[32,3584]{1,0:T(8,128)(2,1)}, u32[]{:S(2)}, u32[]{:S(2)}) collective-permute-start(bf16[32,3584]{1,0:T(8,128)(2,1)} %collective-permute-done.5.refs_6_.refs_7_), channel_id=1, source_target_pairs={{0,2},{4,0},{8,4},{12,8},{14,12},{10,14},{6,10},{2,6},{1,3},{5,1},... | collective-permute-start | bytes 688136 | tf_op jit(solution)/shard_map/ppermute | solution.py:243
  67.7 11.7 %collective-permute-start.9 = (bf16[32,3584]{1,0:T(8,128)(2,1)}, bf16[32,3584]{1,0:T(8,128)(2,1)}, u32[]{:S(2)}, u32[]{:S(2)}) collective-permute-start(bf16[32,3584]{1,0:T(8,128)(2,1)} %collective-permute-done.8.refs_10_.refs_11_), channel_id=1, source_target_pairs={{0,4},{4,8},{8,12},{12,14},{14,10},{10,6},{6,2},{2,0},{1,5},{5,9},... | collective-permute-start | bytes 688136 | tf_op jit(solution)/shard_map/ppermute | solution.py:243
  67.8 13.6 %collective-permute-start.27 = (bf16[32,3584]{1,0:T(8,128)(2,1)S(1)}, bf16[32,3584]{1,0:T(8,128)(2,1)S(1)}, u32[]{:S(2)}, u32[]{:S(2)}) collective-permute-start(bf16[32,3584]{1,0:T(8,128)(2,1)S(1)} %collective-permute-done.26.refs_30_.refs_15_), channel_id=1, source_target_pairs={{0,2},{4,0},{8,4},{12,8},{14,12},{10,14},{6,10},{2,6},{1,3},{5,1},... | collective-permute-start | bytes 688136 | tf_op jit(solution)/shard_map/ppermute | solution.py:243
  72.7 10.4 %collective-permute-start.17 = (bf16[32,3584]{1,0:T(8,128)(2,1)S(1)}, bf16[32,3584]{1,0:T(8,128)(2,1)S(1)}, u32[]{:S(2)}, u32[]{:S(2)}) collective-permute-start(bf16[32,3584]{1,0:T(8,128)(2,1)S(1)} %collective-permute-done.16.refs_19_.refs_4_), channel_id=1, source_target_pairs={{0,4},{4,8},{8,12},{12,14},{14,10},{10,6},{6,2},{2,0},{1,5},{5,9},... | collective-permute-start | bytes 688136 | tf_op jit(solution)/shard_map/ppermute | solution.py:243
  73.1 45.2 %all-to-all-start = ((bf16[8,128,512]{2,1,0:T(8,128)(2,1)}), bf16[8,128,512]{2,1,0:T(8,128)(2,1)S(1)}, u32[]{:S(2)}, u32[]{:S(2)}) async-start(bf16[8,128,512]{2,1,0:T(8,128)(2,1)} %tie.3), calls=%async_computation | async-start | bytes 2097152 | tf_op jit(solution)/shard_map/all_to_all | solution.py:248
  97.9 19.6 %collective-permute-start.34 = (f32[256,512]{1,0:T(8,128)S(1)}, f32[256,512]{1,0:T(8,128)S(1)}, u32[]{:S(2)}, u32[]{:S(2)}) collective-permute-start(f32[256,512]{1,0:T(8,128)S(1)} %get-tuple-element.12), channel_id=1, source_target_pairs={{0,1},{1,0},{2,3},{3,2},{4,5},{5,4},{6,7},{7,6},{8,9},{9,8},{10,11... | collective-permute-start | bytes 1572872 | tf_op jit(solution)/shard_map/ppermute | solution.py:271
  104.1 13.3 %collective-permute-start.31 = (bf16[64,256]{1,0:T(8,128)(2,1)S(1)}, bf16[64,256]{1,0:T(8,128)(2,1)S(1)}, u32[]{:S(2)}, u32[]{:S(2)}) collective-permute-start(bf16[64,256]{1,0:T(8,128)(2,1)S(1)} %add_convert_fusion.refs_0_), channel_id=1, source_target_pairs={{0,4},{2,6},{4,8},{6,10},{8,12},{10,14},{12,0},{14,2},{1,5},{3,7},... | collective-permute-start | bytes 98312 | tf_op jit(solution)/shard_map/ppermute | solution.py:270
  106.2 11.2 %collective-permute-start.32 = (bf16[64,256]{1,0:T(8,128)(2,1)S(1)}, bf16[64,256]{1,0:T(8,128)(2,1)S(1)}, u32[]{:S(2)}, u32[]{:S(2)}) collective-permute-start(bf16[64,256]{1,0:T(8,128)(2,1)S(1)} %add_convert_fusion.refs_0_), channel_id=1, source_target_pairs={{0,8},{2,10},{4,12},{6,14},{8,0},{10,2},{12,4},{14,6},{1,9},{3,11}... | collective-permute-start | bytes 98312 | tf_op jit(solution)/shard_map/ppermute | solution.py:270
  (28 other events, 886.7 us)

commit v14 on v11

--- a/solution.py
+++ b/solution.py
@@ -131,14 +131,13 @@
     rows = chunks[0][0][0].shape[0] * n
     share = down.shape[1] // 2
     ranks = shrink.shape[0]
-    spans = [(base, start, cuts_of(pieces[0].shape[1])) for pieces, base, start in chunks]
+    spans = [(base, start, cuts_of(pieces[0].shape[1])) for pieces, base, start, _ in chunks]
     sizes = [tile for _, _, cuts in spans for _, tile in cuts]
     width = sum(sizes)
     anywhere = pl.BlockSpec(memory_space=pl.ANY)
     held = [
         piece if i in late else in_hbm(piece)
-        for pieces, base, _ in chunks
-        for late in [(3, 4, n - 1) if base == 0 else (3, n - 2, n - 1)]
+        for pieces, _, _, late in chunks
         for i, piece in enumerate(pieces)
     ]
     args = [*after, *held, in_hbm(down), in_hbm(shrink), *(acc or ())]
@@ -168,7 +167,11 @@
     )(scalars, *args)
 
 
-def final_kernel(n, owned, shrunk, slot, factors, kept, other, out, spread):
+def final_kernel(n, owned, shrunk, slot, factors, kept, other, out, spread, factors_here, kept_here, other_here, sems):
+    pairs = [(factors, factors_here), (kept, kept_here), (other, other_here)]
+    copies = [pltpu.make_async_copy(a, b, sems.at[i]) for i, (a, b) in enumerate(pairs)]
+    for copy in copies:
+        copy.start()
     rank = shrunk.shape[0]
     wide = owned * rank
     rows = out.shape[0]
@@ -178,8 +181,11 @@
     place = slot[...] - lane
     for i in range(n):
         spread[:, i * wide:(i + 1) * wide] = jnp.where(place == i * owned, pair, 0.0).astype(BF16)
-    extra = jnp.dot(spread[...], factors[...], preferred_element_type=F32)
-    out[...] = (kept[...] + other[...] + extra).astype(BF16)
+    copies[0].wait()
+    extra = jnp.dot(spread[...], factors_here[...], preferred_element_type=F32)
+    copies[1].wait()
+    copies[2].wait()
+    out[...] = (kept_here[...] + other_here[...] + extra).astype(BF16)
 
 
 def final(shrunk, slot_column, factors, kept, other, owned):
@@ -187,18 +193,24 @@
     rows = kept.shape[0]
     return pl.pallas_call(
         functools.partial(final_kernel, n, owned),
-        in_specs=[pl.BlockSpec(memory_space=pltpu.VMEM)] * 5,
+        in_specs=[pl.BlockSpec(memory_space=pltpu.VMEM)] * 2 + [pl.BlockSpec(memory_space=pl.ANY)] * 3,
         out_specs=pl.BlockSpec(memory_space=pltpu.VMEM),
-        scratch_shapes=[pltpu.VMEM((rows, n * wide), BF16)],
+        scratch_shapes=[
+            pltpu.VMEM((rows, n * wide), BF16),
+            pltpu.VMEM((n * wide, share), BF16),
+            pltpu.VMEM((rows, share), F32),
+            pltpu.VMEM((rows, share), F32),
+            pltpu.SemaphoreType.DMA((3,)),
+        ],
         out_shape=jax.ShapeDtypeStruct((rows, share), BF16),
-        compiler_params=params(8),
+        compiler_params=params(16),
         cost_estimate=pl.CostEstimate(
             flops=2 * rows * share * n * wide,
             bytes_accessed=2 * n * wide * share + 10 * rows * share,
             transcendentals=0,
         ),
         name="expand_and_add",
-    )(shrunk, slot_column, factors.reshape(n * wide, share), kept, other)
+    )(shrunk, slot_column, in_hbm(factors.reshape(n * wide, share)), kept, other)
 
 
 def make_shards(n, cores):
@@ -244,8 +256,9 @@
                     moving = lax.ppermute(moving, "store", pairs)
                     pieces.append(moving)
                 ends.append(moving)
-            chunks.append((pieces, way * n, start))
-        factors = lax.all_to_all(tie(blocks, ends[:4]), "store", 0, 0)
+            late = ((long,), (n - 1,)) if chunk < 2 else ((short, long, n - 1), (short, n - 2, n - 1))
+            chunks.append((pieces, way * n, start, late[way]))
+        factors = lax.all_to_all(tie(blocks, [ends[0], ends[3]]), "store", 0, 0)
 
         call = functools.partial(chunk_matmul, scalars, half)
         first, last = chunks[:CHUNKS // 2], chunks[CHUNKS // 2:]

time: 113 us -> 124 us (1.097)
  waiting for transfers between devices: 17.3 us -> 30.7 us
  local copies, waits for them, and re-layouts: 9.83 us -> 4.85 us
  starting transfers between devices: 53.7 us -> 55.8 us
    ppermute x28, waiting for transfers between devices: 17.3 us -> 30.7 us  [shards(): moving = lax.ppermute(moving, 'store', pairs)]
    unnamed x56 -> x38, local copies, waits for them, and re-layouts: 7.64 us -> 2.66 us
    ppermute x28, starting transfers between devices: 41.7 us -> 36.9 us  [shards(): moving = lax.ppermute(moving, 'store', pairs)]
    ppermute x3, starting transfers between devices: 4.44 us -> 8.99 us  [shards(): lax.ppermute(column, 'store', [(s, (s + ds) % n) for s in range(n)])]
    all_to_all x1, starting transfers between devices: 4.88 us -> 6.27 us  [shards(): factors = lax.all_to_all(tie(blocks, [ends[0], ends[3]]), 'store', 0, 0)]
  transfers between devices with their start and end apart: 36 -> 36, of which waited for: 10 -> 13; matrix products, arithmetic and copies ran while one was open for 1% -> 1% of each run, Pallas kernels for 26% -> 24%
where the time goes in v14:
time: 124 us
  starting transfers between devices  55.8 us (45%)
  Pallas kernels  32 us (26%)
  waiting for transfers between devices  30.7 us (25%)
  local copies, waits for them, and re-layouts  4.85 us (4%)
    ppermute x28, starting transfers between devices, shards(): moving = lax.ppermute(moving, 'store', pairs)  36.9 us
    ppermute x28, waiting for transfers between devices, shards(): moving = lax.ppermute(moving, 'store', pairs)  30.7 us
    pallas_call x4, Pallas kernels, chunk_matmul(): pl.pallas_call(functools.partial(matmul_kernel, n, len(after), spans, hal...  26.2 us
    ppermute x3, starting transfers between devices, shards(): lax.ppermute(column, 'store', [(s, (s + ds) % n) for s in range(n)])  8.99 us
    all_to_all x1, starting transfers between devices, shards(): factors = lax.all_to_all(tie(blocks, [ends[0], ends[3]]), 'store', 0, 0)  6.27 us
    pallas_call x1, Pallas kernels, expand_blocks(): pl.pallas_call(split_kernel, grid_spec=pltpu.PrefetchScalarGridSpec(num_s...  3.31 us
    ppermute x3, starting transfers between devices, shards(): whole = whole + lax.ppermute(mine, ('store', 'tensor'), pairs)  3.12 us
    unnamed x38, local copies, waits for them, and re-layouts  2.66 us
  transfers between devices with their start and end apart: 36, of which 13 were waited for; matrix products, arithmetic and copies ran while one was open for 1% of the time, Pallas kernels for 24%

profile of v14, /device:TPU:0, one launch (start us, length us, event | category | flops | bytes accessed | tf_op | source)
XLA Modules:
  0.0 124.0 jit_solution(8924562423153159738)
XLA Ops:
  1.4 3.0 %collective-permute-start.24 = (bf16[32,3584]{1,0:T(8,128)(2,1)S(1)}, bf16[32,3584]{1,0:T(8,128)(2,1)S(1)}, u32[]{:S(2)}, u32[]{:S(2)}) collective-permute-start(bf16[32,3584]{1,0:T(8,128)(2,1)S(1)} %get-tuple-element.15.refs_8_), channel_id=1, source_target_pairs={{0,2},{4,0},{8,4},{12,8},{14,12},{10,14},{6,10},{2,6},{1,3},{5,1},... | collective-permute-start | bytes 688136 | tf_op jit(solution)/shard_map/ppermute | solution.py:256
  4.5 1.9 %collective-permute-start.18 = (bf16[32,3584]{1,0:T(8,128)(2,1)S(1)}, bf16[32,3584]{1,0:T(8,128)(2,1)S(1)}, u32[]{:S(2)}, u32[]{:S(2)}) collective-permute-start(bf16[32,3584]{1,0:T(8,128)(2,1)S(1)} %get-tuple-element.18.refs_0_), channel_id=1, source_target_pairs={{0,2},{4,0},{8,4},{12,8},{14,12},{10,14},{6,10},{2,6},{1,3},{5,1},... | collective-permute-start | bytes 688136 | tf_op jit(solution)/shard_map/ppermute | solution.py:256
  6.6 1.9 %collective-permute-start.4 = (bf16[32,3584]{1,0:T(8,128)(2,1)S(1)}, bf16[32,3584]{1,0:T(8,128)(2,1)S(1)}, u32[]{:S(2)}, u32[]{:S(2)}) collective-permute-start(bf16[32,3584]{1,0:T(8,128)(2,1)S(1)} %get-tuple-element.17.refs_0_.refs_1_), channel_id=1, source_target_pairs={{0,2},{4,0},{8,4},{12,8},{14,12},{10,14},{6,10},{2,6},{1,3},{5,1},... | collective-permute-start | bytes 688136 | tf_op jit(solution)/shard_map/ppermute | solution.py:256
  10.8 3.3 %expand_blocks.1 = (bf16[8,128,512]{2,1,0:T(8,128)(2,1)}, f32[8,128]{1,0:T(8,128)S(1)}) custom-call(s32[18]{0:T(128)S(1)} %dynamic-slice_bitcast_fusion.scalars, bf16[128,8192]{1,0:T(8,128)(2,1)S(1)} %bitcast.8), custom_call_target="tpu_custom_call" | custom-call | bytes 2097152 | tf_op jit(solution)/shard_map/expand_blocks/pallas_call | solution.py:39
  14.3 1.9 %collective-permute-start.10 = (bf16[32,3584]{1,0:T(8,128)(2,1)S(1)}, bf16[32,3584]{1,0:T(8,128)(2,1)S(1)}, u32[]{:S(2)}, u32[]{:S(2)}) collective-permute-start(bf16[32,3584]{1,0:T(8,128)(2,1)S(1)} %tie.2.refs_8_.refs_9_), channel_id=1, source_target_pairs={{0,2},{4,0},{8,4},{12,8},{14,12},{10,14},{6,10},{2,6},{1,3},{5,1},... | collective-permute-start | bytes 688136 | tf_op jit(solution)/shard_map/ppermute | solution.py:256
  16.2 1.7 %collective-permute-start.25 = (bf16[32,3584]{1,0:T(8,128)(2,1)S(1)}, bf16[32,3584]{1,0:T(8,128)(2,1)S(1)}, u32[]{:S(2)}, u32[]{:S(2)}) collective-permute-start(bf16[32,3584]{1,0:T(8,128)(2,1)S(1)} %collective-permute-done.24.refs_12_), channel_id=1, source_target_pairs={{0,2},{4,0},{8,4},{12,8},{14,12},{10,14},{6,10},{2,6},{1,3},{5,1},... | collective-permute-start | bytes 688136 | tf_op jit(solution)/shard_map/ppermute | solution.py:256
  18.2 2.5 %collective-permute-done.4.refs_5_.refs_6_ = bf16[32,3584]{1,0:T(8,128)(2,1)S(1)} collective-permute-done((bf16[32,3584]{1,0:T(8,128)(2,1)S(1)}, bf16[32,3584]{1,0:T(8,128)(2,1)S(1)}, u32[]{:S(2)}, u32[]{:S(2)}) %collective-permute-start.4) | collective-permute-done | bytes 229408 | tf_op jit(solution)/shard_map/ppermute | solution.py:256
  20.7 2.1 %collective-permute-start.7 = (bf16[32,3584]{1,0:T(8,128)(2,1)S(1)}, bf16[32,3584]{1,0:T(8,128)(2,1)}, u32[]{:S(2)}, u32[]{:S(2)}) collective-permute-start(bf16[32,3584]{1,0:T(8,128)(2,1)S(1)} %tie.2.refs_8_.refs_9_), channel_id=1, source_target_pairs={{0,4},{4,8},{8,12},{12,14},{14,10},{10,6},{6,2},{2,0},{1,5},{5,9},... | collective-permute-start | bytes 688136 | tf_op jit(solution)/shard_map/ppermute | solution.py:256
  25.7 2.0 %collective-permute-start.19 = (bf16[32,3584]{1,0:T(8,128)(2,1)S(1)}, bf16[32,3584]{1,0:T(8,128)(2,1)}, u32[]{:S(2)}, u32[]{:S(2)}) collective-permute-start(bf16[32,3584]{1,0:T(8,128)(2,1)S(1)} %collective-permute-done.18.refs_5_), channel_id=1, source_target_pairs={{0,2},{4,0},{8,4},{12,8},{14,12},{10,14},{6,10},{2,6},{1,3},{5,1},... | collective-permute-start | bytes 688136 | tf_op jit(solution)/shard_map/ppermute | solution.py:256
  27.7 2.9 %collective-permute-done.25.refs_13_ = bf16[32,3584]{1,0:T(8,128)(2,1)S(1)} collective-permute-done((bf16[32,3584]{1,0:T(8,128)(2,1)S(1)}, bf16[32,3584]{1,0:T(8,128)(2,1)S(1)}, u32[]{:S(2)}, u32[]{:S(2)}) %collective-permute-start.25) | collective-permute-done | bytes 229408 | tf_op jit(solution)/shard_map/ppermute | solution.py:256
  30.6 2.0 %collective-permute-start.26 = (bf16[32,3584]{1,0:T(8,128)(2,1)S(1)}, bf16[32,3584]{1,0:T(8,128)(2,1)S(1)}, u32[]{:S(2)}, u32[]{:S(2)}) collective-permute-start(bf16[32,3584]{1,0:T(8,128)(2,1)S(1)} %collective-permute-done.25.refs_13_), channel_id=1, source_target_pairs={{0,2},{4,0},{8,4},{12,8},{14,12},{10,14},{6,10},{2,6},{1,3},{5,1},... | collective-permute-start | bytes 688136 | tf_op jit(solution)/shard_map/ppermute | solution.py:256
  32.7 1.9 %collective-permute-start.5 = (bf16[32,3584]{1,0:T(8,128)(2,1)S(1)}, bf16[32,3584]{1,0:T(8,128)(2,1)}, u32[]{:S(2)}, u32[]{:S(2)}) collective-permute-start(bf16[32,3584]{1,0:T(8,128)(2,1)S(1)} %collective-permute-done.4.refs_5_.refs_6_), channel_id=1, source_target_pairs={{0,2},{4,0},{8,4},{12,8},{14,12},{10,14},{6,10},{2,6},{1,3},{5,1},... | collective-permute-start | bytes 688136 | tf_op jit(solution)/shard_map/ppermute | solution.py:256
  34.6 2.9 %collective-permute-done.22.refs_10_ = bf16[32,3584]{1,0:T(8,128)(2,1)} collective-permute-done((bf16[32,3584]{1,0:T(8,128)(2,1)S(1)}, bf16[32,3584]{1,0:T(8,128)(2,1)}, u32[]{:S(2)}, u32[]{:S(2)}) %collective-permute-start.22) | collective-permute-done | bytes 229408 | tf_op jit(solution)/shard_map/ppermute | solution.py:256
  37.7 1.8 %collective-permute-start.11 = (bf16[32,3584]{1,0:T(8,128)(2,1)S(1)}, bf16[32,3584]{1,0:T(8,128)(2,1)}, u32[]{:S(2)}, u32[]{:S(2)}) collective-permute-start(bf16[32,3584]{1,0:T(8,128)(2,1)S(1)} %collective-permute-done.10.refs_12_.refs_13_), channel_id=1, source_target_pairs={{0,2},{4,0},{8,4},{12,8},{14,12},{10,14},{6,10},{2,6},{1,3},{5,1},... | collective-permute-start | bytes 688136 | tf_op jit(solution)/shard_map/ppermute | solution.py:256
  40.4 2.0 %collective-permute-start.27 = (bf16[32,3584]{1,0:T(8,128)(2,1)S(1)}, bf16[32,3584]{1,0:T(8,128)(2,1)S(1)}, u32[]{:S(2)}, u32[]{:S(2)}) collective-permute-start(bf16[32,3584]{1,0:T(8,128)(2,1)S(1)} %collective-permute-done.26.refs_14_), channel_id=1, source_target_pairs={{0,2},{4,0},{8,4},{12,8},{14,12},{10,14},{6,10},{2,6},{1,3},{5,1},... | collective-permute-start | bytes 688136 | tf_op jit(solution)/shard_map/ppermute | solution.py:256
  42.5 2.9 %collective-permute-done.5.refs_6_.refs_7_ = bf16[32,3584]{1,0:T(8,128)(2,1)} collective-permute-done((bf16[32,3584]{1,0:T(8,128)(2,1)S(1)}, bf16[32,3584]{1,0:T(8,128)(2,1)}, u32[]{:S(2)}, u32[]{:S(2)}) %collective-permute-start.5) | collective-permute-done | bytes 229408 | tf_op jit(solution)/shard_map/ppermute | solution.py:256
  45.4 2.1 %collective-permute-start.8 = (bf16[32,3584]{1,0:T(8,128)(2,1)}, bf16[32,3584]{1,0:T(8,128)(2,1)}, u32[]{:S(2)}, u32[]{:S(2)}) collective-permute-start(bf16[32,3584]{1,0:T(8,128)(2,1)} %collective-permute-done.7.refs_9_.refs_10_), channel_id=1, source_target_pairs={{0,4},{4,8},{8,12},{12,14},{14,10},{10,6},{6,2},{2,0},{1,5},{5,9},... | collective-permute-start | bytes 688136 | tf_op jit(solution)/shard_map/ppermute | solution.py:256
  50.3 2.0 %collective-permute-start.20 = (bf16[32,3584]{1,0:T(8,128)(2,1)}, bf16[32,3584]{1,0:T(8,128)(2,1)}, u32[]{:S(2)}, u32[]{:S(2)}) collective-permute-start(bf16[32,3584]{1,0:T(8,128)(2,1)} %collective-permute-done.19.refs_6_), channel_id=1, source_target_pairs={{0,2},{4,0},{8,4},{12,8},{14,12},{10,14},{6,10},{2,6},{1,3},{5,1},... | collective-permute-start | bytes 688136 | tf_op jit(solution)/shard_map/ppermute | solution.py:256
  52.3 2.8 %collective-permute-done.27.refs_15_.refs_2_ = bf16[32,3584]{1,0:T(8,128)(2,1)S(1)} collective-permute-done((bf16[32,3584]{1,0:T(8,128)(2,1)S(1)}, bf16[32,3584]{1,0:T(8,128)(2,1)S(1)}, u32[]{:S(2)}, u32[]{:S(2)}) %collective-permute-start.27) | collective-permute-done | bytes 229408 | tf_op jit(solution)/shard_map/ppermute | solution.py:256
  55.1 2.1 %collective-permute-start.2 = (bf16[32,3584]{1,0:T(8,128)(2,1)}, bf16[32,3584]{1,0:T(8,128)(2,1)S(1)}, u32[]{:S(2)}, u32[]{:S(2)}) collective-permute-start(bf16[32,3584]{1,0:T(8,128)(2,1)} %collective-permute-done.1.refs_2_.refs_3_), channel_id=1, source_target_pairs={{0,4},{4,8},{8,12},{12,14},{14,10},{10,6},{6,2},{2,0},{1,5},{5,9},... | collective-permute-start | bytes 688136 | tf_op jit(solution)/shard_map/ppermute | solution.py:256
  57.6 6.3 %all-to-all-start = ((bf16[8,128,512]{2,1,0:T(8,128)(2,1)}), bf16[8,128,512]{2,1,0:T(8,128)(2,1)S(1)}, u32[]{:S(2)}, u32[]{:S(2)}) async-start(bf16[8,128,512]{2,1,0:T(8,128)(2,1)} %tie.3), calls=%async_computation | async-start | bytes 2097152 | tf_op jit(solution)/shard_map/all_to_all | solution.py:261
  63.9 2.0 %collective-permute-start.6 = (bf16[32,3584]{1,0:T(8,128)(2,1)}, bf16[32,3584]{1,0:T(8,128)(2,1)S(1)}, u32[]{:S(2)}, u32[]{:S(2)}) collective-permute-start(bf16[32,3584]{1,0:T(8,128)(2,1)} %collective-permute-done.5.refs_6_.refs_7_), channel_id=1, source_target_pairs={{0,2},{4,0},{8,4},{12,8},{14,12},{10,14},{6,10},{2,6},{1,3},{5,1},... | collective-permute-start | bytes 688136 | tf_op jit(solution)/shard_map/ppermute | solution.py:256
  69.5 9.6 %first_chunks.1 = (f32[256,512]{1,0:T(8,128)S(1)}, f32[256,512]{1,0:T(8,128)S(1)}, f32[128,256]{1,0:T(8,128)S(1)}) custom-call(s32[18]{0:T(128)S(1)} %dynamic-slice_bitcast_fusion.scalars, bf16[32,3584]{1,0:T(8,128)(2,1)} %copy-done.8, bf16[32,3584]{1,0:T(8,128)(2,1)} %copy-done.12, bf16[32,3584]{1,0:T(8,128)(2,1)} %copy-done.14, ...), custom_call_target="tpu_custom_call" | custom-call | flops 8455716864 | bytes 22544384 | tf_op jit(solution)/shard_map/first_chunks/pallas_call | solution.py:146
  79.1 7.3 %collective-permute-done.6.refs_7_.refs_8_ = bf16[32,3584]{1,0:T(8,128)(2,1)S(1)} collective-permute-done((bf16[32,3584]{1,0:T(8,128)(2,1)}, bf16[32,3584]{1,0:T(8,128)(2,1)S(1)}, u32[]{:S(2)}, u32[]{:S(2)}) %collective-permute-start.6) | collective-permute-done | bytes 229408 | tf_op jit(solution)/shard_map/ppermute | solution.py:256
  87.1 3.1 %collective-permute-done.3.refs_4_.refs_5_ = bf16[32,3584]{1,0:T(8,128)(2,1)S(1)} collective-permute-done((bf16[32,3584]{1,0:T(8,128)(2,1)S(1)}, bf16[32,3584]{1,0:T(8,128)(2,1)S(1)}, u32[]{:S(2)}, u32[]{:S(2)}) %collective-permute-start.3) | collective-permute-done | bytes 229408 | tf_op jit(solution)/shard_map/ppermute | solution.py:256
  90.9 5.0 %last_narrow.1 = f32[128,256]{1,0:T(8,128)S(1)} custom-call(s32[18]{0:T(128)S(1)} %dynamic-slice_bitcast_fusion.scalars, bf16[32,3584]{1,0:T(8,128)(2,1)} %copy-done.3, bf16[32,3584]{1,0:T(8,128)(2,1)} %copy-done.5, bf16[32,3584]{1,0:T(8,128)(2,1)} %collective-permute-done.1.refs_2_.refs_3_, bf16[32,3584]{1,0:T(8,128)(2,1)S(1)} %collective-permute-done.2.refs_3_.refs_4_, ...), custom_call_target="tpu_custom_call" | custom-call | flops 939524096 | bytes 5767168 | tf_op jit(solution)/shard_map/last_narrow/pallas_call | solution.py:146
  97.3 1.7 %collective-permute-start.29 = (f32[64,256]{1,0:T(8,128)S(1)}, f32[64,256]{1,0:T(8,128)S(1)}, u32[]{:S(2)}, u32[]{:S(2)}) collective-permute-start(f32[64,256]{1,0:T(8,128)S(1)} %fusion.refs_0_), channel_id=1, source_target_pairs={{0,2},{1,3},{2,0},{3,1},{4,6},{5,7},{6,4},{7,5},{8,10},{9,11},{10,... | collective-permute-start | bytes 196616 | tf_op jit(solution)/shard_map/ppermute | solution.py:280
  99.0 5.8 %last_sent.1.refs_0_ = f32[256,512]{1,0:T(8,128)S(1)} custom-call(s32[18]{0:T(128)S(1)} %dynamic-slice_bitcast_fusion.scalars, f32[64,256]{1,0:T(8,128)S(1)} %fusion.refs_0_, bf16[32,3584]{1,0:T(8,128)(2,1)} %copy-done.3, bf16[32,3584]{1,0:T(8,128)(2,1)} %copy-done.5, bf16[32,3584]{1,0:T(8,128)(2,1)} %collective-permute-done.1.refs_2_.refs_3_, ...), custom_call_target="tpu_custom_call" | custom-call | flops 3758096384 | bytes 12058624 | tf_op jit(solution)/shard_map/last_sent/pallas_call | solution.py:146
  105.5 2.4 %collective-permute-start.33 = (bf16[64,256]{1,0:T(8,128)(2,1)S(1)}, bf16[64,256]{1,0:T(8,128)(2,1)S(1)}, u32[]{:S(2)}, u32[]{:S(2)}) collective-permute-start(bf16[64,256]{1,0:T(8,128)(2,1)S(1)} %add_convert_fusion), channel_id=1, source_target_pairs={{0,12},{2,14},{4,0},{6,2},{8,4},{10,6},{12,8},{14,10},{1,13},{3,15... | collective-permute-start | bytes 98312 | tf_op jit(solution)/shard_map/ppermute | solution.py:284
  107.8 6.4 %collective-permute-start.32 = (bf16[64,256]{1,0:T(8,128)(2,1)S(1)}, bf16[64,256]{1,0:T(8,128)(2,1)S(1)}, u32[]{:S(2)}, u32[]{:S(2)}) collective-permute-start(bf16[64,256]{1,0:T(8,128)(2,1)S(1)} %add_convert_fusion), channel_id=1, source_target_pairs={{0,8},{2,10},{4,12},{6,14},{8,0},{10,2},{12,4},{14,6},{1,9},{3,11}... | collective-permute-start | bytes 98312 | tf_op jit(solution)/shard_map/ppermute | solution.py:284
  114.4 5.8 %last_kept.1.kept = f32[256,512]{1,0:T(8,128)S(1)} custom-call(s32[18]{0:T(128)S(1)} %dynamic-slice_bitcast_fusion.scalars, f32[256,512]{1,0:T(8,128)S(1)} %last_sent.1.refs_0_, bf16[32,3584]{1,0:T(8,128)(2,1)} %copy-done.3, bf16[32,3584]{1,0:T(8,128)(2,1)} %copy-done.5, bf16[32,3584]{1,0:T(8,128)(2,1)} %collective-permute-done.1.refs_2_.refs_3_, ...), custom_call_target="tpu_custom_call" | custom-call | flops 3758096384 | bytes 12058624 | tf_op jit(solution)/shard_map/last_kept/pallas_call | solution.py:146
  121.4 2.5 %expand_and_add.1 = bf16[256,512]{1,0:T(8,128)(2,1)} custom-call(bf16[64,256]{1,0:T(8,128)(2,1)S(1)} %add_add_fusion.shrunk, s32[256,1]{1,0:T(8,128)S(1)} %copy.11.slot, bf16[1024,512]{1,0:T(8,128)(2,1)} %bitcast.13, f32[256,512]{1,0:T(8,128)S(1)} %last_kept.1.kept, f32[256,512]{1,0:T(8,128)S(1)} %collective-permute-done.34.other), custom_call_target="tpu_custom_call" | custom-call | flops 268435456 | bytes 2359296 | tf_op jit(solution)/shard_map/expand_and_add/pallas_call | solution.py:194
  (94 shorter events, 20.1 us)
Async XLA Ops:
  1.4 12.7 %collective-permute-start.24 = (bf16[32,3584]{1,0:T(8,128)(2,1)S(1)}, bf16[32,3584]{1,0:T(8,128)(2,1)S(1)}, u32[]{:S(2)}, u32[]{:S(2)}) collective-permute-start(bf16[32,3584]{1,0:T(8,128)(2,1)S(1)} %get-tuple-element.15.refs_8_), channel_id=1, source_target_pairs={{0,2},{4,0},{8,4},{12,8},{14,12},{10,14},{6,10},{2,6},{1,3},{5,1},... | collective-permute-start | bytes 688136 | tf_op jit(solution)/shard_map/ppermute | solution.py:256
  4.4 9.8 %collective-permute-start.21 = (bf16[32,3584]{1,0:T(8,128)(2,1)S(1)}, bf16[32,3584]{1,0:T(8,128)(2,1)S(1)}, u32[]{:S(2)}, u32[]{:S(2)}) collective-permute-start(bf16[32,3584]{1,0:T(8,128)(2,1)S(1)} %get-tuple-element.15.refs_8_), channel_id=1, source_target_pairs={{0,4},{4,8},{8,12},{12,14},{14,10},{10,6},{6,2},{2,0},{1,5},{5,9},... | collective-permute-start | bytes 688136 | tf_op jit(solution)/shard_map/ppermute | solution.py:256
  4.5 11.6 %collective-permute-start.18 = (bf16[32,3584]{1,0:T(8,128)(2,1)S(1)}, bf16[32,3584]{1,0:T(8,128)(2,1)S(1)}, u32[]{:S(2)}, u32[]{:S(2)}) collective-permute-start(bf16[32,3584]{1,0:T(8,128)(2,1)S(1)} %get-tuple-element.18.refs_0_), channel_id=1, source_target_pairs={{0,2},{4,0},{8,4},{12,8},{14,12},{10,14},{6,10},{2,6},{1,3},{5,1},... | collective-permute-start | bytes 688136 | tf_op jit(solution)/shard_map/ppermute | solution.py:256
  6.4 11.4 %collective-permute-start.14 = (bf16[32,3584]{1,0:T(8,128)(2,1)S(1)}, bf16[32,3584]{1,0:T(8,128)(2,1)S(1)}, u32[]{:S(2)}, u32[]{:S(2)}) collective-permute-start(bf16[32,3584]{1,0:T(8,128)(2,1)S(1)} %get-tuple-element.18.refs_0_), channel_id=1, source_target_pairs={{0,4},{4,8},{8,12},{12,14},{14,10},{10,6},{6,2},{2,0},{1,5},{5,9},... | collective-permute-start | bytes 688136 | tf_op jit(solution)/shard_map/ppermute | solution.py:256
  6.6 14.2 %collective-permute-start.4 = (bf16[32,3584]{1,0:T(8,128)(2,1)S(1)}, bf16[32,3584]{1,0:T(8,128)(2,1)S(1)}, u32[]{:S(2)}, u32[]{:S(2)}) collective-permute-start(bf16[32,3584]{1,0:T(8,128)(2,1)S(1)} %get-tuple-element.17.refs_0_.refs_1_), channel_id=1, source_target_pairs={{0,2},{4,0},{8,4},{12,8},{14,12},{10,14},{6,10},{2,6},{1,3},{5,1},... | collective-permute-start | bytes 688136 | tf_op jit(solution)/shard_map/ppermute | solution.py:256
  14.3 11.4 %collective-permute-start.10 = (bf16[32,3584]{1,0:T(8,128)(2,1)S(1)}, bf16[32,3584]{1,0:T(8,128)(2,1)S(1)}, u32[]{:S(2)}, u32[]{:S(2)}) collective-permute-start(bf16[32,3584]{1,0:T(8,128)(2,1)S(1)} %tie.2.refs_8_.refs_9_), channel_id=1, source_target_pairs={{0,2},{4,0},{8,4},{12,8},{14,12},{10,14},{6,10},{2,6},{1,3},{5,1},... | collective-permute-start | bytes 688136 | tf_op jit(solution)/shard_map/ppermute | solution.py:256
  16.2 14.4 %collective-permute-start.25 = (bf16[32,3584]{1,0:T(8,128)(2,1)S(1)}, bf16[32,3584]{1,0:T(8,128)(2,1)S(1)}, u32[]{:S(2)}, u32[]{:S(2)}) collective-permute-start(bf16[32,3584]{1,0:T(8,128)(2,1)S(1)} %collective-permute-done.24.refs_12_), channel_id=1, source_target_pairs={{0,2},{4,0},{8,4},{12,8},{14,12},{10,14},{6,10},{2,6},{1,3},{5,1},... | collective-permute-start | bytes 688136 | tf_op jit(solution)/shard_map/ppermute | solution.py:256
  17.8 14.7 %collective-permute-start.15 = (bf16[32,3584]{1,0:T(8,128)(2,1)S(1)}, bf16[32,3584]{1,0:T(8,128)(2,1)S(1)}, u32[]{:S(2)}, u32[]{:S(2)}) collective-permute-start(bf16[32,3584]{1,0:T(8,128)(2,1)S(1)} %collective-permute-done.14.refs_1_), channel_id=1, source_target_pairs={{0,4},{4,8},{8,12},{12,14},{14,10},{10,6},{6,2},{2,0},{1,5},{5,9},... | collective-permute-start | bytes 688136 | tf_op jit(solution)/shard_map/ppermute | solution.py:256
  20.7 12.0 %collective-permute-start.7 = (bf16[32,3584]{1,0:T(8,128)(2,1)S(1)}, bf16[32,3584]{1,0:T(8,128)(2,1)}, u32[]{:S(2)}, u32[]{:S(2)}) collective-permute-start(bf16[32,3584]{1,0:T(8,128)(2,1)S(1)} %tie.2.refs_8_.refs_9_), channel_id=1, source_target_pairs={{0,4},{4,8},{8,12},{12,14},{14,10},{10,6},{6,2},{2,0},{1,5},{5,9},... | collective-permute-start | bytes 688136 | tf_op jit(solution)/shard_map/ppermute | solution.py:256
  22.8 14.7 %collective-permute-start.22 = (bf16[32,3584]{1,0:T(8,128)(2,1)S(1)}, bf16[32,3584]{1,0:T(8,128)(2,1)}, u32[]{:S(2)}, u32[]{:S(2)}) collective-permute-start(bf16[32,3584]{1,0:T(8,128)(2,1)S(1)} %collective-permute-done.21.refs_9_), channel_id=1, source_target_pairs={{0,4},{4,8},{8,12},{12,14},{14,10},{10,6},{6,2},{2,0},{1,5},{5,9},... | collective-permute-start | bytes 688136 | tf_op jit(solution)/shard_map/ppermute | solution.py:256
  25.7 12.1 %collective-permute-start.19 = (bf16[32,3584]{1,0:T(8,128)(2,1)S(1)}, bf16[32,3584]{1,0:T(8,128)(2,1)}, u32[]{:S(2)}, u32[]{:S(2)}) collective-permute-start(bf16[32,3584]{1,0:T(8,128)(2,1)S(1)} %collective-permute-done.18.refs_5_), channel_id=1, source_target_pairs={{0,2},{4,0},{8,4},{12,8},{14,12},{10,14},{6,10},{2,6},{1,3},{5,1},... | collective-permute-start | bytes 688136 | tf_op jit(solution)/shard_map/ppermute | solution.py:256
  30.6 9.8 %collective-permute-start.26 = (bf16[32,3584]{1,0:T(8,128)(2,1)S(1)}, bf16[32,3584]{1,0:T(8,128)(2,1)S(1)}, u32[]{:S(2)}, u32[]{:S(2)}) collective-permute-start(bf16[32,3584]{1,0:T(8,128)(2,1)S(1)} %collective-permute-done.25.refs_13_), channel_id=1, source_target_pairs={{0,2},{4,0},{8,4},{12,8},{14,12},{10,14},{6,10},{2,6},{1,3},{5,1},... | collective-permute-start | bytes 688136 | tf_op jit(solution)/shard_map/ppermute | solution.py:256
  32.6 9.8 %collective-permute-start.16 = (bf16[32,3584]{1,0:T(8,128)(2,1)S(1)}, bf16[32,3584]{1,0:T(8,128)(2,1)S(1)}, u32[]{:S(2)}, u32[]{:S(2)}) collective-permute-start(bf16[32,3584]{1,0:T(8,128)(2,1)S(1)} %collective-permute-done.15.refs_2_), channel_id=1, source_target_pairs={{0,4},{4,8},{8,12},{12,14},{14,10},{10,6},{6,2},{2,0},{1,5},{5,9},... | collective-permute-start | bytes 688136 | tf_op jit(solution)/shard_map/ppermute | solution.py:256
  32.7 12.7 %collective-permute-start.5 = (bf16[32,3584]{1,0:T(8,128)(2,1)S(1)}, bf16[32,3584]{1,0:T(8,128)(2,1)}, u32[]{:S(2)}, u32[]{:S(2)}) collective-permute-start(bf16[32,3584]{1,0:T(8,128)(2,1)S(1)} %collective-permute-done.4.refs_5_.refs_6_), channel_id=1, source_target_pairs={{0,2},{4,0},{8,4},{12,8},{14,12},{10,14},{6,10},{2,6},{1,3},{5,1},... | collective-permute-start | bytes 688136 | tf_op jit(solution)/shard_map/ppermute | solution.py:256
  37.5 10.0 %collective-permute-start.1 = (bf16[32,3584]{1,0:T(8,128)(2,1)S(1)}, bf16[32,3584]{1,0:T(8,128)(2,1)}, u32[]{:S(2)}, u32[]{:S(2)}) collective-permute-start(bf16[32,3584]{1,0:T(8,128)(2,1)S(1)} %collective-permute-done.refs_1_.refs_2_), channel_id=1, source_target_pairs={{0,4},{4,8},{8,12},{12,14},{14,10},{10,6},{6,2},{2,0},{1,5},{5,9},... | collective-permute-start | bytes 688136 | tf_op jit(solution)/shard_map/ppermute | solution.py:256
  37.7 12.6 %collective-permute-start.11 = (bf16[32,3584]{1,0:T(8,128)(2,1)S(1)}, bf16[32,3584]{1,0:T(8,128)(2,1)}, u32[]{:S(2)}, u32[]{:S(2)}) collective-permute-start(bf16[32,3584]{1,0:T(8,128)(2,1)S(1)} %collective-permute-done.10.refs_12_.refs_13_), channel_id=1, source_target_pairs={{0,2},{4,0},{8,4},{12,8},{14,12},{10,14},{6,10},{2,6},{1,3},{5,1},... | collective-permute-start | bytes 688136 | tf_op jit(solution)/shard_map/ppermute | solution.py:256
  40.4 14.7 %collective-permute-start.27 = (bf16[32,3584]{1,0:T(8,128)(2,1)S(1)}, bf16[32,3584]{1,0:T(8,128)(2,1)S(1)}, u32[]{:S(2)}, u32[]{:S(2)}) collective-permute-start(bf16[32,3584]{1,0:T(8,128)(2,1)S(1)} %collective-permute-done.26.refs_14_), channel_id=1, source_target_pairs={{0,2},{4,0},{8,4},{12,8},{14,12},{10,14},{6,10},{2,6},{1,3},{5,1},... | collective-permute-start | bytes 688136 | tf_op jit(solution)/shard_map/ppermute | solution.py:256
  42.4 14.8 %collective-permute-start.17 = (bf16[32,3584]{1,0:T(8,128)(2,1)S(1)}, bf16[32,3584]{1,0:T(8,128)(2,1)S(1)}, u32[]{:S(2)}, u32[]{:S(2)}) collective-permute-start(bf16[32,3584]{1,0:T(8,128)(2,1)S(1)} %collective-permute-done.16.refs_3_), channel_id=1, source_target_pairs={{0,4},{4,8},{8,12},{12,14},{14,10},{10,6},{6,2},{2,0},{1,5},{5,9},... | collective-permute-start | bytes 688136 | tf_op jit(solution)/shard_map/ppermute | solution.py:256
  45.4 18.5 %collective-permute-start.8 = (bf16[32,3584]{1,0:T(8,128)(2,1)}, bf16[32,3584]{1,0:T(8,128)(2,1)}, u32[]{:S(2)}, u32[]{:S(2)}) collective-permute-start(bf16[32,3584]{1,0:T(8,128)(2,1)} %collective-permute-done.7.refs_9_.refs_10_), channel_id=1, source_target_pairs={{0,4},{4,8},{8,12},{12,14},{14,10},{10,6},{6,2},{2,0},{1,5},{5,9},... | collective-permute-start | bytes 688136 | tf_op jit(solution)/shard_map/ppermute | solution.py:256
  47.5 18.4 %collective-permute-start.23 = (bf16[32,3584]{1,0:T(8,128)(2,1)}, bf16[32,3584]{1,0:T(8,128)(2,1)}, u32[]{:S(2)}, u32[]{:S(2)}) collective-permute-start(bf16[32,3584]{1,0:T(8,128)(2,1)} %collective-permute-done.22.refs_10_), channel_id=1, source_target_pairs={{0,4},{4,8},{8,12},{12,14},{14,10},{10,6},{6,2},{2,0},{1,5},{5,9},... | collective-permute-start | bytes 688136 | tf_op jit(solution)/shard_map/ppermute | solution.py:256
  50.3 19.2 %collective-permute-start.20 = (bf16[32,3584]{1,0:T(8,128)(2,1)}, bf16[32,3584]{1,0:T(8,128)(2,1)}, u32[]{:S(2)}, u32[]{:S(2)}) collective-permute-start(bf16[32,3584]{1,0:T(8,128)(2,1)} %collective-permute-done.19.refs_6_), channel_id=1, source_target_pairs={{0,2},{4,0},{8,4},{12,8},{14,12},{10,14},{6,10},{2,6},{1,3},{5,1},... | collective-permute-start | bytes 688136 | tf_op jit(solution)/shard_map/ppermute | solution.py:256
  55.1 12.3 %collective-permute-start.2 = (bf16[32,3584]{1,0:T(8,128)(2,1)}, bf16[32,3584]{1,0:T(8,128)(2,1)S(1)}, u32[]{:S(2)}, u32[]{:S(2)}) collective-permute-start(bf16[32,3584]{1,0:T(8,128)(2,1)} %collective-permute-done.1.refs_2_.refs_3_), channel_id=1, source_target_pairs={{0,4},{4,8},{8,12},{12,14},{14,10},{10,6},{6,2},{2,0},{1,5},{5,9},... | collective-permute-start | bytes 688136 | tf_op jit(solution)/shard_map/ppermute | solution.py:256
  57.2 11.5 %collective-permute-start.12 = (bf16[32,3584]{1,0:T(8,128)(2,1)}, bf16[32,3584]{1,0:T(8,128)(2,1)S(1)}, u32[]{:S(2)}, u32[]{:S(2)}) collective-permute-start(bf16[32,3584]{1,0:T(8,128)(2,1)} %collective-permute-done.11.refs_13_.refs_14_), channel_id=1, source_target_pairs={{0,2},{4,0},{8,4},{12,8},{14,12},{10,14},{6,10},{2,6},{1,3},{5,1},... | collective-permute-start | bytes 688136 | tf_op jit(solution)/shard_map/ppermute | solution.py:256
  57.6 62.7 %all-to-all-start = ((bf16[8,128,512]{2,1,0:T(8,128)(2,1)}), bf16[8,128,512]{2,1,0:T(8,128)(2,1)S(1)}, u32[]{:S(2)}, u32[]{:S(2)}) async-start(bf16[8,128,512]{2,1,0:T(8,128)(2,1)} %tie.3), calls=%async_computation | async-start | bytes 2097152 | tf_op jit(solution)/shard_map/all_to_all | solution.py:261
  63.9 22.6 %collective-permute-start.6 = (bf16[32,3584]{1,0:T(8,128)(2,1)}, bf16[32,3584]{1,0:T(8,128)(2,1)S(1)}, u32[]{:S(2)}, u32[]{:S(2)}) collective-permute-start(bf16[32,3584]{1,0:T(8,128)(2,1)} %collective-permute-done.5.refs_6_.refs_7_), channel_id=1, source_target_pairs={{0,2},{4,0},{8,4},{12,8},{14,12},{10,14},{6,10},{2,6},{1,3},{5,1},... | collective-permute-start | bytes 688136 | tf_op jit(solution)/shard_map/ppermute | solution.py:256
  65.9 21.2 %collective-permute-start.9 = (bf16[32,3584]{1,0:T(8,128)(2,1)}, bf16[32,3584]{1,0:T(8,128)(2,1)S(1)}, u32[]{:S(2)}, u32[]{:S(2)}) collective-permute-start(bf16[32,3584]{1,0:T(8,128)(2,1)} %collective-permute-done.8.refs_10_.refs_11_), channel_id=1, source_target_pairs={{0,4},{4,8},{8,12},{12,14},{14,10},{10,6},{6,2},{2,0},{1,5},{5,9},... | collective-permute-start | bytes 688136 | tf_op jit(solution)/shard_map/ppermute | solution.py:256
  67.5 22.7 %collective-permute-start.3 = (bf16[32,3584]{1,0:T(8,128)(2,1)S(1)}, bf16[32,3584]{1,0:T(8,128)(2,1)S(1)}, u32[]{:S(2)}, u32[]{:S(2)}) collective-permute-start(bf16[32,3584]{1,0:T(8,128)(2,1)S(1)} %collective-permute-done.2.refs_3_.refs_4_), channel_id=1, source_target_pairs={{0,4},{4,8},{8,12},{12,14},{14,10},{10,6},{6,2},{2,0},{1,5},{5,9},... | collective-permute-start | bytes 688136 | tf_op jit(solution)/shard_map/ppermute | solution.py:256
  68.8 22.1 %collective-permute-start.13 = (bf16[32,3584]{1,0:T(8,128)(2,1)S(1)}, bf16[32,3584]{1,0:T(8,128)(2,1)S(1)}, u32[]{:S(2)}, u32[]{:S(2)}) collective-permute-start(bf16[32,3584]{1,0:T(8,128)(2,1)S(1)} %collective-permute-done.12.refs_14_.refs_15_), channel_id=1, source_target_pairs={{0,2},{4,0},{8,4},{12,8},{14,12},{10,14},{6,10},{2,6},{1,3},{5,1},... | collective-permute-start | bytes 688136 | tf_op jit(solution)/shard_map/ppermute | solution.py:256
  95.9 9.5 %collective-permute-start.30 = (f32[64,256]{1,0:T(8,128)S(1)}, f32[64,256]{1,0:T(8,128)S(1)}, u32[]{:S(2)}, u32[]{:S(2)}) collective-permute-start(f32[64,256]{1,0:T(8,128)S(1)} %fusion.refs_0_), channel_id=1, source_target_pairs={{0,3},{1,2},{2,1},{3,0},{4,7},{5,6},{6,5},{7,4},{8,11},{9,10},{10,... | collective-permute-start | bytes 196616 | tf_op jit(solution)/shard_map/ppermute | solution.py:280
  104.9 15.5 %collective-permute-start.34 = (f32[256,512]{1,0:T(8,128)S(1)}, f32[256,512]{1,0:T(8,128)S(1)}, u32[]{:S(2)}, u32[]{:S(2)}) collective-permute-start(f32[256,512]{1,0:T(8,128)S(1)} %last_sent.1.refs_0_), channel_id=1, source_target_pairs={{0,1},{1,0},{2,3},{3,2},{4,5},{5,4},{6,7},{7,6},{8,9},{9,8},{10,11... | collective-permute-start | bytes 1572872 | tf_op jit(solution)/shard_map/ppermute | solution.py:285
  105.5 14.8 %collective-permute-start.33 = (bf16[64,256]{1,0:T(8,128)(2,1)S(1)}, bf16[64,256]{1,0:T(8,128)(2,1)S(1)}, u32[]{:S(2)}, u32[]{:S(2)}) collective-permute-start(bf16[64,256]{1,0:T(8,128)(2,1)S(1)} %add_convert_fusion), channel_id=1, source_target_pairs={{0,12},{2,14},{4,0},{6,2},{8,4},{10,6},{12,8},{14,10},{1,13},{3,15... | collective-permute-start | bytes 98312 | tf_op jit(solution)/shard_map/ppermute | solution.py:284
  107.8 12.5 %collective-permute-start.32 = (bf16[64,256]{1,0:T(8,128)(2,1)S(1)}, bf16[64,256]{1,0:T(8,128)(2,1)S(1)}, u32[]{:S(2)}, u32[]{:S(2)}) collective-permute-start(bf16[64,256]{1,0:T(8,128)(2,1)S(1)} %add_convert_fusion), channel_id=1, source_target_pairs={{0,8},{2,10},{4,12},{6,14},{8,0},{10,2},{12,4},{14,6},{1,9},{3,11}... | collective-permute-start | bytes 98312 | tf_op jit(solution)/shard_map/ppermute | solution.py:284
  (23 other events, 746.8 us)

commit v15 on v11

--- a/solution.py
+++ b/solution.py
@@ -131,14 +131,13 @@
     rows = chunks[0][0][0].shape[0] * n
     share = down.shape[1] // 2
     ranks = shrink.shape[0]
-    spans = [(base, start, cuts_of(pieces[0].shape[1])) for pieces, base, start in chunks]
+    spans = [(base, start, cuts_of(pieces[0].shape[1])) for pieces, base, start, _ in chunks]
     sizes = [tile for _, _, cuts in spans for _, tile in cuts]
     width = sum(sizes)
     anywhere = pl.BlockSpec(memory_space=pl.ANY)
     held = [
         piece if i in late else in_hbm(piece)
-        for pieces, base, _ in chunks
-        for late in [(3, 4, n - 1) if base == 0 else (3, n - 2, n - 1)]
+        for pieces, _, _, late in chunks
         for i, piece in enumerate(pieces)
     ]
     args = [*after, *held, in_hbm(down), in_hbm(shrink), *(acc or ())]
@@ -244,8 +243,9 @@
                     moving = lax.ppermute(moving, "store", pairs)
                     pieces.append(moving)
                 ends.append(moving)
-            chunks.append((pieces, way * n, start))
-        factors = lax.all_to_all(tie(blocks, ends[:4]), "store", 0, 0)
+            late = ((long,), (n - 1,)) if chunk < 2 else ((short, long, n - 1), (short, n - 2, n - 1))
+            chunks.append((pieces, way * n, start, late[way]))
+        factors = lax.all_to_all(tie(blocks, [ends[0], ends[3], ends[5], ends[6]]), "store", 0, 0)
 
         call = functools.partial(chunk_matmul, scalars, half)
         first, last = chunks[:CHUNKS // 2], chunks[CHUNKS // 2:]

time: 113 us -> 115 us (1.018)
  waiting for transfers between devices: 17.3 us -> 34.2 us
  starting transfers between devices: 53.7 us -> 43.5 us
  local copies, waits for them, and re-layouts: 9.83 us -> 5.69 us
    ppermute x28, waiting for transfers between devices: 17.3 us -> 34.2 us  [shards(): moving = lax.ppermute(moving, 'store', pairs)]
    ppermute x28, starting transfers between devices: 41.7 us -> 30.7 us  [shards(): moving = lax.ppermute(moving, 'store', pairs)]
    unnamed x56 -> x46, local copies, waits for them, and re-layouts: 7.64 us -> 3.5 us
    ppermute x3, starting transfers between devices: 4.44 us -> 5.81 us  [shards(): lax.ppermute(column, 'store', [(s, (s + ds) % n) for s in range(n)])]
  transfers between devices with their start and end apart: 36 -> 36, of which waited for: 10 -> 13; matrix products, arithmetic and copies ran while one was open for 1% -> 1% of each run, Pallas kernels for 26% -> 26%
where the time goes in v15:
time: 115 us
  starting transfers between devices  43.5 us (38%)
  waiting for transfers between devices  34.2 us (30%)
  Pallas kernels  31 us (27%)
  local copies, waits for them, and re-layouts  5.69 us (5%)
    ppermute x28, waiting for transfers between devices, shards(): moving = lax.ppermute(moving, 'store', pairs)  34.2 us
    ppermute x28, starting transfers between devices, shards(): moving = lax.ppermute(moving, 'store', pairs)  30.7 us
    pallas_call x4, Pallas kernels, chunk_matmul(): pl.pallas_call(functools.partial(matmul_kernel, n, len(after), spans, hal...  26.3 us
    ppermute x3, starting transfers between devices, shards(): lax.ppermute(column, 'store', [(s, (s + ds) % n) for s in range(n)])  5.81 us
    all_to_all x1, starting transfers between devices, shards(): lax.all_to_all(tie(blocks, [ends[0], ends[3], ends[5], ends[6]]), 'store'...  4.54 us
    unnamed x46, local copies, waits for them, and re-layouts  3.5 us
    pallas_call x1, Pallas kernels, expand_blocks(): pl.pallas_call(split_kernel, grid_spec=pltpu.PrefetchScalarGridSpec(num_s...  3.33 us
  transfers between devices with their start and end apart: 36, of which 13 were waited for; matrix products, arithmetic and copies ran while one was open for 1% of the time, Pallas kernels for 26%

profile of v15, /device:TPU:0, one launch (start us, length us, event | category | flops | bytes accessed | tf_op | source)
XLA Modules:
  0.0 114.8 jit_solution(9585679952953231707)
XLA Ops:
  1.4 3.1 %collective-permute-start.14 = (bf16[32,3584]{1,0:T(8,128)(2,1)S(1)}, bf16[32,3584]{1,0:T(8,128)(2,1)S(1)}, u32[]{:S(2)}, u32[]{:S(2)}) collective-permute-start(bf16[32,3584]{1,0:T(8,128)(2,1)S(1)} %get-tuple-element.18.refs_0_), channel_id=1, source_target_pairs={{0,4},{4,8},{8,12},{12,14},{14,10},{10,6},{6,2},{2,0},{1,5},{5,9},... | collective-permute-start | bytes 688136 | tf_op jit(solution)/shard_map/ppermute | solution.py:243
  4.5 2.0 %collective-permute-start.24 = (bf16[32,3584]{1,0:T(8,128)(2,1)S(1)}, bf16[32,3584]{1,0:T(8,128)(2,1)S(1)}, u32[]{:S(2)}, u32[]{:S(2)}) collective-permute-start(bf16[32,3584]{1,0:T(8,128)(2,1)S(1)} %get-tuple-element.15.refs_8_), channel_id=1, source_target_pairs={{0,2},{4,0},{8,4},{12,8},{14,12},{10,14},{6,10},{2,6},{1,3},{5,1},... | collective-permute-start | bytes 688136 | tf_op jit(solution)/shard_map/ppermute | solution.py:243
  7.2 1.6 %copy-done.1 = bf16[2,64,8192]{2,1,0:T(8,128)(2,1)S(1)} copy-done((bf16[2,64,8192]{2,1,0:T(8,128)(2,1)S(1)}, bf16[2,64,8192]{2,1,0:T(8,128)(2,1)}, u32[]{:S(2)}) %copy-start.1) | copy-done | bytes 2097176
  8.8 3.3 %expand_blocks.1 = (bf16[8,128,512]{2,1,0:T(8,128)(2,1)}, f32[8,128]{1,0:T(8,128)S(1)}) custom-call(s32[18]{0:T(128)S(1)} %dynamic-slice_bitcast_fusion.scalars, bf16[128,8192]{1,0:T(8,128)(2,1)S(1)} %bitcast.9), custom_call_target="tpu_custom_call" | custom-call | bytes 2097152 | tf_op jit(solution)/shard_map/expand_blocks/pallas_call | solution.py:39
  12.2 1.9 %collective-permute-start.10 = (bf16[32,3584]{1,0:T(8,128)(2,1)S(1)}, bf16[32,3584]{1,0:T(8,128)(2,1)S(1)}, u32[]{:S(2)}, u32[]{:S(2)}) collective-permute-start(bf16[32,3584]{1,0:T(8,128)(2,1)S(1)} %tie.2.refs_8_.refs_9_), channel_id=1, source_target_pairs={{0,2},{4,0},{8,4},{12,8},{14,12},{10,14},{6,10},{2,6},{1,3},{5,1},... | collective-permute-start | bytes 688136 | tf_op jit(solution)/shard_map/ppermute | solution.py:243
  14.2 3.7 %collective-permute-done.24.refs_12_ = bf16[32,3584]{1,0:T(8,128)(2,1)S(1)} collective-permute-done((bf16[32,3584]{1,0:T(8,128)(2,1)S(1)}, bf16[32,3584]{1,0:T(8,128)(2,1)S(1)}, u32[]{:S(2)}, u32[]{:S(2)}) %collective-permute-start.24) | collective-permute-done | bytes 229408 | tf_op jit(solution)/shard_map/ppermute | solution.py:243
  17.9 1.6 %collective-permute-start = (bf16[32,3584]{1,0:T(8,128)(2,1)S(1)}, bf16[32,3584]{1,0:T(8,128)(2,1)S(1)}, u32[]{:S(2)}, u32[]{:S(2)}) collective-permute-start(bf16[32,3584]{1,0:T(8,128)(2,1)S(1)} %get-tuple-element.17.refs_0_.refs_1_), channel_id=1, source_target_pairs={{0,4},{4,8},{8,12},{12,14},{14,10},{10,6},{6,2},{2,0},{1,5},{5,9},... | collective-permute-start | bytes 688136 | tf_op jit(solution)/shard_map/ppermute | solution.py:243
  20.0 1.6 %collective-permute-start.15 = (bf16[32,3584]{1,0:T(8,128)(2,1)S(1)}, bf16[32,3584]{1,0:T(8,128)(2,1)S(1)}, u32[]{:S(2)}, u32[]{:S(2)}) collective-permute-start(bf16[32,3584]{1,0:T(8,128)(2,1)S(1)} %collective-permute-done.14.refs_1_), channel_id=1, source_target_pairs={{0,4},{4,8},{8,12},{12,14},{14,10},{10,6},{6,2},{2,0},{1,5},{5,9},... | collective-permute-start | bytes 688136 | tf_op jit(solution)/shard_map/ppermute | solution.py:243
  22.9 1.9 %collective-permute-start.19 = (bf16[32,3584]{1,0:T(8,128)(2,1)S(1)}, bf16[32,3584]{1,0:T(8,128)(2,1)}, u32[]{:S(2)}, u32[]{:S(2)}) collective-permute-start(bf16[32,3584]{1,0:T(8,128)(2,1)S(1)} %collective-permute-done.18.refs_5_), channel_id=1, source_target_pairs={{0,2},{4,0},{8,4},{12,8},{14,12},{10,14},{6,10},{2,6},{1,3},{5,1},... | collective-permute-start | bytes 688136 | tf_op jit(solution)/shard_map/ppermute | solution.py:243
  24.7 2.7 %collective-permute-done.refs_1_.refs_2_ = bf16[32,3584]{1,0:T(8,128)(2,1)S(1)} collective-permute-done((bf16[32,3584]{1,0:T(8,128)(2,1)S(1)}, bf16[32,3584]{1,0:T(8,128)(2,1)S(1)}, u32[]{:S(2)}, u32[]{:S(2)}) %collective-permute-start) | collective-permute-done | bytes 229408 | tf_op jit(solution)/shard_map/ppermute | solution.py:243
  29.5 2.9 %collective-permute-done.15.refs_2_ = bf16[32,3584]{1,0:T(8,128)(2,1)S(1)} collective-permute-done((bf16[32,3584]{1,0:T(8,128)(2,1)S(1)}, bf16[32,3584]{1,0:T(8,128)(2,1)S(1)}, u32[]{:S(2)}, u32[]{:S(2)}) %collective-permute-start.15) | collective-permute-done | bytes 229408 | tf_op jit(solution)/shard_map/ppermute | solution.py:243
  33.0 1.6 %collective-permute-start.1 = (bf16[32,3584]{1,0:T(8,128)(2,1)S(1)}, bf16[32,3584]{1,0:T(8,128)(2,1)S(1)}, u32[]{:S(2)}, u32[]{:S(2)}) collective-permute-start(bf16[32,3584]{1,0:T(8,128)(2,1)S(1)} %collective-permute-done.refs_1_.refs_2_), channel_id=1, source_target_pairs={{0,4},{4,8},{8,12},{12,14},{14,10},{10,6},{6,2},{2,0},{1,5},{5,9},... | collective-permute-start | bytes 688136 | tf_op jit(solution)/shard_map/ppermute | solution.py:243
  34.6 3.4 %collective-permute-done.19.refs_6_ = bf16[32,3584]{1,0:T(8,128)(2,1)} collective-permute-done((bf16[32,3584]{1,0:T(8,128)(2,1)S(1)}, bf16[32,3584]{1,0:T(8,128)(2,1)}, u32[]{:S(2)}, u32[]{:S(2)}) %collective-permute-start.19) | collective-permute-done | bytes 229408 | tf_op jit(solution)/shard_map/ppermute | solution.py:243
  38.4 1.6 %collective-permute-start.16 = (bf16[32,3584]{1,0:T(8,128)(2,1)S(1)}, bf16[32,3584]{1,0:T(8,128)(2,1)}, u32[]{:S(2)}, u32[]{:S(2)}) collective-permute-start(bf16[32,3584]{1,0:T(8,128)(2,1)S(1)} %collective-permute-done.15.refs_2_), channel_id=1, source_target_pairs={{0,4},{4,8},{8,12},{12,14},{14,10},{10,6},{6,2},{2,0},{1,5},{5,9},... | collective-permute-start | bytes 688136 | tf_op jit(solution)/shard_map/ppermute | solution.py:243
  40.0 2.8 %collective-permute-done.11.refs_13_.refs_14_ = bf16[32,3584]{1,0:T(8,128)(2,1)S(1)} collective-permute-done((bf16[32,3584]{1,0:T(8,128)(2,1)S(1)}, bf16[32,3584]{1,0:T(8,128)(2,1)S(1)}, u32[]{:S(2)}, u32[]{:S(2)}) %collective-permute-start.11) | collective-permute-done | bytes 229408 | tf_op jit(solution)/shard_map/ppermute | solution.py:243
  44.4 2.7 %collective-permute-done.1.refs_2_.refs_3_ = bf16[32,3584]{1,0:T(8,128)(2,1)S(1)} collective-permute-done((bf16[32,3584]{1,0:T(8,128)(2,1)S(1)}, bf16[32,3584]{1,0:T(8,128)(2,1)S(1)}, u32[]{:S(2)}, u32[]{:S(2)}) %collective-permute-start.1) | collective-permute-done | bytes 229408 | tf_op jit(solution)/shard_map/ppermute | solution.py:243
  47.7 1.6 %collective-permute-start.2 = (bf16[32,3584]{1,0:T(8,128)(2,1)S(1)}, bf16[32,3584]{1,0:T(8,128)(2,1)S(1)}, u32[]{:S(2)}, u32[]{:S(2)}) collective-permute-start(bf16[32,3584]{1,0:T(8,128)(2,1)S(1)} %collective-permute-done.1.refs_2_.refs_3_), channel_id=1, source_target_pairs={{0,4},{4,8},{8,12},{12,14},{14,10},{10,6},{6,2},{2,0},{1,5},{5,9},... | collective-permute-start | bytes 688136 | tf_op jit(solution)/shard_map/ppermute | solution.py:243
  49.4 2.8 %collective-permute-done.16.refs_3_ = bf16[32,3584]{1,0:T(8,128)(2,1)} collective-permute-done((bf16[32,3584]{1,0:T(8,128)(2,1)S(1)}, bf16[32,3584]{1,0:T(8,128)(2,1)}, u32[]{:S(2)}, u32[]{:S(2)}) %collective-permute-start.16) | collective-permute-done | bytes 229408 | tf_op jit(solution)/shard_map/ppermute | solution.py:243
  52.1 1.7 %collective-permute-start.20 = (bf16[32,3584]{1,0:T(8,128)(2,1)}, bf16[32,3584]{1,0:T(8,128)(2,1)}, u32[]{:S(2)}, u32[]{:S(2)}) collective-permute-start(bf16[32,3584]{1,0:T(8,128)(2,1)} %collective-permute-done.19.refs_6_), channel_id=1, source_target_pairs={{0,2},{4,0},{8,4},{12,8},{14,12},{10,14},{6,10},{2,6},{1,3},{5,1},... | collective-permute-start | bytes 688136 | tf_op jit(solution)/shard_map/ppermute | solution.py:243
  54.3 3.2 %collective-permute-done.12.refs_14_.refs_15_ = bf16[32,3584]{1,0:T(8,128)(2,1)S(1)} collective-permute-done((bf16[32,3584]{1,0:T(8,128)(2,1)S(1)}, bf16[32,3584]{1,0:T(8,128)(2,1)S(1)}, u32[]{:S(2)}, u32[]{:S(2)}) %collective-permute-start.12) | collective-permute-done | bytes 229408 | tf_op jit(solution)/shard_map/ppermute | solution.py:243
  58.0 1.6 %collective-permute-start.17 = (bf16[32,3584]{1,0:T(8,128)(2,1)}, bf16[32,3584]{1,0:T(8,128)(2,1)S(1)}, u32[]{:S(2)}, u32[]{:S(2)}) collective-permute-start(bf16[32,3584]{1,0:T(8,128)(2,1)} %collective-permute-done.16.refs_3_), channel_id=1, source_target_pairs={{0,4},{4,8},{8,12},{12,14},{14,10},{10,6},{6,2},{2,0},{1,5},{5,9},... | collective-permute-start | bytes 688136 | tf_op jit(solution)/shard_map/ppermute | solution.py:243
  59.6 2.3 %collective-permute-done.2.refs_3_.refs_4_ = bf16[32,3584]{1,0:T(8,128)(2,1)S(1)} collective-permute-done((bf16[32,3584]{1,0:T(8,128)(2,1)S(1)}, bf16[32,3584]{1,0:T(8,128)(2,1)S(1)}, u32[]{:S(2)}, u32[]{:S(2)}) %collective-permute-start.2) | collective-permute-done | bytes 229408 | tf_op jit(solution)/shard_map/ppermute | solution.py:243
  61.9 1.7 %collective-permute-start.27 = (bf16[32,3584]{1,0:T(8,128)(2,1)}, bf16[32,3584]{1,0:T(8,128)(2,1)S(1)}, u32[]{:S(2)}, u32[]{:S(2)}) collective-permute-start(bf16[32,3584]{1,0:T(8,128)(2,1)} %collective-permute-done.26.refs_14_), channel_id=1, source_target_pairs={{0,2},{4,0},{8,4},{12,8},{14,12},{10,14},{6,10},{2,6},{1,3},{5,1},... | collective-permute-start | bytes 688136 | tf_op jit(solution)/shard_map/ppermute | solution.py:243
  63.8 3.6 %collective-permute-done.6.refs_7_.refs_3_.refs_8_ = bf16[32,3584]{1,0:T(8,128)(2,1)S(1)} collective-permute-done((bf16[32,3584]{1,0:T(8,128)(2,1)S(1)}, bf16[32,3584]{1,0:T(8,128)(2,1)S(1)}, u32[]{:S(2)}, u32[]{:S(2)}) %collective-permute-start.6) | collective-permute-done | bytes 229408 | tf_op jit(solution)/shard_map/ppermute | solution.py:243
  72.3 4.5 %all-to-all-start = ((bf16[8,128,512]{2,1,0:T(8,128)(2,1)}), bf16[8,128,512]{2,1,0:T(8,128)(2,1)S(1)}, u32[]{:S(2)}, u32[]{:S(2)}) async-start(bf16[8,128,512]{2,1,0:T(8,128)(2,1)} %tie.3), calls=%async_computation | async-start | bytes 2097152 | tf_op jit(solution)/shard_map/all_to_all | solution.py:248
  76.9 9.6 %first_chunks.1 = (f32[256,512]{1,0:T(8,128)S(1)}, f32[256,512]{1,0:T(8,128)S(1)}, f32[128,256]{1,0:T(8,128)S(1)}) custom-call(s32[18]{0:T(128)S(1)} %dynamic-slice_bitcast_fusion.scalars, bf16[32,3584]{1,0:T(8,128)(2,1)} %copy-done.14, bf16[32,3584]{1,0:T(8,128)(2,1)} %copy-done.15, bf16[32,3584]{1,0:T(8,128)(2,1)} %copy-done.19, ...), custom_call_target="tpu_custom_call" | custom-call | flops 8455716864 | bytes 22544384 | tf_op jit(solution)/shard_map/first_chunks/pallas_call | solution.py:146
  86.5 5.0 %last_narrow.1 = f32[128,256]{1,0:T(8,128)S(1)} custom-call(s32[18]{0:T(128)S(1)} %dynamic-slice_bitcast_fusion.scalars, bf16[32,3584]{1,0:T(8,128)(2,1)} %copy-done.4, bf16[32,3584]{1,0:T(8,128)(2,1)} %copy-done.7, bf16[32,3584]{1,0:T(8,128)(2,1)} %copy-done.11, bf16[32,3584]{1,0:T(8,128)(2,1)S(1)} %collective-permute-done.2.refs_3_.refs_4_, ...), custom_call_target="tpu_custom_call" | custom-call | flops 939524096 | bytes 5767168 | tf_op jit(solution)/shard_map/last_narrow/pallas_call | solution.py:146
  91.6 2.1 %collective-permute-start.29 = (f32[64,256]{1,0:T(8,128)S(1)}, f32[64,256]{1,0:T(8,128)S(1)}, u32[]{:S(2)}, u32[]{:S(2)}) collective-permute-start(f32[64,256]{1,0:T(8,128)S(1)} %fusion.refs_0_), channel_id=1, source_target_pairs={{0,2},{1,3},{2,0},{3,1},{4,6},{5,7},{6,4},{7,5},{8,10},{9,11},{10,... | collective-permute-start | bytes 196616 | tf_op jit(solution)/shard_map/ppermute | solution.py:267
  93.8 5.8 %last_sent.1.refs_0_ = f32[256,512]{1,0:T(8,128)S(1)} custom-call(s32[18]{0:T(128)S(1)} %dynamic-slice_bitcast_fusion.scalars, f32[64,256]{1,0:T(8,128)S(1)} %fusion.refs_0_, bf16[32,3584]{1,0:T(8,128)(2,1)} %copy-done.4, bf16[32,3584]{1,0:T(8,128)(2,1)} %copy-done.7, bf16[32,3584]{1,0:T(8,128)(2,1)} %copy-done.11, ...), custom_call_target="tpu_custom_call" | custom-call | flops 3758096384 | bytes 12058624 | tf_op jit(solution)/shard_map/last_sent/pallas_call | solution.py:146
  99.9 2.0 %collective-permute-start.31 = (bf16[64,256]{1,0:T(8,128)(2,1)S(1)}, bf16[64,256]{1,0:T(8,128)(2,1)S(1)}, u32[]{:S(2)}, u32[]{:S(2)}) collective-permute-start(bf16[64,256]{1,0:T(8,128)(2,1)S(1)} %add_convert_fusion), channel_id=1, source_target_pairs={{0,4},{2,6},{4,8},{6,10},{8,12},{10,14},{12,0},{14,2},{1,5},{3,7},... | collective-permute-start | bytes 98312 | tf_op jit(solution)/shard_map/ppermute | solution.py:271
  101.9 2.4 %collective-permute-start.32 = (bf16[64,256]{1,0:T(8,128)(2,1)S(1)}, bf16[64,256]{1,0:T(8,128)(2,1)S(1)}, u32[]{:S(2)}, u32[]{:S(2)}) collective-permute-start(bf16[64,256]{1,0:T(8,128)(2,1)S(1)} %add_convert_fusion), channel_id=1, source_target_pairs={{0,8},{2,10},{4,12},{6,14},{8,0},{10,2},{12,4},{14,6},{1,9},{3,11}... | collective-permute-start | bytes 98312 | tf_op jit(solution)/shard_map/ppermute | solution.py:271
  105.7 5.8 %last_kept.1.kept = f32[256,512]{1,0:T(8,128)S(1)} custom-call(s32[18]{0:T(128)S(1)} %dynamic-slice_bitcast_fusion.scalars, f32[256,512]{1,0:T(8,128)S(1)} %last_sent.1.refs_0_, bf16[32,3584]{1,0:T(8,128)(2,1)} %copy-done.4, bf16[32,3584]{1,0:T(8,128)(2,1)} %copy-done.7, bf16[32,3584]{1,0:T(8,128)(2,1)} %copy-done.11, ...), custom_call_target="tpu_custom_call" | custom-call | flops 3758096384 | bytes 12058624 | tf_op jit(solution)/shard_map/last_kept/pallas_call | solution.py:146
  (102 shorter events, 20.6 us)
Async XLA Ops:
  1.4 12.7 %collective-permute-start.14 = (bf16[32,3584]{1,0:T(8,128)(2,1)S(1)}, bf16[32,3584]{1,0:T(8,128)(2,1)S(1)}, u32[]{:S(2)}, u32[]{:S(2)}) collective-permute-start(bf16[32,3584]{1,0:T(8,128)(2,1)S(1)} %get-tuple-element.18.refs_0_), channel_id=1, source_target_pairs={{0,4},{4,8},{8,12},{12,14},{14,10},{10,6},{6,2},{2,0},{1,5},{5,9},... | collective-permute-start | bytes 688136 | tf_op jit(solution)/shard_map/ppermute | solution.py:243
  4.5 15.0 %collective-permute-start.18 = (bf16[32,3584]{1,0:T(8,128)(2,1)S(1)}, bf16[32,3584]{1,0:T(8,128)(2,1)S(1)}, u32[]{:S(2)}, u32[]{:S(2)}) collective-permute-start(bf16[32,3584]{1,0:T(8,128)(2,1)S(1)} %get-tuple-element.18.refs_0_), channel_id=1, source_target_pairs={{0,2},{4,0},{8,4},{12,8},{14,12},{10,14},{6,10},{2,6},{1,3},{5,1},... | collective-permute-start | bytes 688136 | tf_op jit(solution)/shard_map/ppermute | solution.py:243
  4.5 13.4 %collective-permute-start.24 = (bf16[32,3584]{1,0:T(8,128)(2,1)S(1)}, bf16[32,3584]{1,0:T(8,128)(2,1)S(1)}, u32[]{:S(2)}, u32[]{:S(2)}) collective-permute-start(bf16[32,3584]{1,0:T(8,128)(2,1)S(1)} %get-tuple-element.15.refs_8_), channel_id=1, source_target_pairs={{0,2},{4,0},{8,4},{12,8},{14,12},{10,14},{6,10},{2,6},{1,3},{5,1},... | collective-permute-start | bytes 688136 | tf_op jit(solution)/shard_map/ppermute | solution.py:243
  6.4 13.5 %collective-permute-start.21 = (bf16[32,3584]{1,0:T(8,128)(2,1)S(1)}, bf16[32,3584]{1,0:T(8,128)(2,1)S(1)}, u32[]{:S(2)}, u32[]{:S(2)}) collective-permute-start(bf16[32,3584]{1,0:T(8,128)(2,1)S(1)} %get-tuple-element.15.refs_8_), channel_id=1, source_target_pairs={{0,4},{4,8},{8,12},{12,14},{14,10},{10,6},{6,2},{2,0},{1,5},{5,9},... | collective-permute-start | bytes 688136 | tf_op jit(solution)/shard_map/ppermute | solution.py:243
  12.2 10.7 %collective-permute-start.10 = (bf16[32,3584]{1,0:T(8,128)(2,1)S(1)}, bf16[32,3584]{1,0:T(8,128)(2,1)S(1)}, u32[]{:S(2)}, u32[]{:S(2)}) collective-permute-start(bf16[32,3584]{1,0:T(8,128)(2,1)S(1)} %tie.2.refs_8_.refs_9_), channel_id=1, source_target_pairs={{0,2},{4,0},{8,4},{12,8},{14,12},{10,14},{6,10},{2,6},{1,3},{5,1},... | collective-permute-start | bytes 688136 | tf_op jit(solution)/shard_map/ppermute | solution.py:243
  14.1 8.8 %collective-permute-start.7 = (bf16[32,3584]{1,0:T(8,128)(2,1)S(1)}, bf16[32,3584]{1,0:T(8,128)(2,1)S(1)}, u32[]{:S(2)}, u32[]{:S(2)}) collective-permute-start(bf16[32,3584]{1,0:T(8,128)(2,1)S(1)} %tie.2.refs_8_.refs_9_), channel_id=1, source_target_pairs={{0,4},{4,8},{8,12},{12,14},{14,10},{10,6},{6,2},{2,0},{1,5},{5,9},... | collective-permute-start | bytes 688136 | tf_op jit(solution)/shard_map/ppermute | solution.py:243
  17.9 9.5 %collective-permute-start = (bf16[32,3584]{1,0:T(8,128)(2,1)S(1)}, bf16[32,3584]{1,0:T(8,128)(2,1)S(1)}, u32[]{:S(2)}, u32[]{:S(2)}) collective-permute-start(bf16[32,3584]{1,0:T(8,128)(2,1)S(1)} %get-tuple-element.17.refs_0_.refs_1_), channel_id=1, source_target_pairs={{0,4},{4,8},{8,12},{12,14},{14,10},{10,6},{6,2},{2,0},{1,5},{5,9},... | collective-permute-start | bytes 688136 | tf_op jit(solution)/shard_map/ppermute | solution.py:243
  19.5 8.5 %collective-permute-start.4 = (bf16[32,3584]{1,0:T(8,128)(2,1)S(1)}, bf16[32,3584]{1,0:T(8,128)(2,1)S(1)}, u32[]{:S(2)}, u32[]{:S(2)}) collective-permute-start(bf16[32,3584]{1,0:T(8,128)(2,1)S(1)} %get-tuple-element.17.refs_0_.refs_1_), channel_id=1, source_target_pairs={{0,2},{4,0},{8,4},{12,8},{14,12},{10,14},{6,10},{2,6},{1,3},{5,1},... | collective-permute-start | bytes 688136 | tf_op jit(solution)/shard_map/ppermute | solution.py:243
  20.0 12.4 %collective-permute-start.15 = (bf16[32,3584]{1,0:T(8,128)(2,1)S(1)}, bf16[32,3584]{1,0:T(8,128)(2,1)S(1)}, u32[]{:S(2)}, u32[]{:S(2)}) collective-permute-start(bf16[32,3584]{1,0:T(8,128)(2,1)S(1)} %collective-permute-done.14.refs_1_), channel_id=1, source_target_pairs={{0,4},{4,8},{8,12},{12,14},{14,10},{10,6},{6,2},{2,0},{1,5},{5,9},... | collective-permute-start | bytes 688136 | tf_op jit(solution)/shard_map/ppermute | solution.py:243
  22.8 10.1 %collective-permute-start.25 = (bf16[32,3584]{1,0:T(8,128)(2,1)S(1)}, bf16[32,3584]{1,0:T(8,128)(2,1)S(1)}, u32[]{:S(2)}, u32[]{:S(2)}) collective-permute-start(bf16[32,3584]{1,0:T(8,128)(2,1)S(1)} %collective-permute-done.24.refs_12_), channel_id=1, source_target_pairs={{0,2},{4,0},{8,4},{12,8},{14,12},{10,14},{6,10},{2,6},{1,3},{5,1},... | collective-permute-start | bytes 688136 | tf_op jit(solution)/shard_map/ppermute | solution.py:243
  22.9 15.1 %collective-permute-start.19 = (bf16[32,3584]{1,0:T(8,128)(2,1)S(1)}, bf16[32,3584]{1,0:T(8,128)(2,1)}, u32[]{:S(2)}, u32[]{:S(2)}) collective-permute-start(bf16[32,3584]{1,0:T(8,128)(2,1)S(1)} %collective-permute-done.18.refs_5_), channel_id=1, source_target_pairs={{0,2},{4,0},{8,4},{12,8},{14,12},{10,14},{6,10},{2,6},{1,3},{5,1},... | collective-permute-start | bytes 688136 | tf_op jit(solution)/shard_map/ppermute | solution.py:243
  27.4 11.0 %collective-permute-start.22 = (bf16[32,3584]{1,0:T(8,128)(2,1)S(1)}, bf16[32,3584]{1,0:T(8,128)(2,1)}, u32[]{:S(2)}, u32[]{:S(2)}) collective-permute-start(bf16[32,3584]{1,0:T(8,128)(2,1)S(1)} %collective-permute-done.21.refs_9_), channel_id=1, source_target_pairs={{0,4},{4,8},{8,12},{12,14},{14,10},{10,6},{6,2},{2,0},{1,5},{5,9},... | collective-permute-start | bytes 688136 | tf_op jit(solution)/shard_map/ppermute | solution.py:243
  28.0 14.7 %collective-permute-start.11 = (bf16[32,3584]{1,0:T(8,128)(2,1)S(1)}, bf16[32,3584]{1,0:T(8,128)(2,1)S(1)}, u32[]{:S(2)}, u32[]{:S(2)}) collective-permute-start(bf16[32,3584]{1,0:T(8,128)(2,1)S(1)} %collective-permute-done.10.refs_12_.refs_13_), channel_id=1, source_target_pairs={{0,2},{4,0},{8,4},{12,8},{14,12},{10,14},{6,10},{2,6},{1,3},{5,1},... | collective-permute-start | bytes 688136 | tf_op jit(solution)/shard_map/ppermute | solution.py:243
  32.4 10.9 %collective-permute-start.8 = (bf16[32,3584]{1,0:T(8,128)(2,1)S(1)}, bf16[32,3584]{1,0:T(8,128)(2,1)S(1)}, u32[]{:S(2)}, u32[]{:S(2)}) collective-permute-start(bf16[32,3584]{1,0:T(8,128)(2,1)S(1)} %collective-permute-done.7.refs_9_.refs_10_), channel_id=1, source_target_pairs={{0,4},{4,8},{8,12},{12,14},{14,10},{10,6},{6,2},{2,0},{1,5},{5,9},... | collective-permute-start | bytes 688136 | tf_op jit(solution)/shard_map/ppermute | solution.py:243
  33.0 14.1 %collective-permute-start.1 = (bf16[32,3584]{1,0:T(8,128)(2,1)S(1)}, bf16[32,3584]{1,0:T(8,128)(2,1)S(1)}, u32[]{:S(2)}, u32[]{:S(2)}) collective-permute-start(bf16[32,3584]{1,0:T(8,128)(2,1)S(1)} %collective-permute-done.refs_1_.refs_2_), channel_id=1, source_target_pairs={{0,4},{4,8},{8,12},{12,14},{14,10},{10,6},{6,2},{2,0},{1,5},{5,9},... | collective-permute-start | bytes 688136 | tf_op jit(solution)/shard_map/ppermute | solution.py:243
  38.0 9.7 %collective-permute-start.5 = (bf16[32,3584]{1,0:T(8,128)(2,1)S(1)}, bf16[32,3584]{1,0:T(8,128)(2,1)S(1)}, u32[]{:S(2)}, u32[]{:S(2)}) collective-permute-start(bf16[32,3584]{1,0:T(8,128)(2,1)S(1)} %collective-permute-done.4.refs_5_.refs_6_), channel_id=1, source_target_pairs={{0,2},{4,0},{8,4},{12,8},{14,12},{10,14},{6,10},{2,6},{1,3},{5,1},... | collective-permute-start | bytes 688136 | tf_op jit(solution)/shard_map/ppermute | solution.py:243
  38.4 13.7 %collective-permute-start.16 = (bf16[32,3584]{1,0:T(8,128)(2,1)S(1)}, bf16[32,3584]{1,0:T(8,128)(2,1)}, u32[]{:S(2)}, u32[]{:S(2)}) collective-permute-start(bf16[32,3584]{1,0:T(8,128)(2,1)S(1)} %collective-permute-done.15.refs_2_), channel_id=1, source_target_pairs={{0,4},{4,8},{8,12},{12,14},{14,10},{10,6},{6,2},{2,0},{1,5},{5,9},... | collective-permute-start | bytes 688136 | tf_op jit(solution)/shard_map/ppermute | solution.py:243
  42.8 11.0 %collective-permute-start.26 = (bf16[32,3584]{1,0:T(8,128)(2,1)S(1)}, bf16[32,3584]{1,0:T(8,128)(2,1)}, u32[]{:S(2)}, u32[]{:S(2)}) collective-permute-start(bf16[32,3584]{1,0:T(8,128)(2,1)S(1)} %collective-permute-done.25.refs_13_), channel_id=1, source_target_pairs={{0,2},{4,0},{8,4},{12,8},{14,12},{10,14},{6,10},{2,6},{1,3},{5,1},... | collective-permute-start | bytes 688136 | tf_op jit(solution)/shard_map/ppermute | solution.py:243
  43.3 14.3 %collective-permute-start.12 = (bf16[32,3584]{1,0:T(8,128)(2,1)S(1)}, bf16[32,3584]{1,0:T(8,128)(2,1)S(1)}, u32[]{:S(2)}, u32[]{:S(2)}) collective-permute-start(bf16[32,3584]{1,0:T(8,128)(2,1)S(1)} %collective-permute-done.11.refs_13_.refs_14_), channel_id=1, source_target_pairs={{0,2},{4,0},{8,4},{12,8},{14,12},{10,14},{6,10},{2,6},{1,3},{5,1},... | collective-permute-start | bytes 688136 | tf_op jit(solution)/shard_map/ppermute | solution.py:243
  47.1 10.9 %collective-permute-start.9 = (bf16[32,3584]{1,0:T(8,128)(2,1)S(1)}, bf16[32,3584]{1,0:T(8,128)(2,1)S(1)}, u32[]{:S(2)}, u32[]{:S(2)}) collective-permute-start(bf16[32,3584]{1,0:T(8,128)(2,1)S(1)} %collective-permute-done.8.refs_10_.refs_11_), channel_id=1, source_target_pairs={{0,4},{4,8},{8,12},{12,14},{14,10},{10,6},{6,2},{2,0},{1,5},{5,9},... | collective-permute-start | bytes 688136 | tf_op jit(solution)/shard_map/ppermute | solution.py:243
  47.7 14.1 %collective-permute-start.2 = (bf16[32,3584]{1,0:T(8,128)(2,1)S(1)}, bf16[32,3584]{1,0:T(8,128)(2,1)S(1)}, u32[]{:S(2)}, u32[]{:S(2)}) collective-permute-start(bf16[32,3584]{1,0:T(8,128)(2,1)S(1)} %collective-permute-done.1.refs_2_.refs_3_), channel_id=1, source_target_pairs={{0,4},{4,8},{8,12},{12,14},{14,10},{10,6},{6,2},{2,0},{1,5},{5,9},... | collective-permute-start | bytes 688136 | tf_op jit(solution)/shard_map/ppermute | solution.py:243
  52.1 24.7 %collective-permute-start.20 = (bf16[32,3584]{1,0:T(8,128)(2,1)}, bf16[32,3584]{1,0:T(8,128)(2,1)}, u32[]{:S(2)}, u32[]{:S(2)}) collective-permute-start(bf16[32,3584]{1,0:T(8,128)(2,1)} %collective-permute-done.19.refs_6_), channel_id=1, source_target_pairs={{0,2},{4,0},{8,4},{12,8},{14,12},{10,14},{6,10},{2,6},{1,3},{5,1},... | collective-permute-start | bytes 688136 | tf_op jit(solution)/shard_map/ppermute | solution.py:243
  53.8 23.0 %collective-permute-start.23 = (bf16[32,3584]{1,0:T(8,128)(2,1)}, bf16[32,3584]{1,0:T(8,128)(2,1)}, u32[]{:S(2)}, u32[]{:S(2)}) collective-permute-start(bf16[32,3584]{1,0:T(8,128)(2,1)} %collective-permute-done.22.refs_10_), channel_id=1, source_target_pairs={{0,4},{4,8},{8,12},{12,14},{14,10},{10,6},{6,2},{2,0},{1,5},{5,9},... | collective-permute-start | bytes 688136 | tf_op jit(solution)/shard_map/ppermute | solution.py:243
  57.5 9.8 %collective-permute-start.6 = (bf16[32,3584]{1,0:T(8,128)(2,1)S(1)}, bf16[32,3584]{1,0:T(8,128)(2,1)S(1)}, u32[]{:S(2)}, u32[]{:S(2)}) collective-permute-start(bf16[32,3584]{1,0:T(8,128)(2,1)S(1)} %collective-permute-done.5.refs_6_.refs_7_), channel_id=1, source_target_pairs={{0,2},{4,0},{8,4},{12,8},{14,12},{10,14},{6,10},{2,6},{1,3},{5,1},... | collective-permute-start | bytes 688136 | tf_op jit(solution)/shard_map/ppermute | solution.py:243
  58.0 11.3 %collective-permute-start.17 = (bf16[32,3584]{1,0:T(8,128)(2,1)}, bf16[32,3584]{1,0:T(8,128)(2,1)S(1)}, u32[]{:S(2)}, u32[]{:S(2)}) collective-permute-start(bf16[32,3584]{1,0:T(8,128)(2,1)} %collective-permute-done.16.refs_3_), channel_id=1, source_target_pairs={{0,4},{4,8},{8,12},{12,14},{14,10},{10,6},{6,2},{2,0},{1,5},{5,9},... | collective-permute-start | bytes 688136 | tf_op jit(solution)/shard_map/ppermute | solution.py:243
  61.9 10.4 %collective-permute-start.27 = (bf16[32,3584]{1,0:T(8,128)(2,1)}, bf16[32,3584]{1,0:T(8,128)(2,1)S(1)}, u32[]{:S(2)}, u32[]{:S(2)}) collective-permute-start(bf16[32,3584]{1,0:T(8,128)(2,1)} %collective-permute-done.26.refs_14_), channel_id=1, source_target_pairs={{0,2},{4,0},{8,4},{12,8},{14,12},{10,14},{6,10},{2,6},{1,3},{5,1},... | collective-permute-start | bytes 688136 | tf_op jit(solution)/shard_map/ppermute | solution.py:243
  67.4 19.1 %collective-permute-start.13 = (bf16[32,3584]{1,0:T(8,128)(2,1)S(1)}, bf16[32,3584]{1,0:T(8,128)(2,1)S(1)}, u32[]{:S(2)}, u32[]{:S(2)}) collective-permute-start(bf16[32,3584]{1,0:T(8,128)(2,1)S(1)} %collective-permute-done.12.refs_14_.refs_15_), channel_id=1, source_target_pairs={{0,2},{4,0},{8,4},{12,8},{14,12},{10,14},{6,10},{2,6},{1,3},{5,1},... | collective-permute-start | bytes 688136 | tf_op jit(solution)/shard_map/ppermute | solution.py:243
  69.3 17.2 %collective-permute-start.3 = (bf16[32,3584]{1,0:T(8,128)(2,1)S(1)}, bf16[32,3584]{1,0:T(8,128)(2,1)S(1)}, u32[]{:S(2)}, u32[]{:S(2)}) collective-permute-start(bf16[32,3584]{1,0:T(8,128)(2,1)S(1)} %collective-permute-done.2.refs_3_.refs_4_), channel_id=1, source_target_pairs={{0,4},{4,8},{8,12},{12,14},{14,10},{10,6},{6,2},{2,0},{1,5},{5,9},... | collective-permute-start | bytes 688136 | tf_op jit(solution)/shard_map/ppermute | solution.py:243
  72.3 40.1 %all-to-all-start = ((bf16[8,128,512]{2,1,0:T(8,128)(2,1)}), bf16[8,128,512]{2,1,0:T(8,128)(2,1)S(1)}, u32[]{:S(2)}, u32[]{:S(2)}) async-start(bf16[8,128,512]{2,1,0:T(8,128)(2,1)} %tie.3), calls=%async_computation | async-start | bytes 2097152 | tf_op jit(solution)/shard_map/all_to_all | solution.py:248
  99.6 11.9 %collective-permute-start.34 = (f32[256,512]{1,0:T(8,128)S(1)}, f32[256,512]{1,0:T(8,128)S(1)}, u32[]{:S(2)}, u32[]{:S(2)}) collective-permute-start(f32[256,512]{1,0:T(8,128)S(1)} %last_sent.1.refs_0_), channel_id=1, source_target_pairs={{0,1},{1,0},{2,3},{3,2},{4,5},{5,4},{6,7},{7,6},{8,9},{9,8},{10,11... | collective-permute-start | bytes 1572872 | tf_op jit(solution)/shard_map/ppermute | solution.py:272
  99.9 11.6 %collective-permute-start.31 = (bf16[64,256]{1,0:T(8,128)(2,1)S(1)}, bf16[64,256]{1,0:T(8,128)(2,1)S(1)}, u32[]{:S(2)}, u32[]{:S(2)}) collective-permute-start(bf16[64,256]{1,0:T(8,128)(2,1)S(1)} %add_convert_fusion), channel_id=1, source_target_pairs={{0,4},{2,6},{4,8},{6,10},{8,12},{10,14},{12,0},{14,2},{1,5},{3,7},... | collective-permute-start | bytes 98312 | tf_op jit(solution)/shard_map/ppermute | solution.py:271
  101.9 9.7 %collective-permute-start.32 = (bf16[64,256]{1,0:T(8,128)(2,1)S(1)}, bf16[64,256]{1,0:T(8,128)(2,1)S(1)}, u32[]{:S(2)}, u32[]{:S(2)}) collective-permute-start(bf16[64,256]{1,0:T(8,128)(2,1)S(1)} %add_convert_fusion), channel_id=1, source_target_pairs={{0,8},{2,10},{4,12},{6,14},{8,0},{10,2},{12,4},{14,6},{1,9},{3,11}... | collective-permute-start | bytes 98312 | tf_op jit(solution)/shard_map/ppermute | solution.py:271
  (27 other events, 793.6 us)

commit v16 on v15

--- a/solution.py
+++ b/solution.py
@@ -245,7 +245,7 @@
                 ends.append(moving)
             late = ((long,), (n - 1,)) if chunk < 2 else ((short, long, n - 1), (short, n - 2, n - 1))
             chunks.append((pieces, way * n, start, late[way]))
-        factors = lax.all_to_all(tie(blocks, [ends[0], ends[3], ends[5], ends[6]]), "store", 0, 0)
+        factors = lax.all_to_all(tie(blocks, ends[:4]), "store", 0, 0)
 
         call = functools.partial(chunk_matmul, scalars, half)
         first, last = chunks[:CHUNKS // 2], chunks[CHUNKS // 2:]

time: 115 us -> 111 us (0.965)
  waiting for transfers between devices: 34.2 us -> 17.9 us
  starting transfers between devices: 43.5 us -> 53.8 us
  local copies, waits for them, and re-layouts: 5.69 us -> 7.28 us
    ppermute x28, waiting for transfers between devices: 34.2 us -> 17.9 us  [shards(): moving = lax.ppermute(moving, 'store', pairs)]
    ppermute x28, starting transfers between devices: 30.7 us -> 41.7 us  [shards(): moving = lax.ppermute(moving, 'store', pairs)]
    unnamed x46 -> x52, local copies, waits for them, and re-layouts: 3.5 us -> 5.1 us
    ppermute x3, starting transfers between devices: 5.81 us -> 4.49 us  [shards(): lax.ppermute(column, 'store', [(s, (s + ds) % n) for s in range(n)])]
  transfers between devices with their start and end apart: 36 -> 36, of which waited for: 13 -> 11; matrix products, arithmetic and copies ran while one was open for 1% -> 1% of each run, Pallas kernels for 26% -> 27%
where the time goes in v16:
time: 111 us; the launch traced here: 110 us
  starting transfers between devices  53.8 us (48%)
  Pallas kernels  30.9 us (28%)
  waiting for transfers between devices  17.9 us (16%)
  local copies, waits for them, and re-layouts  7.28 us (7%)
    ppermute x28, starting transfers between devices, shards(): moving = lax.ppermute(moving, 'store', pairs)  41.7 us
    pallas_call x4, Pallas kernels, chunk_matmul(): pl.pallas_call(functools.partial(matmul_kernel, n, len(after), spans, hal...  26.3 us
    ppermute x28, waiting for transfers between devices, shards(): moving = lax.ppermute(moving, 'store', pairs)  17.9 us
    unnamed x52, local copies, waits for them, and re-layouts  5.1 us
    all_to_all x1, starting transfers between devices, shards(): factors = lax.all_to_all(tie(blocks, ends[:4]), 'store', 0, 0)  4.88 us
    ppermute x3, starting transfers between devices, shards(): lax.ppermute(column, 'store', [(s, (s + ds) % n) for s in range(n)])  4.49 us
    pallas_call x1, Pallas kernels, expand_blocks(): pl.pallas_call(split_kernel, grid_spec=pltpu.PrefetchScalarGridSpec(num_s...  3.34 us
  transfers between devices with their start and end apart: 36, of which 11 were waited for; matrix products, arithmetic and copies ran while one was open for 1% of the time, Pallas kernels for 27%

profile of v16, /device:TPU:0, one launch (start us, length us, event | category | flops | bytes accessed | tf_op | source)
XLA Modules:
  0.0 110.4 jit_solution(13047421903016250423)
XLA Ops:
  1.4 3.0 %collective-permute-start.24 = (bf16[32,3584]{1,0:T(8,128)(2,1)S(1)}, bf16[32,3584]{1,0:T(8,128)(2,1)S(1)}, u32[]{:S(2)}, u32[]{:S(2)}) collective-permute-start(bf16[32,3584]{1,0:T(8,128)(2,1)S(1)} %get-tuple-element.15.refs_8_), channel_id=1, source_target_pairs={{0,2},{4,0},{8,4},{12,8},{14,12},{10,14},{6,10},{2,6},{1,3},{5,1},... | collective-permute-start | bytes 688136 | tf_op jit(solution)/shard_map/ppermute | solution.py:243
  4.5 1.9 %collective-permute-start.18 = (bf16[32,3584]{1,0:T(8,128)(2,1)S(1)}, bf16[32,3584]{1,0:T(8,128)(2,1)S(1)}, u32[]{:S(2)}, u32[]{:S(2)}) collective-permute-start(bf16[32,3584]{1,0:T(8,128)(2,1)S(1)} %get-tuple-element.18.refs_0_), channel_id=1, source_target_pairs={{0,2},{4,0},{8,4},{12,8},{14,12},{10,14},{6,10},{2,6},{1,3},{5,1},... | collective-permute-start | bytes 688136 | tf_op jit(solution)/shard_map/ppermute | solution.py:243
  6.6 1.9 %collective-permute-start.4 = (bf16[32,3584]{1,0:T(8,128)(2,1)S(1)}, bf16[32,3584]{1,0:T(8,128)(2,1)S(1)}, u32[]{:S(2)}, u32[]{:S(2)}) collective-permute-start(bf16[32,3584]{1,0:T(8,128)(2,1)S(1)} %get-tuple-element.17.refs_0_.refs_1_), channel_id=1, source_target_pairs={{0,2},{4,0},{8,4},{12,8},{14,12},{10,14},{6,10},{2,6},{1,3},{5,1},... | collective-permute-start | bytes 688136 | tf_op jit(solution)/shard_map/ppermute | solution.py:243
  9.2 1.6 %copy-done.1 = bf16[2,64,8192]{2,1,0:T(8,128)(2,1)S(1)} copy-done((bf16[2,64,8192]{2,1,0:T(8,128)(2,1)S(1)}, bf16[2,64,8192]{2,1,0:T(8,128)(2,1)}, u32[]{:S(2)}) %copy-start.1) | copy-done | bytes 2097176
  10.8 3.3 %expand_blocks.1 = (bf16[8,128,512]{2,1,0:T(8,128)(2,1)}, f32[8,128]{1,0:T(8,128)S(1)}) custom-call(s32[18]{0:T(128)S(1)} %dynamic-slice_bitcast_fusion.scalars, bf16[128,8192]{1,0:T(8,128)(2,1)S(1)} %bitcast.9), custom_call_target="tpu_custom_call" | custom-call | bytes 2097152 | tf_op jit(solution)/shard_map/expand_blocks/pallas_call | solution.py:39
  14.3 2.0 %collective-permute-start.10 = (bf16[32,3584]{1,0:T(8,128)(2,1)S(1)}, bf16[32,3584]{1,0:T(8,128)(2,1)S(1)}, u32[]{:S(2)}, u32[]{:S(2)}) collective-permute-start(bf16[32,3584]{1,0:T(8,128)(2,1)S(1)} %tie.2.refs_8_.refs_9_), channel_id=1, source_target_pairs={{0,2},{4,0},{8,4},{12,8},{14,12},{10,14},{6,10},{2,6},{1,3},{5,1},... | collective-permute-start | bytes 688136 | tf_op jit(solution)/shard_map/ppermute | solution.py:243
  16.3 1.6 %collective-permute-start.7 = (bf16[32,3584]{1,0:T(8,128)(2,1)S(1)}, bf16[32,3584]{1,0:T(8,128)(2,1)S(1)}, u32[]{:S(2)}, u32[]{:S(2)}) collective-permute-start(bf16[32,3584]{1,0:T(8,128)(2,1)S(1)} %tie.2.refs_8_.refs_9_), channel_id=1, source_target_pairs={{0,4},{4,8},{8,12},{12,14},{14,10},{10,6},{6,2},{2,0},{1,5},{5,9},... | collective-permute-start | bytes 688136 | tf_op jit(solution)/shard_map/ppermute | solution.py:243
  19.1 1.6 %collective-permute-done.4.refs_5_.refs_6_ = bf16[32,3584]{1,0:T(8,128)(2,1)S(1)} collective-permute-done((bf16[32,3584]{1,0:T(8,128)(2,1)S(1)}, bf16[32,3584]{1,0:T(8,128)(2,1)S(1)}, u32[]{:S(2)}, u32[]{:S(2)}) %collective-permute-start.4) | collective-permute-done | bytes 229408 | tf_op jit(solution)/shard_map/ppermute | solution.py:243
  20.7 2.1 %collective-permute-start.22 = (bf16[32,3584]{1,0:T(8,128)(2,1)S(1)}, bf16[32,3584]{1,0:T(8,128)(2,1)S(1)}, u32[]{:S(2)}, u32[]{:S(2)}) collective-permute-start(bf16[32,3584]{1,0:T(8,128)(2,1)S(1)} %collective-permute-done.21.refs_9_), channel_id=1, source_target_pairs={{0,4},{4,8},{8,12},{12,14},{14,10},{10,6},{6,2},{2,0},{1,5},{5,9},... | collective-permute-start | bytes 688136 | tf_op jit(solution)/shard_map/ppermute | solution.py:243
  25.7 2.1 %collective-permute-start.15 = (bf16[32,3584]{1,0:T(8,128)(2,1)S(1)}, bf16[32,3584]{1,0:T(8,128)(2,1)S(1)}, u32[]{:S(2)}, u32[]{:S(2)}) collective-permute-start(bf16[32,3584]{1,0:T(8,128)(2,1)S(1)} %collective-permute-done.14.refs_1_), channel_id=1, source_target_pairs={{0,4},{4,8},{8,12},{12,14},{14,10},{10,6},{6,2},{2,0},{1,5},{5,9},... | collective-permute-start | bytes 688136 | tf_op jit(solution)/shard_map/ppermute | solution.py:243
  30.6 2.1 %collective-permute-start.1 = (bf16[32,3584]{1,0:T(8,128)(2,1)S(1)}, bf16[32,3584]{1,0:T(8,128)(2,1)S(1)}, u32[]{:S(2)}, u32[]{:S(2)}) collective-permute-start(bf16[32,3584]{1,0:T(8,128)(2,1)S(1)} %collective-permute-done.refs_1_.refs_2_), channel_id=1, source_target_pairs={{0,4},{4,8},{8,12},{12,14},{14,10},{10,6},{6,2},{2,0},{1,5},{5,9},... | collective-permute-start | bytes 688136 | tf_op jit(solution)/shard_map/ppermute | solution.py:243
  32.6 1.5 %collective-permute-start.11 = (bf16[32,3584]{1,0:T(8,128)(2,1)S(1)}, bf16[32,3584]{1,0:T(8,128)(2,1)S(1)}, u32[]{:S(2)}, u32[]{:S(2)}) collective-permute-start(bf16[32,3584]{1,0:T(8,128)(2,1)S(1)} %collective-permute-done.10.refs_12_.refs_13_), channel_id=1, source_target_pairs={{0,2},{4,0},{8,4},{12,8},{14,12},{10,14},{6,10},{2,6},{1,3},{5,1},... | collective-permute-start | bytes 688136 | tf_op jit(solution)/shard_map/ppermute | solution.py:243
  34.1 1.5 %collective-permute-done.19.refs_6_ = bf16[32,3584]{1,0:T(8,128)(2,1)} collective-permute-done((bf16[32,3584]{1,0:T(8,128)(2,1)S(1)}, bf16[32,3584]{1,0:T(8,128)(2,1)}, u32[]{:S(2)}, u32[]{:S(2)}) %collective-permute-start.19) | collective-permute-done | bytes 229408 | tf_op jit(solution)/shard_map/ppermute | solution.py:243
  35.6 2.1 %collective-permute-start.8 = (bf16[32,3584]{1,0:T(8,128)(2,1)S(1)}, bf16[32,3584]{1,0:T(8,128)(2,1)}, u32[]{:S(2)}, u32[]{:S(2)}) collective-permute-start(bf16[32,3584]{1,0:T(8,128)(2,1)S(1)} %collective-permute-done.7.refs_9_.refs_10_), channel_id=1, source_target_pairs={{0,4},{4,8},{8,12},{12,14},{14,10},{10,6},{6,2},{2,0},{1,5},{5,9},... | collective-permute-start | bytes 688136 | tf_op jit(solution)/shard_map/ppermute | solution.py:243
  40.5 2.1 %collective-permute-start.23 = (bf16[32,3584]{1,0:T(8,128)(2,1)S(1)}, bf16[32,3584]{1,0:T(8,128)(2,1)S(1)}, u32[]{:S(2)}, u32[]{:S(2)}) collective-permute-start(bf16[32,3584]{1,0:T(8,128)(2,1)S(1)} %collective-permute-done.22.refs_10_), channel_id=1, source_target_pairs={{0,4},{4,8},{8,12},{12,14},{14,10},{10,6},{6,2},{2,0},{1,5},{5,9},... | collective-permute-start | bytes 688136 | tf_op jit(solution)/shard_map/ppermute | solution.py:243
  42.6 1.6 %collective-permute-start.16 = (bf16[32,3584]{1,0:T(8,128)(2,1)S(1)}, bf16[32,3584]{1,0:T(8,128)(2,1)}, u32[]{:S(2)}, u32[]{:S(2)}) collective-permute-start(bf16[32,3584]{1,0:T(8,128)(2,1)S(1)} %collective-permute-done.15.refs_2_), channel_id=1, source_target_pairs={{0,4},{4,8},{8,12},{12,14},{14,10},{10,6},{6,2},{2,0},{1,5},{5,9},... | collective-permute-start | bytes 688136 | tf_op jit(solution)/shard_map/ppermute | solution.py:243
  45.3 2.0 %collective-permute-start.20 = (bf16[32,3584]{1,0:T(8,128)(2,1)}, bf16[32,3584]{1,0:T(8,128)(2,1)S(1)}, u32[]{:S(2)}, u32[]{:S(2)}) collective-permute-start(bf16[32,3584]{1,0:T(8,128)(2,1)} %collective-permute-done.19.refs_6_), channel_id=1, source_target_pairs={{0,2},{4,0},{8,4},{12,8},{14,12},{10,14},{6,10},{2,6},{1,3},{5,1},... | collective-permute-start | bytes 688136 | tf_op jit(solution)/shard_map/ppermute | solution.py:243
  47.5 2.8 %collective-permute-done.26.refs_14_ = bf16[32,3584]{1,0:T(8,128)(2,1)} collective-permute-done((bf16[32,3584]{1,0:T(8,128)(2,1)S(1)}, bf16[32,3584]{1,0:T(8,128)(2,1)}, u32[]{:S(2)}, u32[]{:S(2)}) %collective-permute-start.26) | collective-permute-done | bytes 229408 | tf_op jit(solution)/shard_map/ppermute | solution.py:243
  50.3 2.0 %collective-permute-start.12 = (bf16[32,3584]{1,0:T(8,128)(2,1)S(1)}, bf16[32,3584]{1,0:T(8,128)(2,1)S(1)}, u32[]{:S(2)}, u32[]{:S(2)}) collective-permute-start(bf16[32,3584]{1,0:T(8,128)(2,1)S(1)} %collective-permute-done.11.refs_13_.refs_14_), channel_id=1, source_target_pairs={{0,2},{4,0},{8,4},{12,8},{14,12},{10,14},{6,10},{2,6},{1,3},{5,1},... | collective-permute-start | bytes 688136 | tf_op jit(solution)/shard_map/ppermute | solution.py:243
  52.3 1.6 %collective-permute-start.27 = (bf16[32,3584]{1,0:T(8,128)(2,1)}, bf16[32,3584]{1,0:T(8,128)(2,1)S(1)}, u32[]{:S(2)}, u32[]{:S(2)}) collective-permute-start(bf16[32,3584]{1,0:T(8,128)(2,1)} %collective-permute-done.26.refs_14_), channel_id=1, source_target_pairs={{0,2},{4,0},{8,4},{12,8},{14,12},{10,14},{6,10},{2,6},{1,3},{5,1},... | collective-permute-start | bytes 688136 | tf_op jit(solution)/shard_map/ppermute | solution.py:243
  54.0 3.2 %collective-permute-done.16.refs_3_ = bf16[32,3584]{1,0:T(8,128)(2,1)} collective-permute-done((bf16[32,3584]{1,0:T(8,128)(2,1)S(1)}, bf16[32,3584]{1,0:T(8,128)(2,1)}, u32[]{:S(2)}, u32[]{:S(2)}) %collective-permute-start.16) | collective-permute-done | bytes 229408 | tf_op jit(solution)/shard_map/ppermute | solution.py:243
  57.7 1.9 %collective-permute-start.6 = (bf16[32,3584]{1,0:T(8,128)(2,1)}, bf16[32,3584]{1,0:T(8,128)(2,1)S(1)}, u32[]{:S(2)}, u32[]{:S(2)}) collective-permute-start(bf16[32,3584]{1,0:T(8,128)(2,1)} %collective-permute-done.5.refs_6_.refs_7_), channel_id=1, source_target_pairs={{0,2},{4,0},{8,4},{12,8},{14,12},{10,14},{6,10},{2,6},{1,3},{5,1},... | collective-permute-start | bytes 688136 | tf_op jit(solution)/shard_map/ppermute | solution.py:243
  59.6 2.4 %collective-permute-done.2.refs_3_.refs_4_ = bf16[32,3584]{1,0:T(8,128)(2,1)S(1)} collective-permute-done((bf16[32,3584]{1,0:T(8,128)(2,1)S(1)}, bf16[32,3584]{1,0:T(8,128)(2,1)S(1)}, u32[]{:S(2)}, u32[]{:S(2)}) %collective-permute-start.2) | collective-permute-done | bytes 229408 | tf_op jit(solution)/shard_map/ppermute | solution.py:243
  62.2 1.9 %collective-permute-start.3 = (bf16[32,3584]{1,0:T(8,128)(2,1)S(1)}, bf16[32,3584]{1,0:T(8,128)(2,1)S(1)}, u32[]{:S(2)}, u32[]{:S(2)}) collective-permute-start(bf16[32,3584]{1,0:T(8,128)(2,1)S(1)} %collective-permute-done.2.refs_3_.refs_4_), channel_id=1, source_target_pairs={{0,4},{4,8},{8,12},{12,14},{14,10},{10,6},{6,2},{2,0},{1,5},{5,9},... | collective-permute-start | bytes 688136 | tf_op jit(solution)/shard_map/ppermute | solution.py:243
  65.0 2.0 %collective-permute-start.13 = (bf16[32,3584]{1,0:T(8,128)(2,1)S(1)}, bf16[32,3584]{1,0:T(8,128)(2,1)S(1)}, u32[]{:S(2)}, u32[]{:S(2)}) collective-permute-start(bf16[32,3584]{1,0:T(8,128)(2,1)S(1)} %collective-permute-done.12.refs_14_.refs_15_), channel_id=1, source_target_pairs={{0,2},{4,0},{8,4},{12,8},{14,12},{10,14},{6,10},{2,6},{1,3},{5,1},... | collective-permute-start | bytes 688136 | tf_op jit(solution)/shard_map/ppermute | solution.py:243
  67.7 4.9 %all-to-all-start = ((bf16[8,128,512]{2,1,0:T(8,128)(2,1)}), bf16[8,128,512]{2,1,0:T(8,128)(2,1)S(1)}, u32[]{:S(2)}, u32[]{:S(2)}) async-start(bf16[8,128,512]{2,1,0:T(8,128)(2,1)} %tie.3), calls=%async_computation | async-start | bytes 2097152 | tf_op jit(solution)/shard_map/all_to_all | solution.py:248
  73.5 9.6 %first_chunks.1 = (f32[256,512]{1,0:T(8,128)S(1)}, f32[256,512]{1,0:T(8,128)S(1)}, f32[128,256]{1,0:T(8,128)S(1)}) custom-call(s32[18]{0:T(128)S(1)} %dynamic-slice_bitcast_fusion.scalars, bf16[32,3584]{1,0:T(8,128)(2,1)} %copy-done.16, bf16[32,3584]{1,0:T(8,128)(2,1)} %copy-done.20, bf16[32,3584]{1,0:T(8,128)(2,1)} %copy-done.23, ...), custom_call_target="tpu_custom_call" | custom-call | flops 8455716864 | bytes 22544384 | tf_op jit(solution)/shard_map/first_chunks/pallas_call | solution.py:146
  83.1 5.0 %last_narrow.1 = f32[128,256]{1,0:T(8,128)S(1)} custom-call(s32[18]{0:T(128)S(1)} %dynamic-slice_bitcast_fusion.scalars, bf16[32,3584]{1,0:T(8,128)(2,1)} %copy-done.8, bf16[32,3584]{1,0:T(8,128)(2,1)} %copy-done.10, bf16[32,3584]{1,0:T(8,128)(2,1)} %copy-done.13, bf16[32,3584]{1,0:T(8,128)(2,1)S(1)} %collective-permute-done.2.refs_3_.refs_4_, ...), custom_call_target="tpu_custom_call" | custom-call | flops 939524096 | bytes 5767168 | tf_op jit(solution)/shard_map/last_narrow/pallas_call | solution.py:146
  88.3 2.1 %collective-permute-start.29 = (f32[64,256]{1,0:T(8,128)S(1)}, f32[64,256]{1,0:T(8,128)S(1)}, u32[]{:S(2)}, u32[]{:S(2)}) collective-permute-start(f32[64,256]{1,0:T(8,128)S(1)} %fusion.refs_0_), channel_id=1, source_target_pairs={{0,2},{1,3},{2,0},{3,1},{4,6},{5,7},{6,4},{7,5},{8,10},{9,11},{10,... | collective-permute-start | bytes 196616 | tf_op jit(solution)/shard_map/ppermute | solution.py:267
  90.4 5.8 %last_sent.1.refs_0_ = f32[256,512]{1,0:T(8,128)S(1)} custom-call(s32[18]{0:T(128)S(1)} %dynamic-slice_bitcast_fusion.scalars, f32[64,256]{1,0:T(8,128)S(1)} %fusion.refs_0_, bf16[32,3584]{1,0:T(8,128)(2,1)} %copy-done.8, bf16[32,3584]{1,0:T(8,128)(2,1)} %copy-done.10, bf16[32,3584]{1,0:T(8,128)(2,1)} %copy-done.13, ...), custom_call_target="tpu_custom_call" | custom-call | flops 3758096384 | bytes 12058624 | tf_op jit(solution)/shard_map/last_sent/pallas_call | solution.py:146
  96.8 3.3 %collective-permute-start.33 = (bf16[64,256]{1,0:T(8,128)(2,1)S(1)}, bf16[64,256]{1,0:T(8,128)(2,1)S(1)}, u32[]{:S(2)}, u32[]{:S(2)}) collective-permute-start(bf16[64,256]{1,0:T(8,128)(2,1)S(1)} %add_convert_fusion), channel_id=1, source_target_pairs={{0,12},{2,14},{4,0},{6,2},{8,4},{10,6},{12,8},{14,10},{1,13},{3,15... | collective-permute-start | bytes 98312 | tf_op jit(solution)/shard_map/ppermute | solution.py:271
  101.3 5.8 %last_kept.1.kept = f32[256,512]{1,0:T(8,128)S(1)} custom-call(s32[18]{0:T(128)S(1)} %dynamic-slice_bitcast_fusion.scalars, f32[256,512]{1,0:T(8,128)S(1)} %last_sent.1.refs_0_, bf16[32,3584]{1,0:T(8,128)(2,1)} %copy-done.8, bf16[32,3584]{1,0:T(8,128)(2,1)} %copy-done.10, bf16[32,3584]{1,0:T(8,128)(2,1)} %copy-done.13, ...), custom_call_target="tpu_custom_call" | custom-call | flops 3758096384 | bytes 12058624 | tf_op jit(solution)/shard_map/last_kept/pallas_call | solution.py:146
  (108 shorter events, 21.8 us)
Async XLA Ops:
  1.4 12.7 %collective-permute-start.24 = (bf16[32,3584]{1,0:T(8,128)(2,1)S(1)}, bf16[32,3584]{1,0:T(8,128)(2,1)S(1)}, u32[]{:S(2)}, u32[]{:S(2)}) collective-permute-start(bf16[32,3584]{1,0:T(8,128)(2,1)S(1)} %get-tuple-element.15.refs_8_), channel_id=1, source_target_pairs={{0,2},{4,0},{8,4},{12,8},{14,12},{10,14},{6,10},{2,6},{1,3},{5,1},... | collective-permute-start | bytes 688136 | tf_op jit(solution)/shard_map/ppermute | solution.py:243
  4.4 9.9 %collective-permute-start.21 = (bf16[32,3584]{1,0:T(8,128)(2,1)S(1)}, bf16[32,3584]{1,0:T(8,128)(2,1)S(1)}, u32[]{:S(2)}, u32[]{:S(2)}) collective-permute-start(bf16[32,3584]{1,0:T(8,128)(2,1)S(1)} %get-tuple-element.15.refs_8_), channel_id=1, source_target_pairs={{0,4},{4,8},{8,12},{12,14},{14,10},{10,6},{6,2},{2,0},{1,5},{5,9},... | collective-permute-start | bytes 688136 | tf_op jit(solution)/shard_map/ppermute | solution.py:243
  4.5 11.7 %collective-permute-start.18 = (bf16[32,3584]{1,0:T(8,128)(2,1)S(1)}, bf16[32,3584]{1,0:T(8,128)(2,1)S(1)}, u32[]{:S(2)}, u32[]{:S(2)}) collective-permute-start(bf16[32,3584]{1,0:T(8,128)(2,1)S(1)} %get-tuple-element.18.refs_0_), channel_id=1, source_target_pairs={{0,2},{4,0},{8,4},{12,8},{14,12},{10,14},{6,10},{2,6},{1,3},{5,1},... | collective-permute-start | bytes 688136 | tf_op jit(solution)/shard_map/ppermute | solution.py:243
  6.4 11.4 %collective-permute-start.14 = (bf16[32,3584]{1,0:T(8,128)(2,1)S(1)}, bf16[32,3584]{1,0:T(8,128)(2,1)S(1)}, u32[]{:S(2)}, u32[]{:S(2)}) collective-permute-start(bf16[32,3584]{1,0:T(8,128)(2,1)S(1)} %get-tuple-element.18.refs_0_), channel_id=1, source_target_pairs={{0,4},{4,8},{8,12},{12,14},{14,10},{10,6},{6,2},{2,0},{1,5},{5,9},... | collective-permute-start | bytes 688136 | tf_op jit(solution)/shard_map/ppermute | solution.py:243
  6.6 14.2 %collective-permute-start.4 = (bf16[32,3584]{1,0:T(8,128)(2,1)S(1)}, bf16[32,3584]{1,0:T(8,128)(2,1)S(1)}, u32[]{:S(2)}, u32[]{:S(2)}) collective-permute-start(bf16[32,3584]{1,0:T(8,128)(2,1)S(1)} %get-tuple-element.17.refs_0_.refs_1_), channel_id=1, source_target_pairs={{0,2},{4,0},{8,4},{12,8},{14,12},{10,14},{6,10},{2,6},{1,3},{5,1},... | collective-permute-start | bytes 688136 | tf_op jit(solution)/shard_map/ppermute | solution.py:243
  14.1 8.7 %collective-permute-start = (bf16[32,3584]{1,0:T(8,128)(2,1)S(1)}, bf16[32,3584]{1,0:T(8,128)(2,1)S(1)}, u32[]{:S(2)}, u32[]{:S(2)}) collective-permute-start(bf16[32,3584]{1,0:T(8,128)(2,1)S(1)} %get-tuple-element.17.refs_0_.refs_1_), channel_id=1, source_target_pairs={{0,4},{4,8},{8,12},{12,14},{14,10},{10,6},{6,2},{2,0},{1,5},{5,9},... | collective-permute-start | bytes 688136 | tf_op jit(solution)/shard_map/ppermute | solution.py:243
  14.3 11.4 %collective-permute-start.10 = (bf16[32,3584]{1,0:T(8,128)(2,1)S(1)}, bf16[32,3584]{1,0:T(8,128)(2,1)S(1)}, u32[]{:S(2)}, u32[]{:S(2)}) collective-permute-start(bf16[32,3584]{1,0:T(8,128)(2,1)S(1)} %tie.2.refs_8_.refs_9_), channel_id=1, source_target_pairs={{0,2},{4,0},{8,4},{12,8},{14,12},{10,14},{6,10},{2,6},{1,3},{5,1},... | collective-permute-start | bytes 688136 | tf_op jit(solution)/shard_map/ppermute | solution.py:243
  16.3 11.5 %collective-permute-start.7 = (bf16[32,3584]{1,0:T(8,128)(2,1)S(1)}, bf16[32,3584]{1,0:T(8,128)(2,1)S(1)}, u32[]{:S(2)}, u32[]{:S(2)}) collective-permute-start(bf16[32,3584]{1,0:T(8,128)(2,1)S(1)} %tie.2.refs_8_.refs_9_), channel_id=1, source_target_pairs={{0,4},{4,8},{8,12},{12,14},{14,10},{10,6},{6,2},{2,0},{1,5},{5,9},... | collective-permute-start | bytes 688136 | tf_op jit(solution)/shard_map/ppermute | solution.py:243
  17.9 12.7 %collective-permute-start.25 = (bf16[32,3584]{1,0:T(8,128)(2,1)S(1)}, bf16[32,3584]{1,0:T(8,128)(2,1)S(1)}, u32[]{:S(2)}, u32[]{:S(2)}) collective-permute-start(bf16[32,3584]{1,0:T(8,128)(2,1)S(1)} %collective-permute-done.24.refs_12_), channel_id=1, source_target_pairs={{0,2},{4,0},{8,4},{12,8},{14,12},{10,14},{6,10},{2,6},{1,3},{5,1},... | collective-permute-start | bytes 688136 | tf_op jit(solution)/shard_map/ppermute | solution.py:243
  20.7 11.9 %collective-permute-start.22 = (bf16[32,3584]{1,0:T(8,128)(2,1)S(1)}, bf16[32,3584]{1,0:T(8,128)(2,1)S(1)}, u32[]{:S(2)}, u32[]{:S(2)}) collective-permute-start(bf16[32,3584]{1,0:T(8,128)(2,1)S(1)} %collective-permute-done.21.refs_9_), channel_id=1, source_target_pairs={{0,4},{4,8},{8,12},{12,14},{14,10},{10,6},{6,2},{2,0},{1,5},{5,9},... | collective-permute-start | bytes 688136 | tf_op jit(solution)/shard_map/ppermute | solution.py:243
  22.8 12.8 %collective-permute-start.19 = (bf16[32,3584]{1,0:T(8,128)(2,1)S(1)}, bf16[32,3584]{1,0:T(8,128)(2,1)}, u32[]{:S(2)}, u32[]{:S(2)}) collective-permute-start(bf16[32,3584]{1,0:T(8,128)(2,1)S(1)} %collective-permute-done.18.refs_5_), channel_id=1, source_target_pairs={{0,2},{4,0},{8,4},{12,8},{14,12},{10,14},{6,10},{2,6},{1,3},{5,1},... | collective-permute-start | bytes 688136 | tf_op jit(solution)/shard_map/ppermute | solution.py:243
  25.7 12.0 %collective-permute-start.15 = (bf16[32,3584]{1,0:T(8,128)(2,1)S(1)}, bf16[32,3584]{1,0:T(8,128)(2,1)S(1)}, u32[]{:S(2)}, u32[]{:S(2)}) collective-permute-start(bf16[32,3584]{1,0:T(8,128)(2,1)S(1)} %collective-permute-done.14.refs_1_), channel_id=1, source_target_pairs={{0,4},{4,8},{8,12},{12,14},{14,10},{10,6},{6,2},{2,0},{1,5},{5,9},... | collective-permute-start | bytes 688136 | tf_op jit(solution)/shard_map/ppermute | solution.py:243
  27.7 12.8 %collective-permute-start.5 = (bf16[32,3584]{1,0:T(8,128)(2,1)S(1)}, bf16[32,3584]{1,0:T(8,128)(2,1)}, u32[]{:S(2)}, u32[]{:S(2)}) collective-permute-start(bf16[32,3584]{1,0:T(8,128)(2,1)S(1)} %collective-permute-done.4.refs_5_.refs_6_), channel_id=1, source_target_pairs={{0,2},{4,0},{8,4},{12,8},{14,12},{10,14},{6,10},{2,6},{1,3},{5,1},... | collective-permute-start | bytes 688136 | tf_op jit(solution)/shard_map/ppermute | solution.py:243
  30.6 12.0 %collective-permute-start.1 = (bf16[32,3584]{1,0:T(8,128)(2,1)S(1)}, bf16[32,3584]{1,0:T(8,128)(2,1)S(1)}, u32[]{:S(2)}, u32[]{:S(2)}) collective-permute-start(bf16[32,3584]{1,0:T(8,128)(2,1)S(1)} %collective-permute-done.refs_1_.refs_2_), channel_id=1, source_target_pairs={{0,4},{4,8},{8,12},{12,14},{14,10},{10,6},{6,2},{2,0},{1,5},{5,9},... | collective-permute-start | bytes 688136 | tf_op jit(solution)/shard_map/ppermute | solution.py:243
  32.6 12.7 %collective-permute-start.11 = (bf16[32,3584]{1,0:T(8,128)(2,1)S(1)}, bf16[32,3584]{1,0:T(8,128)(2,1)S(1)}, u32[]{:S(2)}, u32[]{:S(2)}) collective-permute-start(bf16[32,3584]{1,0:T(8,128)(2,1)S(1)} %collective-permute-done.10.refs_12_.refs_13_), channel_id=1, source_target_pairs={{0,2},{4,0},{8,4},{12,8},{14,12},{10,14},{6,10},{2,6},{1,3},{5,1},... | collective-permute-start | bytes 688136 | tf_op jit(solution)/shard_map/ppermute | solution.py:243
  35.6 11.8 %collective-permute-start.8 = (bf16[32,3584]{1,0:T(8,128)(2,1)S(1)}, bf16[32,3584]{1,0:T(8,128)(2,1)}, u32[]{:S(2)}, u32[]{:S(2)}) collective-permute-start(bf16[32,3584]{1,0:T(8,128)(2,1)S(1)} %collective-permute-done.7.refs_9_.refs_10_), channel_id=1, source_target_pairs={{0,4},{4,8},{8,12},{12,14},{14,10},{10,6},{6,2},{2,0},{1,5},{5,9},... | collective-permute-start | bytes 688136 | tf_op jit(solution)/shard_map/ppermute | solution.py:243
  37.7 12.7 %collective-permute-start.26 = (bf16[32,3584]{1,0:T(8,128)(2,1)S(1)}, bf16[32,3584]{1,0:T(8,128)(2,1)}, u32[]{:S(2)}, u32[]{:S(2)}) collective-permute-start(bf16[32,3584]{1,0:T(8,128)(2,1)S(1)} %collective-permute-done.25.refs_13_), channel_id=1, source_target_pairs={{0,2},{4,0},{8,4},{12,8},{14,12},{10,14},{6,10},{2,6},{1,3},{5,1},... | collective-permute-start | bytes 688136 | tf_op jit(solution)/shard_map/ppermute | solution.py:243
  40.5 11.8 %collective-permute-start.23 = (bf16[32,3584]{1,0:T(8,128)(2,1)S(1)}, bf16[32,3584]{1,0:T(8,128)(2,1)S(1)}, u32[]{:S(2)}, u32[]{:S(2)}) collective-permute-start(bf16[32,3584]{1,0:T(8,128)(2,1)S(1)} %collective-permute-done.22.refs_10_), channel_id=1, source_target_pairs={{0,4},{4,8},{8,12},{12,14},{14,10},{10,6},{6,2},{2,0},{1,5},{5,9},... | collective-permute-start | bytes 688136 | tf_op jit(solution)/shard_map/ppermute | solution.py:243
  42.6 14.6 %collective-permute-start.16 = (bf16[32,3584]{1,0:T(8,128)(2,1)S(1)}, bf16[32,3584]{1,0:T(8,128)(2,1)}, u32[]{:S(2)}, u32[]{:S(2)}) collective-permute-start(bf16[32,3584]{1,0:T(8,128)(2,1)S(1)} %collective-permute-done.15.refs_2_), channel_id=1, source_target_pairs={{0,4},{4,8},{8,12},{12,14},{14,10},{10,6},{6,2},{2,0},{1,5},{5,9},... | collective-permute-start | bytes 688136 | tf_op jit(solution)/shard_map/ppermute | solution.py:243
  45.3 12.3 %collective-permute-start.20 = (bf16[32,3584]{1,0:T(8,128)(2,1)}, bf16[32,3584]{1,0:T(8,128)(2,1)S(1)}, u32[]{:S(2)}, u32[]{:S(2)}) collective-permute-start(bf16[32,3584]{1,0:T(8,128)(2,1)} %collective-permute-done.19.refs_6_), channel_id=1, source_target_pairs={{0,2},{4,0},{8,4},{12,8},{14,12},{10,14},{6,10},{2,6},{1,3},{5,1},... | collective-permute-start | bytes 688136 | tf_op jit(solution)/shard_map/ppermute | solution.py:243
  47.4 14.6 %collective-permute-start.2 = (bf16[32,3584]{1,0:T(8,128)(2,1)S(1)}, bf16[32,3584]{1,0:T(8,128)(2,1)S(1)}, u32[]{:S(2)}, u32[]{:S(2)}) collective-permute-start(bf16[32,3584]{1,0:T(8,128)(2,1)S(1)} %collective-permute-done.1.refs_2_.refs_3_), channel_id=1, source_target_pairs={{0,4},{4,8},{8,12},{12,14},{14,10},{10,6},{6,2},{2,0},{1,5},{5,9},... | collective-permute-start | bytes 688136 | tf_op jit(solution)/shard_map/ppermute | solution.py:243
  50.3 11.9 %collective-permute-start.12 = (bf16[32,3584]{1,0:T(8,128)(2,1)S(1)}, bf16[32,3584]{1,0:T(8,128)(2,1)S(1)}, u32[]{:S(2)}, u32[]{:S(2)}) collective-permute-start(bf16[32,3584]{1,0:T(8,128)(2,1)S(1)} %collective-permute-done.11.refs_13_.refs_14_), channel_id=1, source_target_pairs={{0,2},{4,0},{8,4},{12,8},{14,12},{10,14},{6,10},{2,6},{1,3},{5,1},... | collective-permute-start | bytes 688136 | tf_op jit(solution)/shard_map/ppermute | solution.py:243
  52.3 12.6 %collective-permute-start.27 = (bf16[32,3584]{1,0:T(8,128)(2,1)}, bf16[32,3584]{1,0:T(8,128)(2,1)S(1)}, u32[]{:S(2)}, u32[]{:S(2)}) collective-permute-start(bf16[32,3584]{1,0:T(8,128)(2,1)} %collective-permute-done.26.refs_14_), channel_id=1, source_target_pairs={{0,2},{4,0},{8,4},{12,8},{14,12},{10,14},{6,10},{2,6},{1,3},{5,1},... | collective-permute-start | bytes 688136 | tf_op jit(solution)/shard_map/ppermute | solution.py:243
  57.2 9.8 %collective-permute-start.17 = (bf16[32,3584]{1,0:T(8,128)(2,1)}, bf16[32,3584]{1,0:T(8,128)(2,1)S(1)}, u32[]{:S(2)}, u32[]{:S(2)}) collective-permute-start(bf16[32,3584]{1,0:T(8,128)(2,1)} %collective-permute-done.16.refs_3_), channel_id=1, source_target_pairs={{0,4},{4,8},{8,12},{12,14},{14,10},{10,6},{6,2},{2,0},{1,5},{5,9},... | collective-permute-start | bytes 688136 | tf_op jit(solution)/shard_map/ppermute | solution.py:243
  57.7 25.5 %collective-permute-start.6 = (bf16[32,3584]{1,0:T(8,128)(2,1)}, bf16[32,3584]{1,0:T(8,128)(2,1)S(1)}, u32[]{:S(2)}, u32[]{:S(2)}) collective-permute-start(bf16[32,3584]{1,0:T(8,128)(2,1)} %collective-permute-done.5.refs_6_.refs_7_), channel_id=1, source_target_pairs={{0,2},{4,0},{8,4},{12,8},{14,12},{10,14},{6,10},{2,6},{1,3},{5,1},... | collective-permute-start | bytes 688136 | tf_op jit(solution)/shard_map/ppermute | solution.py:243
  62.0 21.1 %collective-permute-start.9 = (bf16[32,3584]{1,0:T(8,128)(2,1)}, bf16[32,3584]{1,0:T(8,128)(2,1)S(1)}, u32[]{:S(2)}, u32[]{:S(2)}) collective-permute-start(bf16[32,3584]{1,0:T(8,128)(2,1)} %collective-permute-done.8.refs_10_.refs_11_), channel_id=1, source_target_pairs={{0,4},{4,8},{8,12},{12,14},{14,10},{10,6},{6,2},{2,0},{1,5},{5,9},... | collective-permute-start | bytes 688136 | tf_op jit(solution)/shard_map/ppermute | solution.py:243
  62.2 20.9 %collective-permute-start.3 = (bf16[32,3584]{1,0:T(8,128)(2,1)S(1)}, bf16[32,3584]{1,0:T(8,128)(2,1)S(1)}, u32[]{:S(2)}, u32[]{:S(2)}) collective-permute-start(bf16[32,3584]{1,0:T(8,128)(2,1)S(1)} %collective-permute-done.2.refs_3_.refs_4_), channel_id=1, source_target_pairs={{0,4},{4,8},{8,12},{12,14},{14,10},{10,6},{6,2},{2,0},{1,5},{5,9},... | collective-permute-start | bytes 688136 | tf_op jit(solution)/shard_map/ppermute | solution.py:243
  65.0 18.2 %collective-permute-start.13 = (bf16[32,3584]{1,0:T(8,128)(2,1)S(1)}, bf16[32,3584]{1,0:T(8,128)(2,1)S(1)}, u32[]{:S(2)}, u32[]{:S(2)}) collective-permute-start(bf16[32,3584]{1,0:T(8,128)(2,1)S(1)} %collective-permute-done.12.refs_14_.refs_15_), channel_id=1, source_target_pairs={{0,2},{4,0},{8,4},{12,8},{14,12},{10,14},{6,10},{2,6},{1,3},{5,1},... | collective-permute-start | bytes 688136 | tf_op jit(solution)/shard_map/ppermute | solution.py:243
  67.7 40.3 %all-to-all-start = ((bf16[8,128,512]{2,1,0:T(8,128)(2,1)}), bf16[8,128,512]{2,1,0:T(8,128)(2,1)S(1)}, u32[]{:S(2)}, u32[]{:S(2)}) async-start(bf16[8,128,512]{2,1,0:T(8,128)(2,1)} %tie.3), calls=%async_computation | async-start | bytes 2097152 | tf_op jit(solution)/shard_map/all_to_all | solution.py:248
  88.2 8.6 %collective-permute-start.30 = (f32[64,256]{1,0:T(8,128)S(1)}, f32[64,256]{1,0:T(8,128)S(1)}, u32[]{:S(2)}, u32[]{:S(2)}) collective-permute-start(f32[64,256]{1,0:T(8,128)S(1)} %fusion.refs_0_), channel_id=1, source_target_pairs={{0,3},{1,2},{2,1},{3,0},{4,7},{5,6},{6,5},{7,4},{8,11},{9,10},{10,... | collective-permute-start | bytes 196616 | tf_op jit(solution)/shard_map/ppermute | solution.py:267
  96.2 11.0 %collective-permute-start.34 = (f32[256,512]{1,0:T(8,128)S(1)}, f32[256,512]{1,0:T(8,128)S(1)}, u32[]{:S(2)}, u32[]{:S(2)}) collective-permute-start(f32[256,512]{1,0:T(8,128)S(1)} %last_sent.1.refs_0_), channel_id=1, source_target_pairs={{0,1},{1,0},{2,3},{3,2},{4,5},{5,4},{6,7},{7,6},{8,9},{9,8},{10,11... | collective-permute-start | bytes 1572872 | tf_op jit(solution)/shard_map/ppermute | solution.py:272
  96.8 10.3 %collective-permute-start.33 = (bf16[64,256]{1,0:T(8,128)(2,1)S(1)}, bf16[64,256]{1,0:T(8,128)(2,1)S(1)}, u32[]{:S(2)}, u32[]{:S(2)}) collective-permute-start(bf16[64,256]{1,0:T(8,128)(2,1)S(1)} %add_convert_fusion), channel_id=1, source_target_pairs={{0,12},{2,14},{4,0},{6,2},{8,4},{10,6},{12,8},{14,10},{1,13},{3,15... | collective-permute-start | bytes 98312 | tf_op jit(solution)/shard_map/ppermute | solution.py:271
  (30 other events, 742.8 us)
